TPU v7x, 32 devices: a whole 2x2x4 slice. The times are simulated.
32 devices in a mesh: layer: 2 (over y), blk: 4 (over z), tok: 2 (over x), rep: 2 (over core).
Axes of the slice: x: 2, y: 2, z: 4, core: 2. Of those that a mesh axis runs over, the one named last changes fastest.
Arguments:
- tokens: bfloat16 [1024, 8192], P(('layer', 'tok', 'rep'), 'blk'), parts along dimension 0, may hold values from -6 to 6
- teacher: bfloat16 [16384, 14336], P(('layer', 'blk'), ('tok', 'rep')), parts along dimension 0, may hold values from -0.0625 to 0.0625
- left_blocks: bfloat16 [128, 8192], P(('layer', 'blk')), parts along dimension 0, may hold values from -0.5 to 0.5
- right_blocks: bfloat16 [128, 14336], P(('layer', 'blk')), parts along dimension 0, may hold values from -0.75 to 0.75
Outputs:
- grad_left: float32 [128, 8192], P(('layer', 'blk'), ('tok', 'rep')), parts along dimension 0
- grad_right: float32 [128, 14336], P(('layer', 'blk'), ('tok', 'rep')), parts along dimension 0
There are 2 independent parts, one for each index of `layer`. A program takes and returns all parts, laid end to end along the dimension named above; each array names one. Nothing has to cross between parts.
All inputs are finite; a program needn't handle non-finite values.
Results may differ from a plain program's by a relative error of at most 0.009.
Values may be sent and summed in bfloat16 or wider, within the bound.
No kernel may reach another device: no remote copies, remote signals or barrier semaphores. Data moves between devices by JAX's collectives and lax.ppermute only.
A program may use at most 64 MiB of HBM per device.

v0:
```python
import jax
import jax.numpy as jnp
from jax import lax
from jax.sharding import PartitionSpec as P

D = 8192
F = 14336
NB = 64


def per_device(tokens, teacher, left_blocks, right_blocks):
    tok_dev = tokens.shape[0]
    block_in = D // NB
    block_out = F // NB
    local_blocks = left_blocks.shape[0]
    n_tok = lax.axis_size("tok")
    n_rep = lax.axis_size("rep")
    x_blocks = tokens.reshape(tok_dev, local_blocks, block_in)
    right = right_blocks.reshape(local_blocks, NB, block_out)
    partials = jnp.dot(
        lax.all_gather(tokens, ("tok", "rep"), axis=0, tiled=True),
        teacher,
        preferred_element_type=jnp.float32,
    ).astype(jnp.bfloat16)
    rows_full = lax.all_to_all(partials, ("tok", "rep"), split_axis=0, concat_axis=1, tiled=True)
    rows_full = lax.optimization_barrier(rows_full)
    target = lax.psum_scatter(
        rows_full.astype(jnp.float32).astype(jnp.bfloat16), "blk", scatter_dimension=1, tiled=True
    ).astype(jnp.float32)
    left = left_blocks.reshape(local_blocks, block_in, NB)
    hidden = jnp.einsum("tbj,bjk->bkt", x_blocks, left, preferred_element_type=jnp.float32).astype(
        jnp.bfloat16
    )
    permuted = lax.all_to_all(hidden, "blk", split_axis=1, concat_axis=0, tiled=True)
    student = jnp.einsum("bkt,kbo->tko", permuted, right, preferred_element_type=jnp.float32)
    permuted, student = (permuted, student)
    scale = float(tok_dev * n_tok * n_rep) ** (-0.5)
    target_blocks = target.reshape(tok_dev, local_blocks, block_out)
    grad_out = ((student - target_blocks) * scale).astype(jnp.bfloat16)
    right_term = jnp.einsum("bkt,tko->kbo", permuted, grad_out, preferred_element_type=jnp.float32)
    grad_right = lax.psum_scatter(
        right_term.reshape(local_blocks, NB * block_out).astype(jnp.bfloat16),
        ("tok", "rep"),
        scatter_dimension=1,
        tiled=True,
    ).astype(jnp.float32)
    back = jnp.einsum("tko,kbo->bkt", grad_out, right, preferred_element_type=jnp.float32).astype(
        jnp.bfloat16
    )
    returned = lax.all_to_all(back, "blk", split_axis=0, concat_axis=1, tiled=True)
    left_term = jnp.einsum("tbj,bkt->bjk", x_blocks, returned, preferred_element_type=jnp.float32)
    grad_left = lax.psum_scatter(
        left_term.reshape(local_blocks, block_in * NB).astype(jnp.bfloat16),
        ("tok", "rep"),
        scatter_dimension=1,
        tiled=True,
    ).astype(jnp.float32)
    return (grad_left, grad_right)


def solution(mesh):
    return jax.shard_map(
        per_device,
        mesh=mesh,
        in_specs=(
            P(("layer", "tok", "rep"), "blk"),
            P(("layer", "blk"), ("tok", "rep")),
            P(("layer", "blk"), None),
            P(("layer", "blk"), None),
        ),
        out_specs=(P(("layer", "blk"), ("tok", "rep")), P(("layer", "blk"), ("tok", "rep"))),
        check_vma=False,
    )
```

profile of v0, /device:TPU:0, one launch (start us, length us, event | category | flops | bytes accessed | tf_op | source)
XLA Modules:
  0.0 239.5 jit_solution(15720977778453289763)
XLA Ops:
  7.2 0.7 all-gather.2.cloned.1.call-update
  7.9 26.9 %all-gather.2.cloned.1.call-done = bf16[512,2048]{1,0:T(8,128)(2,1)} async-done(((bf16[128,2048]{1,0:T(8,128)(2,1)}), bf16[512,2048]{1,0:T(8,128)(2,1)}) %all-gather.2.cloned.1.call-update) | async-done | bytes 2097168 | tf_op jit(solution)/shard_map/all_gather | solution.py:21
  34.9 11.7 %convolution_convert_fusion = bf16[512,3584]{1,0:T(8,128)(2,1)S(1)} fusion(bf16[512,2048]{1,0:T(8,128)(2,1)} %all-gather.2.cloned.1.call-done, bf16[2048,3584]{1,0:T(8,128)(2,1)} %param.5), kind=kOutput, calls=%fused_computation | convolution fusion | flops 7518027776 | bytes 20447232 | tf_op jit(solution)/shard_map/dot_general | solution.py:20
  46.6 45.9 %all_to_all.55 = bf16[4,128,3584]{2,1,0:T(8,128)(2,1)} all-to-all(bf16[4,128,3584]{2,1,0:T(8,128)(2,1)S(1)} %bitcast.43), channel_id=1, replica_groups=mesh['layer'=2,'blk'=4,'tok'=2,'rep'=2] {'tok','rep'}, dimensions={0} | all-to-all | bytes 7340032 | tf_op jit(solution)/shard_map/all_to_all | solution.py:25
  92.6 6.0 %copy.23 = bf16[128,4,3584]{0,2,1:T(8,128)(2,1)} copy(bf16[128,4,3584]{2,0,1:T(8,128)(2,1)} %bitcast.42) | data formatting | bytes 7340032 | tf_op jit(solution)/shard_map/all_to_all | solution.py:25
  98.6 0.9 copy-done.2
  99.5 0.5 reshape.26
  100.0 0.5 convolution_convert_fusion.4
  100.5 0.9 copy.21
  101.4 4.6 %all-to-all-start = ((bf16[16,64,128]{2,0,1:T(8,128)(2,1)}), bf16[16,64,128]{2,0,1:T(8,128)(2,1)S(1)}, u32[]{:S(2)}, u32[]{:S(2)}) async-start(bf16[16,64,128]{2,0,1:T(8,128)(2,1)} %copy.21), calls=%async_computation | async-start | bytes 524288 | tf_op jit(solution)/shard_map/all_to_all | solution.py:34
  106.0 0.7 reshape.28
  106.8 15.0 %all-to-all-done = bf16[16,64,128]{2,0,1:T(8,128)(2,1)S(1)} async-done(((bf16[16,64,128]{2,0,1:T(8,128)(2,1)}), bf16[16,64,128]{2,0,1:T(8,128)(2,1)S(1)}, u32[]{:S(2)}, u32[]{:S(2)}) %all-to-all-start) | async-done | bytes 262176 | tf_op jit(solution)/shard_map/all_to_all | solution.py:34
  121.8 49.6 %reduce-scatter.4.cloned.1.call-done = bf16[128,3584]{0,1:T(8,128)(2,1)} async-done(((bf16[128,14336]{0,1:T(8,128)(2,1)}), bf16[128,3584]{0,1:T(8,128)(2,1)}) %reduce-scatter.4.cloned.1.call-update) | async-done | bytes 917520 | tf_op jit(solution)/shard_map/reduce_scatter | solution.py:27
  171.3 1.7 fusion.1
  173.0 0.4 fusion.3
  173.6 12.9 %all_to_all.56 = bf16[64,16,128]{2,1,0:T(8,128)(2,1)S(1)} all-to-all(bf16[64,16,128]{2,1,0:T(8,128)(2,1)S(1)} %copy.24), channel_id=1, replica_groups=mesh['layer'=2,'blk'=4,'tok'=2,'rep'=2] {'blk'}, dimensions={0} | all-to-all | bytes 524288 | tf_op jit(solution)/shard_map/all_to_all | solution.py:50
  186.9 0.3 copy.27
  187.2 1.2 convert_element_type.46
  188.4 0.7 convolution_convert_fusion.1
  189.1 1.6 convert_element_type.49
  190.7 16.8 %reduce-scatter.6.cloned.1.call-done = bf16[16,2048]{1,0:T(8,128)(2,1)} async-done(((bf16[16,8192]{1,0:T(8,128)(2,1)}), bf16[16,2048]{1,0:T(8,128)(2,1)}) %reduce-scatter.6.cloned.1.call-update) | async-done | bytes 65552 | tf_op jit(solution)/shard_map/reduce_scatter | solution.py:52
  207.6 1.5 convert_element_type.47
  209.1 22.3 %reduce-scatter.8.cloned.1.call-done = bf16[16,3584]{1,0:T(8,128)(2,1)} async-done(((bf16[16,14336]{1,0:T(8,128)(2,1)}), bf16[16,3584]{1,0:T(8,128)(2,1)}) %reduce-scatter.8.cloned.1.call-update) | async-done | bytes 114704 | tf_op jit(solution)/shard_map/reduce_scatter | solution.py:41
  231.4 1.6 convert_element_type.50
  (16 shorter events, 0.7 us)
Async XLA Ops:
  7.2 27.7 %all-gather.2.cloned.1.call-start = ((), (), s32[]{:S(2)}) async-start(), calls=%async_computation.6 | async-start | bytes 2621440 | tf_op jit(solution)/shard_map/all_gather | solution.py:21
  7.9 163.4 %reduce-scatter.4.cloned.1.call-start = ((), (), s32[]{:S(2)}) async-start(), calls=%async_computation.7 | async-start | bytes 4587520 | tf_op jit(solution)/shard_map/reduce_scatter | solution.py:27
  98.5 0.9 copy-start.2
  98.5 1.5 copy-start
  98.5 7.5 %copy-start.1 = (bf16[16,14336]{1,0:T(8,128)(2,1)S(1)}, bf16[16,14336]{1,0:T(8,128)(2,1)}, u32[]{:S(2)}) copy-start(bf16[16,14336]{1,0:T(8,128)(2,1)} %param.7) | copy-start | bytes 1376260
  101.4 20.3 %all-to-all-start = ((bf16[16,64,128]{2,0,1:T(8,128)(2,1)}), bf16[16,64,128]{2,0,1:T(8,128)(2,1)S(1)}, u32[]{:S(2)}, u32[]{:S(2)}) async-start(bf16[16,64,128]{2,0,1:T(8,128)(2,1)} %copy.21), calls=%async_computation | async-start | bytes 524288 | tf_op jit(solution)/shard_map/all_to_all | solution.py:34
  106.0 101.6 %reduce-scatter.6.cloned.1.call-start = ((), (), s32[]{:S(2)}) async-start(), calls=%async_computation.8 | async-start | bytes 327680 | tf_op jit(solution)/shard_map/reduce_scatter | solution.py:52
  188.4 43.0 %reduce-scatter.8.cloned.1.call-start = ((), (), s32[]{:S(2)}) async-start(), calls=%async_computation.9 | async-start | bytes 573440 | tf_op jit(solution)/shard_map/reduce_scatter | solution.py:41
Sparse Core Ops, SparseCore 0:
  9.6 25.2 all-gather.1
  98.7 72.5 reduce-scatter.3
  188.5 19.0 reduce-scatter.5
  210.1 21.2 reduce-scatter.7
where the time goes:
time: 240 us; the launch traced here: 239 us
  waiting for transfers between devices  131 us (55%)
  blocking collectives  58.9 us (25%)
  matrix products  15.3 us (6%)
  between operations  13.8 us (6%)
  local copies, waits for them, and re-layouts  12.4 us (5%)
  starting transfers between devices  4.71 us (2%)
  other arithmetic  3.1 us (1%)
    reduce_scatter x1, waiting for transfers between devices, per_device(): lax.psum_scatter(rows_full.astype(jnp.float32).astype(jnp.bfloat16), 'blk...  49.6 us
    all_to_all x1, blocking collectives, per_device(): lax.all_to_all(partials, ('tok', 'rep'), split_axis=0, concat_axis=1, til...  45.9 us
    all_gather x1, waiting for transfers between devices, per_device(): lax.all_gather(tokens, ('tok', 'rep'), axis=0, tiled=True)  26.9 us
    reduce_scatter x1, waiting for transfers between devices, per_device(): lax.psum_scatter(right_term.reshape(local_blocks, NB * block_out).astype(...  22.3 us
    reduce_scatter x1, waiting for transfers between devices, per_device(): lax.psum_scatter(left_term.reshape(local_blocks, block_in * NB).astype(jn...  16.8 us
    all_to_all x1, waiting for transfers between devices, per_device(): lax.all_to_all(hidden, 'blk', split_axis=1, concat_axis=0, tiled=True)  15 us
    all_to_all x1, blocking collectives, per_device(): lax.all_to_all(back, 'blk', split_axis=0, concat_axis=1, tiled=True)  12.9 us
    dot_general x1, matrix products, per_device(): jnp.dot(lax.all_gather(tokens, ('tok', 'rep'), axis=0, tiled=True), teach...  11.7 us
  transfers between devices with their start and end apart: 5, of which 5 were waited for; matrix products, arithmetic and copies ran while one was open for 3% of the time, Pallas kernels for 0%

commit v1 on v0

v1 whole, which is shorter than its diff:
```python
import functools

import jax
import jax.numpy as jnp
from jax import lax
from jax.experimental import pallas as pl
from jax.experimental.pallas import tpu as pltpu
from jax.sharding import PartitionSpec as P

D = 8192
F = 14336
NB = 64
BI = D // NB
FB = F // NB
GROUP = 4
COLS = GROUP * FB
BF = jnp.bfloat16
F32 = jnp.float32
NT = (((1,), (1,)), ((), ()))
TN = (((0,), (0,)), ((), ()))


def residual_kernel(scale, z_ref, tok_ref, teacher_ref, hid_ref, own_ref, right_ref, resid_ref, back_ref):
    target = jnp.dot(tok_ref[...], teacher_ref[...], preferred_element_type=F32)
    student = lax.dot_general(hid_ref[...], own_ref[0, 0], TN, preferred_element_type=F32)
    resid = ((student - target) * scale).astype(BF)
    resid_ref[...] = resid
    n_z, rows, _ = right_ref.shape[1:]
    right = right_ref[0].reshape(n_z * rows, COLS)
    back = lax.dot_general(right, resid, NT, preferred_element_type=F32)
    back_ref[...] = back.astype(BF).reshape(back_ref.shape)


def residual(z, tokens, teacher, hidden, right, scale):
    t, depth = tokens.shape
    n_q, n_z, rows, _ = right.shape
    cols = teacher.shape[1]
    return pl.pallas_call(
        functools.partial(residual_kernel, scale),
        grid_spec=pltpu.PrefetchScalarGridSpec(
            num_scalar_prefetch=1,
            grid=(n_q,),
            in_specs=[
                pl.BlockSpec((t, depth), lambda q, z: (0, 0)),
                pl.BlockSpec((depth, COLS), lambda q, z: (0, q)),
                pl.BlockSpec((rows, t), lambda q, z: (q, 0)),
                pl.BlockSpec((1, 1, rows, COLS), lambda q, z: (q, z[0], 0, 0)),
                pl.BlockSpec((1, n_z, rows, COLS), lambda q, z: (q, 0, 0, 0)),
            ],
            out_specs=[
                pl.BlockSpec((t, COLS), lambda q, z: (0, q)),
                pl.BlockSpec((n_z, rows, t), lambda q, z: (0, q, 0)),
            ],
        ),
        out_shape=[
            jax.ShapeDtypeStruct((t, cols), BF),
            jax.ShapeDtypeStruct((n_z, n_q * rows, t), BF),
        ],
        compiler_params=pltpu.CompilerParams(vmem_limit_bytes=40 * 1024 * 1024),
        cost_estimate=pl.CostEstimate(
            flops=2 * t * cols * (depth + 256), bytes_accessed=2 * depth * cols, transcendentals=0
        ),
        name="residual",
    )(z, tokens, teacher, hidden, right, right)


def grad_right_kernel(hid_ref, resid_ref, out_ref):
    n_z, rows, t = hid_ref.shape
    per_z = rows // GROUP
    prod = jnp.dot(hid_ref[...].reshape(n_z * rows, t), resid_ref[...], preferred_element_type=F32)
    prod = prod.reshape(n_z, GROUP, per_z, COLS)
    block = lax.broadcasted_iota(jnp.int32, (n_z, per_z, COLS), 2) // FB
    total = prod[:, 0]
    for k in range(1, GROUP):
        total = jnp.where(block == k, prod[:, k], total)
    out_ref[...] = total.astype(BF)


def grad_right_partial(hidden, resid):
    n_z, rows, t = hidden.shape
    cols = resid.shape[1]
    n_q = cols // COLS
    per_z = rows // (n_q * GROUP)
    return pl.pallas_call(
        grad_right_kernel,
        grid=(n_q,),
        in_specs=[
            pl.BlockSpec((n_z, rows // n_q, t), lambda q: (0, q, 0)),
            pl.BlockSpec((t, COLS), lambda q: (0, q)),
        ],
        out_specs=pl.BlockSpec((n_z, per_z, COLS), lambda q: (0, 0, q)),
        out_shape=jax.ShapeDtypeStruct((n_z, per_z, cols), BF),
        compiler_params=pltpu.CompilerParams(vmem_limit_bytes=40 * 1024 * 1024),
        cost_estimate=pl.CostEstimate(
            flops=2 * t * cols * 256, bytes_accessed=2 * t * cols, transcendentals=0
        ),
        name="grad_right",
    )(hidden, resid)


def per_device(tokens, teacher, left_blocks, right_blocks):
    n_z = lax.axis_size("blk")
    n_tok = lax.axis_size("tok")
    n_rep = lax.axis_size("rep")
    n_c = n_tok * n_rep
    z = lax.axis_index("blk")
    c = lax.axis_index(("tok", "rep"))
    tok_dev, depth = tokens.shape
    n_b = left_blocks.shape[0]
    n_k = teacher.shape[1] // FB
    n_q = n_k // GROUP
    scale = float(tok_dev * n_c) ** (-0.5)
    plane = ("blk", "tok", "rep")

    def swap(x, axis, s):
        n = lax.axis_size(axis)
        return lax.ppermute(x, axis, [(i, i ^ s) for i in range(n)])

    right_here = lax.ppermute(
        right_blocks, plane, [(a * n_c + b, b * n_c + a) for a in range(n_z) for b in range(n_c)]
    )

    chips = []
    for s in range(n_tok):
        own = tokens if s == 0 else swap(tokens, "tok", s)
        if n_rep == 1:
            chips.append(own)
        else:
            chips.append(jnp.concatenate([own] + [swap(own, "rep", r) for r in range(1, n_rep)], axis=0))

    left = left_blocks.reshape(n_b * BI, NB)
    rows_kb = n_k * n_b
    pick = (
        lax.broadcasted_iota(jnp.int32, (rows_kb, NB), 0) // n_b + c * n_k
        == lax.broadcasted_iota(jnp.int32, (rows_kb, NB), 1)
    ).astype(BF)
    diag = (
        lax.broadcasted_iota(jnp.int32, (rows_kb, n_b * BI), 0) % n_b
        == lax.broadcasted_iota(jnp.int32, (rows_kb, n_b * BI), 1) // BI
    )
    spread = lax.dot_general(pick, left, NT, preferred_element_type=F32)
    spread = jnp.where(diag, spread, 0.0).astype(BF)

    r = right_here.reshape(n_q, GROUP, n_z, n_b, FB).transpose(0, 2, 1, 3, 4)
    eye = jnp.eye(GROUP, dtype=BF)
    right_diag = (r[:, :, :, :, None, :] * eye[None, None, :, None, :, None]).reshape(
        n_q, n_z, GROUP * n_b, COLS
    )

    z_scalar = jnp.reshape(z, (1,)).astype(jnp.int32)
    hid_all, resids, backs = [], [], []
    for x in chips:
        hid = lax.dot_general(spread, x, NT, preferred_element_type=F32).astype(BF)
        hid_all.append([hid] + [swap(hid, "blk", s) for s in range(1, n_z)])
        resid, back = residual(z_scalar, x, teacher, hid, right_diag, scale)
        resids.append(resid)
        total = None
        for s in range(n_z):
            piece = lax.dynamic_index_in_dim(back, z ^ s, 0, keepdims=False)
            if s:
                piece = swap(piece, "blk", s)
            piece = piece.astype(F32)
            total = piece if total is None else total + piece
        backs.append(total.astype(BF))

    x_all = jnp.concatenate(chips, axis=0)
    back_all = jnp.concatenate(backs, axis=1)
    prod = jnp.dot(back_all, x_all, preferred_element_type=F32)
    gl = jnp.where(diag, prod, 0.0).reshape(n_k, n_b, n_b * BI).sum(1).astype(BF)
    gl = gl.reshape(n_k, n_b, n_c, BI // n_c).transpose(2, 1, 3, 0)
    got = []
    for s in range(n_c):
        piece = lax.dynamic_index_in_dim(gl, c ^ s, 0, keepdims=False)
        if s:
            piece = lax.ppermute(piece, ("tok", "rep"), [(i, i ^ s) for i in range(n_c)])
        got.append(piece)
    got = jnp.stack(got, 0)
    order = jnp.arange(n_c) ^ c
    grad_left = jnp.take(got, order, axis=0).transpose(1, 2, 0, 3).reshape(n_b, -1).astype(F32)

    hid_cat = jnp.stack(
        [jnp.concatenate([h[s] for h in hid_all], axis=1) for s in range(n_z)], axis=0
    )
    gr = grad_right_partial(hid_cat, jnp.concatenate(resids, axis=0))
    total = None
    for s in range(n_z):
        perm = [(a * n_c + b, b * n_c + (a ^ s)) for a in range(n_z) for b in range(n_c)]
        piece = lax.ppermute(gr[s], plane, perm).astype(F32)
        total = piece if total is None else total + piece
    grad_right = total.reshape(n_b, n_k, FB).transpose(1, 0, 2).reshape(n_k, n_b * FB)
    return grad_left, grad_right


def solution(mesh):
    return jax.shard_map(
        per_device,
        mesh=mesh,
        in_specs=(
            P(("layer", "tok", "rep"), "blk"),
            P(("layer", "blk"), ("tok", "rep")),
            P(("layer", "blk"), None),
            P(("layer", "blk"), None),
        ),
        out_specs=(P(("layer", "blk"), ("tok", "rep")), P(("layer", "blk"), ("tok", "rep"))),
        check_vma=False,
    )
```

time: 240 us -> 125 us (0.52)
  the two profiles are of different devices: /device:TPU:0 before, /device:TPU:2 now
where the time goes in v1:
time: 125 us
  starting transfers between devices  40.9 us (33%)
  waiting for transfers between devices  38.8 us (31%)
  Pallas kernels  21.5 us (17%)
  local copies, waits for them, and re-layouts  13.2 us (11%)
  matrix products  4.65 us (4%)
  other arithmetic  4.41 us (4%)
    ppermute x15, starting transfers between devices, swap(): return lax.ppermute(x, axis, [(i, i ^ s) for i in range(n)])  23.7 us
    pallas_call x2, Pallas kernels, residual(): pl.pallas_call(functools.partial(residual_kernel, scale), grid_spec=pltpu...  19.3 us
    ppermute x1, waiting for transfers between devices, per_device(): lax.ppermute(right_blocks, plane, [(a * n_c + b, b * n_c + a) for a in ra...  17.8 us
    ppermute x4, waiting for transfers between devices, per_device(): piece = lax.ppermute(gr[s], plane, perm).astype(F32)  11.1 us
    ppermute x15, waiting for transfers between devices, swap(): return lax.ppermute(x, axis, [(i, i ^ s) for i in range(n)])  9.85 us
    ppermute x4, starting transfers between devices, per_device(): piece = lax.ppermute(gr[s], plane, perm).astype(F32)  9.03 us
    ppermute x1, starting transfers between devices, per_device(): lax.ppermute(right_blocks, plane, [(a * n_c + b, b * n_c + a) for a in ra...  5.85 us
    mul x4, local copies, waits for them, and re-layouts, per_device(): r[:, :, :, :, None, :] * eye[None, None, :, None, :, None]  3.85 us
  transfers between devices with their start and end apart: 23, of which 9 were waited for; matrix products, arithmetic and copies ran while one was open for 17% of the time, Pallas kernels for 17%

profile of v1, /device:TPU:2, one launch (start us, length us, event | category | flops | bytes accessed | tf_op | source)
XLA Modules:
  0.0 124.6 jit_solution(16621914545621490665)
XLA Ops:
  0.8 5.9 %collective-permute-start.1 = (bf16[16,14336]{1,0:T(8,128)(2,1)}, bf16[16,14336]{1,0:T(8,128)(2,1)S(1)}, u32[]{:S(2)}, u32[]{:S(2)}) collective-permute-start(bf16[16,14336]{1,0:T(8,128)(2,1)} %param.7), channel_id=1, source_target_pairs={{0,0},{1,4},{2,8},{3,12},{4,1},{5,5},{6,9},{7,13},{8,2},{9,6},{10,... | collective-permute-start | bytes 1376264 | tf_op jit(solution)/shard_map/ppermute | solution.py:119
  6.8 1.5 %reshape.66 = bf16[2048,64]{1,0:T(8,128)(2,1)S(1)} reshape(bf16[16,8192]{1,0:T(8,128)(2,1)} %param.6) | data formatting | bytes 524288 | tf_op jit(solution)/shard_map/reshape | solution.py:131
  8.6 1.5 %fusion = bf16[256,2048]{1,0:T(8,128)(2,1)} fusion(bf16[2048,64]{1,0:T(8,128)(2,1)S(1)} %reshape.66, s32[2048]{0:T(1024)S(1)} %get-tuple-element.26, s32[2048]{0:T(1024)S(1)} %get-tuple-element.27, s32[256]{0:T(256)S(1)} %get-tuple-element.29, s32[256]{0:T(256)S(1)} %get-tuple-element.30, pred[256]{0:T(512)(128)(4,1)S(1)} %get-tuple-element.25, ...), kind=kOutput, calls=%fused_computation.4 | convolution fusion | flops 69779456 | bytes 1333764 | tf_op jit(solution)/shard_map/dot_general | solution.py:141
  10.1 17.8 %collective-permute-done.1 = bf16[16,14336]{1,0:T(8,128)(2,1)S(1)} collective-permute-done((bf16[16,14336]{1,0:T(8,128)(2,1)}, bf16[16,14336]{1,0:T(8,128)(2,1)S(1)}, u32[]{:S(2)}, u32[]{:S(2)}) %collective-permute-start.1) | collective-permute-done | bytes 458784 | tf_op jit(solution)/shard_map/ppermute | solution.py:119
  29.8 2.5 %mul.29 = bf16[4,4,64,896]{3,2,1,0:T(8,128)(2,1)} reshape(bf16[4,4,4,16,4,224]{5,4,3,2,1,0:T(4,128)(2,1)S(1)} %mul.28) | data formatting | bytes 3670016 | tf_op jit(solution)/shard_map/mul | solution.py:146
  32.3 1.8 %broadcast_multiply_fusion.own_ref.right_ref = bf16[4,4,64,896]{3,2,1,0:T(8,128)(2,1)S(1)} fusion(bf16[4,4,64,896]{3,2,1,0:T(8,128)(2,1)} %mul.29, bf16[64,896]{1,0:T(8,128)(2,1)S(1)} %mul.31), kind=kLoop, calls=%fused_computation.17 | loop fusion | flops 917504 | bytes 3784704 | tf_op jit(solution)/shard_map/mul | solution.py:146
  35.8 9.6 %residual.2 = (bf16[256,3584]{1,0:T(8,128)(2,1)S(1)}, bf16[4,256,256]{2,1,0:T(8,128)(2,1)S(1)}) custom-call(s32[1]{0:T(128)} %bitcast.z_ref, bf16[256,2048]{1,0:T(8,128)(2,1)S(1)} %constant_dynamic-update-slice_fusion.tok_ref, bf16[2048,3584]{1,0:T(8,128)(2,1)} %teacher_ref.3, bf16[256,256]{1,0:T(8,128)(2,1)S(1)} %convolution_convert_fusion.1.hid_ref, ...), custom_call_target="tpu_custom_call" | custom-call | flops 4227858432 | bytes 14680064 | tf_op jit(solution)/shard_map/residual/pallas_call | solution.py:38
  45.6 3.9 %collective-permute-start.4 = (bf16[256,256]{1,0:T(8,128)(2,1)S(1)}, bf16[256,256]{1,0:T(8,128)(2,1)S(1)}, u32[]{:S(2)}, u32[]{:S(2)}) collective-permute-start(bf16[256,256]{1,0:T(8,128)(2,1)S(1)} %get-tuple-element.11), channel_id=1, source_target_pairs={{0,12},{4,8},{8,4},{12,0},{1,13},{5,9},{9,5},{13,1},{2,14},{6,10},... | collective-permute-start | bytes 393224 | tf_op jit(solution)/shard_map/ppermute | solution.py:117
  51.2 2.7 %collective-permute-done.4 = bf16[256,256]{1,0:T(8,128)(2,1)S(1)} collective-permute-done((bf16[256,256]{1,0:T(8,128)(2,1)S(1)}, bf16[256,256]{1,0:T(8,128)(2,1)S(1)}, u32[]{:S(2)}, u32[]{:S(2)}) %collective-permute-start.4) | collective-permute-done | bytes 131104 | tf_op jit(solution)/shard_map/ppermute | solution.py:117
  53.9 5.4 %collective-permute-start.15 = (bf16[256,256]{1,0:T(8,128)(2,1)S(1)}, bf16[256,256]{1,0:T(8,128)(2,1)S(1)}, u32[]{:S(2)}, u32[]{:S(2)}) collective-permute-start(bf16[256,256]{1,0:T(8,128)(2,1)S(1)} %convolution_convert_fusion.1.hid_ref), channel_id=1, source_target_pairs={{0,8},{4,12},{8,0},{12,4},{1,9},{5,13},{9,1},{13,5},{2,10},{6,14},... | collective-permute-start | bytes 393224 | tf_op jit(solution)/shard_map/ppermute | solution.py:117
  61.1 9.6 %residual.3 = (bf16[256,3584]{1,0:T(8,128)(2,1)S(1)}, bf16[4,256,256]{2,1,0:T(8,128)(2,1)S(1)}) custom-call(s32[1]{0:T(128)} %bitcast.z_ref, bf16[256,2048]{1,0:T(8,128)(2,1)S(1)} %constant_dynamic-update-slice_fusion.2.tok_ref, bf16[2048,3584]{1,0:T(8,128)(2,1)} %teacher_ref.3, bf16[256,256]{1,0:T(8,128)(2,1)S(1)} %convolution_convert_fusion.hid_ref, ...), custom_call_target="tpu_custom_call" | custom-call | flops 4227858432 | bytes 14680064 | tf_op jit(solution)/shard_map/residual/pallas_call | solution.py:38
  70.8 4.2 %collective-permute-start.9 = (bf16[256,256]{1,0:T(8,128)(2,1)S(1)}, bf16[256,256]{1,0:T(8,128)(2,1)S(1)}, u32[]{:S(2)}, u32[]{:S(2)}) collective-permute-start(bf16[256,256]{1,0:T(8,128)(2,1)S(1)} %get-tuple-element.14), channel_id=1, source_target_pairs={{0,12},{4,8},{8,4},{12,0},{1,13},{5,9},{9,5},{13,1},{2,14},{6,10},... | collective-permute-start | bytes 393224 | tf_op jit(solution)/shard_map/ppermute | solution.py:117
  75.6 2.0 %pad_maximum_fusion.resid_ref = bf16[512,3584]{1,0:T(8,128)(2,1)} fusion(bf16[256,3584]{1,0:T(8,128)(2,1)S(1)} %get-tuple-element.9, bf16[256,3584]{1,0:T(8,128)(2,1)S(1)} %get-tuple-element.8), kind=kLoop, calls=%fused_computation.1 | loop fusion | flops 7340032 | bytes 7340032 | tf_op jit(solution)/shard_map/concatenate | solution.py:184
  77.7 1.8 %collective-permute-done.9 = bf16[256,256]{1,0:T(8,128)(2,1)S(1)} collective-permute-done((bf16[256,256]{1,0:T(8,128)(2,1)S(1)}, bf16[256,256]{1,0:T(8,128)(2,1)S(1)}, u32[]{:S(2)}, u32[]{:S(2)}) %collective-permute-start.9) | collective-permute-done | bytes 131104 | tf_op jit(solution)/shard_map/ppermute | solution.py:117
  79.4 4.2 %collective-permute-start.13 = (bf16[256,256]{1,0:T(8,128)(2,1)S(1)}, bf16[256,256]{1,0:T(8,128)(2,1)S(1)}, u32[]{:S(2)}, u32[]{:S(2)}) collective-permute-start(bf16[256,256]{1,0:T(8,128)(2,1)S(1)} %convolution_convert_fusion.1.hid_ref), channel_id=1, source_target_pairs={{0,4},{4,0},{8,12},{12,8},{1,5},{5,1},{9,13},{13,9},{2,6},{6,2},{1... | collective-permute-start | bytes 393224 | tf_op jit(solution)/shard_map/ppermute | solution.py:117
  85.5 2.1 %bitcast_reduce_fusion = bf16[16,2048]{1,0:T(8,128)(2,1)S(1)} fusion(bf16[128,2048]{1,0:T(8,128)(2,1)S(1)} %collective-permute-done.6, bf16[128,2048]{1,0:T(8,128)(2,1)} %collective-permute-done.5, bf16[128,2048]{1,0:T(8,128)(2,1)} %collective-permute-done, bf16[128,2048]{1,0:T(8,128)(2,1)S(1)} %copy-done.3, s32[2048]{0:T(1024)S(1)} %get-tuple-element.26, ...), kind=kOutput, calls=%fused_computation.12 | convolution fusion | flops 548372480 | bytes 2445568 | tf_op jit(solution)/shard_map/dot_general | solution.py:168
  88.4 3.9 %collective-permute-start.14 = (bf16[256,256]{1,0:T(8,128)(2,1)S(1)}, bf16[256,256]{1,0:T(8,128)(2,1)S(1)}, u32[]{:S(2)}, u32[]{:S(2)}) collective-permute-start(bf16[256,256]{1,0:T(8,128)(2,1)S(1)} %convolution_convert_fusion.hid_ref), channel_id=1, source_target_pairs={{0,4},{4,0},{8,12},{12,8},{1,5},{5,1},{9,13},{13,9},{2,6},{6,2},{1... | collective-permute-start | bytes 393224 | tf_op jit(solution)/shard_map/ppermute | solution.py:117
  92.5 2.3 %collective-permute-start.11 = (bf16[16,32,16]{1,2,0:T(8,128)(2,1)S(1)}, bf16[16,32,16]{1,2,0:T(8,128)(2,1)S(1)}, u32[]{:S(2)}, u32[]{:S(2)}) collective-permute-start(bf16[16,32,16]{1,2,0:T(8,128)(2,1)S(1)} %bitcast.74), channel_id=1, source_target_pairs={{0,2},{1,3},{2,0},{3,1},{4,6},{5,7},{6,4},{7,5},{8,10},{9,11},{10,... | collective-permute-start | bytes 49160 | tf_op jit(solution)/shard_map/ppermute | solution.py:175
  94.8 1.7 %collective-permute-done.16 = bf16[256,256]{1,0:T(8,128)(2,1)S(1)} collective-permute-done((bf16[256,256]{1,0:T(8,128)(2,1)S(1)}, bf16[256,256]{1,0:T(8,128)(2,1)S(1)}, u32[]{:S(2)}, u32[]{:S(2)}) %collective-permute-start.16) | collective-permute-done | bytes 131104 | tf_op jit(solution)/shard_map/ppermute | solution.py:117
  98.0 2.2 %grad_right.1 = bf16[4,16,3584]{2,1,0:T(8,128)(2,1)S(1)} custom-call(bf16[4,256,512]{2,1,0:T(8,128)(2,1)S(1)} %pad_maximum_fusion.1.hid_ref, bf16[512,3584]{1,0:T(8,128)(2,1)S(1)} %copy-done), custom_call_target="tpu_custom_call" | custom-call | flops 939524096 | bytes 3670016 | tf_op jit(solution)/shard_map/grad_right/pallas_call | solution.py:84
  101.3 3.2 %collective-permute-start.20 = (bf16[16,3584]{1,0:T(8,128)(2,1)S(1)}, bf16[16,3584]{1,0:T(8,128)(2,1)S(1)}, u32[]{:S(2)}, u32[]{:S(2)}) collective-permute-start(bf16[16,3584]{1,0:T(8,128)(2,1)S(1)} %get-tuple-element.19), channel_id=1, source_target_pairs={{0,1},{1,5},{2,9},{3,13},{4,0},{5,4},{6,8},{7,12},{8,3},{9,7},{10,... | collective-permute-start | bytes 344072 | tf_op jit(solution)/shard_map/ppermute | solution.py:188
  104.5 4.9 %collective-permute-start.19 = (bf16[16,3584]{1,0:T(8,128)(2,1)S(1)}, bf16[16,3584]{1,0:T(8,128)(2,1)S(1)}, u32[]{:S(2)}, u32[]{:S(2)}) collective-permute-start(bf16[16,3584]{1,0:T(8,128)(2,1)S(1)} %get-tuple-element.16), channel_id=1, source_target_pairs={{0,0},{1,4},{2,8},{3,12},{4,1},{5,5},{6,9},{7,13},{8,2},{9,6},{10,... | collective-permute-start | bytes 344072 | tf_op jit(solution)/shard_map/ppermute | solution.py:188
  110.6 1.6 %reshape.73 = f32[16,2048]{1,0:T(8,128)} reshape(f32[16,32,4,16]{3,2,1,0:T(4,128)S(1)} %copy.25) | data formatting | bytes 262144 | tf_op jit(solution)/shard_map/convert_element_type | solution.py:179
  112.4 10.9 %collective-permute-done.19 = bf16[16,3584]{1,0:T(8,128)(2,1)S(1)} collective-permute-done((bf16[16,3584]{1,0:T(8,128)(2,1)S(1)}, bf16[16,3584]{1,0:T(8,128)(2,1)S(1)}, u32[]{:S(2)}, u32[]{:S(2)}) %collective-permute-start.19) | collective-permute-done | bytes 114720 | tf_op jit(solution)/shard_map/ppermute | solution.py:188
  (84 shorter events, 16.4 us)
Async XLA Ops:
  0.6 44.8 %collective-permute-start.5 = (bf16[128,2048]{1,0:T(8,128)(2,1)}, bf16[128,2048]{1,0:T(8,128)(2,1)}, u32[]{:S(2)}, u32[]{:S(2)}) collective-permute-start(bf16[128,2048]{1,0:T(8,128)(2,1)} %param.4), channel_id=1, source_target_pairs={{0,2},{2,0},{1,3},{3,1},{4,6},{6,4},{5,7},{7,5},{8,10},{10,8},{9,1... | collective-permute-start | bytes 1572872 | tf_op jit(solution)/shard_map/ppermute | solution.py:117
  0.7 33.4 %collective-permute-start = (bf16[128,2048]{1,0:T(8,128)(2,1)}, bf16[128,2048]{1,0:T(8,128)(2,1)}, u32[]{:S(2)}, u32[]{:S(2)}) collective-permute-start(bf16[128,2048]{1,0:T(8,128)(2,1)} %param.4), channel_id=1, source_target_pairs={{0,1},{1,0},{2,3},{3,2},{4,5},{5,4},{6,7},{7,6},{8,9},{9,8},{10,11... | collective-permute-start | bytes 1572872 | tf_op jit(solution)/shard_map/ppermute | solution.py:117
  0.8 27.1 %collective-permute-start.1 = (bf16[16,14336]{1,0:T(8,128)(2,1)}, bf16[16,14336]{1,0:T(8,128)(2,1)S(1)}, u32[]{:S(2)}, u32[]{:S(2)}) collective-permute-start(bf16[16,14336]{1,0:T(8,128)(2,1)} %param.7), channel_id=1, source_target_pairs={{0,0},{1,4},{2,8},{3,12},{4,1},{5,5},{6,9},{7,13},{8,2},{9,6},{10,... | collective-permute-start | bytes 1376264 | tf_op jit(solution)/shard_map/ppermute | solution.py:119
  35.7 52.7 %collective-permute-start.17 = (bf16[256,256]{1,0:T(8,128)(2,1)S(1)}, bf16[256,256]{1,0:T(8,128)(2,1)S(1)}, u32[]{:S(2)}, u32[]{:S(2)}) collective-permute-start(bf16[256,256]{1,0:T(8,128)(2,1)S(1)} %convolution_convert_fusion.1.hid_ref), channel_id=1, source_target_pairs={{0,12},{4,8},{8,4},{12,0},{1,13},{5,9},{9,5},{13,1},{2,14},{6,10},... | collective-permute-start | bytes 393224 | tf_op jit(solution)/shard_map/ppermute | solution.py:117
  45.5 15.0 %collective-permute-start.6 = (bf16[128,2048]{1,0:T(8,128)(2,1)}, bf16[128,2048]{1,0:T(8,128)(2,1)S(1)}, u32[]{:S(2)}, u32[]{:S(2)}) collective-permute-start(bf16[128,2048]{1,0:T(8,128)(2,1)} %collective-permute-done.5), channel_id=1, source_target_pairs={{0,1},{1,0},{2,3},{3,2},{4,5},{5,4},{6,7},{7,6},{8,9},{9,8},{10,11... | collective-permute-start | bytes 1572872 | tf_op jit(solution)/shard_map/ppermute | solution.py:117
  45.6 8.3 %collective-permute-start.4 = (bf16[256,256]{1,0:T(8,128)(2,1)S(1)}, bf16[256,256]{1,0:T(8,128)(2,1)S(1)}, u32[]{:S(2)}, u32[]{:S(2)}) collective-permute-start(bf16[256,256]{1,0:T(8,128)(2,1)S(1)} %get-tuple-element.11), channel_id=1, source_target_pairs={{0,12},{4,8},{8,4},{12,0},{1,13},{5,9},{9,5},{13,1},{2,14},{6,10},... | collective-permute-start | bytes 393224 | tf_op jit(solution)/shard_map/ppermute | solution.py:117
  49.5 10.9 %collective-permute-start.3 = (bf16[256,256]{1,0:T(8,128)(2,1)S(1)}, bf16[256,256]{1,0:T(8,128)(2,1)S(1)}, u32[]{:S(2)}, u32[]{:S(2)}) collective-permute-start(bf16[256,256]{1,0:T(8,128)(2,1)S(1)} %get-tuple-element.12), channel_id=1, source_target_pairs={{0,8},{4,12},{8,0},{12,4},{1,9},{5,13},{9,1},{13,5},{2,10},{6,14},... | collective-permute-start | bytes 393224 | tf_op jit(solution)/shard_map/ppermute | solution.py:117
  49.5 10.9 %collective-permute-start.2 = (bf16[256,256]{1,0:T(8,128)(2,1)S(1)}, bf16[256,256]{1,0:T(8,128)(2,1)S(1)}, u32[]{:S(2)}, u32[]{:S(2)}) collective-permute-start(bf16[256,256]{1,0:T(8,128)(2,1)S(1)} %get-tuple-element.10), channel_id=1, source_target_pairs={{0,4},{4,0},{8,12},{12,8},{1,5},{5,1},{9,13},{13,9},{2,6},{6,2},{1... | collective-permute-start | bytes 393224 | tf_op jit(solution)/shard_map/ppermute | solution.py:117
  53.9 38.5 %collective-permute-start.15 = (bf16[256,256]{1,0:T(8,128)(2,1)S(1)}, bf16[256,256]{1,0:T(8,128)(2,1)S(1)}, u32[]{:S(2)}, u32[]{:S(2)}) collective-permute-start(bf16[256,256]{1,0:T(8,128)(2,1)S(1)} %convolution_convert_fusion.1.hid_ref), channel_id=1, source_target_pairs={{0,8},{4,12},{8,0},{12,4},{1,9},{5,13},{9,1},{13,5},{2,10},{6,14},... | collective-permute-start | bytes 393224 | tf_op jit(solution)/shard_map/ppermute | solution.py:117
  70.8 8.7 %collective-permute-start.9 = (bf16[256,256]{1,0:T(8,128)(2,1)S(1)}, bf16[256,256]{1,0:T(8,128)(2,1)S(1)}, u32[]{:S(2)}, u32[]{:S(2)}) collective-permute-start(bf16[256,256]{1,0:T(8,128)(2,1)S(1)} %get-tuple-element.14), channel_id=1, source_target_pairs={{0,12},{4,8},{8,4},{12,0},{1,13},{5,9},{9,5},{13,1},{2,14},{6,10},... | collective-permute-start | bytes 393224 | tf_op jit(solution)/shard_map/ppermute | solution.py:117
  75.0 9.9 %collective-permute-start.8 = (bf16[256,256]{1,0:T(8,128)(2,1)S(1)}, bf16[256,256]{1,0:T(8,128)(2,1)S(1)}, u32[]{:S(2)}, u32[]{:S(2)}) collective-permute-start(bf16[256,256]{1,0:T(8,128)(2,1)S(1)} %get-tuple-element.15), channel_id=1, source_target_pairs={{0,8},{4,12},{8,0},{12,4},{1,9},{5,13},{9,1},{13,5},{2,10},{6,14},... | collective-permute-start | bytes 393224 | tf_op jit(solution)/shard_map/ppermute | solution.py:117
  75.0 10.5 %collective-permute-start.7 = (bf16[256,256]{1,0:T(8,128)(2,1)S(1)}, bf16[256,256]{1,0:T(8,128)(2,1)S(1)}, u32[]{:S(2)}, u32[]{:S(2)}) collective-permute-start(bf16[256,256]{1,0:T(8,128)(2,1)S(1)} %get-tuple-element.13), channel_id=1, source_target_pairs={{0,4},{4,0},{8,12},{12,8},{1,5},{5,1},{9,13},{13,9},{2,6},{6,2},{1... | collective-permute-start | bytes 393224 | tf_op jit(solution)/shard_map/ppermute | solution.py:117
  75.6 9.9 %copy-start.3 = (bf16[128,2048]{1,0:T(8,128)(2,1)S(1)}, bf16[128,2048]{1,0:T(8,128)(2,1)}, u32[]{:S(2)}) copy-start(bf16[128,2048]{1,0:T(8,128)(2,1)} %param.4) | copy-start | bytes 1572868
  79.4 17.1 %collective-permute-start.13 = (bf16[256,256]{1,0:T(8,128)(2,1)S(1)}, bf16[256,256]{1,0:T(8,128)(2,1)S(1)}, u32[]{:S(2)}, u32[]{:S(2)}) collective-permute-start(bf16[256,256]{1,0:T(8,128)(2,1)S(1)} %convolution_convert_fusion.1.hid_ref), channel_id=1, source_target_pairs={{0,4},{4,0},{8,12},{12,8},{1,5},{5,1},{9,13},{13,9},{2,6},{6,2},{1... | collective-permute-start | bytes 393224 | tf_op jit(solution)/shard_map/ppermute | solution.py:117
  84.9 7.4 %collective-permute-start.18 = (bf16[256,256]{1,0:T(8,128)(2,1)S(1)}, bf16[256,256]{1,0:T(8,128)(2,1)S(1)}, u32[]{:S(2)}, u32[]{:S(2)}) collective-permute-start(bf16[256,256]{1,0:T(8,128)(2,1)S(1)} %convolution_convert_fusion.hid_ref), channel_id=1, source_target_pairs={{0,12},{4,8},{8,4},{12,0},{1,13},{5,9},{9,5},{13,1},{2,14},{6,10},... | collective-permute-start | bytes 393224 | tf_op jit(solution)/shard_map/ppermute | solution.py:117
  85.5 11.1 %collective-permute-start.16 = (bf16[256,256]{1,0:T(8,128)(2,1)S(1)}, bf16[256,256]{1,0:T(8,128)(2,1)S(1)}, u32[]{:S(2)}, u32[]{:S(2)}) collective-permute-start(bf16[256,256]{1,0:T(8,128)(2,1)S(1)} %convolution_convert_fusion.hid_ref), channel_id=1, source_target_pairs={{0,8},{4,12},{8,0},{12,4},{1,9},{5,13},{9,1},{13,5},{2,10},{6,14},... | collective-permute-start | bytes 393224 | tf_op jit(solution)/shard_map/ppermute | solution.py:117
  88.4 9.4 %collective-permute-start.14 = (bf16[256,256]{1,0:T(8,128)(2,1)S(1)}, bf16[256,256]{1,0:T(8,128)(2,1)S(1)}, u32[]{:S(2)}, u32[]{:S(2)}) collective-permute-start(bf16[256,256]{1,0:T(8,128)(2,1)S(1)} %convolution_convert_fusion.hid_ref), channel_id=1, source_target_pairs={{0,4},{4,0},{8,12},{12,8},{1,5},{5,1},{9,13},{13,9},{2,6},{6,2},{1... | collective-permute-start | bytes 393224 | tf_op jit(solution)/shard_map/ppermute | solution.py:117
  92.3 9.0 %collective-permute-start.12 = (bf16[16,32,16]{1,2,0:T(8,128)(2,1)S(1)}, bf16[16,32,16]{1,2,0:T(8,128)(2,1)S(1)}, u32[]{:S(2)}, u32[]{:S(2)}) collective-permute-start(bf16[16,32,16]{1,2,0:T(8,128)(2,1)S(1)} %bitcast.72), channel_id=1, source_target_pairs={{0,3},{1,2},{2,1},{3,0},{4,7},{5,6},{6,5},{7,4},{8,11},{9,10},{10,... | collective-permute-start | bytes 49160 | tf_op jit(solution)/shard_map/ppermute | solution.py:175
  92.5 12.0 %collective-permute-start.11 = (bf16[16,32,16]{1,2,0:T(8,128)(2,1)S(1)}, bf16[16,32,16]{1,2,0:T(8,128)(2,1)S(1)}, u32[]{:S(2)}, u32[]{:S(2)}) collective-permute-start(bf16[16,32,16]{1,2,0:T(8,128)(2,1)S(1)} %bitcast.74), channel_id=1, source_target_pairs={{0,2},{1,3},{2,0},{3,1},{4,6},{5,7},{6,4},{7,5},{8,10},{9,11},{10,... | collective-permute-start | bytes 49160 | tf_op jit(solution)/shard_map/ppermute | solution.py:175
  96.5 12.8 %collective-permute-start.10 = (bf16[16,32,16]{1,2,0:T(8,128)(2,1)S(1)}, bf16[16,32,16]{1,2,0:T(8,128)(2,1)S(1)}, u32[]{:S(2)}, u32[]{:S(2)}) collective-permute-start(bf16[16,32,16]{1,2,0:T(8,128)(2,1)S(1)} %bitcast.73), channel_id=1, source_target_pairs={{0,1},{1,0},{2,3},{3,2},{4,5},{5,4},{6,7},{7,6},{8,9},{9,8},{10,11... | collective-permute-start | bytes 49160 | tf_op jit(solution)/shard_map/ppermute | solution.py:175
  100.3 11.9 %collective-permute-start.22 = (bf16[16,3584]{1,0:T(8,128)(2,1)S(1)}, bf16[16,3584]{1,0:T(8,128)(2,1)S(1)}, u32[]{:S(2)}, u32[]{:S(2)}) collective-permute-start(bf16[16,3584]{1,0:T(8,128)(2,1)S(1)} %get-tuple-element.17), channel_id=1, source_target_pairs={{0,3},{1,7},{2,11},{3,15},{4,2},{5,6},{6,10},{7,14},{8,1},{9,5},{1... | collective-permute-start | bytes 344072 | tf_op jit(solution)/shard_map/ppermute | solution.py:188
  100.4 11.8 %collective-permute-start.21 = (bf16[16,3584]{1,0:T(8,128)(2,1)S(1)}, bf16[16,3584]{1,0:T(8,128)(2,1)S(1)}, u32[]{:S(2)}, u32[]{:S(2)}) collective-permute-start(bf16[16,3584]{1,0:T(8,128)(2,1)S(1)} %get-tuple-element.18), channel_id=1, source_target_pairs={{0,2},{1,6},{2,10},{3,14},{4,3},{5,7},{6,11},{7,15},{8,0},{9,4},{1... | collective-permute-start | bytes 344072 | tf_op jit(solution)/shard_map/ppermute | solution.py:188
  101.3 11.1 %collective-permute-start.20 = (bf16[16,3584]{1,0:T(8,128)(2,1)S(1)}, bf16[16,3584]{1,0:T(8,128)(2,1)S(1)}, u32[]{:S(2)}, u32[]{:S(2)}) collective-permute-start(bf16[16,3584]{1,0:T(8,128)(2,1)S(1)} %get-tuple-element.19), channel_id=1, source_target_pairs={{0,1},{1,5},{2,9},{3,13},{4,0},{5,4},{6,8},{7,12},{8,3},{9,7},{10,... | collective-permute-start | bytes 344072 | tf_op jit(solution)/shard_map/ppermute | solution.py:188
  104.5 18.8 %collective-permute-start.19 = (bf16[16,3584]{1,0:T(8,128)(2,1)S(1)}, bf16[16,3584]{1,0:T(8,128)(2,1)S(1)}, u32[]{:S(2)}, u32[]{:S(2)}) collective-permute-start(bf16[16,3584]{1,0:T(8,128)(2,1)S(1)} %get-tuple-element.16), channel_id=1, source_target_pairs={{0,0},{1,4},{2,8},{3,12},{4,1},{5,5},{6,9},{7,13},{8,2},{9,6},{10,... | collective-permute-start | bytes 344072 | tf_op jit(solution)/shard_map/ppermute | solution.py:188
  (3 other events, 14.0 us)

commit v2 on v0

v2 whole, which is shorter than its diff:
```python
import functools

import jax
import jax.numpy as jnp
from jax import lax
from jax.experimental import pallas as pl
from jax.experimental.pallas import tpu as pltpu
from jax.sharding import PartitionSpec as P

D = 8192
F = 14336
NB = 64
BI = D // NB
FB = F // NB
GROUP = 4
COLS = GROUP * FB
BF = jnp.bfloat16
F32 = jnp.float32
NT = (((1,), (1,)), ((), ()))
TN = (((0,), (0,)), ((), ()))
VMEM = 40 * 1024 * 1024


def cost(flops, nbytes):
    return pl.CostEstimate(flops=flops, bytes_accessed=nbytes, transcendentals=0)


def rows_of(refs):
    return jnp.concatenate([r[...] for r in refs], axis=0) if len(refs) > 1 else refs[0][...]


def target_kernel(*refs):
    *tok_refs, teacher_ref, out_ref = refs
    out_ref[...] = jnp.dot(rows_of(tok_refs), teacher_ref[...], preferred_element_type=F32).astype(BF)


def target(tokens, teacher):
    t, depth = tokens[0].shape
    cols = teacher.shape[1]
    block = 512 if cols % 512 == 0 else COLS
    total = t * len(tokens)
    return pl.pallas_call(
        target_kernel,
        grid=(cols // block,),
        in_specs=[pl.BlockSpec((t, depth), lambda q: (0, 0))] * len(tokens)
        + [pl.BlockSpec((depth, block), lambda q: (0, q))],
        out_specs=pl.BlockSpec((total, block), lambda q: (0, q)),
        out_shape=jax.ShapeDtypeStruct((total, cols), BF),
        compiler_params=pltpu.CompilerParams(vmem_limit_bytes=VMEM),
        cost_estimate=cost(2 * total * cols * depth, 2 * depth * cols),
        name="target",
    )(*tokens, teacher)


def spread_kernel(in_ref, out_ref):
    n_z, rows, _ = in_ref.shape
    tile = (
        lax.broadcasted_iota(jnp.int32, (FB, COLS), 0)
        == lax.broadcasted_iota(jnp.int32, (FB, COLS), 1) % FB
    )
    wide = jnp.dot(
        in_ref[...].reshape(n_z * rows, FB), tile.astype(F32).astype(BF), preferred_element_type=F32
    ).reshape(n_z, rows, COLS)
    shape = (n_z, rows, COLS)
    own = lax.broadcasted_iota(jnp.int32, shape, 1) // (rows // GROUP) == lax.broadcasted_iota(
        jnp.int32, shape, 2
    ) // FB
    out_ref[0] = jnp.where(own, wide, 0.0).astype(BF)


def spread_right(right, n_q):
    n_z, rows, _ = right.shape
    return pl.pallas_call(
        spread_kernel,
        grid=(n_q,),
        in_specs=[pl.BlockSpec((n_z, rows // n_q, FB), lambda q: (0, q, 0))],
        out_specs=pl.BlockSpec((1, n_z, rows // n_q, COLS), lambda q: (q, 0, 0, 0)),
        out_shape=jax.ShapeDtypeStruct((n_q, n_z, rows // n_q, COLS), BF),
        compiler_params=pltpu.CompilerParams(vmem_limit_bytes=VMEM),
        cost_estimate=cost(2 * n_z * rows * FB * COLS, 4 * n_z * rows * COLS),
        name="spread_right",
    )(right)


def project_kernel(scale, part_ref, hid_ref, right_ref, resid_ref, back_ref):
    n_z, rows, _ = right_ref.shape[1:]
    student = lax.dot_general(hid_ref[...], right_ref[0, 0], TN, preferred_element_type=F32)
    resid = ((student - part_ref[...].astype(F32)) * scale).astype(BF)
    resid_ref[...] = resid
    right = right_ref[0].reshape(n_z * rows, COLS)
    back = lax.dot_general(right, resid, NT, preferred_element_type=F32)
    back_ref[...] = back.astype(BF).reshape(back_ref.shape)


def project(part, hidden, right, scale):
    t, cols = part.shape
    n_q, n_z, rows, _ = right.shape
    return pl.pallas_call(
        functools.partial(project_kernel, scale),
        grid=(n_q,),
        in_specs=[
            pl.BlockSpec((t, COLS), lambda q: (0, q)),
            pl.BlockSpec((rows, t), lambda q: (q, 0)),
            pl.BlockSpec((1, n_z, rows, COLS), lambda q: (q, 0, 0, 0)),
        ],
        out_specs=[
            pl.BlockSpec((t, COLS), lambda q: (0, q)),
            pl.BlockSpec((n_z, rows, t), lambda q: (0, q, 0)),
        ],
        out_shape=[
            jax.ShapeDtypeStruct((t, cols), BF),
            jax.ShapeDtypeStruct((n_z, n_q * rows, t), BF),
        ],
        compiler_params=pltpu.CompilerParams(vmem_limit_bytes=VMEM),
        cost_estimate=cost(2 * t * cols * n_z * rows * 2, 6 * t * cols),
        name="project",
    )(part, hidden, right)


def grad_right_kernel(n_z, halves, *refs):
    hid_refs, resid_refs, out_ref = refs[: n_z * halves], refs[n_z * halves : -1], refs[-1]
    rows = hid_refs[0].shape[0]
    per_z = rows // GROUP
    prod = None
    for h in range(halves):
        hid = rows_of(hid_refs[h * n_z : (h + 1) * n_z])
        term = jnp.dot(hid, resid_refs[h][...], preferred_element_type=F32)
        prod = term if prod is None else prod + term
    prod = prod.reshape(n_z, GROUP, per_z, COLS)
    block = lax.broadcasted_iota(jnp.int32, (n_z, per_z, COLS), 2) // FB
    total = prod[:, 0]
    for k in range(1, GROUP):
        total = jnp.where(block == k, prod[:, k], total)
    out_ref[...] = total.astype(BF)


def grad_right_partial(hidden, resids):
    halves, n_z = len(hidden), len(hidden[0])
    rows, t = hidden[0][0].shape
    cols = resids[0].shape[1]
    n_q = cols // COLS
    per_z = rows // (n_q * GROUP)
    return pl.pallas_call(
        functools.partial(grad_right_kernel, n_z, halves),
        grid=(n_q,),
        in_specs=[pl.BlockSpec((rows // n_q, t), lambda q: (q, 0))] * (halves * n_z)
        + [pl.BlockSpec((t, COLS), lambda q: (0, q))] * halves,
        out_specs=pl.BlockSpec((n_z, per_z, COLS), lambda q: (0, 0, q)),
        out_shape=jax.ShapeDtypeStruct((n_z, per_z, cols), BF),
        compiler_params=pltpu.CompilerParams(vmem_limit_bytes=VMEM),
        cost_estimate=cost(2 * halves * t * cols * n_z * rows // n_q, 2 * halves * t * cols),
        name="grad_right",
    )(*[h for hs in hidden for h in hs], *resids)


def grad_left_kernel(n_z, halves, n_k, *refs):
    per = halves * n_z
    back_refs, tok_refs, out_ref = refs[:per], refs[per:-1], refs[-1]
    pieces = len(tok_refs) // halves
    prod = None
    for h in range(halves):
        total = back_refs[h * n_z][0].astype(F32)
        for s in range(1, n_z):
            total = total + back_refs[h * n_z + s][...].astype(F32)
        term = jnp.dot(
            total.astype(BF),
            rows_of(tok_refs[h * pieces : (h + 1) * pieces]),
            preferred_element_type=F32,
        )
        prod = term if prod is None else prod + term
    rows, block = prod.shape
    n_b = rows // n_k
    prod = prod.reshape(n_k, n_b, block)
    at = pl.program_id(0) * (block // BI)
    own = lax.broadcasted_iota(jnp.int32, prod.shape, 1) == at + lax.broadcasted_iota(
        jnp.int32, prod.shape, 2
    ) // BI
    out_ref[...] = jnp.where(own, prod, 0.0).sum(1).astype(BF)


def grad_left_of(backs, tokens, n_k):
    halves, n_z = len(backs), len(backs[0])
    rows, t = backs[0][1].shape
    piece, depth = tokens[0][0].shape
    block = min(depth, 1024)
    first = pl.BlockSpec((1, rows, t), lambda q: (0, 0, 0))
    rest = pl.BlockSpec((rows, t), lambda q: (0, 0))
    flat = [x for h in tokens for x in h]
    return pl.pallas_call(
        functools.partial(grad_left_kernel, n_z, halves, n_k),
        grid=(depth // block,),
        in_specs=([first] + [rest] * (n_z - 1)) * halves
        + [pl.BlockSpec((piece, block), lambda q: (0, q))] * len(flat),
        out_specs=pl.BlockSpec((n_k, block), lambda q: (0, q)),
        out_shape=jax.ShapeDtypeStruct((n_k, depth), BF),
        compiler_params=pltpu.CompilerParams(vmem_limit_bytes=VMEM),
        cost_estimate=cost(2 * halves * t * rows * depth, 2 * halves * t * depth),
        name="grad_left",
    )(*[b for h in backs for b in h], *flat)


def place_kernel(n_b, c_ref, *refs):
    in_refs, out_ref = refs[:-1], refs[-1]
    n_c, n_k = len(in_refs), in_refs[0].shape[0]
    x = rows_of(in_refs)
    row = lax.broadcasted_iota(jnp.int32, (NB, NB), 0)
    col = lax.broadcasted_iota(jnp.int32, (NB, NB), 1)
    pick = row == ((col // n_k) ^ c_ref[0]) * n_k + col % n_k
    got = lax.dot_general(
        x, pick.astype(F32).astype(BF), (((0,), (1,)), ((), ())), preferred_element_type=F32
    )
    for j in range(got.shape[0] // n_b):
        out_ref[:, j * NB : (j + 1) * NB] = got[j * n_b : (j + 1) * n_b]


def place(c, pieces, n_b):
    n = pieces[0].shape[1] // n_b
    return pl.pallas_call(
        functools.partial(place_kernel, n_b),
        in_specs=[pl.BlockSpec(memory_space=pltpu.SMEM)]
        + [pl.BlockSpec(memory_space=pltpu.VMEM)] * len(pieces),
        out_specs=pl.BlockSpec(memory_space=pltpu.VMEM),
        out_shape=jax.ShapeDtypeStruct((n_b, n * NB), F32),
        name="place",
    )(c, *pieces)


def swap(x, axes, s):
    n = lax.axis_size(axes)
    return lax.ppermute(x, axes, [(i, i ^ s) for i in range(n)])


def gather(x, axes):
    got = [x]
    for s in range(1, lax.axis_size(axes)):
        got.append(swap(got[s & (s - 1)], axes, s & -s))
    return got


def pick(x, at):
    return lax.dynamic_index_in_dim(x, at, 0, keepdims=False)


def per_device(tokens, teacher, left_blocks, right_blocks):
    n_z = lax.axis_size("blk")
    n_c = lax.axis_size(("tok", "rep"))
    n_rep = lax.axis_size("rep")
    z = lax.axis_index("blk")
    c = lax.axis_index(("tok", "rep"))
    plane = ("tok", "rep")
    n_b = left_blocks.shape[0]
    n_k = teacher.shape[1] // FB
    n_q = n_k // GROUP
    scale = float(tokens.shape[0] * n_c) ** (-0.5)

    chips = [[own] + [swap(own, "rep", r) for r in range(1, n_rep)] for own in gather(tokens, "tok")]

    share = n_b * FB
    quarter = lax.dynamic_slice_in_dim(right_blocks, c * share, share, 1)
    quarters = jnp.stack(gather(quarter, "blk"), 0)
    here = []
    for s in range(n_c):
        piece = pick(quarters, z ^ c ^ s)
        here.append(swap(piece, plane, s) if s else piece)
    here = jnp.stack(here, 0)
    right = jnp.stack([pick(here, c ^ z ^ s) for s in range(n_z)], 0)
    right = spread_right(right.reshape(n_z, n_k * n_b, FB), n_q)

    left = left_blocks.reshape(n_b * BI, NB)
    rows_kb = n_k * n_b
    take = (
        lax.broadcasted_iota(jnp.int32, (rows_kb, NB), 0) // n_b + c * n_k
        == lax.broadcasted_iota(jnp.int32, (rows_kb, NB), 1)
    ).astype(BF)
    diag = (
        lax.broadcasted_iota(jnp.int32, (rows_kb, n_b * BI), 0) % n_b
        == lax.broadcasted_iota(jnp.int32, (rows_kb, n_b * BI), 1) // BI
    )
    left = lax.dot_general(take, left, NT, preferred_element_type=F32)
    left = jnp.where(diag, left, 0.0).astype(BF)

    hidden, resids, backs = [], [], []
    for x in chips:
        hid = jnp.concatenate(
            [lax.dot_general(left, p, NT, preferred_element_type=F32).astype(BF) for p in x], axis=1
        )
        hidden.append(gather(hid, "blk"))
        resid, back = project(target(x, teacher), hid, right, scale)
        resids.append(resid)
        backs.append([back] + [swap(back[s], "blk", s) for s in range(1, n_z)])

    gl = grad_left_of(backs, chips, n_k)
    gl = gl.reshape(n_k, n_b, n_c, BI // n_c).transpose(2, 0, 3, 1).reshape(n_c, n_k, -1)
    got = []
    for s in range(n_c):
        piece = pick(gl, c ^ s)
        got.append(swap(piece, plane, s) if s else piece)
    grad_left = place(jnp.reshape(c, (1,)).astype(jnp.int32), got, n_b)

    gr = grad_right_partial(hidden, resids)
    there = []
    for s in range(n_c):
        piece = pick(gr, z ^ c ^ s)
        there.append(swap(piece, plane, s) if s else piece)
    there = jnp.stack(there, 0)
    total = None
    for s in range(n_z):
        piece = pick(there, c ^ z ^ s)
        piece = (swap(piece, "blk", s) if s else piece).astype(F32)
        total = piece if total is None else total + piece
    grad_right = total.reshape(n_b, n_k, FB).transpose(1, 0, 2).reshape(n_k, n_b * FB)
    return grad_left, grad_right


def solution(mesh):
    return jax.shard_map(
        per_device,
        mesh=mesh,
        in_specs=(
            P(("layer", "tok", "rep"), "blk"),
            P(("layer", "blk"), ("tok", "rep")),
            P(("layer", "blk"), None),
            P(("layer", "blk"), None),
        ),
        out_specs=(P(("layer", "blk"), ("tok", "rep")), P(("layer", "blk"), ("tok", "rep"))),
        check_vma=False,
    )
```

time: 240 us -> 108 us (0.45)
  waiting for transfers between devices: 131 us -> 18.5 us
  blocking collectives: 58.9 us -> 0 us
  starting transfers between devices: 4.71 us -> 37.5 us
  Pallas kernels: 0 us -> 31.9 us
  between operations: 13.8 us -> 1.03 us
  matrix products: 15.3 us -> 3.36 us
    reduce_scatter x3 -> x0, waiting for transfers between devices: 88.6 us -> none  [the longest x1 49.6 us: per_device(): lax.psum_scatter(rows_full.astype(jnp.float32).astype(jnp.bfloat16), 'blk...]
    all_to_all x2 -> x0, blocking collectives: 58.9 us -> none  [the longest x1 45.9 us: per_device(): lax.all_to_all(partials, ('tok', 'rep'), split_axis=0, concat_axis=1, til...]
    ppermute x0 -> x30, starting transfers between devices: none -> 37.5 us  [swap(): return lax.ppermute(x, axes, [(i, i ^ s) for i in range(n)])]
    pallas_call x0 -> x8, Pallas kernels: none -> 31.9 us  [the longest x2 18.7 us: target(): pl.pallas_call(target_kernel, grid=(cols // block,), in_specs=[pl.BlockSp...]
    all_gather x1 -> x0, waiting for transfers between devices: 26.9 us -> none  [per_device(): lax.all_gather(tokens, ('tok', 'rep'), axis=0, tiled=True)]
    ppermute x0 -> x30, waiting for transfers between devices: none -> 18.5 us  [swap(): return lax.ppermute(x, axes, [(i, i ^ s) for i in range(n)])]
    all_to_all x1 -> x0, waiting for transfers between devices: 15 us -> none  [per_device(): lax.all_to_all(hidden, 'blk', split_axis=1, concat_axis=0, tiled=True)]
    dot_general x6 -> x5, matrix products: 15.3 us -> 3.36 us  [the longest x4 1.73 us: per_device(): lax.dot_general(left, p, NT, preferred_element_type=F32).astype(BF)]
  transfers between devices with their start and end apart: 5 -> 30, of which waited for: 5 -> 9; matrix products, arithmetic and copies ran while one was open for 3% -> 10% of each run, Pallas kernels for 0% -> 30%
where the time goes in v2:
time: 108 us
  starting transfers between devices  37.5 us (35%)
  Pallas kernels  31.9 us (30%)
  waiting for transfers between devices  18.5 us (17%)
  local copies, waits for them, and re-layouts  12.6 us (12%)
  matrix products  3.36 us (3%)
  other arithmetic  2.56 us (2%)
    ppermute x30, starting transfers between devices, swap(): return lax.ppermute(x, axes, [(i, i ^ s) for i in range(n)])  37.5 us
    pallas_call x2, Pallas kernels, target(): pl.pallas_call(target_kernel, grid=(cols // block,), in_specs=[pl.BlockSp...  18.7 us
    ppermute x30, waiting for transfers between devices, swap(): return lax.ppermute(x, axes, [(i, i ^ s) for i in range(n)])  18.5 us
    pallas_call x2, Pallas kernels, project(): pl.pallas_call(functools.partial(project_kernel, scale), grid=(n_q,), in_...  5.87 us
    unnamed x22, local copies, waits for them, and re-layouts  4.22 us
    reshape x1, local copies, waits for them, and re-layouts, per_device(): left = left_blocks.reshape(n_b * BI, NB)  2.26 us
    pallas_call x1, Pallas kernels, grad_right_partial(): pl.pallas_call(functools.partial(grad_right_kernel, n_z, halves), grid=(n...  2.16 us
  transfers between devices with their start and end apart: 30, of which 9 were waited for; matrix products, arithmetic and copies ran while one was open for 10% of the time, Pallas kernels for 30%

profile of v2, /device:TPU:0, one launch (start us, length us, event | category | flops | bytes accessed | tf_op | source)
XLA Modules:
  0.0 107.5 jit_solution(12901580013397172907)
XLA Ops:
  2.3 4.0 %collective-permute-start.2 = (bf16[16,3584]{1,0:T(8,128)(2,1)}, bf16[16,3584]{1,0:T(8,128)(2,1)S(1)}, u32[]{:S(2)}, u32[]{:S(2)}) collective-permute-start(bf16[16,3584]{1,0:T(8,128)(2,1)} %constant_dynamic-slice_fusion.6), channel_id=1, source_target_pairs={{0,8},{4,12},{8,0},{12,4},{1,9},{5,13},{9,1},{13,5},{2,10},{6,14},... | collective-permute-start | bytes 344072 | tf_op jit(solution)/shard_map/ppermute | solution.py:230
  6.3 1.6 %collective-permute-start.1 = (bf16[16,3584]{1,0:T(8,128)(2,1)}, bf16[16,3584]{1,0:T(8,128)(2,1)S(1)}, u32[]{:S(2)}, u32[]{:S(2)}) collective-permute-start(bf16[16,3584]{1,0:T(8,128)(2,1)} %constant_dynamic-slice_fusion.6), channel_id=1, source_target_pairs={{0,4},{4,0},{8,12},{12,8},{1,5},{5,1},{9,13},{13,9},{2,6},{6,2},{1... | collective-permute-start | bytes 344072 | tf_op jit(solution)/shard_map/ppermute | solution.py:230
  10.6 2.3 %reshape.28 = bf16[2048,64]{1,0:T(8,128)(2,1)} reshape(bf16[16,8192]{1,0:T(8,128)(2,1)} %param.6) | data formatting | bytes 524288 | tf_op jit(solution)/shard_map/reshape | solution.py:269
  13.3 1.6 %fusion = bf16[256,2048]{1,0:T(8,128)(2,1)S(1)} fusion(bf16[2048,64]{1,0:T(8,128)(2,1)} %reshape.28, s32[2048]{0:T(1024)S(1)} %get-tuple-element.37, s32[2048]{0:T(1024)S(1)} %get-tuple-element.38, s32[256]{0:T(256)S(1)} %get-tuple-element.40, s32[256]{0:T(256)S(1)} %get-tuple-element.41, pred[256]{0:T(512)(128)(4,1)} %get-tuple-element.36, ...), kind=kOutput, calls=%fused_computation.1 | convolution fusion | flops 69779456 | bytes 1333764 | tf_op jit(solution)/shard_map/dot_general | solution.py:279
  15.0 3.4 %collective-permute-done.3 = bf16[16,3584]{1,0:T(8,128)(2,1)S(1)} collective-permute-done((bf16[16,3584]{1,0:T(8,128)(2,1)S(1)}, bf16[16,3584]{1,0:T(8,128)(2,1)S(1)}, u32[]{:S(2)}, u32[]{:S(2)}) %collective-permute-start.3) | collective-permute-done | bytes 114720 | tf_op jit(solution)/shard_map/ppermute | solution.py:230
  21.2 2.9 %collective-permute-done.6 = bf16[16,3584]{1,0:T(8,128)(2,1)S(1)} collective-permute-done((bf16[16,3584]{1,0:T(8,128)(2,1)S(1)}, bf16[16,3584]{1,0:T(8,128)(2,1)S(1)}, u32[]{:S(2)}, u32[]{:S(2)}) %collective-permute-start.6) | collective-permute-done | bytes 114720 | tf_op jit(solution)/shard_map/ppermute | solution.py:230
  24.0 2.3 %collective-permute-done.5 = bf16[16,3584]{1,0:T(8,128)(2,1)S(1)} collective-permute-done((bf16[16,3584]{1,0:T(8,128)(2,1)S(1)}, bf16[16,3584]{1,0:T(8,128)(2,1)S(1)}, u32[]{:S(2)}, u32[]{:S(2)}) %collective-permute-start.5) | collective-permute-done | bytes 114720 | tf_op jit(solution)/shard_map/ppermute | solution.py:230
  30.5 1.7 %collective-permute-start.18 = (bf16[256,256]{1,0:T(8,128)(2,1)S(1)}, bf16[256,256]{1,0:T(8,128)(2,1)S(1)}, u32[]{:S(2)}, u32[]{:S(2)}) collective-permute-start(bf16[256,256]{1,0:T(8,128)(2,1)S(1)} %pad_maximum_fusion.4.hid_ref.refs_0_), channel_id=1, source_target_pairs={{0,4},{4,0},{8,12},{12,8},{1,5},{5,1},{9,13},{13,9},{2,6},{6,2},{1... | collective-permute-start | bytes 393224 | tf_op jit(solution)/shard_map/ppermute | solution.py:230
  32.3 9.4 %target.2.part_ref = bf16[256,3584]{1,0:T(8,128)(2,1)S(1)} custom-call(bf16[128,2048]{1,0:T(8,128)(2,1)S(1)} %copy-done.1, bf16[128,2048]{1,0:T(8,128)(2,1)S(1)} %collective-permute-done.refs_1_.refs_9_, bf16[2048,3584]{1,0:T(8,128)(2,1)} %refs_2_.3), custom_call_target="tpu_custom_call" | custom-call | flops 3758096384 | bytes 14680064 | tf_op jit(solution)/shard_map/target/pallas_call | solution.py:42
  41.6 2.9 %project.2 = (bf16[256,3584]{1,0:T(8,128)(2,1)S(1)}, bf16[4,256,256]{2,1,0:T(8,128)(2,1)S(1)}) custom-call(bf16[256,3584]{1,0:T(8,128)(2,1)S(1)} %target.2.part_ref, bf16[256,256]{1,0:T(8,128)(2,1)S(1)} %pad_maximum_fusion.4.hid_ref.refs_0_, bf16[4,4,64,896]{3,2,1,0:T(8,128)(2,1)S(1)} %spread_right.1.right_ref), custom_call_target="tpu_custom_call" | custom-call | flops 939524096 | bytes 5505024 | tf_op jit(solution)/shard_map/project/pallas_call | solution.py:98
  45.4 1.8 %collective-permute-start.20 = (bf16[256,256]{1,0:T(8,128)(2,1)S(1)}, bf16[256,256]{1,0:T(8,128)(2,1)S(1)}, u32[]{:S(2)}, u32[]{:S(2)}) collective-permute-start(bf16[256,256]{1,0:T(8,128)(2,1)S(1)} %collective-permute-done.19.refs_2_), channel_id=1, source_target_pairs={{0,4},{4,0},{8,12},{12,8},{1,5},{5,1},{9,13},{13,9},{2,6},{6,2},{1... | collective-permute-start | bytes 393224 | tf_op jit(solution)/shard_map/ppermute | solution.py:230
  48.0 1.6 %collective-permute-start.21 = (bf16[256,256]{1,0:T(8,128)(2,1)S(1)}, bf16[256,256]{1,0:T(8,128)(2,1)S(1)}, u32[]{:S(2)}, u32[]{:S(2)}) collective-permute-start(bf16[256,256]{1,0:T(8,128)(2,1)S(1)} %pad_maximum_fusion.5.hid_ref.refs_4_), channel_id=1, source_target_pairs={{0,4},{4,0},{8,12},{12,8},{1,5},{5,1},{9,13},{13,9},{2,6},{6,2},{1... | collective-permute-start | bytes 393224 | tf_op jit(solution)/shard_map/ppermute | solution.py:230
  49.6 9.3 %target.3.part_ref = bf16[256,3584]{1,0:T(8,128)(2,1)S(1)} custom-call(bf16[128,2048]{1,0:T(8,128)(2,1)S(1)} %collective-permute-done.10.refs_0_.refs_10_, bf16[128,2048]{1,0:T(8,128)(2,1)S(1)} %collective-permute-done.11.refs_1_.refs_11_, bf16[2048,3584]{1,0:T(8,128)(2,1)} %refs_2_.3), custom_call_target="tpu_custom_call" | custom-call | flops 3758096384 | bytes 14680064 | tf_op jit(solution)/shard_map/target/pallas_call | solution.py:42
  59.0 2.9 %project.3 = (bf16[256,3584]{1,0:T(8,128)(2,1)S(1)}, bf16[4,256,256]{2,1,0:T(8,128)(2,1)S(1)}) custom-call(bf16[256,3584]{1,0:T(8,128)(2,1)S(1)} %target.3.part_ref, bf16[256,256]{1,0:T(8,128)(2,1)S(1)} %pad_maximum_fusion.5.hid_ref.refs_4_, bf16[4,4,64,896]{3,2,1,0:T(8,128)(2,1)S(1)} %spread_right.1.right_ref), custom_call_target="tpu_custom_call" | custom-call | flops 939524096 | bytes 5505024 | tf_op jit(solution)/shard_map/project/pallas_call | solution.py:98
  63.2 2.6 %collective-permute-start.8 = (bf16[256,256]{1,0:T(8,128)(2,1)S(1)}, bf16[256,256]{1,0:T(8,128)(2,1)S(1)}, u32[]{:S(2)}, u32[]{:S(2)}) collective-permute-start(bf16[256,256]{1,0:T(8,128)(2,1)S(1)} %get-tuple-element.14), channel_id=1, source_target_pairs={{0,8},{4,12},{8,0},{12,4},{1,9},{5,13},{9,1},{13,5},{2,10},{6,14},... | collective-permute-start | bytes 393224 | tf_op jit(solution)/shard_map/ppermute | solution.py:230
  67.1 1.6 %collective-permute-done.23.refs_7_ = bf16[256,256]{1,0:T(8,128)(2,1)S(1)} collective-permute-done((bf16[256,256]{1,0:T(8,128)(2,1)S(1)}, bf16[256,256]{1,0:T(8,128)(2,1)S(1)}, u32[]{:S(2)}, u32[]{:S(2)}) %collective-permute-start.23) | collective-permute-done | bytes 131104 | tf_op jit(solution)/shard_map/ppermute | solution.py:230
  70.2 2.2 %grad_right.1 = bf16[4,16,3584]{2,1,0:T(8,128)(2,1)S(1)} custom-call(bf16[256,256]{1,0:T(8,128)(2,1)S(1)} %pad_maximum_fusion.4.hid_ref.refs_0_, bf16[256,256]{1,0:T(8,128)(2,1)S(1)} %collective-permute-done.18.refs_1_, bf16[256,256]{1,0:T(8,128)(2,1)S(1)} %collective-permute-done.19.refs_2_, bf16[256,256]{1,0:T(8,128)(2,1)S(1)} %collective-permute-done.20.refs_3_, ...), custom_call_target="tpu_custom_call" | custom-call | flops 939524096 | bytes 3670016 | tf_op jit(solution)/shard_map/grad_right/pallas_call | solution.py:143
  74.5 1.7 %collective-permute-done.8.refs_2_ = bf16[256,256]{1,0:T(8,128)(2,1)S(1)} collective-permute-done((bf16[256,256]{1,0:T(8,128)(2,1)S(1)}, bf16[256,256]{1,0:T(8,128)(2,1)S(1)}, u32[]{:S(2)}, u32[]{:S(2)}) %collective-permute-start.8) | collective-permute-done | bytes 131104 | tf_op jit(solution)/shard_map/ppermute | solution.py:230
  76.2 6.5 %collective-permute-start.25 = (bf16[16,3584]{1,0:T(8,128)(2,1)}, bf16[16,3584]{1,0:T(8,128)(2,1)}, u32[]{:S(2)}, u32[]{:S(2)}) collective-permute-start(bf16[16,3584]{1,0:T(8,128)(2,1)} %get-tuple-element.21), channel_id=1, source_target_pairs={{0,2},{1,3},{2,0},{3,1},{4,6},{5,7},{6,4},{7,5},{8,10},{9,11},{10,... | collective-permute-start | bytes 344072 | tf_op jit(solution)/shard_map/ppermute | solution.py:230
  83.4 3.6 %collective-permute-done.13.refs_6_ = bf16[256,256]{1,0:T(8,128)(2,1)} collective-permute-done((bf16[256,256]{1,0:T(8,128)(2,1)}, bf16[256,256]{1,0:T(8,128)(2,1)}, u32[]{:S(2)}, u32[]{:S(2)}) %collective-permute-start.13) | collective-permute-done | bytes 131104 | tf_op jit(solution)/shard_map/ppermute | solution.py:230
  89.0 2.2 %grad_left.1 = bf16[16,2048]{1,0:T(8,128)(2,1)S(1)} custom-call(bf16[4,256,256]{2,1,0:T(8,128)(2,1)S(1)} %get-tuple-element.6.refs_0_, bf16[256,256]{1,0:T(8,128)(2,1)S(1)} %collective-permute-done.7.refs_1_, bf16[256,256]{1,0:T(8,128)(2,1)S(1)} %collective-permute-done.8.refs_2_, bf16[256,256]{1,0:T(8,128)(2,1)S(1)} %collective-permute-done.9.refs_3_, ...), custom_call_target="tpu_custom_call" | custom-call | flops 536870912 | bytes 2097152 | tf_op jit(solution)/shard_map/grad_left/pallas_call | solution.py:189
  93.6 2.1 %collective-permute-start.27 = (bf16[16,3584]{1,0:T(8,128)(2,1)S(1)}, bf16[16,3584]{1,0:T(8,128)(2,1)S(1)}, u32[]{:S(2)}, u32[]{:S(2)}) collective-permute-start(bf16[16,3584]{1,0:T(8,128)(2,1)S(1)} %get-tuple-element.16), channel_id=1, source_target_pairs={{0,4},{4,0},{8,12},{12,8},{1,5},{5,1},{9,13},{13,9},{2,6},{6,2},{1... | collective-permute-start | bytes 344072 | tf_op jit(solution)/shard_map/ppermute | solution.py:230
  100.9 1.5 %collective-permute-done.16.refs_2_ = bf16[16,512]{1,0:T(8,128)(2,1)S(1)} collective-permute-done((bf16[16,512]{1,0:T(8,128)(2,1)S(1)}, bf16[16,512]{1,0:T(8,128)(2,1)S(1)}, u32[]{:S(2)}, u32[]{:S(2)}) %collective-permute-start.16) | collective-permute-done | bytes 16416 | tf_op jit(solution)/shard_map/ppermute | solution.py:230
  103.8 1.7 %place.1 = f32[16,2048]{1,0:T(8,128)} custom-call(s32[1]{0:T(128)} %bitcast.c_ref, bf16[16,512]{1,0:T(8,128)(2,1)} %get-tuple-element.34.refs_0_, bf16[16,512]{1,0:T(8,128)(2,1)} %copy-done.8, bf16[16,512]{1,0:T(8,128)(2,1)} %copy-done.9, bf16[16,512]{1,0:T(8,128)(2,1)} %copy-done.10), custom_call_target="tpu_custom_call" | custom-call | tf_op jit(solution)/shard_map/place/pallas_call | solution.py:218
  (100 shorter events, 33.2 us)
Async XLA Ops:
  2.3 10.6 %collective-permute-start.2 = (bf16[16,3584]{1,0:T(8,128)(2,1)}, bf16[16,3584]{1,0:T(8,128)(2,1)S(1)}, u32[]{:S(2)}, u32[]{:S(2)}) collective-permute-start(bf16[16,3584]{1,0:T(8,128)(2,1)} %constant_dynamic-slice_fusion.6), channel_id=1, source_target_pairs={{0,8},{4,12},{8,0},{12,4},{1,9},{5,13},{9,1},{13,5},{2,10},{6,14},... | collective-permute-start | bytes 344072 | tf_op jit(solution)/shard_map/ppermute | solution.py:230
  6.3 8.6 %collective-permute-start.1 = (bf16[16,3584]{1,0:T(8,128)(2,1)}, bf16[16,3584]{1,0:T(8,128)(2,1)S(1)}, u32[]{:S(2)}, u32[]{:S(2)}) collective-permute-start(bf16[16,3584]{1,0:T(8,128)(2,1)} %constant_dynamic-slice_fusion.6), channel_id=1, source_target_pairs={{0,4},{4,0},{8,12},{12,8},{1,5},{5,1},{9,13},{13,9},{2,6},{6,2},{1... | collective-permute-start | bytes 344072 | tf_op jit(solution)/shard_map/ppermute | solution.py:230
  7.9 24.3 %collective-permute-start.10 = (bf16[128,2048]{1,0:T(8,128)(2,1)}, bf16[128,2048]{1,0:T(8,128)(2,1)S(1)}, u32[]{:S(2)}, u32[]{:S(2)}) collective-permute-start(bf16[128,2048]{1,0:T(8,128)(2,1)} %refs_8_.1), channel_id=1, source_target_pairs={{0,2},{2,0},{1,3},{3,1},{4,6},{6,4},{5,7},{7,5},{8,10},{10,8},{9,1... | collective-permute-start | bytes 1572872 | tf_op jit(solution)/shard_map/ppermute | solution.py:230
  9.4 19.2 %collective-permute-start = (bf16[128,2048]{1,0:T(8,128)(2,1)}, bf16[128,2048]{1,0:T(8,128)(2,1)S(1)}, u32[]{:S(2)}, u32[]{:S(2)}) collective-permute-start(bf16[128,2048]{1,0:T(8,128)(2,1)} %refs_8_.1), channel_id=1, source_target_pairs={{0,1},{1,0},{2,3},{3,2},{4,5},{5,4},{6,7},{7,6},{8,9},{9,8},{10,11... | collective-permute-start | bytes 1572872 | tf_op jit(solution)/shard_map/ppermute | solution.py:230
  19.3 7.1 %collective-permute-start.5 = (bf16[16,3584]{1,0:T(8,128)(2,1)S(1)}, bf16[16,3584]{1,0:T(8,128)(2,1)S(1)}, u32[]{:S(2)}, u32[]{:S(2)}) collective-permute-start(bf16[16,3584]{1,0:T(8,128)(2,1)S(1)} %get-tuple-element.29), channel_id=1, source_target_pairs={{0,2},{1,3},{2,0},{3,1},{4,6},{5,7},{6,4},{7,5},{8,10},{9,11},{10,... | collective-permute-start | bytes 344072 | tf_op jit(solution)/shard_map/ppermute | solution.py:230
  29.1 16.3 %collective-permute-start.19 = (bf16[256,256]{1,0:T(8,128)(2,1)S(1)}, bf16[256,256]{1,0:T(8,128)(2,1)S(1)}, u32[]{:S(2)}, u32[]{:S(2)}) collective-permute-start(bf16[256,256]{1,0:T(8,128)(2,1)S(1)} %pad_maximum_fusion.4.hid_ref.refs_0_), channel_id=1, source_target_pairs={{0,8},{4,12},{8,0},{12,4},{1,9},{5,13},{9,1},{13,5},{2,10},{6,14},... | collective-permute-start | bytes 393224 | tf_op jit(solution)/shard_map/ppermute | solution.py:230
  30.5 32.7 %collective-permute-start.18 = (bf16[256,256]{1,0:T(8,128)(2,1)S(1)}, bf16[256,256]{1,0:T(8,128)(2,1)S(1)}, u32[]{:S(2)}, u32[]{:S(2)}) collective-permute-start(bf16[256,256]{1,0:T(8,128)(2,1)S(1)} %pad_maximum_fusion.4.hid_ref.refs_0_), channel_id=1, source_target_pairs={{0,4},{4,0},{8,12},{12,8},{1,5},{5,1},{9,13},{13,9},{2,6},{6,2},{1... | collective-permute-start | bytes 393224 | tf_op jit(solution)/shard_map/ppermute | solution.py:230
  32.3 15.0 %collective-permute-start.11 = (bf16[128,2048]{1,0:T(8,128)(2,1)S(1)}, bf16[128,2048]{1,0:T(8,128)(2,1)S(1)}, u32[]{:S(2)}, u32[]{:S(2)}) collective-permute-start(bf16[128,2048]{1,0:T(8,128)(2,1)S(1)} %collective-permute-done.10.refs_0_.refs_10_), channel_id=1, source_target_pairs={{0,1},{1,0},{2,3},{3,2},{4,5},{5,4},{6,7},{7,6},{8,9},{9,8},{10,11... | collective-permute-start | bytes 1572872 | tf_op jit(solution)/shard_map/ppermute | solution.py:230
  44.6 27.8 %collective-permute-start.7 = (bf16[256,256]{1,0:T(8,128)(2,1)S(1)}, bf16[256,256]{1,0:T(8,128)(2,1)S(1)}, u32[]{:S(2)}, u32[]{:S(2)}) collective-permute-start(bf16[256,256]{1,0:T(8,128)(2,1)S(1)} %get-tuple-element.15), channel_id=1, source_target_pairs={{0,4},{4,0},{8,12},{12,8},{1,5},{5,1},{9,13},{13,9},{2,6},{6,2},{1... | collective-permute-start | bytes 393224 | tf_op jit(solution)/shard_map/ppermute | solution.py:230
  45.4 20.4 %collective-permute-start.20 = (bf16[256,256]{1,0:T(8,128)(2,1)S(1)}, bf16[256,256]{1,0:T(8,128)(2,1)S(1)}, u32[]{:S(2)}, u32[]{:S(2)}) collective-permute-start(bf16[256,256]{1,0:T(8,128)(2,1)S(1)} %collective-permute-done.19.refs_2_), channel_id=1, source_target_pairs={{0,4},{4,0},{8,12},{12,8},{1,5},{5,1},{9,13},{13,9},{2,6},{6,2},{1... | collective-permute-start | bytes 393224 | tf_op jit(solution)/shard_map/ppermute | solution.py:230
  47.7 14.2 %collective-permute-start.22 = (bf16[256,256]{1,0:T(8,128)(2,1)S(1)}, bf16[256,256]{1,0:T(8,128)(2,1)S(1)}, u32[]{:S(2)}, u32[]{:S(2)}) collective-permute-start(bf16[256,256]{1,0:T(8,128)(2,1)S(1)} %pad_maximum_fusion.5.hid_ref.refs_4_), channel_id=1, source_target_pairs={{0,8},{4,12},{8,0},{12,4},{1,9},{5,13},{9,1},{13,5},{2,10},{6,14},... | collective-permute-start | bytes 393224 | tf_op jit(solution)/shard_map/ppermute | solution.py:230
  48.0 19.1 %collective-permute-start.21 = (bf16[256,256]{1,0:T(8,128)(2,1)S(1)}, bf16[256,256]{1,0:T(8,128)(2,1)S(1)}, u32[]{:S(2)}, u32[]{:S(2)}) collective-permute-start(bf16[256,256]{1,0:T(8,128)(2,1)S(1)} %pad_maximum_fusion.5.hid_ref.refs_4_), channel_id=1, source_target_pairs={{0,4},{4,0},{8,12},{12,8},{1,5},{5,1},{9,13},{13,9},{2,6},{6,2},{1... | collective-permute-start | bytes 393224 | tf_op jit(solution)/shard_map/ppermute | solution.py:230
  61.9 6.8 %collective-permute-start.23 = (bf16[256,256]{1,0:T(8,128)(2,1)S(1)}, bf16[256,256]{1,0:T(8,128)(2,1)S(1)}, u32[]{:S(2)}, u32[]{:S(2)}) collective-permute-start(bf16[256,256]{1,0:T(8,128)(2,1)S(1)} %collective-permute-done.22.refs_6_), channel_id=1, source_target_pairs={{0,4},{4,0},{8,12},{12,8},{1,5},{5,1},{9,13},{13,9},{2,6},{6,2},{1... | collective-permute-start | bytes 393224 | tf_op jit(solution)/shard_map/ppermute | solution.py:230
  63.2 13.0 %collective-permute-start.8 = (bf16[256,256]{1,0:T(8,128)(2,1)S(1)}, bf16[256,256]{1,0:T(8,128)(2,1)S(1)}, u32[]{:S(2)}, u32[]{:S(2)}) collective-permute-start(bf16[256,256]{1,0:T(8,128)(2,1)S(1)} %get-tuple-element.14), channel_id=1, source_target_pairs={{0,8},{4,12},{8,0},{12,4},{1,9},{5,13},{9,1},{13,5},{2,10},{6,14},... | collective-permute-start | bytes 393224 | tf_op jit(solution)/shard_map/ppermute | solution.py:230
  65.8 10.4 %collective-permute-start.9 = (bf16[256,256]{1,0:T(8,128)(2,1)S(1)}, bf16[256,256]{1,0:T(8,128)(2,1)S(1)}, u32[]{:S(2)}, u32[]{:S(2)}) collective-permute-start(bf16[256,256]{1,0:T(8,128)(2,1)S(1)} %get-tuple-element.13), channel_id=1, source_target_pairs={{0,12},{4,8},{8,4},{12,0},{1,13},{5,9},{9,5},{13,1},{2,14},{6,10},... | collective-permute-start | bytes 393224 | tf_op jit(solution)/shard_map/ppermute | solution.py:230
  67.1 15.5 %collective-permute-start.12 = (bf16[256,256]{1,0:T(8,128)(2,1)S(1)}, bf16[256,256]{1,0:T(8,128)(2,1)S(1)}, u32[]{:S(2)}, u32[]{:S(2)}) collective-permute-start(bf16[256,256]{1,0:T(8,128)(2,1)S(1)} %get-tuple-element.12), channel_id=1, source_target_pairs={{0,4},{4,0},{8,12},{12,8},{1,5},{5,1},{9,13},{13,9},{2,6},{6,2},{1... | collective-permute-start | bytes 393224 | tf_op jit(solution)/shard_map/ppermute | solution.py:230
  68.8 18.2 %collective-permute-start.13 = (bf16[256,256]{1,0:T(8,128)(2,1)}, bf16[256,256]{1,0:T(8,128)(2,1)}, u32[]{:S(2)}, u32[]{:S(2)}) collective-permute-start(bf16[256,256]{1,0:T(8,128)(2,1)} %get-tuple-element.11), channel_id=1, source_target_pairs={{0,8},{4,12},{8,0},{12,4},{1,9},{5,13},{9,1},{13,5},{2,10},{6,14},... | collective-permute-start | bytes 393224 | tf_op jit(solution)/shard_map/ppermute | solution.py:230
  72.4 14.6 %collective-permute-start.14 = (bf16[256,256]{1,0:T(8,128)(2,1)}, bf16[256,256]{1,0:T(8,128)(2,1)}, u32[]{:S(2)}, u32[]{:S(2)}) collective-permute-start(bf16[256,256]{1,0:T(8,128)(2,1)} %get-tuple-element.10), channel_id=1, source_target_pairs={{0,12},{4,8},{8,4},{12,0},{1,13},{5,9},{9,5},{13,1},{2,14},{6,10},... | collective-permute-start | bytes 393224 | tf_op jit(solution)/shard_map/ppermute | solution.py:230
  76.2 16.2 %collective-permute-start.24 = (bf16[16,3584]{1,0:T(8,128)(2,1)}, bf16[16,3584]{1,0:T(8,128)(2,1)}, u32[]{:S(2)}, u32[]{:S(2)}) collective-permute-start(bf16[16,3584]{1,0:T(8,128)(2,1)} %get-tuple-element.22), channel_id=1, source_target_pairs={{0,1},{1,0},{2,3},{3,2},{4,5},{5,4},{6,7},{7,6},{8,9},{9,8},{10,11... | collective-permute-start | bytes 344072 | tf_op jit(solution)/shard_map/ppermute | solution.py:230
  76.2 16.2 %collective-permute-start.25 = (bf16[16,3584]{1,0:T(8,128)(2,1)}, bf16[16,3584]{1,0:T(8,128)(2,1)}, u32[]{:S(2)}, u32[]{:S(2)}) collective-permute-start(bf16[16,3584]{1,0:T(8,128)(2,1)} %get-tuple-element.21), channel_id=1, source_target_pairs={{0,2},{1,3},{2,0},{3,1},{4,6},{5,7},{6,4},{7,5},{8,10},{9,11},{10,... | collective-permute-start | bytes 344072 | tf_op jit(solution)/shard_map/ppermute | solution.py:230
  83.3 9.1 %collective-permute-start.26 = (bf16[16,3584]{1,0:T(8,128)(2,1)}, bf16[16,3584]{1,0:T(8,128)(2,1)}, u32[]{:S(2)}, u32[]{:S(2)}) collective-permute-start(bf16[16,3584]{1,0:T(8,128)(2,1)} %get-tuple-element.20), channel_id=1, source_target_pairs={{0,3},{1,2},{2,1},{3,0},{4,7},{5,6},{6,5},{7,4},{8,11},{9,10},{10,... | collective-permute-start | bytes 344072 | tf_op jit(solution)/shard_map/ppermute | solution.py:230
  93.6 11.9 %collective-permute-start.27 = (bf16[16,3584]{1,0:T(8,128)(2,1)S(1)}, bf16[16,3584]{1,0:T(8,128)(2,1)S(1)}, u32[]{:S(2)}, u32[]{:S(2)}) collective-permute-start(bf16[16,3584]{1,0:T(8,128)(2,1)S(1)} %get-tuple-element.16), channel_id=1, source_target_pairs={{0,4},{4,0},{8,12},{12,8},{1,5},{5,1},{9,13},{13,9},{2,6},{6,2},{1... | collective-permute-start | bytes 344072 | tf_op jit(solution)/shard_map/ppermute | solution.py:230
  95.7 10.6 %collective-permute-start.28 = (bf16[16,3584]{1,0:T(8,128)(2,1)S(1)}, bf16[16,3584]{1,0:T(8,128)(2,1)S(1)}, u32[]{:S(2)}, u32[]{:S(2)}) collective-permute-start(bf16[16,3584]{1,0:T(8,128)(2,1)S(1)} %get-tuple-element.18), channel_id=1, source_target_pairs={{0,8},{4,12},{8,0},{12,4},{1,9},{5,13},{9,1},{13,5},{2,10},{6,14},... | collective-permute-start | bytes 344072 | tf_op jit(solution)/shard_map/ppermute | solution.py:230
  96.6 9.6 %collective-permute-start.29 = (bf16[16,3584]{1,0:T(8,128)(2,1)S(1)}, bf16[16,3584]{1,0:T(8,128)(2,1)S(1)}, u32[]{:S(2)}, u32[]{:S(2)}) collective-permute-start(bf16[16,3584]{1,0:T(8,128)(2,1)S(1)} %get-tuple-element.17), channel_id=1, source_target_pairs={{0,12},{4,8},{8,4},{12,0},{1,13},{5,9},{9,5},{13,1},{2,14},{6,10},... | collective-permute-start | bytes 344072 | tf_op jit(solution)/shard_map/ppermute | solution.py:230
  (17 other events, 63.5 us)

commit v3 on v2

--- a/solution.py
+++ b/solution.py
@@ -18,6 +18,7 @@
 F32 = jnp.float32
 NT = (((1,), (1,)), ((), ()))
 TN = (((0,), (0,)), ((), ()))
+SPLIT = 4
 VMEM = 40 * 1024 * 1024
 
 
@@ -29,9 +30,11 @@
     return jnp.concatenate([r[...] for r in refs], axis=0) if len(refs) > 1 else refs[0][...]
 
 
-def target_kernel(*refs):
-    *tok_refs, teacher_ref, out_ref = refs
-    out_ref[...] = jnp.dot(rows_of(tok_refs), teacher_ref[...], preferred_element_type=F32).astype(BF)
+def target_kernel(pieces, *refs):
+    tok_refs, teacher_refs, out_ref = refs[:pieces], refs[pieces:-1], refs[-1]
+    out_ref[...] = jnp.dot(
+        rows_of(tok_refs), rows_of(teacher_refs), preferred_element_type=F32
+    ).astype(BF)
 
 
 def target(tokens, teacher):
@@ -40,16 +43,16 @@
     block = 512 if cols % 512 == 0 else COLS
     total = t * len(tokens)
     return pl.pallas_call(
-        target_kernel,
+        functools.partial(target_kernel, len(tokens)),
         grid=(cols // block,),
         in_specs=[pl.BlockSpec((t, depth), lambda q: (0, 0))] * len(tokens)
-        + [pl.BlockSpec((depth, block), lambda q: (0, q))],
+        + [pl.BlockSpec((depth // SPLIT, block), lambda q, i=i: (i, q)) for i in range(SPLIT)],
         out_specs=pl.BlockSpec((total, block), lambda q: (0, q)),
         out_shape=jax.ShapeDtypeStruct((total, cols), BF),
         compiler_params=pltpu.CompilerParams(vmem_limit_bytes=VMEM),
         cost_estimate=cost(2 * total * cols * depth, 2 * depth * cols),
         name="target",
-    )(*tokens, teacher)
+    )(*tokens, *[teacher] * SPLIT)
 
 
 def spread_kernel(in_ref, out_ref):
@@ -117,15 +120,10 @@
     )(part, hidden, right)
 
 
-def grad_right_kernel(n_z, halves, *refs):
-    hid_refs, resid_refs, out_ref = refs[: n_z * halves], refs[n_z * halves : -1], refs[-1]
-    rows = hid_refs[0].shape[0]
-    per_z = rows // GROUP
-    prod = None
-    for h in range(halves):
-        hid = rows_of(hid_refs[h * n_z : (h + 1) * n_z])
-        term = jnp.dot(hid, resid_refs[h][...], preferred_element_type=F32)
-        prod = term if prod is None else prod + term
+def grad_right_kernel(*refs):
+    *hid_refs, resid_ref, out_ref = refs
+    n_z, per_z = len(hid_refs), hid_refs[0].shape[0] // GROUP
+    prod = jnp.dot(rows_of(hid_refs), resid_ref[...], preferred_element_type=F32)
     prod = prod.reshape(n_z, GROUP, per_z, COLS)
     block = lax.broadcasted_iota(jnp.int32, (n_z, per_z, COLS), 2) // FB
     total = prod[:, 0]
@@ -134,43 +132,33 @@
     out_ref[...] = total.astype(BF)
 
 
-def grad_right_partial(hidden, resids):
-    halves, n_z = len(hidden), len(hidden[0])
-    rows, t = hidden[0][0].shape
-    cols = resids[0].shape[1]
+def grad_right_partial(hidden, resid):
+    n_z = len(hidden)
+    rows, t = hidden[0].shape
+    cols = resid.shape[1]
     n_q = cols // COLS
     per_z = rows // (n_q * GROUP)
     return pl.pallas_call(
-        functools.partial(grad_right_kernel, n_z, halves),
+        grad_right_kernel,
         grid=(n_q,),
-        in_specs=[pl.BlockSpec((rows // n_q, t), lambda q: (q, 0))] * (halves * n_z)
-        + [pl.BlockSpec((t, COLS), lambda q: (0, q))] * halves,
+        in_specs=[pl.BlockSpec((rows // n_q, t), lambda q: (q, 0))] * n_z
+        + [pl.BlockSpec((t, COLS), lambda q: (0, q))],
         out_specs=pl.BlockSpec((n_z, per_z, COLS), lambda q: (0, 0, q)),
         out_shape=jax.ShapeDtypeStruct((n_z, per_z, cols), BF),
         compiler_params=pltpu.CompilerParams(vmem_limit_bytes=VMEM),
-        cost_estimate=cost(2 * halves * t * cols * n_z * rows // n_q, 2 * halves * t * cols),
+        cost_estimate=cost(2 * t * cols * n_z * rows // n_q, 2 * t * cols),
         name="grad_right",
-    )(*[h for hs in hidden for h in hs], *resids)
-
-
-def grad_left_kernel(n_z, halves, n_k, *refs):
-    per = halves * n_z
-    back_refs, tok_refs, out_ref = refs[:per], refs[per:-1], refs[-1]
-    pieces = len(tok_refs) // halves
-    prod = None
-    for h in range(halves):
-        total = back_refs[h * n_z][0].astype(F32)
-        for s in range(1, n_z):
-            total = total + back_refs[h * n_z + s][...].astype(F32)
-        term = jnp.dot(
-            total.astype(BF),
-            rows_of(tok_refs[h * pieces : (h + 1) * pieces]),
-            preferred_element_type=F32,
-        )
-        prod = term if prod is None else prod + term
+    )(*hidden, resid)
+
+
+def grad_left_kernel(n_z, n_k, *refs):
+    back_refs, tok_refs, out_ref = refs[:n_z], refs[n_z:-1], refs[-1]
+    total = back_refs[0][0].astype(F32)
+    for ref in back_refs[1:]:
+        total = total + ref[...].astype(F32)
+    prod = jnp.dot(total.astype(BF), rows_of(tok_refs), preferred_element_type=F32)
     rows, block = prod.shape
-    n_b = rows // n_k
-    prod = prod.reshape(n_k, n_b, block)
+    prod = prod.reshape(n_k, rows // n_k, block)
     at = pl.program_id(0) * (block // BI)
     own = lax.broadcasted_iota(jnp.int32, prod.shape, 1) == at + lax.broadcasted_iota(
         jnp.int32, prod.shape, 2
@@ -179,24 +167,22 @@
 
 
 def grad_left_of(backs, tokens, n_k):
-    halves, n_z = len(backs), len(backs[0])
-    rows, t = backs[0][1].shape
-    piece, depth = tokens[0][0].shape
+    n_z = len(backs)
+    rows, t = backs[1].shape
+    piece, depth = tokens[0].shape
     block = min(depth, 1024)
-    first = pl.BlockSpec((1, rows, t), lambda q: (0, 0, 0))
-    rest = pl.BlockSpec((rows, t), lambda q: (0, 0))
-    flat = [x for h in tokens for x in h]
-    return pl.pallas_call(
-        functools.partial(grad_left_kernel, n_z, halves, n_k),
+    return pl.pallas_call(
+        functools.partial(grad_left_kernel, n_z, n_k),
         grid=(depth // block,),
-        in_specs=([first] + [rest] * (n_z - 1)) * halves
-        + [pl.BlockSpec((piece, block), lambda q: (0, q))] * len(flat),
+        in_specs=[pl.BlockSpec((1, rows, t), lambda q: (0, 0, 0))]
+        + [pl.BlockSpec((rows, t), lambda q: (0, 0))] * (n_z - 1)
+        + [pl.BlockSpec((piece, block), lambda q: (0, q))] * len(tokens),
         out_specs=pl.BlockSpec((n_k, block), lambda q: (0, q)),
         out_shape=jax.ShapeDtypeStruct((n_k, depth), BF),
         compiler_params=pltpu.CompilerParams(vmem_limit_bytes=VMEM),
-        cost_estimate=cost(2 * halves * t * rows * depth, 2 * halves * t * depth),
+        cost_estimate=cost(2 * t * rows * depth, 2 * t * depth),
         name="grad_left",
-    )(*[b for h in backs for b in h], *flat)
+    )(*backs, *tokens)
 
 
 def place_kernel(n_b, c_ref, *refs):
@@ -244,7 +230,6 @@
 def per_device(tokens, teacher, left_blocks, right_blocks):
     n_z = lax.axis_size("blk")
     n_c = lax.axis_size(("tok", "rep"))
-    n_rep = lax.axis_size("rep")
     z = lax.axis_index("blk")
     c = lax.axis_index(("tok", "rep"))
     plane = ("tok", "rep")
@@ -253,17 +238,15 @@
     n_q = n_k // GROUP
     scale = float(tokens.shape[0] * n_c) ** (-0.5)
 
-    chips = [[own] + [swap(own, "rep", r) for r in range(1, n_rep)] for own in gather(tokens, "tok")]
-
-    share = n_b * FB
-    quarter = lax.dynamic_slice_in_dim(right_blocks, c * share, share, 1)
-    quarters = jnp.stack(gather(quarter, "blk"), 0)
-    here = []
-    for s in range(n_c):
-        piece = pick(quarters, z ^ c ^ s)
-        here.append(swap(piece, plane, s) if s else piece)
-    here = jnp.stack(here, 0)
-    right = jnp.stack([pick(here, c ^ z ^ s) for s in range(n_z)], 0)
+    pieces = [p for own in gather(tokens, "tok") for p in gather(own, "rep")]
+
+    half = n_k // 2
+    sides = []
+    for i, side in enumerate((0, n_c // 2)):
+        perm = [(a * n_c + b, (b ^ side) * n_c + a) for a in range(n_z) for b in range(n_c)]
+        sides.append(lax.ppermute(right_blocks[i * half : (i + 1) * half], ("blk",) + plane, perm))
+    right = jnp.concatenate(sides, axis=0).reshape(n_k, n_z, n_b * FB)
+    right = jnp.stack([lax.dynamic_index_in_dim(right, z ^ s, 1, keepdims=False) for s in range(n_z)], 0)
     right = spread_right(right.reshape(n_z, n_k * n_b, FB), n_q)
 
     left = left_blocks.reshape(n_b * BI, NB)
@@ -279,17 +262,14 @@
     left = lax.dot_general(take, left, NT, preferred_element_type=F32)
     left = jnp.where(diag, left, 0.0).astype(BF)
 
-    hidden, resids, backs = [], [], []
-    for x in chips:
-        hid = jnp.concatenate(
-            [lax.dot_general(left, p, NT, preferred_element_type=F32).astype(BF) for p in x], axis=1
-        )
-        hidden.append(gather(hid, "blk"))
-        resid, back = project(target(x, teacher), hid, right, scale)
-        resids.append(resid)
-        backs.append([back] + [swap(back[s], "blk", s) for s in range(1, n_z)])
-
-    gl = grad_left_of(backs, chips, n_k)
+    hid = jnp.concatenate(
+        [lax.dot_general(left, p, NT, preferred_element_type=F32).astype(BF) for p in pieces], axis=1
+    )
+    hidden = gather(hid, "blk")
+    resid, back = project(target(pieces, teacher), hid, right, scale)
+    backs = [back] + [swap(back[s], "blk", s) for s in range(1, n_z)]
+
+    gl = grad_left_of(backs, pieces, n_k)
     gl = gl.reshape(n_k, n_b, n_c, BI // n_c).transpose(2, 0, 3, 1).reshape(n_c, n_k, -1)
     got = []
     for s in range(n_c):
@@ -297,7 +277,7 @@
         got.append(swap(piece, plane, s) if s else piece)
     grad_left = place(jnp.reshape(c, (1,)).astype(jnp.int32), got, n_b)
 
-    gr = grad_right_partial(hidden, resids)
+    gr = grad_right_partial(hidden, resid)
     there = []
     for s in range(n_c):
         piece = pick(gr, z ^ c ^ s)

time: 108 us -> 101 us (0.935)
  waiting for transfers between devices: 18.5 us -> 28.1 us
  Pallas kernels: 31.9 us -> 22.4 us
  starting transfers between devices: 37.5 us -> 28.4 us
  local copies, waits for them, and re-layouts: 12.6 us -> 15.5 us
  matrix products: 3.36 us -> 2.24 us
    ppermute x30 -> x18, starting transfers between devices: 37.5 us -> 23.8 us  [swap(): return lax.ppermute(x, axes, [(i, i ^ s) for i in range(n)])]
    ppermute x0 -> x2, waiting for transfers between devices: none -> 7.69 us  [per_device(): lax.ppermute(right_blocks[i * half:(i + 1) * half], ('blk',) + plane, perm)]
    pallas_call x4 -> x3, Pallas kernels: 23 us -> 15.6 us  [the longest x1 11.3 us: target(): pl.pallas_call(functools.partial(target_kernel, len(tokens)), grid=(cols...]
    ppermute x0 -> x2, starting transfers between devices: none -> 4.56 us  [per_device(): lax.ppermute(right_blocks[i * half:(i + 1) * half], ('blk',) + plane, perm)]
    unnamed x22 -> x8, local copies, waits for them, and re-layouts: 4.22 us -> 1.12 us
    dynamic_slice x1, local copies, waits for them, and re-layouts: 0.65 us -> 3.3 us  [per_device(): lax.dynamic_index_in_dim(right, z ^ s, 1, keepdims=False)]
    pallas_call x2 -> x1, Pallas kernels: 5.87 us -> 3.6 us  [project(): pl.pallas_call(functools.partial(project_kernel, scale), grid=(n_q,), in_...]
    ppermute x30 -> x18, waiting for transfers between devices: 18.5 us -> 20.4 us  [swap(): return lax.ppermute(x, axes, [(i, i ^ s) for i in range(n)])]
  transfers between devices with their start and end apart: 30 -> 20, of which waited for: 9 -> 6; matrix products, arithmetic and copies ran while one was open for 10% -> 17% of each run, Pallas kernels for 30% -> 22%
where the time goes in v3:
time: 101 us
  starting transfers between devices  28.4 us (28%)
  waiting for transfers between devices  28.1 us (28%)
  Pallas kernels  22.4 us (22%)
  local copies, waits for them, and re-layouts  15.5 us (15%)
  other arithmetic  3.11 us (3%)
  matrix products  2.24 us (2%)
    ppermute x18, starting transfers between devices, swap(): return lax.ppermute(x, axes, [(i, i ^ s) for i in range(n)])  23.8 us
    ppermute x18, waiting for transfers between devices, swap(): return lax.ppermute(x, axes, [(i, i ^ s) for i in range(n)])  20.4 us
    pallas_call x1, Pallas kernels, target(): pl.pallas_call(functools.partial(target_kernel, len(tokens)), grid=(cols...  11.3 us
    ppermute x2, waiting for transfers between devices, per_device(): lax.ppermute(right_blocks[i * half:(i + 1) * half], ('blk',) + plane, perm)  7.69 us
    ppermute x2, starting transfers between devices, per_device(): lax.ppermute(right_blocks[i * half:(i + 1) * half], ('blk',) + plane, perm)  4.56 us
    pallas_call x1, Pallas kernels, project(): pl.pallas_call(functools.partial(project_kernel, scale), grid=(n_q,), in_...  3.6 us
    dynamic_slice x1, local copies, waits for them, and re-layouts, per_device(): lax.dynamic_index_in_dim(right, z ^ s, 1, keepdims=False)  3.3 us
    pallas_call x1, Pallas kernels, grad_left_of(): pl.pallas_call(functools.partial(grad_left_kernel, n_z, n_k), grid=(depth...  2.16 us
  transfers between devices with their start and end apart: 20, of which 6 were waited for; matrix products, arithmetic and copies ran while one was open for 17% of the time, Pallas kernels for 22%

profile of v3, /device:TPU:0, one launch (start us, length us, event | category | flops | bytes accessed | tf_op | source)
XLA Modules:
  0.0 100.7 jit_solution(13248421645804227389)
XLA Ops:
  0.6 3.0 %collective-permute-start.1 = (bf16[128,2048]{1,0:T(8,128)(2,1)}, bf16[128,2048]{1,0:T(8,128)(2,1)S(1)}, u32[]{:S(2)}, u32[]{:S(2)}) collective-permute-start(bf16[128,2048]{1,0:T(8,128)(2,1)} %refs_4_.3), channel_id=1, source_target_pairs={{0,2},{2,0},{1,3},{3,1},{4,6},{6,4},{5,7},{7,5},{8,10},{10,8},{9,1... | collective-permute-start | bytes 1572872 | tf_op jit(solution)/shard_map/ppermute | solution.py:216
  3.6 1.8 %fusion.12 = (bf16[8,14336]{1,0:T(8,128)(2,1)}, bf16[8,14336]{1,0:T(8,128)(2,1)}) fusion(bf16[16,14336]{1,0:T(8,128)(2,1)} %param.7), kind=kLoop, calls=%fused_computation.52 | loop fusion | bytes 917504 | tf_op jit(solution)/shard_map/slice | solution.py:247
  5.5 1.6 %collective-permute-start.3 = (bf16[8,14336]{1,0:T(8,128)(2,1)}, bf16[8,14336]{1,0:T(8,128)(2,1)S(1)}, u32[]{:S(2)}, u32[]{:S(2)}) collective-permute-start(bf16[8,14336]{1,0:T(8,128)(2,1)} %get-tuple-element.20), channel_id=1, source_target_pairs={{0,0},{1,4},{2,8},{3,12},{4,1},{5,5},{6,9},{7,13},{8,2},{9,6},{10,... | collective-permute-start | bytes 688136 | tf_op jit(solution)/shard_map/ppermute | solution.py:247
  7.1 3.0 %collective-permute-start.4 = (bf16[8,14336]{1,0:T(8,128)(2,1)}, bf16[8,14336]{1,0:T(8,128)(2,1)}, u32[]{:S(2)}, u32[]{:S(2)}) collective-permute-start(bf16[8,14336]{1,0:T(8,128)(2,1)} %get-tuple-element.21), channel_id=1, source_target_pairs={{0,8},{1,12},{2,0},{3,4},{4,9},{5,13},{6,1},{7,5},{8,10},{9,14},{1... | collective-permute-start | bytes 688136 | tf_op jit(solution)/shard_map/ppermute | solution.py:247
  10.1 1.5 %reshape.41 = bf16[2048,64]{1,0:T(8,128)(2,1)S(1)} reshape(bf16[16,8192]{1,0:T(8,128)(2,1)} %param.6) | data formatting | bytes 524288 | tf_op jit(solution)/shard_map/reshape | solution.py:252
  13.1 7.7 %collective-permute-done.4 = bf16[8,14336]{1,0:T(8,128)(2,1)} collective-permute-done((bf16[8,14336]{1,0:T(8,128)(2,1)}, bf16[8,14336]{1,0:T(8,128)(2,1)}, u32[]{:S(2)}, u32[]{:S(2)}) %collective-permute-start.4) | collective-permute-done | bytes 229408 | tf_op jit(solution)/shard_map/ppermute | solution.py:247
  20.8 1.7 %pad_maximum_fusion.1 = bf16[16,14336]{1,0:T(8,128)(2,1)} fusion(bf16[8,14336]{1,0:T(8,128)(2,1)} %collective-permute-done.4, bf16[8,14336]{1,0:T(8,128)(2,1)S(1)} %collective-permute-done.3), kind=kLoop, calls=%fused_computation.8 | loop fusion | flops 917504 | bytes 917504 | tf_op jit(solution)/shard_map/concatenate | solution.py:248
  23.9 3.3 %dynamic-slice_reduce_fusion.3 = (bf16[16,3584]{1,0:T(8,128)(2,1)}, bf16[16,3584]{1,0:T(8,128)(2,1)S(1)}, bf16[16,3584]{1,0:T(8,128)(2,1)S(1)}, bf16[16,3584]{1,0:T(8,128)(2,1)S(1)}) fusion(bf16[16,4,3584]{2,1,0:T(4,128)(2,1)S(1)} %reshape.42, s32[]{:T(128)S(6)} %select_n.68, s32[]{:T(128)S(6)} %select_n.70, s32[]{:T(128)S(6)} %select_n.69, s32[]{:T(128)S(6)} %select_n.71), kind=kLoop, calls=%fused_computation.20 | loop fusion | bytes 917520 | tf_op jit(solution)/shard_map/jit(dynamic_index_in_dim)/dynamic_slice | solution.py:249
  29.0 1.5 %spread_right.1.right_ref = bf16[4,4,64,896]{3,2,1,0:T(8,128)(2,1)S(1)} custom-call(bf16[4,256,224]{2,1,0:T(8,128)(2,1)S(1)} %pad_maximum_fusion.in_ref), custom_call_target="tpu_custom_call" | custom-call | flops 411041792 | bytes 3670016 | tf_op jit(solution)/shard_map/spread_right/pallas_call | solution.py:76
  33.0 2.9 %collective-permute-start.12 = (bf16[256,512]{1,0:T(8,128)(2,1)S(1)}, bf16[256,512]{1,0:T(8,128)(2,1)S(1)}, u32[]{:S(2)}, u32[]{:S(2)}) collective-permute-start(bf16[256,512]{1,0:T(8,128)(2,1)S(1)} %pad_maximum_fusion.3.hid_ref.refs_0_), channel_id=1, source_target_pairs={{0,8},{4,12},{8,0},{12,4},{1,9},{5,13},{9,1},{13,5},{2,10},{6,14},... | collective-permute-start | bytes 786440 | tf_op jit(solution)/shard_map/ppermute | solution.py:216
  36.0 1.8 %collective-permute-start.11 = (bf16[256,512]{1,0:T(8,128)(2,1)S(1)}, bf16[256,512]{1,0:T(8,128)(2,1)S(1)}, u32[]{:S(2)}, u32[]{:S(2)}) collective-permute-start(bf16[256,512]{1,0:T(8,128)(2,1)S(1)} %pad_maximum_fusion.3.hid_ref.refs_0_), channel_id=1, source_target_pairs={{0,4},{4,0},{8,12},{12,8},{1,5},{5,1},{9,13},{13,9},{2,6},{6,2},{1... | collective-permute-start | bytes 786440 | tf_op jit(solution)/shard_map/ppermute | solution.py:216
  37.8 11.3 %target.1.part_ref = bf16[512,3584]{1,0:T(8,128)(2,1)S(1)} custom-call(bf16[128,2048]{1,0:T(8,128)(2,1)S(1)} %copy-done, bf16[128,2048]{1,0:T(8,128)(2,1)S(1)} %collective-permute-done.refs_1_.refs_5_, bf16[128,2048]{1,0:T(8,128)(2,1)S(1)} %collective-permute-done.1.refs_2_.refs_6_, bf16[128,2048]{1,0:T(8,128)(2,1)S(1)} %collective-permute-done.2.refs_3_.refs_7_, ...), custom_call_target="tpu_custom_call" | custom-call | flops 7516192768 | bytes 14680064 | tf_op jit(solution)/shard_map/target/pallas_call | solution.py:45
  49.4 3.6 %project.1 = (bf16[512,3584]{1,0:T(8,128)(2,1)S(1)}, bf16[4,256,512]{2,1,0:T(8,128)(2,1)S(1)}) custom-call(bf16[512,3584]{1,0:T(8,128)(2,1)S(1)} %target.1.part_ref, bf16[256,512]{1,0:T(8,128)(2,1)S(1)} %pad_maximum_fusion.3.hid_ref.refs_0_, bf16[4,4,64,896]{3,2,1,0:T(8,128)(2,1)S(1)} %spread_right.1.right_ref), custom_call_target="tpu_custom_call" | custom-call | flops 1879048192 | bytes 11010048 | tf_op jit(solution)/shard_map/project/pallas_call | solution.py:101
  53.8 1.8 %collective-permute-start.5 = (bf16[256,512]{1,0:T(8,128)(2,1)S(1)}, bf16[256,512]{1,0:T(8,128)(2,1)S(1)}, u32[]{:S(2)}, u32[]{:S(2)}) collective-permute-start(bf16[256,512]{1,0:T(8,128)(2,1)S(1)} %get-tuple-element.12), channel_id=1, source_target_pairs={{0,4},{4,0},{8,12},{12,8},{1,5},{5,1},{9,13},{13,9},{2,6},{6,2},{1... | collective-permute-start | bytes 786440 | tf_op jit(solution)/shard_map/ppermute | solution.py:216
  57.0 1.5 %collective-permute-start.7 = (bf16[256,512]{1,0:T(8,128)(2,1)}, bf16[256,512]{1,0:T(8,128)(2,1)}, u32[]{:S(2)}, u32[]{:S(2)}) collective-permute-start(bf16[256,512]{1,0:T(8,128)(2,1)} %get-tuple-element.10), channel_id=1, source_target_pairs={{0,12},{4,8},{8,4},{12,0},{1,13},{5,9},{9,5},{13,1},{2,14},{6,10},... | collective-permute-start | bytes 786440 | tf_op jit(solution)/shard_map/ppermute | solution.py:216
  58.5 2.2 %grad_right.1 = bf16[4,16,3584]{2,1,0:T(8,128)(2,1)S(1)} custom-call(bf16[256,512]{1,0:T(8,128)(2,1)S(1)} %pad_maximum_fusion.3.hid_ref.refs_0_, bf16[256,512]{1,0:T(8,128)(2,1)S(1)} %collective-permute-done.11.refs_1_, bf16[256,512]{1,0:T(8,128)(2,1)S(1)} %collective-permute-done.12.refs_2_, bf16[256,512]{1,0:T(8,128)(2,1)S(1)} %collective-permute-done.13.refs_3_, ...), custom_call_target="tpu_custom_call" | custom-call | flops 939524096 | bytes 3670016 | tf_op jit(solution)/shard_map/grad_right/pallas_call | solution.py:141
  62.7 5.0 %collective-permute-done.5.refs_1_ = bf16[256,512]{1,0:T(8,128)(2,1)S(1)} collective-permute-done((bf16[256,512]{1,0:T(8,128)(2,1)S(1)}, bf16[256,512]{1,0:T(8,128)(2,1)S(1)}, u32[]{:S(2)}, u32[]{:S(2)}) %collective-permute-start.5) | collective-permute-done | bytes 262176 | tf_op jit(solution)/shard_map/ppermute | solution.py:216
  67.8 9.5 %collective-permute-done.6.refs_2_ = bf16[256,512]{1,0:T(8,128)(2,1)} collective-permute-done((bf16[256,512]{1,0:T(8,128)(2,1)}, bf16[256,512]{1,0:T(8,128)(2,1)}, u32[]{:S(2)}, u32[]{:S(2)}) %collective-permute-start.6) | collective-permute-done | bytes 262176 | tf_op jit(solution)/shard_map/ppermute | solution.py:216
  77.3 2.2 %grad_left.1 = bf16[16,2048]{1,0:T(8,128)(2,1)S(1)} custom-call(bf16[4,256,512]{2,1,0:T(8,128)(2,1)S(1)} %get-tuple-element.4.refs_0_, bf16[256,512]{1,0:T(8,128)(2,1)S(1)} %collective-permute-done.5.refs_1_, bf16[256,512]{1,0:T(8,128)(2,1)} %collective-permute-done.6.refs_2_, bf16[256,512]{1,0:T(8,128)(2,1)} %collective-permute-done.7.refs_3_, ...), custom_call_target="tpu_custom_call" | custom-call | flops 536870912 | bytes 2097152 | tf_op jit(solution)/shard_map/grad_left/pallas_call | solution.py:174
  82.0 4.5 %collective-permute-start.17 = (bf16[16,3584]{1,0:T(8,128)(2,1)S(1)}, bf16[16,3584]{1,0:T(8,128)(2,1)S(1)}, u32[]{:S(2)}, u32[]{:S(2)}) collective-permute-start(bf16[16,3584]{1,0:T(8,128)(2,1)S(1)} %get-tuple-element.13), channel_id=1, source_target_pairs={{0,4},{4,0},{8,12},{12,8},{1,5},{5,1},{9,13},{13,9},{2,6},{6,2},{1... | collective-permute-start | bytes 344072 | tf_op jit(solution)/shard_map/ppermute | solution.py:216
  86.5 1.7 %collective-permute-start.18 = (bf16[16,3584]{1,0:T(8,128)(2,1)S(1)}, bf16[16,3584]{1,0:T(8,128)(2,1)S(1)}, u32[]{:S(2)}, u32[]{:S(2)}) collective-permute-start(bf16[16,3584]{1,0:T(8,128)(2,1)S(1)} %get-tuple-element.15), channel_id=1, source_target_pairs={{0,8},{4,12},{8,0},{12,4},{1,9},{5,13},{9,1},{13,5},{2,10},{6,14},... | collective-permute-start | bytes 344072 | tf_op jit(solution)/shard_map/ppermute | solution.py:216
  91.3 2.1 %collective-permute-done.10.refs_3_ = bf16[16,512]{1,0:T(8,128)(2,1)S(1)} collective-permute-done((bf16[16,512]{1,0:T(8,128)(2,1)S(1)}, bf16[16,512]{1,0:T(8,128)(2,1)S(1)}, u32[]{:S(2)}, u32[]{:S(2)}) %collective-permute-start.10) | collective-permute-done | bytes 16416 | tf_op jit(solution)/shard_map/ppermute | solution.py:216
  94.3 2.8 %collective-permute-done.9.refs_2_ = bf16[16,512]{1,0:T(8,128)(2,1)S(1)} collective-permute-done((bf16[16,512]{1,0:T(8,128)(2,1)S(1)}, bf16[16,512]{1,0:T(8,128)(2,1)S(1)}, u32[]{:S(2)}, u32[]{:S(2)}) %collective-permute-start.9) | collective-permute-done | bytes 16416 | tf_op jit(solution)/shard_map/ppermute | solution.py:216
  97.7 1.7 %place.1 = f32[16,2048]{1,0:T(8,128)} custom-call(s32[1]{0:T(128)} %bitcast.c_ref, bf16[16,512]{1,0:T(8,128)(2,1)} %get-tuple-element.25.refs_0_, bf16[16,512]{1,0:T(8,128)(2,1)} %copy-done.2, bf16[16,512]{1,0:T(8,128)(2,1)} %copy-done.3, bf16[16,512]{1,0:T(8,128)(2,1)} %copy-done.1), custom_call_target="tpu_custom_call" | custom-call | tf_op jit(solution)/shard_map/place/pallas_call | solution.py:204
  (63 shorter events, 20.1 us)
Async XLA Ops:
  0.6 29.9 %collective-permute-start.1 = (bf16[128,2048]{1,0:T(8,128)(2,1)}, bf16[128,2048]{1,0:T(8,128)(2,1)S(1)}, u32[]{:S(2)}, u32[]{:S(2)}) collective-permute-start(bf16[128,2048]{1,0:T(8,128)(2,1)} %refs_4_.3), channel_id=1, source_target_pairs={{0,2},{2,0},{1,3},{3,1},{4,6},{6,4},{5,7},{7,5},{8,10},{10,8},{9,1... | collective-permute-start | bytes 1572872 | tf_op jit(solution)/shard_map/ppermute | solution.py:216
  3.6 27.5 %collective-permute-start = (bf16[128,2048]{1,0:T(8,128)(2,1)}, bf16[128,2048]{1,0:T(8,128)(2,1)S(1)}, u32[]{:S(2)}, u32[]{:S(2)}) collective-permute-start(bf16[128,2048]{1,0:T(8,128)(2,1)} %refs_4_.3), channel_id=1, source_target_pairs={{0,1},{1,0},{2,3},{3,2},{4,5},{5,4},{6,7},{7,6},{8,9},{9,8},{10,11... | collective-permute-start | bytes 1572872 | tf_op jit(solution)/shard_map/ppermute | solution.py:216
  5.5 7.6 %collective-permute-start.3 = (bf16[8,14336]{1,0:T(8,128)(2,1)}, bf16[8,14336]{1,0:T(8,128)(2,1)S(1)}, u32[]{:S(2)}, u32[]{:S(2)}) collective-permute-start(bf16[8,14336]{1,0:T(8,128)(2,1)} %get-tuple-element.20), channel_id=1, source_target_pairs={{0,0},{1,4},{2,8},{3,12},{4,1},{5,5},{6,9},{7,13},{8,2},{9,6},{10,... | collective-permute-start | bytes 688136 | tf_op jit(solution)/shard_map/ppermute | solution.py:247
  7.1 13.7 %collective-permute-start.4 = (bf16[8,14336]{1,0:T(8,128)(2,1)}, bf16[8,14336]{1,0:T(8,128)(2,1)}, u32[]{:S(2)}, u32[]{:S(2)}) collective-permute-start(bf16[8,14336]{1,0:T(8,128)(2,1)} %get-tuple-element.21), channel_id=1, source_target_pairs={{0,8},{1,12},{2,0},{3,4},{4,9},{5,13},{6,1},{7,5},{8,10},{9,14},{1... | collective-permute-start | bytes 688136 | tf_op jit(solution)/shard_map/ppermute | solution.py:247
  11.6 1.0 %copy-start = (bf16[128,2048]{1,0:T(8,128)(2,1)S(1)}, bf16[128,2048]{1,0:T(8,128)(2,1)}, u32[]{:S(2)}) copy-start(bf16[128,2048]{1,0:T(8,128)(2,1)} %refs_4_.3) | copy-start | bytes 1572868
  30.6 2.0 %collective-permute-start.2 = (bf16[128,2048]{1,0:T(8,128)(2,1)S(1)}, bf16[128,2048]{1,0:T(8,128)(2,1)S(1)}, u32[]{:S(2)}, u32[]{:S(2)}) collective-permute-start(bf16[128,2048]{1,0:T(8,128)(2,1)S(1)} %collective-permute-done.1.refs_2_.refs_6_), channel_id=1, source_target_pairs={{0,1},{1,0},{2,3},{3,2},{4,5},{5,4},{6,7},{7,6},{8,9},{9,8},{10,11... | collective-permute-start | bytes 1572872 | tf_op jit(solution)/shard_map/ppermute | solution.py:216
  33.0 16.0 %collective-permute-start.12 = (bf16[256,512]{1,0:T(8,128)(2,1)S(1)}, bf16[256,512]{1,0:T(8,128)(2,1)S(1)}, u32[]{:S(2)}, u32[]{:S(2)}) collective-permute-start(bf16[256,512]{1,0:T(8,128)(2,1)S(1)} %pad_maximum_fusion.3.hid_ref.refs_0_), channel_id=1, source_target_pairs={{0,8},{4,12},{8,0},{12,4},{1,9},{5,13},{9,1},{13,5},{2,10},{6,14},... | collective-permute-start | bytes 786440 | tf_op jit(solution)/shard_map/ppermute | solution.py:216
  36.0 22.5 %collective-permute-start.11 = (bf16[256,512]{1,0:T(8,128)(2,1)S(1)}, bf16[256,512]{1,0:T(8,128)(2,1)S(1)}, u32[]{:S(2)}, u32[]{:S(2)}) collective-permute-start(bf16[256,512]{1,0:T(8,128)(2,1)S(1)} %pad_maximum_fusion.3.hid_ref.refs_0_), channel_id=1, source_target_pairs={{0,4},{4,0},{8,12},{12,8},{1,5},{5,1},{9,13},{13,9},{2,6},{6,2},{1... | collective-permute-start | bytes 786440 | tf_op jit(solution)/shard_map/ppermute | solution.py:216
  49.1 9.4 %collective-permute-start.13 = (bf16[256,512]{1,0:T(8,128)(2,1)S(1)}, bf16[256,512]{1,0:T(8,128)(2,1)S(1)}, u32[]{:S(2)}, u32[]{:S(2)}) collective-permute-start(bf16[256,512]{1,0:T(8,128)(2,1)S(1)} %collective-permute-done.12.refs_2_), channel_id=1, source_target_pairs={{0,4},{4,0},{8,12},{12,8},{1,5},{5,1},{9,13},{13,9},{2,6},{6,2},{1... | collective-permute-start | bytes 786440 | tf_op jit(solution)/shard_map/ppermute | solution.py:216
  53.8 13.8 %collective-permute-start.5 = (bf16[256,512]{1,0:T(8,128)(2,1)S(1)}, bf16[256,512]{1,0:T(8,128)(2,1)S(1)}, u32[]{:S(2)}, u32[]{:S(2)}) collective-permute-start(bf16[256,512]{1,0:T(8,128)(2,1)S(1)} %get-tuple-element.12), channel_id=1, source_target_pairs={{0,4},{4,0},{8,12},{12,8},{1,5},{5,1},{9,13},{13,9},{2,6},{6,2},{1... | collective-permute-start | bytes 786440 | tf_op jit(solution)/shard_map/ppermute | solution.py:216
  55.6 21.7 %collective-permute-start.6 = (bf16[256,512]{1,0:T(8,128)(2,1)}, bf16[256,512]{1,0:T(8,128)(2,1)}, u32[]{:S(2)}, u32[]{:S(2)}) collective-permute-start(bf16[256,512]{1,0:T(8,128)(2,1)} %get-tuple-element.11), channel_id=1, source_target_pairs={{0,8},{4,12},{8,0},{12,4},{1,9},{5,13},{9,1},{13,5},{2,10},{6,14},... | collective-permute-start | bytes 786440 | tf_op jit(solution)/shard_map/ppermute | solution.py:216
  57.0 20.3 %collective-permute-start.7 = (bf16[256,512]{1,0:T(8,128)(2,1)}, bf16[256,512]{1,0:T(8,128)(2,1)}, u32[]{:S(2)}, u32[]{:S(2)}) collective-permute-start(bf16[256,512]{1,0:T(8,128)(2,1)} %get-tuple-element.10), channel_id=1, source_target_pairs={{0,12},{4,8},{8,4},{12,0},{1,13},{5,9},{9,5},{13,1},{2,14},{6,10},... | collective-permute-start | bytes 786440 | tf_op jit(solution)/shard_map/ppermute | solution.py:216
  61.4 19.4 %collective-permute-start.14 = (bf16[16,3584]{1,0:T(8,128)(2,1)}, bf16[16,3584]{1,0:T(8,128)(2,1)}, u32[]{:S(2)}, u32[]{:S(2)}) collective-permute-start(bf16[16,3584]{1,0:T(8,128)(2,1)} %get-tuple-element.19), channel_id=1, source_target_pairs={{0,1},{1,0},{2,3},{3,2},{4,5},{5,4},{6,7},{7,6},{8,9},{9,8},{10,11... | collective-permute-start | bytes 344072 | tf_op jit(solution)/shard_map/ppermute | solution.py:216
  61.4 19.4 %collective-permute-start.15 = (bf16[16,3584]{1,0:T(8,128)(2,1)}, bf16[16,3584]{1,0:T(8,128)(2,1)}, u32[]{:S(2)}, u32[]{:S(2)}) collective-permute-start(bf16[16,3584]{1,0:T(8,128)(2,1)} %get-tuple-element.18), channel_id=1, source_target_pairs={{0,2},{1,3},{2,0},{3,1},{4,6},{5,7},{6,4},{7,5},{8,10},{9,11},{10,... | collective-permute-start | bytes 344072 | tf_op jit(solution)/shard_map/ppermute | solution.py:216
  67.7 13.1 %collective-permute-start.16 = (bf16[16,3584]{1,0:T(8,128)(2,1)}, bf16[16,3584]{1,0:T(8,128)(2,1)}, u32[]{:S(2)}, u32[]{:S(2)}) collective-permute-start(bf16[16,3584]{1,0:T(8,128)(2,1)} %get-tuple-element.17), channel_id=1, source_target_pairs={{0,3},{1,2},{2,1},{3,0},{4,7},{5,6},{6,5},{7,4},{8,11},{9,10},{10,... | collective-permute-start | bytes 344072 | tf_op jit(solution)/shard_map/ppermute | solution.py:216
  82.0 17.4 %collective-permute-start.17 = (bf16[16,3584]{1,0:T(8,128)(2,1)S(1)}, bf16[16,3584]{1,0:T(8,128)(2,1)S(1)}, u32[]{:S(2)}, u32[]{:S(2)}) collective-permute-start(bf16[16,3584]{1,0:T(8,128)(2,1)S(1)} %get-tuple-element.13), channel_id=1, source_target_pairs={{0,4},{4,0},{8,12},{12,8},{1,5},{5,1},{9,13},{13,9},{2,6},{6,2},{1... | collective-permute-start | bytes 344072 | tf_op jit(solution)/shard_map/ppermute | solution.py:216
  86.5 12.9 %collective-permute-start.18 = (bf16[16,3584]{1,0:T(8,128)(2,1)S(1)}, bf16[16,3584]{1,0:T(8,128)(2,1)S(1)}, u32[]{:S(2)}, u32[]{:S(2)}) collective-permute-start(bf16[16,3584]{1,0:T(8,128)(2,1)S(1)} %get-tuple-element.15), channel_id=1, source_target_pairs={{0,8},{4,12},{8,0},{12,4},{1,9},{5,13},{9,1},{13,5},{2,10},{6,14},... | collective-permute-start | bytes 344072 | tf_op jit(solution)/shard_map/ppermute | solution.py:216
  88.2 11.2 %collective-permute-start.19 = (bf16[16,3584]{1,0:T(8,128)(2,1)S(1)}, bf16[16,3584]{1,0:T(8,128)(2,1)S(1)}, u32[]{:S(2)}, u32[]{:S(2)}) collective-permute-start(bf16[16,3584]{1,0:T(8,128)(2,1)S(1)} %get-tuple-element.14), channel_id=1, source_target_pairs={{0,12},{4,8},{8,4},{12,0},{1,13},{5,9},{9,5},{13,1},{2,14},{6,10},... | collective-permute-start | bytes 344072 | tf_op jit(solution)/shard_map/ppermute | solution.py:216
  90.2 3.2 %collective-permute-start.10 = (bf16[16,512]{1,0:T(8,128)(2,1)S(1)}, bf16[16,512]{1,0:T(8,128)(2,1)S(1)}, u32[]{:S(2)}, u32[]{:S(2)}) collective-permute-start(bf16[16,512]{1,0:T(8,128)(2,1)S(1)} %get-tuple-element.22), channel_id=1, source_target_pairs={{0,3},{1,2},{2,1},{3,0},{4,7},{5,6},{6,5},{7,4},{8,11},{9,10},{10,... | collective-permute-start | bytes 49160 | tf_op jit(solution)/shard_map/ppermute | solution.py:216
  90.2 4.1 %collective-permute-start.8 = (bf16[16,512]{1,0:T(8,128)(2,1)S(1)}, bf16[16,512]{1,0:T(8,128)(2,1)S(1)}, u32[]{:S(2)}, u32[]{:S(2)}) collective-permute-start(bf16[16,512]{1,0:T(8,128)(2,1)S(1)} %get-tuple-element.24), channel_id=1, source_target_pairs={{0,1},{1,0},{2,3},{3,2},{4,5},{5,4},{6,7},{7,6},{8,9},{9,8},{10,11... | collective-permute-start | bytes 49160 | tf_op jit(solution)/shard_map/ppermute | solution.py:216
  93.3 3.7 %copy-start.1 = (bf16[16,512]{1,0:T(8,128)(2,1)}, bf16[16,512]{1,0:T(8,128)(2,1)S(1)}, u32[]{:S(2)}) copy-start(bf16[16,512]{1,0:T(8,128)(2,1)S(1)} %collective-permute-done.10.refs_3_) | copy-start | bytes 49156
  93.3 3.7 %collective-permute-start.9 = (bf16[16,512]{1,0:T(8,128)(2,1)S(1)}, bf16[16,512]{1,0:T(8,128)(2,1)S(1)}, u32[]{:S(2)}, u32[]{:S(2)}) collective-permute-start(bf16[16,512]{1,0:T(8,128)(2,1)S(1)} %get-tuple-element.23), channel_id=1, source_target_pairs={{0,2},{1,3},{2,0},{3,1},{4,6},{5,7},{6,4},{7,5},{8,10},{9,11},{10,... | collective-permute-start | bytes 49160 | tf_op jit(solution)/shard_map/ppermute | solution.py:216
  94.3 2.8 %copy-start.2 = (bf16[16,512]{1,0:T(8,128)(2,1)}, bf16[16,512]{1,0:T(8,128)(2,1)S(1)}, u32[]{:S(2)}) copy-start(bf16[16,512]{1,0:T(8,128)(2,1)S(1)} %collective-permute-done.8.refs_1_) | copy-start | bytes 49156
  97.1 0.6 copy-start.3

commit v4 on v3

v4 whole, which is shorter than its diff:
```python
import functools

import jax
import jax.numpy as jnp
from jax import lax
from jax.experimental import pallas as pl
from jax.experimental.pallas import tpu as pltpu
from jax.sharding import PartitionSpec as P

D = 8192
F = 14336
NB = 64
BI = D // NB
FB = F // NB
GROUP = 4
COLS = GROUP * FB
BF = jnp.bfloat16
F32 = jnp.float32
NT = (((1,), (1,)), ((), ()))
TN = (((0,), (0,)), ((), ()))
SPLIT = 4
VMEM = 40 * 1024 * 1024


def cost(flops, nbytes):
    return pl.CostEstimate(flops=flops, bytes_accessed=nbytes, transcendentals=0)


def rows_of(refs):
    return jnp.concatenate([r[...] for r in refs], axis=0) if len(refs) > 1 else refs[0][...]


def spread(right):
    n_z, n_k, n_b, _ = right.shape
    rows = n_z * n_k * n_b
    tile = (
        lax.broadcasted_iota(jnp.int32, (FB, COLS), 0)
        == lax.broadcasted_iota(jnp.int32, (FB, COLS), 1) % FB
    )
    wide = jnp.dot(right.reshape(rows, FB), tile.astype(F32).astype(BF), preferred_element_type=F32)
    k_row = lax.broadcasted_iota(jnp.int32, (rows, COLS), 0) // n_b % n_k
    k_col = lax.broadcasted_iota(jnp.int32, (rows, COLS), 1) // FB
    return jnp.where(k_row == k_col, wide, 0.0).astype(BF)


def back_kernel(scale, n_tok, n_hid, n_z, z_ref, *refs):
    tok_refs, refs = refs[:n_tok], refs[n_tok:]
    hid_refs, refs = refs[:n_hid], refs[n_hid:]
    teacher_refs, right_refs, (back_ref, own_ref) = refs[:SPLIT], refs[SPLIT:-2], refs[-2:]
    right = jnp.stack(
        [jnp.concatenate([a[0, :, 0], b[0, :, 0]], axis=0) for a, b in zip(right_refs[:n_z], right_refs[n_z:])],
        axis=0,
    )
    right = spread(right)
    rows = right.shape[0] // n_z
    own_ref[0] = right[:rows]
    folded = jnp.concatenate(
        [lax.dot_general(t[...], right, NT, preferred_element_type=F32).astype(BF) for t in teacher_refs],
        axis=0,
    )
    square = lax.dot_general(right[:rows], right, NT, preferred_element_type=F32).astype(BF)
    hid = jnp.concatenate([h[...] for h in hid_refs], axis=1)
    back = lax.dot_general(hid, square, TN, preferred_element_type=F32) - jnp.dot(
        rows_of(tok_refs), folded, preferred_element_type=F32
    )
    back_ref[...] = (back * scale).T.astype(BF).reshape(back_ref.shape)


def back_partial(z, tokens, hidden, teacher, sides, scale):
    piece, depth = tokens[0].shape
    t = piece * len(tokens)
    cols = teacher.shape[1]
    n_q, half, n_z, n_b, _ = sides[0].shape
    rows = GROUP * n_b
    right_specs = [
        pl.BlockSpec((1, half, 1, n_b, FB), lambda q, z, s=s: (q, 0, z[0] ^ s, 0, 0)) for s in range(n_z)
    ]
    return pl.pallas_call(
        functools.partial(back_kernel, scale, len(tokens), len(hidden), n_z),
        grid_spec=pltpu.PrefetchScalarGridSpec(
            num_scalar_prefetch=1,
            grid=(n_q,),
            in_specs=[pl.BlockSpec((piece, depth), lambda q, z: (0, 0))] * len(tokens)
            + [pl.BlockSpec((rows, h.shape[1]), lambda q, z: (q, 0)) for h in hidden]
            + [pl.BlockSpec((depth // SPLIT, COLS), lambda q, z, i=i: (i, q)) for i in range(SPLIT)]
            + right_specs * 2,
            out_specs=[
                pl.BlockSpec((n_z, rows, t), lambda q, z: (0, q, 0)),
                pl.BlockSpec((1, rows, COLS), lambda q, z: (q, 0, 0)),
            ],
        ),
        out_shape=[
            jax.ShapeDtypeStruct((n_z, n_q * rows, t), BF),
            jax.ShapeDtypeStruct((n_q, rows, COLS), BF),
        ],
        compiler_params=pltpu.CompilerParams(vmem_limit_bytes=VMEM),
        cost_estimate=cost(4 * t * depth * n_z * rows * n_q, 2 * depth * cols),
        name="back",
    )(z, *tokens, *hidden, *[teacher] * SPLIT, *[sides[0]] * n_z, *[sides[1]] * n_z)


def grad_right_kernel(scale, n_tok, n_z, parts, *refs):
    tok_refs, teacher_refs, refs = refs[:n_tok], refs[n_tok : n_tok + SPLIT], refs[n_tok + SPLIT :]
    hid_refs, (right_ref, out_ref) = refs[:-2], refs[-2:]
    target = jnp.dot(rows_of(tok_refs), rows_of(teacher_refs), preferred_element_type=F32)
    hid = [
        jnp.concatenate([r[...] for r in hid_refs[s * parts : (s + 1) * parts]], axis=1) for s in range(n_z)
    ]
    student = lax.dot_general(hid[0], right_ref[0], TN, preferred_element_type=F32)
    resid = ((student - target) * scale).astype(BF)
    prod = jnp.dot(jnp.concatenate(hid, axis=0), resid, preferred_element_type=F32)
    per_z = hid[0].shape[0] // GROUP
    prod = prod.reshape(n_z, GROUP, per_z, COLS)
    block = lax.broadcasted_iota(jnp.int32, (n_z, per_z, COLS), 2) // FB
    total = prod[:, 0]
    for k in range(1, GROUP):
        total = jnp.where(block == k, prod[:, k], total)
    out_ref[...] = total.astype(BF)


def grad_right_partial(tokens, teacher, hidden, right, scale):
    piece, depth = tokens[0].shape
    t = piece * len(tokens)
    cols = teacher.shape[1]
    n_z, parts = len(hidden), len(hidden[0])
    n_q, rows, _ = right.shape
    return pl.pallas_call(
        functools.partial(grad_right_kernel, scale, len(tokens), n_z, parts),
        grid=(n_q,),
        in_specs=[pl.BlockSpec((piece, depth), lambda q: (0, 0))] * len(tokens)
        + [pl.BlockSpec((depth // SPLIT, COLS), lambda q, i=i: (i, q)) for i in range(SPLIT)]
        + [pl.BlockSpec((rows, h.shape[1]), lambda q: (q, 0)) for hs in hidden for h in hs]
        + [pl.BlockSpec((1, rows, COLS), lambda q: (q, 0, 0))],
        out_specs=pl.BlockSpec((n_z, rows // GROUP, COLS), lambda q: (0, 0, q)),
        out_shape=jax.ShapeDtypeStruct((n_z, rows // GROUP, cols), BF),
        compiler_params=pltpu.CompilerParams(vmem_limit_bytes=VMEM),
        cost_estimate=cost(2 * t * cols * (depth + n_z * rows), 2 * depth * cols),
        name="grad_right",
    )(*tokens, *[teacher] * SPLIT, *[h for hs in hidden for h in hs], right)


def grad_left_kernel(n_z, n_k, *refs):
    back_refs, tok_refs, out_ref = refs[:n_z], refs[n_z:-1], refs[-1]
    total = back_refs[0][0].astype(F32)
    for ref in back_refs[1:]:
        total = total + ref[...].astype(F32)
    prod = jnp.dot(total.astype(BF), rows_of(tok_refs), preferred_element_type=F32)
    rows, block = prod.shape
    prod = prod.reshape(n_k, rows // n_k, block)
    at = pl.program_id(0) * (block // BI)
    own = lax.broadcasted_iota(jnp.int32, prod.shape, 1) == at + lax.broadcasted_iota(
        jnp.int32, prod.shape, 2
    ) // BI
    out_ref[...] = jnp.where(own, prod, 0.0).sum(1).astype(BF)


def grad_left_of(backs, tokens, n_k):
    n_z = len(backs)
    rows, t = backs[1].shape
    piece, depth = tokens[0].shape
    block = min(depth, 1024)
    return pl.pallas_call(
        functools.partial(grad_left_kernel, n_z, n_k),
        grid=(depth // block,),
        in_specs=[pl.BlockSpec((1, rows, t), lambda q: (0, 0, 0))]
        + [pl.BlockSpec((rows, t), lambda q: (0, 0))] * (n_z - 1)
        + [pl.BlockSpec((piece, block), lambda q: (0, q))] * len(tokens),
        out_specs=pl.BlockSpec((n_k, block), lambda q: (0, q)),
        out_shape=jax.ShapeDtypeStruct((n_k, depth), BF),
        compiler_params=pltpu.CompilerParams(vmem_limit_bytes=VMEM),
        cost_estimate=cost(2 * t * rows * depth, 2 * t * depth),
        name="grad_left",
    )(*backs, *tokens)


def place_kernel(n_b, c_ref, *refs):
    in_refs, out_ref = refs[:-1], refs[-1]
    n_c, n_k = len(in_refs), in_refs[0].shape[0]
    x = rows_of(in_refs)
    row = lax.broadcasted_iota(jnp.int32, (NB, NB), 0)
    col = lax.broadcasted_iota(jnp.int32, (NB, NB), 1)
    pick = row == ((col // n_k) ^ c_ref[0]) * n_k + col % n_k
    got = lax.dot_general(
        x, pick.astype(F32).astype(BF), (((0,), (1,)), ((), ())), preferred_element_type=F32
    )
    for j in range(got.shape[0] // n_b):
        out_ref[:, j * NB : (j + 1) * NB] = got[j * n_b : (j + 1) * n_b]


def place(c, pieces, n_b):
    n = pieces[0].shape[1] // n_b
    return pl.pallas_call(
        functools.partial(place_kernel, n_b),
        in_specs=[pl.BlockSpec(memory_space=pltpu.SMEM)]
        + [pl.BlockSpec(memory_space=pltpu.VMEM)] * len(pieces),
        out_specs=pl.BlockSpec(memory_space=pltpu.VMEM),
        out_shape=jax.ShapeDtypeStruct((n_b, n * NB), F32),
        name="place",
    )(c, *pieces)


def swap(x, axes, s):
    n = lax.axis_size(axes)
    return lax.ppermute(x, axes, [(i, i ^ s) for i in range(n)])


def gather(x, axes):
    got = [x]
    for s in range(1, lax.axis_size(axes)):
        got.append(swap(got[s & (s - 1)], axes, s & -s))
    return got


def pick(x, at):
    return lax.dynamic_index_in_dim(x, at, 0, keepdims=False)


def per_device(tokens, teacher, left_blocks, right_blocks):
    n_z = lax.axis_size("blk")
    n_c = lax.axis_size(("tok", "rep"))
    z = lax.axis_index("blk")
    c = lax.axis_index(("tok", "rep"))
    plane = ("tok", "rep")
    n_b = left_blocks.shape[0]
    n_k = teacher.shape[1] // FB
    n_q = n_k // GROUP
    scale = float(tokens.shape[0] * n_c) ** (-0.5)

    sides = right_blocks.reshape(n_q, 2, GROUP // 2, n_z, n_b, FB)
    perms = [
        [(a * n_c + b, (b ^ side) * n_c + a) for a in range(n_z) for b in range(n_c)] for side in (0, n_c // 2)
    ]
    sides = [lax.ppermute(sides[:, i], ("blk",) + plane, perm) for i, perm in enumerate(perms)]

    chips = [gather(own, "rep") for own in gather(tokens, "tok")]
    pieces = [p for chip in chips for p in chip]

    left = left_blocks.reshape(n_b * BI, NB)
    rows_kb = n_k * n_b
    take = (
        lax.broadcasted_iota(jnp.int32, (rows_kb, NB), 0) // n_b + c * n_k
        == lax.broadcasted_iota(jnp.int32, (rows_kb, NB), 1)
    ).astype(BF)
    diag = (
        lax.broadcasted_iota(jnp.int32, (rows_kb, n_b * BI), 0) % n_b
        == lax.broadcasted_iota(jnp.int32, (rows_kb, n_b * BI), 1) // BI
    )
    left = lax.dot_general(take, left, NT, preferred_element_type=F32)
    left = jnp.where(diag, left, 0.0).astype(BF)

    hid = [
        jnp.concatenate(
            [lax.dot_general(left, p, NT, preferred_element_type=F32).astype(BF) for p in chip], axis=1
        )
        for chip in chips
    ]
    hidden = list(zip(*[gather(h, "blk") for h in hid]))
    back, own = back_partial(jnp.reshape(z, (1,)).astype(jnp.int32), pieces, hid, teacher, sides, scale)
    backs = [back] + [swap(back[s], "blk", s) for s in range(1, n_z)]

    gl = grad_left_of(backs, pieces, n_k)
    gl = gl.reshape(n_k, n_b, n_c, BI // n_c).transpose(2, 0, 3, 1).reshape(n_c, n_k, -1)
    got = []
    for s in range(n_c):
        piece = pick(gl, c ^ s)
        got.append(swap(piece, plane, s) if s else piece)
    grad_left = place(jnp.reshape(c, (1,)).astype(jnp.int32), got, n_b)

    gr = grad_right_partial(pieces, teacher, hidden, own, scale)
    there = []
    for s in range(n_c):
        piece = pick(gr, z ^ c ^ s)
        there.append(swap(piece, plane, s) if s else piece)
    there = jnp.stack(there, 0)
    total = None
    for s in range(n_z):
        piece = pick(there, c ^ z ^ s)
        piece = (swap(piece, "blk", s) if s else piece).astype(F32)
        total = piece if total is None else total + piece
    grad_right = total.reshape(n_b, n_k, FB).transpose(1, 0, 2).reshape(n_k, n_b * FB)
    return grad_left, grad_right


def solution(mesh):
    return jax.shard_map(
        per_device,
        mesh=mesh,
        in_specs=(
            P(("layer", "tok", "rep"), "blk"),
            P(("layer", "blk"), ("tok", "rep")),
            P(("layer", "blk"), None),
            P(("layer", "blk"), None),
        ),
        out_specs=(P(("layer", "blk"), ("tok", "rep")), P(("layer", "blk"), ("tok", "rep"))),
        check_vma=False,
    )
```

time: 101 us -> 101 us (level)
  Pallas kernels: 22.4 us -> 34.2 us
  waiting for transfers between devices: 28.1 us -> 18.7 us
  local copies, waits for them, and re-layouts: 15.5 us -> 9.15 us
  starting transfers between devices: 28.4 us -> 33.7 us
  other arithmetic: 3.11 us -> 1.24 us
    pallas_call x4 -> x2, Pallas kernels: 18.5 us -> 30.3 us  [the longest x1 16.7 us: back_partial(): pl.pallas_call(functools.partial(back_kernel, scale, len(tokens), len(hid...]
    ppermute x2, waiting for transfers between devices: 7.69 us -> 0.01 us  [per_device(): lax.ppermute(sides[:, i], ('blk',) + plane, perm)]
    ppermute x18 -> x21, starting transfers between devices: 23.8 us -> 29.1 us  [swap(): return lax.ppermute(x, axes, [(i, i ^ s) for i in range(n)])]
    dynamic_slice x1 -> x0, local copies, waits for them, and re-layouts: 3.3 us -> none  [per_device(): lax.dynamic_index_in_dim(right, z ^ s, 1, keepdims=False)]
    slice x1 -> x0, local copies, waits for them, and re-layouts: 1.84 us -> none  [per_device(): right_blocks[i * half:(i + 1) * half]]
    concatenate x1 -> x0, other arithmetic: 1.74 us -> none  [per_device(): right = jnp.concatenate(sides, axis=0).reshape(n_k, n_z, n_b * FB)]
    another operation x4 -> x0, local copies, waits for them, and re-layouts: 1.69 us -> none  [per_device(): jnp.stack([lax.dynamic_index_in_dim(right, z ^ s, 1, keepdims=False) for...]
    ppermute x18 -> x21, waiting for transfers between devices: 20.4 us -> 18.7 us  [swap(): return lax.ppermute(x, axes, [(i, i ^ s) for i in range(n)])]
  transfers between devices with their start and end apart: 20 -> 23, of which waited for: 6 -> 8; matrix products, arithmetic and copies ran while one was open for 17% -> 8% of each run, Pallas kernels for 22% -> 34%
where the time goes in v4:
time: 101 us; the launch traced here: 100 us
  Pallas kernels  34.2 us (34%)
  starting transfers between devices  33.7 us (33%)
  waiting for transfers between devices  18.7 us (19%)
  local copies, waits for them, and re-layouts  9.15 us (9%)
  matrix products  2.23 us (2%)
  other arithmetic  1.24 us (1%)
    ppermute x21, starting transfers between devices, swap(): return lax.ppermute(x, axes, [(i, i ^ s) for i in range(n)])  29.1 us
    ppermute x21, waiting for transfers between devices, swap(): return lax.ppermute(x, axes, [(i, i ^ s) for i in range(n)])  18.7 us
    pallas_call x1, Pallas kernels, back_partial(): pl.pallas_call(functools.partial(back_kernel, scale, len(tokens), len(hid...  16.7 us
    pallas_call x1, Pallas kernels, grad_right_partial(): pl.pallas_call(functools.partial(grad_right_kernel, scale, len(tokens), n...  13.6 us
    ppermute x2, starting transfers between devices, per_device(): lax.ppermute(sides[:, i], ('blk',) + plane, perm)  4.56 us
    pallas_call x1, Pallas kernels, grad_left_of(): pl.pallas_call(functools.partial(grad_left_kernel, n_z, n_k), grid=(depth...  2.17 us
    unnamed x14, local copies, waits for them, and re-layouts  2.11 us
  transfers between devices with their start and end apart: 23, of which 8 were waited for; matrix products, arithmetic and copies ran while one was open for 8% of the time, Pallas kernels for 34%

profile of v4, /device:TPU:0, one launch (start us, length us, event | category | flops | bytes accessed | tf_op | source)
XLA Modules:
  0.0 100.2 jit_solution(11845535051446402313)
XLA Ops:
  1.2 2.6 %collective-permute-start.1 = (bf16[128,2048]{1,0:T(8,128)(2,1)}, bf16[128,2048]{1,0:T(8,128)(2,1)S(1)}, u32[]{:S(2)}, u32[]{:S(2)}) collective-permute-start(bf16[128,2048]{1,0:T(8,128)(2,1)} %refs_0_.3), channel_id=1, source_target_pairs={{0,2},{2,0},{1,3},{3,1},{4,6},{6,4},{5,7},{7,5},{8,10},{10,8},{9,1... | collective-permute-start | bytes 1572872 | tf_op jit(solution)/shard_map/ppermute | solution.py:204
  3.7 1.8 %reshape.33 = bf16[4,2,2,4,16,224]{5,4,3,2,1,0:T(8,128)(2,1)S(1)} reshape(bf16[16,14336]{1,0:T(8,128)(2,1)} %param.7) | data formatting | bytes 917504 | tf_op jit(solution)/shard_map/reshape | solution.py:229
  6.2 3.9 %collective-permute-start.4 = (bf16[4,2,4,16,224]{4,3,2,1,0:T(8,128)(2,1)S(1)}, bf16[4,2,4,16,224]{4,3,2,1,0:T(8,128)(2,1)S(1)}, u32[]{:S(2)}, u32[]{:S(2)}) collective-permute-start(bf16[4,2,4,16,224]{4,3,2,1,0:T(8,128)(2,1)S(1)} %get-tuple-element.9), channel_id=1, source_target_pairs={{0,8},{1,12},{2,0},{3,4},{4,9},{5,13},{6,1},{7,5},{8,10},{9,14},{1... | collective-permute-start | bytes 688136 | tf_op jit(solution)/shard_map/ppermute | solution.py:233
  12.2 8.6 %collective-permute-done.1.refs_2_.refs_6_ = bf16[128,2048]{1,0:T(8,128)(2,1)S(1)} collective-permute-done((bf16[128,2048]{1,0:T(8,128)(2,1)}, bf16[128,2048]{1,0:T(8,128)(2,1)S(1)}, u32[]{:S(2)}, u32[]{:S(2)}) %collective-permute-start.1) | collective-permute-done | bytes 524320 | tf_op jit(solution)/shard_map/ppermute | solution.py:204
  21.3 2.2 %collective-permute-start.11 = (bf16[256,256]{1,0:T(8,128)(2,1)S(1)}, bf16[256,256]{1,0:T(8,128)(2,1)S(1)}, u32[]{:S(2)}, u32[]{:S(2)}) collective-permute-start(bf16[256,256]{1,0:T(8,128)(2,1)S(1)} %pad_maximum_fusion.1.refs_4_.refs_8_), channel_id=1, source_target_pairs={{0,4},{4,0},{8,12},{12,8},{1,5},{5,1},{9,13},{13,9},{2,6},{6,2},{1... | collective-permute-start | bytes 393224 | tf_op jit(solution)/shard_map/ppermute | solution.py:204
  23.6 2.7 %collective-permute-start.13 = (bf16[256,256]{1,0:T(8,128)(2,1)S(1)}, bf16[256,256]{1,0:T(8,128)(2,1)S(1)}, u32[]{:S(2)}, u32[]{:S(2)}) collective-permute-start(bf16[256,256]{1,0:T(8,128)(2,1)S(1)} %pad_maximum_fusion.1.refs_4_.refs_8_), channel_id=1, source_target_pairs={{0,8},{4,12},{8,0},{12,4},{1,9},{5,13},{9,1},{13,5},{2,10},{6,14},... | collective-permute-start | bytes 393224 | tf_op jit(solution)/shard_map/ppermute | solution.py:204
  26.7 3.6 %collective-permute-done.13.refs_12_ = bf16[256,256]{1,0:T(8,128)(2,1)S(1)} collective-permute-done((bf16[256,256]{1,0:T(8,128)(2,1)S(1)}, bf16[256,256]{1,0:T(8,128)(2,1)S(1)}, u32[]{:S(2)}, u32[]{:S(2)}) %collective-permute-start.13) | collective-permute-done | bytes 131104 | tf_op jit(solution)/shard_map/ppermute | solution.py:204
  30.2 3.7 %collective-permute-start.15 = (bf16[256,256]{1,0:T(8,128)(2,1)S(1)}, bf16[256,256]{1,0:T(8,128)(2,1)S(1)}, u32[]{:S(2)}, u32[]{:S(2)}) collective-permute-start(bf16[256,256]{1,0:T(8,128)(2,1)S(1)} %collective-permute-done.13.refs_12_), channel_id=1, source_target_pairs={{0,4},{4,0},{8,12},{12,8},{1,5},{5,1},{9,13},{13,9},{2,6},{6,2},{1... | collective-permute-start | bytes 393224 | tf_op jit(solution)/shard_map/ppermute | solution.py:204
  34.5 2.7 %collective-permute-start.14 = (bf16[256,256]{1,0:T(8,128)(2,1)S(1)}, bf16[256,256]{1,0:T(8,128)(2,1)S(1)}, u32[]{:S(2)}, u32[]{:S(2)}) collective-permute-start(bf16[256,256]{1,0:T(8,128)(2,1)S(1)} %pad_maximum_fusion.2.refs_5_.refs_9_), channel_id=1, source_target_pairs={{0,8},{4,12},{8,0},{12,4},{1,9},{5,13},{9,1},{13,5},{2,10},{6,14},... | collective-permute-start | bytes 393224 | tf_op jit(solution)/shard_map/ppermute | solution.py:204
  37.2 16.7 %back.1 = (bf16[4,256,512]{2,1,0:T(8,128)(2,1)S(1)}, bf16[4,64,896]{2,1,0:T(8,128)(2,1)S(1)}) custom-call(s32[1]{0:T(128)} %bitcast.1.z_ref, bf16[128,2048]{1,0:T(8,128)(2,1)S(1)} %copy-done, bf16[128,2048]{1,0:T(8,128)(2,1)S(1)} %collective-permute-done.refs_1_.refs_5_, bf16[128,2048]{1,0:T(8,128)(2,1)S(1)} %collective-permute-done.1.refs_2_.refs_6_, ...), custom_call_target="tpu_custom_call" | custom-call | flops 4294967296 | bytes 14680064 | tf_op jit(solution)/shard_map/back/pallas_call | solution.py:78
  54.0 2.0 %collective-permute-start.16 = (bf16[256,256]{1,0:T(8,128)(2,1)S(1)}, bf16[256,256]{1,0:T(8,128)(2,1)S(1)}, u32[]{:S(2)}, u32[]{:S(2)}) collective-permute-start(bf16[256,256]{1,0:T(8,128)(2,1)S(1)} %collective-permute-done.14.refs_13_), channel_id=1, source_target_pairs={{0,4},{4,0},{8,12},{12,8},{1,5},{5,1},{9,13},{13,9},{2,6},{6,2},{1... | collective-permute-start | bytes 393224 | tf_op jit(solution)/shard_map/ppermute | solution.py:204
  56.8 1.0 copy-done.1
  58.2 4.0 %collective-permute-start.7 = (bf16[256,512]{1,0:T(8,128)(2,1)}, bf16[256,512]{1,0:T(8,128)(2,1)}, u32[]{:S(2)}, u32[]{:S(2)}) collective-permute-start(bf16[256,512]{1,0:T(8,128)(2,1)} %get-tuple-element.6), channel_id=1, source_target_pairs={{0,12},{4,8},{8,4},{12,0},{1,13},{5,9},{9,5},{13,1},{2,14},{6,10},... | collective-permute-start | bytes 786440 | tf_op jit(solution)/shard_map/ppermute | solution.py:204
  62.2 13.6 %grad_right.1 = bf16[4,16,3584]{2,1,0:T(8,128)(2,1)S(1)} custom-call(bf16[128,2048]{1,0:T(8,128)(2,1)S(1)} %copy-done, bf16[128,2048]{1,0:T(8,128)(2,1)S(1)} %collective-permute-done.refs_1_.refs_5_, bf16[128,2048]{1,0:T(8,128)(2,1)S(1)} %collective-permute-done.1.refs_2_.refs_6_, bf16[128,2048]{1,0:T(8,128)(2,1)S(1)} %collective-permute-done.2.refs_3_.refs_7_, ...), custom_call_target="tpu_custom_call" | custom-call | flops 8455716864 | bytes 14680064 | tf_op jit(solution)/shard_map/grad_right/pallas_call | solution.py:127
  76.6 2.5 %collective-permute-start.18 = (bf16[16,3584]{1,0:T(8,128)(2,1)}, bf16[16,3584]{1,0:T(8,128)(2,1)}, u32[]{:S(2)}, u32[]{:S(2)}) collective-permute-start(bf16[16,3584]{1,0:T(8,128)(2,1)} %get-tuple-element.16), channel_id=1, source_target_pairs={{0,2},{1,3},{2,0},{3,1},{4,6},{5,7},{6,4},{7,5},{8,10},{9,11},{10,... | collective-permute-start | bytes 344072 | tf_op jit(solution)/shard_map/ppermute | solution.py:204
  79.3 2.2 %grad_left.1 = bf16[16,2048]{1,0:T(8,128)(2,1)S(1)} custom-call(bf16[4,256,512]{2,1,0:T(8,128)(2,1)S(1)} %copy-done.2, bf16[256,512]{1,0:T(8,128)(2,1)S(1)} %collective-permute-done.5.refs_1_, bf16[256,512]{1,0:T(8,128)(2,1)} %collective-permute-done.6.refs_2_, bf16[256,512]{1,0:T(8,128)(2,1)} %collective-permute-done.7.refs_3_, ...), custom_call_target="tpu_custom_call" | custom-call | flops 536870912 | bytes 2097152 | tf_op jit(solution)/shard_map/grad_left/pallas_call | solution.py:162
  82.7 2.1 %collective-permute-done.18 = bf16[16,3584]{1,0:T(8,128)(2,1)} collective-permute-done((bf16[16,3584]{1,0:T(8,128)(2,1)}, bf16[16,3584]{1,0:T(8,128)(2,1)}, u32[]{:S(2)}, u32[]{:S(2)}) %collective-permute-start.18) | collective-permute-done | bytes 114720 | tf_op jit(solution)/shard_map/ppermute | solution.py:204
  84.8 1.1 %pad_maximum_fusion = bf16[4,16,3584]{2,1,0:T(8,128)(2,1)S(1)} fusion(bf16[1,16,3584]{2,1,0:T(8,128)(2,1)} %bitcast.17, bf16[1,16,3584]{2,1,0:T(8,128)(2,1)} %bitcast.15, bf16[1,16,3584]{2,1,0:T(8,128)(2,1)} %bitcast.13, bf16[1,16,3584]{2,1,0:T(8,128)(2,1)} %get-tuple-element.14), kind=kLoop, calls=%fused_computation.7 | loop fusion | flops 688128 | bytes 917504 | tf_op jit(solution)/shard_map/stack | solution.py:274
  86.0 1.4 %collective-permute-start.22 = (bf16[16,3584]{1,0:T(8,128)(2,1)S(1)}, bf16[16,3584]{1,0:T(8,128)(2,1)S(1)}, u32[]{:S(2)}, u32[]{:S(2)}) collective-permute-start(bf16[16,3584]{1,0:T(8,128)(2,1)S(1)} %get-tuple-element.12), channel_id=1, source_target_pairs={{0,12},{4,8},{8,4},{12,0},{1,13},{5,9},{9,5},{13,1},{2,14},{6,10},... | collective-permute-start | bytes 344072 | tf_op jit(solution)/shard_map/ppermute | solution.py:204
  87.4 2.0 %collective-permute-start.21 = (bf16[16,3584]{1,0:T(8,128)(2,1)S(1)}, bf16[16,3584]{1,0:T(8,128)(2,1)S(1)}, u32[]{:S(2)}, u32[]{:S(2)}) collective-permute-start(bf16[16,3584]{1,0:T(8,128)(2,1)S(1)} %get-tuple-element.13), channel_id=1, source_target_pairs={{0,8},{4,12},{8,0},{12,4},{1,9},{5,13},{9,1},{13,5},{2,10},{6,14},... | collective-permute-start | bytes 344072 | tf_op jit(solution)/shard_map/ppermute | solution.py:204
  89.4 1.1 %collective-permute-start.20 = (bf16[16,3584]{1,0:T(8,128)(2,1)S(1)}, bf16[16,3584]{1,0:T(8,128)(2,1)S(1)}, u32[]{:S(2)}, u32[]{:S(2)}) collective-permute-start(bf16[16,3584]{1,0:T(8,128)(2,1)S(1)} %get-tuple-element.11), channel_id=1, source_target_pairs={{0,4},{4,0},{8,12},{12,8},{1,5},{5,1},{9,13},{13,9},{2,6},{6,2},{1... | collective-permute-start | bytes 344072 | tf_op jit(solution)/shard_map/ppermute | solution.py:204
  92.9 1.9 %collective-permute-done.9.refs_2_ = bf16[16,512]{1,0:T(8,128)(2,1)S(1)} collective-permute-done((bf16[16,512]{1,0:T(8,128)(2,1)S(1)}, bf16[16,512]{1,0:T(8,128)(2,1)S(1)}, u32[]{:S(2)}, u32[]{:S(2)}) %collective-permute-start.9) | collective-permute-done | bytes 16416 | tf_op jit(solution)/shard_map/ppermute | solution.py:204
  96.0 1.7 %place.1 = f32[16,2048]{1,0:T(8,128)} custom-call(s32[1]{0:T(128)} %bitcast.c_ref, bf16[16,512]{1,0:T(8,128)(2,1)} %get-tuple-element.21.refs_0_, bf16[16,512]{1,0:T(8,128)(2,1)} %copy-done.4, bf16[16,512]{1,0:T(8,128)(2,1)} %copy-done.5, bf16[16,512]{1,0:T(8,128)(2,1)} %copy-done.6), custom_call_target="tpu_custom_call" | custom-call | tf_op jit(solution)/shard_map/place/pallas_call | solution.py:192
  97.7 1.2 %collective-permute-done.21 = bf16[16,3584]{1,0:T(8,128)(2,1)S(1)} collective-permute-done((bf16[16,3584]{1,0:T(8,128)(2,1)S(1)}, bf16[16,3584]{1,0:T(8,128)(2,1)S(1)}, u32[]{:S(2)}, u32[]{:S(2)}) %collective-permute-start.21) | collective-permute-done | bytes 114720 | tf_op jit(solution)/shard_map/ppermute | solution.py:204
  (67 shorter events, 13.1 us)
Async XLA Ops:
  0.6 20.2 %collective-permute-start = (bf16[128,2048]{1,0:T(8,128)(2,1)}, bf16[128,2048]{1,0:T(8,128)(2,1)S(1)}, u32[]{:S(2)}, u32[]{:S(2)}) collective-permute-start(bf16[128,2048]{1,0:T(8,128)(2,1)} %refs_0_.3), channel_id=1, source_target_pairs={{0,1},{1,0},{2,3},{3,2},{4,5},{5,4},{6,7},{7,6},{8,9},{9,8},{10,11... | collective-permute-start | bytes 1572872 | tf_op jit(solution)/shard_map/ppermute | solution.py:204
  1.2 19.7 %collective-permute-start.1 = (bf16[128,2048]{1,0:T(8,128)(2,1)}, bf16[128,2048]{1,0:T(8,128)(2,1)S(1)}, u32[]{:S(2)}, u32[]{:S(2)}) collective-permute-start(bf16[128,2048]{1,0:T(8,128)(2,1)} %refs_0_.3), channel_id=1, source_target_pairs={{0,2},{2,0},{1,3},{3,1},{4,6},{6,4},{5,7},{7,5},{8,10},{10,8},{9,1... | collective-permute-start | bytes 1572872 | tf_op jit(solution)/shard_map/ppermute | solution.py:204
  5.5 29.0 %collective-permute-start.3 = (bf16[4,2,4,16,224]{4,3,2,1,0:T(8,128)(2,1)S(1)}, bf16[4,2,4,16,224]{4,3,2,1,0:T(8,128)(2,1)S(1)}, u32[]{:S(2)}, u32[]{:S(2)}) collective-permute-start(bf16[4,2,4,16,224]{4,3,2,1,0:T(8,128)(2,1)S(1)} %get-tuple-element.10), channel_id=1, source_target_pairs={{0,0},{1,4},{2,8},{3,12},{4,1},{5,5},{6,9},{7,13},{8,2},{9,6},{10,... | collective-permute-start | bytes 688136 | tf_op jit(solution)/shard_map/ppermute | solution.py:233
  6.2 31.0 %collective-permute-start.4 = (bf16[4,2,4,16,224]{4,3,2,1,0:T(8,128)(2,1)S(1)}, bf16[4,2,4,16,224]{4,3,2,1,0:T(8,128)(2,1)S(1)}, u32[]{:S(2)}, u32[]{:S(2)}) collective-permute-start(bf16[4,2,4,16,224]{4,3,2,1,0:T(8,128)(2,1)S(1)} %get-tuple-element.9), channel_id=1, source_target_pairs={{0,8},{1,12},{2,0},{3,4},{4,9},{5,13},{6,1},{7,5},{8,10},{9,14},{1... | collective-permute-start | bytes 688136 | tf_op jit(solution)/shard_map/ppermute | solution.py:233
  20.9 13.1 %collective-permute-start.2 = (bf16[128,2048]{1,0:T(8,128)(2,1)S(1)}, bf16[128,2048]{1,0:T(8,128)(2,1)S(1)}, u32[]{:S(2)}, u32[]{:S(2)}) collective-permute-start(bf16[128,2048]{1,0:T(8,128)(2,1)S(1)} %collective-permute-done.1.refs_2_.refs_6_), channel_id=1, source_target_pairs={{0,1},{1,0},{2,3},{3,2},{4,5},{5,4},{6,7},{7,6},{8,9},{9,8},{10,11... | collective-permute-start | bytes 1572872 | tf_op jit(solution)/shard_map/ppermute | solution.py:204
  21.3 36.6 %collective-permute-start.11 = (bf16[256,256]{1,0:T(8,128)(2,1)S(1)}, bf16[256,256]{1,0:T(8,128)(2,1)S(1)}, u32[]{:S(2)}, u32[]{:S(2)}) collective-permute-start(bf16[256,256]{1,0:T(8,128)(2,1)S(1)} %pad_maximum_fusion.1.refs_4_.refs_8_), channel_id=1, source_target_pairs={{0,4},{4,0},{8,12},{12,8},{1,5},{5,1},{9,13},{13,9},{2,6},{6,2},{1... | collective-permute-start | bytes 393224 | tf_op jit(solution)/shard_map/ppermute | solution.py:204
  23.6 6.7 %collective-permute-start.13 = (bf16[256,256]{1,0:T(8,128)(2,1)S(1)}, bf16[256,256]{1,0:T(8,128)(2,1)S(1)}, u32[]{:S(2)}, u32[]{:S(2)}) collective-permute-start(bf16[256,256]{1,0:T(8,128)(2,1)S(1)} %pad_maximum_fusion.1.refs_4_.refs_8_), channel_id=1, source_target_pairs={{0,8},{4,12},{8,0},{12,4},{1,9},{5,13},{9,1},{13,5},{2,10},{6,14},... | collective-permute-start | bytes 393224 | tf_op jit(solution)/shard_map/ppermute | solution.py:204
  30.2 27.9 %collective-permute-start.15 = (bf16[256,256]{1,0:T(8,128)(2,1)S(1)}, bf16[256,256]{1,0:T(8,128)(2,1)S(1)}, u32[]{:S(2)}, u32[]{:S(2)}) collective-permute-start(bf16[256,256]{1,0:T(8,128)(2,1)S(1)} %collective-permute-done.13.refs_12_), channel_id=1, source_target_pairs={{0,4},{4,0},{8,12},{12,8},{1,5},{5,1},{9,13},{13,9},{2,6},{6,2},{1... | collective-permute-start | bytes 393224 | tf_op jit(solution)/shard_map/ppermute | solution.py:204
  34.4 27.8 %collective-permute-start.12 = (bf16[256,256]{1,0:T(8,128)(2,1)S(1)}, bf16[256,256]{1,0:T(8,128)(2,1)S(1)}, u32[]{:S(2)}, u32[]{:S(2)}) collective-permute-start(bf16[256,256]{1,0:T(8,128)(2,1)S(1)} %pad_maximum_fusion.2.refs_5_.refs_9_), channel_id=1, source_target_pairs={{0,4},{4,0},{8,12},{12,8},{1,5},{5,1},{9,13},{13,9},{2,6},{6,2},{1... | collective-permute-start | bytes 393224 | tf_op jit(solution)/shard_map/ppermute | solution.py:204
  34.5 19.4 %collective-permute-start.14 = (bf16[256,256]{1,0:T(8,128)(2,1)S(1)}, bf16[256,256]{1,0:T(8,128)(2,1)S(1)}, u32[]{:S(2)}, u32[]{:S(2)}) collective-permute-start(bf16[256,256]{1,0:T(8,128)(2,1)S(1)} %pad_maximum_fusion.2.refs_5_.refs_9_), channel_id=1, source_target_pairs={{0,8},{4,12},{8,0},{12,4},{1,9},{5,13},{9,1},{13,5},{2,10},{6,14},... | collective-permute-start | bytes 393224 | tf_op jit(solution)/shard_map/ppermute | solution.py:204
  54.0 8.2 %collective-permute-start.16 = (bf16[256,256]{1,0:T(8,128)(2,1)S(1)}, bf16[256,256]{1,0:T(8,128)(2,1)S(1)}, u32[]{:S(2)}, u32[]{:S(2)}) collective-permute-start(bf16[256,256]{1,0:T(8,128)(2,1)S(1)} %collective-permute-done.14.refs_13_), channel_id=1, source_target_pairs={{0,4},{4,0},{8,12},{12,8},{1,5},{5,1},{9,13},{13,9},{2,6},{6,2},{1... | collective-permute-start | bytes 393224 | tf_op jit(solution)/shard_map/ppermute | solution.py:204
  57.8 21.3 %collective-permute-start.5 = (bf16[256,512]{1,0:T(8,128)(2,1)S(1)}, bf16[256,512]{1,0:T(8,128)(2,1)S(1)}, u32[]{:S(2)}, u32[]{:S(2)}) collective-permute-start(bf16[256,512]{1,0:T(8,128)(2,1)S(1)} %get-tuple-element.8), channel_id=1, source_target_pairs={{0,4},{4,0},{8,12},{12,8},{1,5},{5,1},{9,13},{13,9},{2,6},{6,2},{1... | collective-permute-start | bytes 786440 | tf_op jit(solution)/shard_map/ppermute | solution.py:204
  57.9 21.4 %collective-permute-start.6 = (bf16[256,512]{1,0:T(8,128)(2,1)}, bf16[256,512]{1,0:T(8,128)(2,1)}, u32[]{:S(2)}, u32[]{:S(2)}) collective-permute-start(bf16[256,512]{1,0:T(8,128)(2,1)} %get-tuple-element.7), channel_id=1, source_target_pairs={{0,8},{4,12},{8,0},{12,4},{1,9},{5,13},{9,1},{13,5},{2,10},{6,14},... | collective-permute-start | bytes 786440 | tf_op jit(solution)/shard_map/ppermute | solution.py:204
  58.2 21.1 %collective-permute-start.7 = (bf16[256,512]{1,0:T(8,128)(2,1)}, bf16[256,512]{1,0:T(8,128)(2,1)}, u32[]{:S(2)}, u32[]{:S(2)}) collective-permute-start(bf16[256,512]{1,0:T(8,128)(2,1)} %get-tuple-element.6), channel_id=1, source_target_pairs={{0,12},{4,8},{8,4},{12,0},{1,13},{5,9},{9,5},{13,1},{2,14},{6,10},... | collective-permute-start | bytes 786440 | tf_op jit(solution)/shard_map/ppermute | solution.py:204
  62.2 17.1 %copy-start.2 = (bf16[4,256,512]{2,1,0:T(8,128)(2,1)S(1)}, bf16[4,256,512]{2,1,0:T(8,128)(2,1)}, u32[]{:S(2)}) copy-start(bf16[4,256,512]{2,1,0:T(8,128)(2,1)} %copy-done.1) | copy-start | bytes 3145732
  76.6 6.1 %collective-permute-start.19 = (bf16[16,3584]{1,0:T(8,128)(2,1)}, bf16[16,3584]{1,0:T(8,128)(2,1)}, u32[]{:S(2)}, u32[]{:S(2)}) collective-permute-start(bf16[16,3584]{1,0:T(8,128)(2,1)} %get-tuple-element.15), channel_id=1, source_target_pairs={{0,3},{1,2},{2,1},{3,0},{4,7},{5,6},{6,5},{7,4},{8,11},{9,10},{10,... | collective-permute-start | bytes 344072 | tf_op jit(solution)/shard_map/ppermute | solution.py:204
  76.6 8.2 %collective-permute-start.18 = (bf16[16,3584]{1,0:T(8,128)(2,1)}, bf16[16,3584]{1,0:T(8,128)(2,1)}, u32[]{:S(2)}, u32[]{:S(2)}) collective-permute-start(bf16[16,3584]{1,0:T(8,128)(2,1)} %get-tuple-element.16), channel_id=1, source_target_pairs={{0,2},{1,3},{2,0},{3,1},{4,6},{5,7},{6,4},{7,5},{8,10},{9,11},{10,... | collective-permute-start | bytes 344072 | tf_op jit(solution)/shard_map/ppermute | solution.py:204
  79.1 5.7 %collective-permute-start.17 = (bf16[16,3584]{1,0:T(8,128)(2,1)}, bf16[16,3584]{1,0:T(8,128)(2,1)}, u32[]{:S(2)}, u32[]{:S(2)}) collective-permute-start(bf16[16,3584]{1,0:T(8,128)(2,1)} %get-tuple-element.17), channel_id=1, source_target_pairs={{0,1},{1,0},{2,3},{3,2},{4,5},{5,4},{6,7},{7,6},{8,9},{9,8},{10,11... | collective-permute-start | bytes 344072 | tf_op jit(solution)/shard_map/ppermute | solution.py:204
  86.0 11.7 %collective-permute-start.22 = (bf16[16,3584]{1,0:T(8,128)(2,1)S(1)}, bf16[16,3584]{1,0:T(8,128)(2,1)S(1)}, u32[]{:S(2)}, u32[]{:S(2)}) collective-permute-start(bf16[16,3584]{1,0:T(8,128)(2,1)S(1)} %get-tuple-element.12), channel_id=1, source_target_pairs={{0,12},{4,8},{8,4},{12,0},{1,13},{5,9},{9,5},{13,1},{2,14},{6,10},... | collective-permute-start | bytes 344072 | tf_op jit(solution)/shard_map/ppermute | solution.py:204
  87.4 11.5 %collective-permute-start.21 = (bf16[16,3584]{1,0:T(8,128)(2,1)S(1)}, bf16[16,3584]{1,0:T(8,128)(2,1)S(1)}, u32[]{:S(2)}, u32[]{:S(2)}) collective-permute-start(bf16[16,3584]{1,0:T(8,128)(2,1)S(1)} %get-tuple-element.13), channel_id=1, source_target_pairs={{0,8},{4,12},{8,0},{12,4},{1,9},{5,13},{9,1},{13,5},{2,10},{6,14},... | collective-permute-start | bytes 344072 | tf_op jit(solution)/shard_map/ppermute | solution.py:204
  89.4 9.5 %collective-permute-start.20 = (bf16[16,3584]{1,0:T(8,128)(2,1)S(1)}, bf16[16,3584]{1,0:T(8,128)(2,1)S(1)}, u32[]{:S(2)}, u32[]{:S(2)}) collective-permute-start(bf16[16,3584]{1,0:T(8,128)(2,1)S(1)} %get-tuple-element.11), channel_id=1, source_target_pairs={{0,4},{4,0},{8,12},{12,8},{1,5},{5,1},{9,13},{13,9},{2,6},{6,2},{1... | collective-permute-start | bytes 344072 | tf_op jit(solution)/shard_map/ppermute | solution.py:204
  91.1 1.2 %collective-permute-start.8 = (bf16[16,512]{1,0:T(8,128)(2,1)S(1)}, bf16[16,512]{1,0:T(8,128)(2,1)S(1)}, u32[]{:S(2)}, u32[]{:S(2)}) collective-permute-start(bf16[16,512]{1,0:T(8,128)(2,1)S(1)} %get-tuple-element.20), channel_id=1, source_target_pairs={{0,1},{1,0},{2,3},{3,2},{4,5},{5,4},{6,7},{7,6},{8,9},{9,8},{10,11... | collective-permute-start | bytes 49160 | tf_op jit(solution)/shard_map/ppermute | solution.py:204
  91.1 3.7 %collective-permute-start.9 = (bf16[16,512]{1,0:T(8,128)(2,1)S(1)}, bf16[16,512]{1,0:T(8,128)(2,1)S(1)}, u32[]{:S(2)}, u32[]{:S(2)}) collective-permute-start(bf16[16,512]{1,0:T(8,128)(2,1)S(1)} %get-tuple-element.19), channel_id=1, source_target_pairs={{0,2},{1,3},{2,0},{3,1},{4,6},{5,7},{6,4},{7,5},{8,10},{9,11},{10,... | collective-permute-start | bytes 49160 | tf_op jit(solution)/shard_map/ppermute | solution.py:204
  92.3 3.2 %collective-permute-start.10 = (bf16[16,512]{1,0:T(8,128)(2,1)S(1)}, bf16[16,512]{1,0:T(8,128)(2,1)S(1)}, u32[]{:S(2)}, u32[]{:S(2)}) collective-permute-start(bf16[16,512]{1,0:T(8,128)(2,1)S(1)} %get-tuple-element.18), channel_id=1, source_target_pairs={{0,3},{1,2},{2,1},{3,0},{4,7},{5,6},{6,5},{7,4},{8,11},{9,10},{10,... | collective-permute-start | bytes 49160 | tf_op jit(solution)/shard_map/ppermute | solution.py:204
  (6 other events, 16.0 us)

commit v5 on v4

v5 whole, which is shorter than its diff:
```python
import functools

import jax
import jax.numpy as jnp
from jax import lax
from jax.experimental import pallas as pl
from jax.experimental.pallas import tpu as pltpu
from jax.sharding import PartitionSpec as P

D = 8192
F = 14336
NB = 64
BI = D // NB
FB = F // NB
GROUP = 4
COLS = GROUP * FB
BF = jnp.bfloat16
F32 = jnp.float32
NT = (((1,), (1,)), ((), ()))
TN = (((0,), (0,)), ((), ()))
SPLIT = 4
VMEM = 40 * 1024 * 1024


def cost(flops, nbytes):
    return pl.CostEstimate(flops=flops, bytes_accessed=nbytes, transcendentals=0)


def rows_of(refs):
    return jnp.concatenate([r[...] for r in refs], axis=0) if len(refs) > 1 else refs[0][...]


def spread(right):
    n_z, n_k, n_b, _ = right.shape
    rows = n_z * n_k * n_b
    col = lax.broadcasted_iota(jnp.int32, (1, COLS), 1)
    tile = (lax.broadcasted_iota(jnp.int32, (FB, 1), 0) == col % FB).astype(F32).astype(BF)
    wide = jnp.dot(right.reshape(rows, FB), tile, preferred_element_type=F32)
    k_row = lax.broadcasted_iota(jnp.int32, (rows, 1), 0) // n_b % n_k
    return jnp.where(k_row == col // FB, wide, 0.0).astype(BF)


def residual_kernel(scale, n_tok, n_hid, n_z, z_ref, *refs):
    tok_refs, refs = refs[:n_tok], refs[n_tok:]
    hid_refs, refs = refs[:n_hid], refs[n_hid:]
    teacher_refs, right_refs, (resid_ref, back_ref) = refs[:SPLIT], refs[SPLIT:-2], refs[-2:]
    right = jnp.stack(
        [jnp.concatenate([a[0, :, 0], b[0, :, 0]], axis=0) for a, b in zip(right_refs[:n_z], right_refs[n_z:])],
        axis=0,
    )
    right = spread(right)
    rows = right.shape[0] // n_z
    hid = jnp.concatenate([h[...] for h in hid_refs], axis=1)
    resid = lax.dot_general(hid, right[:rows], TN, preferred_element_type=F32) - jnp.dot(
        rows_of(tok_refs), rows_of(teacher_refs), preferred_element_type=F32
    )
    resid = (resid * scale).astype(BF)
    resid_ref[...] = resid
    back = lax.dot_general(right, resid, NT, preferred_element_type=F32)
    back_ref[...] = back.astype(BF).reshape(back_ref.shape)


def residual(z, tokens, hidden, teacher, sides, scale):
    piece, depth = tokens[0].shape
    t = piece * len(tokens)
    cols = teacher.shape[1]
    n_q, half, n_z, n_b, _ = sides[0].shape
    rows = GROUP * n_b
    right_specs = [
        pl.BlockSpec((1, half, 1, n_b, FB), lambda q, z, s=s: (q, 0, z[0] ^ s, 0, 0)) for s in range(n_z)
    ]
    return pl.pallas_call(
        functools.partial(residual_kernel, scale, len(tokens), len(hidden), n_z),
        grid_spec=pltpu.PrefetchScalarGridSpec(
            num_scalar_prefetch=1,
            grid=(n_q,),
            in_specs=[pl.BlockSpec((piece, depth), lambda q, z: (0, 0))] * len(tokens)
            + [pl.BlockSpec((rows, h.shape[1]), lambda q, z: (q, 0)) for h in hidden]
            + [pl.BlockSpec((depth // SPLIT, COLS), lambda q, z, i=i: (i, q)) for i in range(SPLIT)]
            + right_specs * 2,
            out_specs=[
                pl.BlockSpec((t, COLS), lambda q, z: (0, q)),
                pl.BlockSpec((n_z, rows, t), lambda q, z: (0, q, 0)),
            ],
        ),
        out_shape=[
            jax.ShapeDtypeStruct((t, cols), BF),
            jax.ShapeDtypeStruct((n_z, n_q * rows, t), BF),
        ],
        compiler_params=pltpu.CompilerParams(vmem_limit_bytes=VMEM),
        cost_estimate=cost(2 * t * cols * (depth + n_z * rows), 2 * depth * cols),
        name="residual",
    )(z, *tokens, *hidden, *[teacher] * SPLIT, *[sides[0]] * n_z, *[sides[1]] * n_z)


def grad_right_kernel(n_z, parts, *refs):
    hid_refs, (resid_ref, out_ref) = refs[:-2], refs[-2:]
    hid = jnp.concatenate(
        [
            jnp.concatenate([r[...] for r in hid_refs[s * parts : (s + 1) * parts]], axis=1)
            for s in range(n_z)
        ],
        axis=0,
    )
    prod = jnp.dot(hid, resid_ref[...], preferred_element_type=F32)
    prod = prod.reshape(n_z, GROUP, prod.shape[0] // (n_z * GROUP), COLS)
    block = lax.broadcasted_iota(jnp.int32, (1, 1, COLS), 2) // FB
    total = prod[:, 0]
    for k in range(1, GROUP):
        total = jnp.where(block == k, prod[:, k], total)
    out_ref[...] = total.astype(BF)


def grad_right_partial(hidden, resid):
    t, cols = resid.shape
    n_z, parts = len(hidden), len(hidden[0])
    n_q = cols // COLS
    rows = hidden[0][0].shape[0] // n_q
    return pl.pallas_call(
        functools.partial(grad_right_kernel, n_z, parts),
        grid=(n_q,),
        in_specs=[pl.BlockSpec((rows, h.shape[1]), lambda q: (q, 0)) for hs in hidden for h in hs]
        + [pl.BlockSpec((t, COLS), lambda q: (0, q))],
        out_specs=pl.BlockSpec((n_z, rows // GROUP, COLS), lambda q: (0, 0, q)),
        out_shape=jax.ShapeDtypeStruct((n_z, rows // GROUP, cols), BF),
        compiler_params=pltpu.CompilerParams(vmem_limit_bytes=VMEM),
        cost_estimate=cost(2 * t * cols * n_z * rows, 2 * t * cols),
        name="grad_right",
    )(*[h for hs in hidden for h in hs], resid)


def grad_left_kernel(n_z, n_k, *refs):
    back_refs, tok_refs, out_ref = refs[:n_z], refs[n_z:-1], refs[-1]
    total = back_refs[0][0].astype(F32)
    for ref in back_refs[1:]:
        total = total + ref[...].astype(F32)
    prod = jnp.dot(total.astype(BF), rows_of(tok_refs), preferred_element_type=F32)
    rows, block = prod.shape
    prod = prod.reshape(n_k, rows // n_k, block)
    at = pl.program_id(0) * (block // BI)
    own = lax.broadcasted_iota(jnp.int32, prod.shape, 1) == at + lax.broadcasted_iota(
        jnp.int32, prod.shape, 2
    ) // BI
    out_ref[...] = jnp.where(own, prod, 0.0).sum(1).astype(BF)


def grad_left_of(backs, tokens, n_k):
    n_z = len(backs)
    rows, t = backs[1].shape
    piece, depth = tokens[0].shape
    block = min(depth, 1024)
    return pl.pallas_call(
        functools.partial(grad_left_kernel, n_z, n_k),
        grid=(depth // block,),
        in_specs=[pl.BlockSpec((1, rows, t), lambda q: (0, 0, 0))]
        + [pl.BlockSpec((rows, t), lambda q: (0, 0))] * (n_z - 1)
        + [pl.BlockSpec((piece, block), lambda q: (0, q))] * len(tokens),
        out_specs=pl.BlockSpec((n_k, block), lambda q: (0, q)),
        out_shape=jax.ShapeDtypeStruct((n_k, depth), BF),
        compiler_params=pltpu.CompilerParams(vmem_limit_bytes=VMEM),
        cost_estimate=cost(2 * t * rows * depth, 2 * t * depth),
        name="grad_left",
    )(*backs, *tokens)


def place_kernel(n_b, c_ref, *refs):
    in_refs, out_ref = refs[:-1], refs[-1]
    n_c, n_k = len(in_refs), in_refs[0].shape[0]
    x = rows_of(in_refs)
    row = lax.broadcasted_iota(jnp.int32, (NB, NB), 0)
    col = lax.broadcasted_iota(jnp.int32, (NB, NB), 1)
    pick = row == ((col // n_k) ^ c_ref[0]) * n_k + col % n_k
    got = lax.dot_general(
        x, pick.astype(F32).astype(BF), (((0,), (1,)), ((), ())), preferred_element_type=F32
    )
    for j in range(got.shape[0] // n_b):
        out_ref[:, j * NB : (j + 1) * NB] = got[j * n_b : (j + 1) * n_b]


def place(c, pieces, n_b):
    n = pieces[0].shape[1] // n_b
    return pl.pallas_call(
        functools.partial(place_kernel, n_b),
        in_specs=[pl.BlockSpec(memory_space=pltpu.SMEM)]
        + [pl.BlockSpec(memory_space=pltpu.VMEM)] * len(pieces),
        out_specs=pl.BlockSpec(memory_space=pltpu.VMEM),
        out_shape=jax.ShapeDtypeStruct((n_b, n * NB), F32),
        name="place",
    )(c, *pieces)


def swap(x, axes, s):
    n = lax.axis_size(axes)
    return lax.ppermute(x, axes, [(i, i ^ s) for i in range(n)])


def gather(x, axes):
    got = [x]
    for s in range(1, lax.axis_size(axes)):
        got.append(swap(got[s & (s - 1)], axes, s & -s))
    return got


def pick(x, at):
    return lax.dynamic_index_in_dim(x, at, 0, keepdims=False)


def per_device(tokens, teacher, left_blocks, right_blocks):
    n_z = lax.axis_size("blk")
    n_tok = lax.axis_size("tok")
    n_c = lax.axis_size(("tok", "rep"))
    z = lax.axis_index("blk")
    c = lax.axis_index(("tok", "rep"))
    plane = ("tok", "rep")
    n_b = left_blocks.shape[0]
    n_k = teacher.shape[1] // FB
    n_q = n_k // GROUP
    scale = float(tokens.shape[0] * n_c) ** (-0.5)

    left = left_blocks.reshape(n_b * BI, NB)
    rows_kb = n_k * n_b
    take = (
        lax.broadcasted_iota(jnp.int32, (rows_kb, NB), 0) // n_b + c * n_k
        == lax.broadcasted_iota(jnp.int32, (rows_kb, NB), 1)
    ).astype(BF)
    diag = (
        lax.broadcasted_iota(jnp.int32, (rows_kb, n_b * BI), 0) % n_b
        == lax.broadcasted_iota(jnp.int32, (rows_kb, n_b * BI), 1) // BI
    )
    left = lax.dot_general(take, left, NT, preferred_element_type=F32)
    left = jnp.where(diag, left, 0.0).astype(BF)

    def hidden_of(chip):
        return jnp.concatenate(
            [lax.dot_general(left, p, NT, preferred_element_type=F32).astype(BF) for p in chip], axis=1
        )

    far = [swap(tokens, "tok", s) for s in range(1, n_tok)]
    near = gather(tokens, "rep")
    sides = right_blocks.reshape(n_q, 2, GROUP // 2, n_z, n_b, FB)
    turn = [
        [(a * n_c + b, (b ^ side) * n_c + a) for a in range(n_z) for b in range(n_c)] for side in (0, n_c // 2)
    ]
    sides = [lax.ppermute(sides[:, i], ("blk",) + plane, perm) for i, perm in enumerate(turn)]

    first = hidden_of(near)
    early = gather(first, "blk")
    far, early[1:], _ = lax.optimization_barrier((far, early[1:], sides))
    chips = [near] + [gather(x, "rep") for x in far]
    pieces = [p for chip in chips for p in chip]
    hid = [first] + [hidden_of(chip) for chip in chips[1:]]
    late = [[h] + [swap(h, "blk", s) for s in range(1, n_z)] for h in hid[1:]]
    hidden = list(zip(early, *late))
    resid, back = residual(jnp.reshape(z, (1,)).astype(jnp.int32), pieces, hid, teacher, sides, scale)
    backs = [back] + [swap(back[s], "blk", s) for s in range(1, n_z)]

    gl = grad_left_of(backs, pieces, n_k)
    gl = gl.reshape(n_k, n_b, n_c, BI // n_c).transpose(2, 0, 3, 1).reshape(n_c, n_k, -1)
    got = []
    for s in range(n_c):
        piece = pick(gl, c ^ s)
        got.append(swap(piece, plane, s) if s else piece)
    grad_left = place(jnp.reshape(c, (1,)).astype(jnp.int32), got, n_b)

    hidden[0], _ = lax.optimization_barrier((hidden[0], backs[1:]))
    gr = grad_right_partial(hidden, resid)
    total = gr[0].astype(F32)
    for s in range(1, n_z):
        total = total + swap(gr[s], "blk", s).astype(F32)
    total = lax.ppermute(total.astype(BF), ("blk",) + plane, turn[0])
    total = total.reshape(n_b, n_k, FB).transpose(1, 0, 2).reshape(n_k, n_b * FB)
    grad_right = total.astype(F32)
    return grad_left, grad_right


def solution(mesh):
    return jax.shard_map(
        per_device,
        mesh=mesh,
        in_specs=(
            P(("layer", "tok", "rep"), "blk"),
            P(("layer", "blk"), ("tok", "rep")),
            P(("layer", "blk"), None),
            P(("layer", "blk"), None),
        ),
        out_specs=(P(("layer", "blk"), ("tok", "rep")), P(("layer", "blk"), ("tok", "rep"))),
        check_vma=False,
    )
```

time: 101 us -> 123 us (1.22)
  waiting for transfers between devices: 18.7 us -> 48.2 us
  Pallas kernels: 34.2 us -> 19.9 us
  local copies, waits for them, and re-layouts: 9.15 us -> 16 us
  starting transfers between devices: 33.7 us -> 31.1 us
  matrix products: 2.23 us -> 4.73 us
    ppermute x21 -> x18, waiting for transfers between devices: 18.7 us -> 48.2 us  [swap(): return lax.ppermute(x, axes, [(i, i ^ s) for i in range(n)])]
    pallas_call x2, Pallas kernels: 30.3 us -> 17 us  [the longest x1 14.8 us: residual(): pl.pallas_call(functools.partial(residual_kernel, scale, len(tokens), len...]
    unnamed x14 -> x36, local copies, waits for them, and re-layouts: 2.11 us -> 8.91 us
    ppermute x21 -> x18, starting transfers between devices: 29.1 us -> 25.5 us  [swap(): return lax.ppermute(x, axes, [(i, i ^ s) for i in range(n)])]
    dot_general x4, matrix products: 1.73 us -> 4.22 us  [hidden_of(): lax.dot_general(left, p, NT, preferred_element_type=F32).astype(BF)]
  transfers between devices with their start and end apart: 23 -> 21, of which waited for: 8 -> 10; matrix products, arithmetic and copies ran while one was open for 8% -> 7% of each run, Pallas kernels for 34% -> 2%
where the time goes in v5:
time: 123 us; the launch traced here: 122 us
  waiting for transfers between devices  48.2 us (39%)
  starting transfers between devices  31.1 us (25%)
  Pallas kernels  19.9 us (16%)
  local copies, waits for them, and re-layouts  16 us (13%)
  matrix products  4.73 us (4%)
    ppermute x18, waiting for transfers between devices, swap(): return lax.ppermute(x, axes, [(i, i ^ s) for i in range(n)])  48.2 us
    ppermute x18, starting transfers between devices, swap(): return lax.ppermute(x, axes, [(i, i ^ s) for i in range(n)])  25.5 us
    pallas_call x1, Pallas kernels, residual(): pl.pallas_call(functools.partial(residual_kernel, scale, len(tokens), len...  14.8 us
    unnamed x36, local copies, waits for them, and re-layouts  8.91 us
    ppermute x2, starting transfers between devices, per_device(): lax.ppermute(sides[:, i], ('blk',) + plane, perm)  4.86 us
    dot_general x4, matrix products, hidden_of(): lax.dot_general(left, p, NT, preferred_element_type=F32).astype(BF)  4.22 us
  transfers between devices with their start and end apart: 21, of which 10 were waited for; matrix products, arithmetic and copies ran while one was open for 7% of the time, Pallas kernels for 2%

profile of v5, /device:TPU:0, one launch (start us, length us, event | category | flops | bytes accessed | tf_op | source)
XLA Modules:
  0.0 122.0 jit_solution(17979940568044135491)
XLA Ops:
  1.1 2.6 %collective-permute-start.1 = (bf16[128,2048]{1,0:T(8,128)(2,1)}, bf16[128,2048]{1,0:T(8,128)(2,1)S(1)}, u32[]{:S(2)}, u32[]{:S(2)}) collective-permute-start(bf16[128,2048]{1,0:T(8,128)(2,1)} %refs_4_.1), channel_id=1, source_target_pairs={{0,2},{2,0},{1,3},{3,1},{4,6},{6,4},{5,7},{7,5},{8,10},{10,8},{9,1... | collective-permute-start | bytes 1572872 | tf_op jit(solution)/shard_map/ppermute | solution.py:194
  3.8 1.5 %reshape.32 = bf16[2048,64]{1,0:T(8,128)(2,1)S(1)} reshape(bf16[16,8192]{1,0:T(8,128)(2,1)} %param.6) | data formatting | bytes 524288 | tf_op jit(solution)/shard_map/reshape | solution.py:220
  5.2 1.8 %reshape.33 = bf16[4,2,2,4,16,224]{5,4,3,2,1,0:T(8,128)(2,1)S(1)} reshape(bf16[16,14336]{1,0:T(8,128)(2,1)} %param.7) | data formatting | bytes 917504 | tf_op jit(solution)/shard_map/reshape | solution.py:240
  9.0 2.7 %collective-permute-start.3 = (bf16[256,256]{1,0:T(8,128)(2,1)S(1)}, bf16[256,256]{1,0:T(8,128)(2,1)S(1)}, u32[]{:S(2)}, u32[]{:S(2)}) collective-permute-start(bf16[256,256]{1,0:T(8,128)(2,1)S(1)} %pad_maximum_fusion.refs_4_.refs_0_), channel_id=1, source_target_pairs={{0,8},{4,12},{8,0},{12,4},{1,9},{5,13},{9,1},{13,5},{2,10},{6,14},... | collective-permute-start | bytes 393224 | tf_op jit(solution)/shard_map/ppermute | solution.py:194
  12.4 4.2 %collective-permute-start.6 = (bf16[4,2,4,16,224]{4,3,2,1,0:T(8,128)(2,1)S(1)}, bf16[4,2,4,16,224]{4,3,2,1,0:T(8,128)(2,1)S(1)}, u32[]{:S(2)}, u32[]{:S(2)}) collective-permute-start(bf16[4,2,4,16,224]{4,3,2,1,0:T(8,128)(2,1)S(1)} %get-tuple-element.21), channel_id=1, source_target_pairs={{0,8},{1,12},{2,0},{3,4},{4,9},{5,13},{6,1},{7,5},{8,10},{9,14},{1... | collective-permute-start | bytes 688136 | tf_op jit(solution)/shard_map/ppermute | solution.py:244
  16.9 7.7 %collective-permute-done.3.refs_4_ = bf16[256,256]{1,0:T(8,128)(2,1)S(1)} collective-permute-done((bf16[256,256]{1,0:T(8,128)(2,1)S(1)}, bf16[256,256]{1,0:T(8,128)(2,1)S(1)}, u32[]{:S(2)}, u32[]{:S(2)}) %collective-permute-start.3) | collective-permute-done | bytes 131104 | tf_op jit(solution)/shard_map/ppermute | solution.py:194
  24.7 6.3 %collective-permute-done.2.refs_2_ = bf16[256,256]{1,0:T(8,128)(2,1)S(1)} collective-permute-done((bf16[256,256]{1,0:T(8,128)(2,1)S(1)}, bf16[256,256]{1,0:T(8,128)(2,1)S(1)}, u32[]{:S(2)}, u32[]{:S(2)}) %collective-permute-start.2) | collective-permute-done | bytes 131104 | tf_op jit(solution)/shard_map/ppermute | solution.py:194
  32.4 1.7 %convolution_convert_fusion.1 = bf16[256,128]{1,0:T(8,128)(2,1)S(1)} fusion(bf16[256,2048]{1,0:T(8,128)(2,1)} %copy-done.14, bf16[128,2048]{1,0:T(8,128)(2,1)S(1)} %collective-permute-done.1.refs_2_.refs_6_), kind=kOutput, calls=%fused_computation.4 | convolution fusion | flops 134250496 | bytes 1638400 | tf_op jit(solution)/shard_map/dot_general | solution.py:235
  34.3 1.7 %convolution_convert_fusion = bf16[256,128]{1,0:T(8,128)(2,1)S(1)} fusion(bf16[256,2048]{1,0:T(8,128)(2,1)} %copy-done.14, bf16[128,2048]{1,0:T(8,128)(2,1)S(1)} %collective-permute-done.7.refs_3_.refs_7_), kind=kOutput, calls=%fused_computation.3 | convolution fusion | flops 134250496 | bytes 1638400 | tf_op jit(solution)/shard_map/dot_general | solution.py:235
  36.0 14.8 %residual.1 = (bf16[512,3584]{1,0:T(8,128)(2,1)S(1)}, bf16[4,256,512]{2,1,0:T(8,128)(2,1)S(1)}) custom-call(s32[1]{0:T(128)} %bitcast.1.z_ref, bf16[128,2048]{1,0:T(8,128)(2,1)S(1)} %copy-done, bf16[128,2048]{1,0:T(8,128)(2,1)S(1)} %collective-permute-done.refs_1_.refs_5_, bf16[128,2048]{1,0:T(8,128)(2,1)S(1)} %collective-permute-done.1.refs_2_.refs_6_, ...), custom_call_target="tpu_custom_call" | custom-call | flops 8455716864 | bytes 14680064 | tf_op jit(solution)/shard_map/residual/pallas_call | solution.py:72
  51.9 3.6 %collective-permute-start.9 = (bf16[256,512]{1,0:T(8,128)(2,1)S(1)}, bf16[256,512]{1,0:T(8,128)(2,1)S(1)}, u32[]{:S(2)}, u32[]{:S(2)}) collective-permute-start(bf16[256,512]{1,0:T(8,128)(2,1)S(1)} %get-tuple-element.19), channel_id=1, source_target_pairs={{0,8},{4,12},{8,0},{12,4},{1,9},{5,13},{9,1},{13,5},{2,10},{6,14},... | collective-permute-start | bytes 786440 | tf_op jit(solution)/shard_map/ppermute | solution.py:194
  56.3 3.6 %collective-permute-start.15 = (bf16[256,256]{1,0:T(8,128)(2,1)S(1)}, bf16[256,256]{1,0:T(8,128)(2,1)S(1)}, u32[]{:S(2)}, u32[]{:S(2)}) collective-permute-start(bf16[256,256]{1,0:T(8,128)(2,1)S(1)} %pad_maximum_fusion.1.refs_5_.refs_1_), channel_id=1, source_target_pairs={{0,8},{4,12},{8,0},{12,4},{1,9},{5,13},{9,1},{13,5},{2,10},{6,14},... | collective-permute-start | bytes 393224 | tf_op jit(solution)/shard_map/ppermute | solution.py:194
  59.9 6.3 %collective-permute-done.8.refs_1_ = bf16[256,512]{1,0:T(8,128)(2,1)S(1)} collective-permute-done((bf16[256,512]{1,0:T(8,128)(2,1)S(1)}, bf16[256,512]{1,0:T(8,128)(2,1)S(1)}, u32[]{:S(2)}, u32[]{:S(2)}) %collective-permute-start.8) | collective-permute-done | bytes 262176 | tf_op jit(solution)/shard_map/ppermute | solution.py:194
  66.2 1.8 %collective-permute-start.16 = (bf16[256,256]{1,0:T(8,128)(2,1)S(1)}, bf16[256,256]{1,0:T(8,128)(2,1)S(1)}, u32[]{:S(2)}, u32[]{:S(2)}) collective-permute-start(bf16[256,256]{1,0:T(8,128)(2,1)S(1)} %pad_maximum_fusion.1.refs_5_.refs_1_), channel_id=1, source_target_pairs={{0,12},{4,8},{8,4},{12,0},{1,13},{5,9},{9,5},{13,1},{2,14},{6,10},... | collective-permute-start | bytes 393224 | tf_op jit(solution)/shard_map/ppermute | solution.py:194
  68.0 6.0 %collective-permute-done.9.refs_2_ = bf16[256,512]{1,0:T(8,128)(2,1)S(1)} collective-permute-done((bf16[256,512]{1,0:T(8,128)(2,1)S(1)}, bf16[256,512]{1,0:T(8,128)(2,1)S(1)}, u32[]{:S(2)}, u32[]{:S(2)}) %collective-permute-start.9) | collective-permute-done | bytes 262176 | tf_op jit(solution)/shard_map/ppermute | solution.py:194
  75.3 12.6 %collective-permute-done.15.refs_5_ = bf16[256,256]{1,0:T(8,128)(2,1)S(1)} collective-permute-done((bf16[256,256]{1,0:T(8,128)(2,1)S(1)}, bf16[256,256]{1,0:T(8,128)(2,1)S(1)}, u32[]{:S(2)}, u32[]{:S(2)}) %collective-permute-start.15) | collective-permute-done | bytes 131104 | tf_op jit(solution)/shard_map/ppermute | solution.py:194
  90.7 2.2 %grad_right.1 = bf16[4,16,3584]{2,1,0:T(8,128)(2,1)S(1)} custom-call(bf16[256,256]{1,0:T(8,128)(2,1)S(1)} %pad_maximum_fusion.refs_4_.refs_0_, bf16[256,256]{1,0:T(8,128)(2,1)S(1)} %pad_maximum_fusion.1.refs_5_.refs_1_, bf16[256,256]{1,0:T(8,128)(2,1)S(1)} %copy-done.11, bf16[256,256]{1,0:T(8,128)(2,1)S(1)} %collective-permute-done.14.refs_3_, ...), custom_call_target="tpu_custom_call" | custom-call | flops 939524096 | bytes 3670016 | tf_op jit(solution)/shard_map/grad_right/pallas_call | solution.py:119
  94.4 2.4 %collective-permute-start.19 = (bf16[16,3584]{1,0:T(8,128)(2,1)}, bf16[16,3584]{1,0:T(8,128)(2,1)}, u32[]{:S(2)}, u32[]{:S(2)}) collective-permute-start(bf16[16,3584]{1,0:T(8,128)(2,1)} %get-tuple-element.24), channel_id=1, source_target_pairs={{0,12},{4,8},{8,4},{12,0},{1,13},{5,9},{9,5},{13,1},{2,14},{6,10},... | collective-permute-start | bytes 344072 | tf_op jit(solution)/shard_map/ppermute | solution.py:194
  96.7 1.8 %collective-permute-start.18 = (bf16[16,3584]{1,0:T(8,128)(2,1)}, bf16[16,3584]{1,0:T(8,128)(2,1)}, u32[]{:S(2)}, u32[]{:S(2)}) collective-permute-start(bf16[16,3584]{1,0:T(8,128)(2,1)} %get-tuple-element.25), channel_id=1, source_target_pairs={{0,8},{4,12},{8,0},{12,4},{1,9},{5,13},{9,1},{13,5},{2,10},{6,14},... | collective-permute-start | bytes 344072 | tf_op jit(solution)/shard_map/ppermute | solution.py:194
  103.1 4.5 %collective-permute-done.18 = bf16[16,3584]{1,0:T(8,128)(2,1)} collective-permute-done((bf16[16,3584]{1,0:T(8,128)(2,1)}, bf16[16,3584]{1,0:T(8,128)(2,1)}, u32[]{:S(2)}, u32[]{:S(2)}) %collective-permute-start.18) | collective-permute-done | bytes 114720 | tf_op jit(solution)/shard_map/ppermute | solution.py:194
  111.0 4.3 %collective-permute-start.12 = (bf16[16,512]{1,0:T(8,128)(2,1)S(1)}, bf16[16,512]{1,0:T(8,128)(2,1)S(1)}, u32[]{:S(2)}, u32[]{:S(2)}) collective-permute-start(bf16[16,512]{1,0:T(8,128)(2,1)S(1)} %get-tuple-element.27), channel_id=1, source_target_pairs={{0,2},{1,3},{2,0},{3,1},{4,6},{5,7},{6,4},{7,5},{8,10},{9,11},{10,... | collective-permute-start | bytes 49160 | tf_op jit(solution)/shard_map/ppermute | solution.py:194
  115.3 1.7 %collective-permute-done.12.refs_2_ = bf16[16,512]{1,0:T(8,128)(2,1)S(1)} collective-permute-done((bf16[16,512]{1,0:T(8,128)(2,1)S(1)}, bf16[16,512]{1,0:T(8,128)(2,1)S(1)}, u32[]{:S(2)}, u32[]{:S(2)}) %collective-permute-start.12) | collective-permute-done | bytes 16416 | tf_op jit(solution)/shard_map/ppermute | solution.py:194
  117.0 1.5 %collective-permute-done.13.refs_3_ = bf16[16,512]{1,0:T(8,128)(2,1)S(1)} collective-permute-done((bf16[16,512]{1,0:T(8,128)(2,1)S(1)}, bf16[16,512]{1,0:T(8,128)(2,1)S(1)}, u32[]{:S(2)}, u32[]{:S(2)}) %collective-permute-start.13) | collective-permute-done | bytes 16416 | tf_op jit(solution)/shard_map/ppermute | solution.py:194
  119.1 1.7 %place.1 = f32[16,2048]{1,0:T(8,128)} custom-call(s32[1]{0:T(128)} %bitcast.c_ref, bf16[16,512]{1,0:T(8,128)(2,1)} %get-tuple-element.29.refs_0_, bf16[16,512]{1,0:T(8,128)(2,1)} %copy-done.15, bf16[16,512]{1,0:T(8,128)(2,1)} %copy-done.16, bf16[16,512]{1,0:T(8,128)(2,1)} %copy-done.17), custom_call_target="tpu_custom_call" | custom-call | tf_op jit(solution)/shard_map/place/pallas_call | solution.py:182
  (83 shorter events, 22.4 us)
Async XLA Ops:
  0.6 7.9 %collective-permute-start = (bf16[128,2048]{1,0:T(8,128)(2,1)}, bf16[128,2048]{1,0:T(8,128)(2,1)S(1)}, u32[]{:S(2)}, u32[]{:S(2)}) collective-permute-start(bf16[128,2048]{1,0:T(8,128)(2,1)} %refs_4_.1), channel_id=1, source_target_pairs={{0,1},{1,0},{2,3},{3,2},{4,5},{5,4},{6,7},{7,6},{8,9},{9,8},{10,11... | collective-permute-start | bytes 1572872 | tf_op jit(solution)/shard_map/ppermute | solution.py:194
  1.1 23.5 %collective-permute-start.1 = (bf16[128,2048]{1,0:T(8,128)(2,1)}, bf16[128,2048]{1,0:T(8,128)(2,1)S(1)}, u32[]{:S(2)}, u32[]{:S(2)}) collective-permute-start(bf16[128,2048]{1,0:T(8,128)(2,1)} %refs_4_.1), channel_id=1, source_target_pairs={{0,2},{2,0},{1,3},{3,1},{4,6},{6,4},{5,7},{7,5},{8,10},{10,8},{9,1... | collective-permute-start | bytes 1572872 | tf_op jit(solution)/shard_map/ppermute | solution.py:194
  9.0 15.7 %collective-permute-start.3 = (bf16[256,256]{1,0:T(8,128)(2,1)S(1)}, bf16[256,256]{1,0:T(8,128)(2,1)S(1)}, u32[]{:S(2)}, u32[]{:S(2)}) collective-permute-start(bf16[256,256]{1,0:T(8,128)(2,1)S(1)} %pad_maximum_fusion.refs_4_.refs_0_), channel_id=1, source_target_pairs={{0,8},{4,12},{8,0},{12,4},{1,9},{5,13},{9,1},{13,5},{2,10},{6,14},... | collective-permute-start | bytes 393224 | tf_op jit(solution)/shard_map/ppermute | solution.py:194
  11.7 13.0 %collective-permute-start.5 = (bf16[4,2,4,16,224]{4,3,2,1,0:T(8,128)(2,1)S(1)}, bf16[4,2,4,16,224]{4,3,2,1,0:T(8,128)(2,1)S(1)}, u32[]{:S(2)}, u32[]{:S(2)}) collective-permute-start(bf16[4,2,4,16,224]{4,3,2,1,0:T(8,128)(2,1)S(1)} %get-tuple-element.22), channel_id=1, source_target_pairs={{0,0},{1,4},{2,8},{3,12},{4,1},{5,5},{6,9},{7,13},{8,2},{9,6},{10,... | collective-permute-start | bytes 688136 | tf_op jit(solution)/shard_map/ppermute | solution.py:244
  12.4 12.3 %collective-permute-start.6 = (bf16[4,2,4,16,224]{4,3,2,1,0:T(8,128)(2,1)S(1)}, bf16[4,2,4,16,224]{4,3,2,1,0:T(8,128)(2,1)S(1)}, u32[]{:S(2)}, u32[]{:S(2)}) collective-permute-start(bf16[4,2,4,16,224]{4,3,2,1,0:T(8,128)(2,1)S(1)} %get-tuple-element.21), channel_id=1, source_target_pairs={{0,8},{1,12},{2,0},{3,4},{4,9},{5,13},{6,1},{7,5},{8,10},{9,14},{1... | collective-permute-start | bytes 688136 | tf_op jit(solution)/shard_map/ppermute | solution.py:244
  16.5 14.4 %collective-permute-start.2 = (bf16[256,256]{1,0:T(8,128)(2,1)S(1)}, bf16[256,256]{1,0:T(8,128)(2,1)S(1)}, u32[]{:S(2)}, u32[]{:S(2)}) collective-permute-start(bf16[256,256]{1,0:T(8,128)(2,1)S(1)} %pad_maximum_fusion.refs_4_.refs_0_), channel_id=1, source_target_pairs={{0,4},{4,0},{8,12},{12,8},{1,5},{5,1},{9,13},{13,9},{2,6},{6,2},{1... | collective-permute-start | bytes 393224 | tf_op jit(solution)/shard_map/ppermute | solution.py:194
  24.6 26.1 %copy-start.8 = (bf16[256,256]{1,0:T(8,128)(2,1)}, bf16[256,256]{1,0:T(8,128)(2,1)S(1)}, u32[]{:S(2)}) copy-start(bf16[256,256]{1,0:T(8,128)(2,1)S(1)} %collective-permute-done.3.refs_4_) | copy-start | bytes 393220
  24.6 7.7 %collective-permute-start.4 = (bf16[256,256]{1,0:T(8,128)(2,1)S(1)}, bf16[256,256]{1,0:T(8,128)(2,1)S(1)}, u32[]{:S(2)}, u32[]{:S(2)}) collective-permute-start(bf16[256,256]{1,0:T(8,128)(2,1)S(1)} %collective-permute-done.3.refs_4_), channel_id=1, source_target_pairs={{0,4},{4,0},{8,12},{12,8},{1,5},{5,1},{9,13},{13,9},{2,6},{6,2},{1... | collective-permute-start | bytes 393224 | tf_op jit(solution)/shard_map/ppermute | solution.py:194
  31.0 19.8 %copy-start.10 = (bf16[256,256]{1,0:T(8,128)(2,1)}, bf16[256,256]{1,0:T(8,128)(2,1)S(1)}, u32[]{:S(2)}) copy-start(bf16[256,256]{1,0:T(8,128)(2,1)S(1)} %collective-permute-done.2.refs_2_) | copy-start | bytes 393220
  32.4 18.4 %copy-start.12 = (bf16[256,256]{1,0:T(8,128)(2,1)}, bf16[256,256]{1,0:T(8,128)(2,1)S(1)}, u32[]{:S(2)}) copy-start(bf16[256,256]{1,0:T(8,128)(2,1)S(1)} %collective-permute-done.4.refs_6_) | copy-start | bytes 393220
  32.4 1.9 %collective-permute-start.7 = (bf16[128,2048]{1,0:T(8,128)(2,1)S(1)}, bf16[128,2048]{1,0:T(8,128)(2,1)S(1)}, u32[]{:S(2)}, u32[]{:S(2)}) collective-permute-start(bf16[128,2048]{1,0:T(8,128)(2,1)S(1)} %collective-permute-done.1.refs_2_.refs_6_), channel_id=1, source_target_pairs={{0,1},{1,0},{2,3},{3,2},{4,5},{5,4},{6,7},{7,6},{8,9},{9,8},{10,11... | collective-permute-start | bytes 1572872 | tf_op jit(solution)/shard_map/ppermute | solution.py:194
  51.9 14.3 %collective-permute-start.8 = (bf16[256,512]{1,0:T(8,128)(2,1)S(1)}, bf16[256,512]{1,0:T(8,128)(2,1)S(1)}, u32[]{:S(2)}, u32[]{:S(2)}) collective-permute-start(bf16[256,512]{1,0:T(8,128)(2,1)S(1)} %get-tuple-element.20), channel_id=1, source_target_pairs={{0,4},{4,0},{8,12},{12,8},{1,5},{5,1},{9,13},{13,9},{2,6},{6,2},{1... | collective-permute-start | bytes 786440 | tf_op jit(solution)/shard_map/ppermute | solution.py:194
  51.9 22.1 %collective-permute-start.9 = (bf16[256,512]{1,0:T(8,128)(2,1)S(1)}, bf16[256,512]{1,0:T(8,128)(2,1)S(1)}, u32[]{:S(2)}, u32[]{:S(2)}) collective-permute-start(bf16[256,512]{1,0:T(8,128)(2,1)S(1)} %get-tuple-element.19), channel_id=1, source_target_pairs={{0,8},{4,12},{8,0},{12,4},{1,9},{5,13},{9,1},{13,5},{2,10},{6,14},... | collective-permute-start | bytes 786440 | tf_op jit(solution)/shard_map/ppermute | solution.py:194
  55.5 19.1 %collective-permute-start.10 = (bf16[256,512]{1,0:T(8,128)(2,1)S(1)}, bf16[256,512]{1,0:T(8,128)(2,1)S(1)}, u32[]{:S(2)}, u32[]{:S(2)}) collective-permute-start(bf16[256,512]{1,0:T(8,128)(2,1)S(1)} %get-tuple-element.18), channel_id=1, source_target_pairs={{0,12},{4,8},{8,4},{12,0},{1,13},{5,9},{9,5},{13,1},{2,14},{6,10},... | collective-permute-start | bytes 786440 | tf_op jit(solution)/shard_map/ppermute | solution.py:194
  56.3 19.1 %collective-permute-start.14 = (bf16[256,256]{1,0:T(8,128)(2,1)S(1)}, bf16[256,256]{1,0:T(8,128)(2,1)S(1)}, u32[]{:S(2)}, u32[]{:S(2)}) collective-permute-start(bf16[256,256]{1,0:T(8,128)(2,1)S(1)} %pad_maximum_fusion.1.refs_5_.refs_1_), channel_id=1, source_target_pairs={{0,4},{4,0},{8,12},{12,8},{1,5},{5,1},{9,13},{13,9},{2,6},{6,2},{1... | collective-permute-start | bytes 393224 | tf_op jit(solution)/shard_map/ppermute | solution.py:194
  56.3 31.7 %collective-permute-start.15 = (bf16[256,256]{1,0:T(8,128)(2,1)S(1)}, bf16[256,256]{1,0:T(8,128)(2,1)S(1)}, u32[]{:S(2)}, u32[]{:S(2)}) collective-permute-start(bf16[256,256]{1,0:T(8,128)(2,1)S(1)} %pad_maximum_fusion.1.refs_5_.refs_1_), channel_id=1, source_target_pairs={{0,8},{4,12},{8,0},{12,4},{1,9},{5,13},{9,1},{13,5},{2,10},{6,14},... | collective-permute-start | bytes 393224 | tf_op jit(solution)/shard_map/ppermute | solution.py:194
  66.2 21.8 %collective-permute-start.16 = (bf16[256,256]{1,0:T(8,128)(2,1)S(1)}, bf16[256,256]{1,0:T(8,128)(2,1)S(1)}, u32[]{:S(2)}, u32[]{:S(2)}) collective-permute-start(bf16[256,256]{1,0:T(8,128)(2,1)S(1)} %pad_maximum_fusion.1.refs_5_.refs_1_), channel_id=1, source_target_pairs={{0,12},{4,8},{8,4},{12,0},{1,13},{5,9},{9,5},{13,1},{2,14},{6,10},... | collective-permute-start | bytes 393224 | tf_op jit(solution)/shard_map/ppermute | solution.py:194
  94.4 8.8 %collective-permute-start.19 = (bf16[16,3584]{1,0:T(8,128)(2,1)}, bf16[16,3584]{1,0:T(8,128)(2,1)}, u32[]{:S(2)}, u32[]{:S(2)}) collective-permute-start(bf16[16,3584]{1,0:T(8,128)(2,1)} %get-tuple-element.24), channel_id=1, source_target_pairs={{0,12},{4,8},{8,4},{12,0},{1,13},{5,9},{9,5},{13,1},{2,14},{6,10},... | collective-permute-start | bytes 344072 | tf_op jit(solution)/shard_map/ppermute | solution.py:194
  96.7 10.9 %collective-permute-start.18 = (bf16[16,3584]{1,0:T(8,128)(2,1)}, bf16[16,3584]{1,0:T(8,128)(2,1)}, u32[]{:S(2)}, u32[]{:S(2)}) collective-permute-start(bf16[16,3584]{1,0:T(8,128)(2,1)} %get-tuple-element.25), channel_id=1, source_target_pairs={{0,8},{4,12},{8,0},{12,4},{1,9},{5,13},{9,1},{13,5},{2,10},{6,14},... | collective-permute-start | bytes 344072 | tf_op jit(solution)/shard_map/ppermute | solution.py:194
  98.5 9.1 %collective-permute-start.17 = (bf16[16,3584]{1,0:T(8,128)(2,1)}, bf16[16,3584]{1,0:T(8,128)(2,1)}, u32[]{:S(2)}, u32[]{:S(2)}) collective-permute-start(bf16[16,3584]{1,0:T(8,128)(2,1)} %get-tuple-element.23), channel_id=1, source_target_pairs={{0,4},{4,0},{8,12},{12,8},{1,5},{5,1},{9,13},{13,9},{2,6},{6,2},{1... | collective-permute-start | bytes 344072 | tf_op jit(solution)/shard_map/ppermute | solution.py:194
  108.8 12.0 %collective-permute-start.20 = (bf16[16,3584]{1,0:T(8,128)(2,1)S(1)}, bf16[16,3584]{1,0:T(8,128)(2,1)S(1)}, u32[]{:S(2)}, u32[]{:S(2)}) collective-permute-start(bf16[16,3584]{1,0:T(8,128)(2,1)S(1)} %fusion.3), channel_id=1, source_target_pairs={{0,0},{1,4},{2,8},{3,12},{4,1},{5,5},{6,9},{7,13},{8,2},{9,6},{10,... | collective-permute-start | bytes 344072 | tf_op jit(solution)/shard_map/ppermute | solution.py:270
  110.1 5.2 %collective-permute-start.11 = (bf16[16,512]{1,0:T(8,128)(2,1)S(1)}, bf16[16,512]{1,0:T(8,128)(2,1)S(1)}, u32[]{:S(2)}, u32[]{:S(2)}) collective-permute-start(bf16[16,512]{1,0:T(8,128)(2,1)S(1)} %get-tuple-element.28), channel_id=1, source_target_pairs={{0,1},{1,0},{2,3},{3,2},{4,5},{5,4},{6,7},{7,6},{8,9},{9,8},{10,11... | collective-permute-start | bytes 49160 | tf_op jit(solution)/shard_map/ppermute | solution.py:194
  111.0 6.0 %collective-permute-start.12 = (bf16[16,512]{1,0:T(8,128)(2,1)S(1)}, bf16[16,512]{1,0:T(8,128)(2,1)S(1)}, u32[]{:S(2)}, u32[]{:S(2)}) collective-permute-start(bf16[16,512]{1,0:T(8,128)(2,1)S(1)} %get-tuple-element.27), channel_id=1, source_target_pairs={{0,2},{1,3},{2,0},{3,1},{4,6},{5,7},{6,4},{7,5},{8,10},{9,11},{10,... | collective-permute-start | bytes 49160 | tf_op jit(solution)/shard_map/ppermute | solution.py:194
  115.2 3.2 %collective-permute-start.13 = (bf16[16,512]{1,0:T(8,128)(2,1)S(1)}, bf16[16,512]{1,0:T(8,128)(2,1)S(1)}, u32[]{:S(2)}, u32[]{:S(2)}) collective-permute-start(bf16[16,512]{1,0:T(8,128)(2,1)S(1)} %get-tuple-element.26), channel_id=1, source_target_pairs={{0,3},{1,2},{2,1},{3,0},{4,7},{5,6},{6,5},{7,4},{8,11},{9,10},{10,... | collective-permute-start | bytes 49160 | tf_op jit(solution)/shard_map/ppermute | solution.py:194
  (15 other events, 25.9 us)

commit v6 on v5

--- a/solution.py
+++ b/solution.py
@@ -40,10 +40,31 @@
     return jnp.where(k_row == col // FB, wide, 0.0).astype(BF)
 
 
-def residual_kernel(scale, n_tok, n_hid, n_z, z_ref, *refs):
-    tok_refs, refs = refs[:n_tok], refs[n_tok:]
-    hid_refs, refs = refs[:n_hid], refs[n_hid:]
-    teacher_refs, right_refs, (resid_ref, back_ref) = refs[:SPLIT], refs[SPLIT:-2], refs[-2:]
+def target_kernel(pieces, *refs):
+    tok_refs, teacher_refs, out_ref = refs[:pieces], refs[pieces:-1], refs[-1]
+    out_ref[...] = jnp.dot(rows_of(tok_refs), rows_of(teacher_refs), preferred_element_type=F32).astype(BF)
+
+
+def target(tokens, teacher):
+    t, depth = tokens[0].shape
+    cols = teacher.shape[1]
+    block = 512 if cols % 512 == 0 else COLS
+    total = t * len(tokens)
+    return pl.pallas_call(
+        functools.partial(target_kernel, len(tokens)),
+        grid=(cols // block,),
+        in_specs=[pl.BlockSpec((t, depth), lambda q: (0, 0))] * len(tokens)
+        + [pl.BlockSpec((depth // SPLIT, block), lambda q, i=i: (i, q)) for i in range(SPLIT)],
+        out_specs=pl.BlockSpec((total, block), lambda q: (0, q)),
+        out_shape=jax.ShapeDtypeStruct((total, cols), BF),
+        compiler_params=pltpu.CompilerParams(vmem_limit_bytes=VMEM),
+        cost_estimate=cost(2 * total * cols * depth, 2 * depth * cols),
+        name="target",
+    )(*tokens, *[teacher] * SPLIT)
+
+
+def project_kernel(scale, n_hid, n_z, z_ref, part_ref, *refs):
+    hid_refs, right_refs, (resid_ref, back_ref) = refs[:n_hid], refs[n_hid:-2], refs[-2:]
     right = jnp.stack(
         [jnp.concatenate([a[0, :, 0], b[0, :, 0]], axis=0) for a, b in zip(right_refs[:n_z], right_refs[n_z:])],
         axis=0,
@@ -51,32 +72,27 @@
     right = spread(right)
     rows = right.shape[0] // n_z
     hid = jnp.concatenate([h[...] for h in hid_refs], axis=1)
-    resid = lax.dot_general(hid, right[:rows], TN, preferred_element_type=F32) - jnp.dot(
-        rows_of(tok_refs), rows_of(teacher_refs), preferred_element_type=F32
-    )
-    resid = (resid * scale).astype(BF)
+    student = lax.dot_general(hid, right[:rows], TN, preferred_element_type=F32)
+    resid = ((student - part_ref[...].astype(F32)) * scale).astype(BF)
     resid_ref[...] = resid
     back = lax.dot_general(right, resid, NT, preferred_element_type=F32)
     back_ref[...] = back.astype(BF).reshape(back_ref.shape)
 
 
-def residual(z, tokens, hidden, teacher, sides, scale):
-    piece, depth = tokens[0].shape
-    t = piece * len(tokens)
-    cols = teacher.shape[1]
+def project(z, part, hidden, sides, scale):
+    t, cols = part.shape
     n_q, half, n_z, n_b, _ = sides[0].shape
     rows = GROUP * n_b
     right_specs = [
         pl.BlockSpec((1, half, 1, n_b, FB), lambda q, z, s=s: (q, 0, z[0] ^ s, 0, 0)) for s in range(n_z)
     ]
     return pl.pallas_call(
-        functools.partial(residual_kernel, scale, len(tokens), len(hidden), n_z),
+        functools.partial(project_kernel, scale, len(hidden), n_z),
         grid_spec=pltpu.PrefetchScalarGridSpec(
             num_scalar_prefetch=1,
             grid=(n_q,),
-            in_specs=[pl.BlockSpec((piece, depth), lambda q, z: (0, 0))] * len(tokens)
+            in_specs=[pl.BlockSpec((t, COLS), lambda q, z: (0, q))]
             + [pl.BlockSpec((rows, h.shape[1]), lambda q, z: (q, 0)) for h in hidden]
-            + [pl.BlockSpec((depth // SPLIT, COLS), lambda q, z, i=i: (i, q)) for i in range(SPLIT)]
             + right_specs * 2,
             out_specs=[
                 pl.BlockSpec((t, COLS), lambda q, z: (0, q)),
@@ -88,9 +104,9 @@
             jax.ShapeDtypeStruct((n_z, n_q * rows, t), BF),
         ],
         compiler_params=pltpu.CompilerParams(vmem_limit_bytes=VMEM),
-        cost_estimate=cost(2 * t * cols * (depth + n_z * rows), 2 * depth * cols),
-        name="residual",
-    )(z, *tokens, *hidden, *[teacher] * SPLIT, *[sides[0]] * n_z, *[sides[1]] * n_z)
+        cost_estimate=cost(2 * t * cols * n_z * rows * 2, 6 * t * cols),
+        name="project",
+    )(z, part, *hidden, *[sides[0]] * n_z, *[sides[1]] * n_z)
 
 
 def grad_right_kernel(n_z, parts, *refs):
@@ -237,22 +253,32 @@
 
     far = [swap(tokens, "tok", s) for s in range(1, n_tok)]
     near = gather(tokens, "rep")
+    first = hidden_of(near)
+    early = gather(first, "blk")
     sides = right_blocks.reshape(n_q, 2, GROUP // 2, n_z, n_b, FB)
+    sides = [sides[:, i] for i in range(2)]
+    far, early[1:3], sides = lax.optimization_barrier((far, early[1:3], sides))
+
     turn = [
         [(a * n_c + b, (b ^ side) * n_c + a) for a in range(n_z) for b in range(n_c)] for side in (0, n_c // 2)
     ]
-    sides = [lax.ppermute(sides[:, i], ("blk",) + plane, perm) for i, perm in enumerate(turn)]
-
-    first = hidden_of(near)
-    early = gather(first, "blk")
-    far, early[1:], _ = lax.optimization_barrier((far, early[1:], sides))
+    sides = [lax.ppermute(x, ("blk",) + plane, perm) for x, perm in zip(sides, turn)]
+
     chips = [near] + [gather(x, "rep") for x in far]
     pieces = [p for chip in chips for p in chip]
     hid = [first] + [hidden_of(chip) for chip in chips[1:]]
-    late = [[h] + [swap(h, "blk", s) for s in range(1, n_z)] for h in hid[1:]]
-    hidden = list(zip(early, *late))
-    resid, back = residual(jnp.reshape(z, (1,)).astype(jnp.int32), pieces, hid, teacher, sides, scale)
+    late = [[swap(h, "blk", s) for s in range(1, n_z)] for h in hid[1:]]
+    part, late, sides = lax.optimization_barrier((target(pieces, teacher), late, sides))
+    resid, back = project(jnp.reshape(z, (1,)).astype(jnp.int32), part, hid, sides, scale)
     backs = [back] + [swap(back[s], "blk", s) for s in range(1, n_z)]
+    hidden = list(zip(early, *[[h] + x for h, x in zip(hid[1:], late)]))
+
+    gr = grad_right_partial(hidden, resid)
+    total = gr[0].astype(F32)
+    for s in range(1, n_z):
+        total = total + swap(gr[s], "blk", s).astype(F32)
+    total = lax.ppermute(total.astype(BF), ("blk",) + plane, turn[0])
+    grad_right = total.reshape(n_b, n_k, FB).transpose(1, 0, 2).reshape(n_k, n_b * FB).astype(F32)
 
     gl = grad_left_of(backs, pieces, n_k)
     gl = gl.reshape(n_k, n_b, n_c, BI // n_c).transpose(2, 0, 3, 1).reshape(n_c, n_k, -1)
@@ -262,14 +288,6 @@
         got.append(swap(piece, plane, s) if s else piece)
     grad_left = place(jnp.reshape(c, (1,)).astype(jnp.int32), got, n_b)
 
-    hidden[0], _ = lax.optimization_barrier((hidden[0], backs[1:]))
-    gr = grad_right_partial(hidden, resid)
-    total = gr[0].astype(F32)
-    for s in range(1, n_z):
-        total = total + swap(gr[s], "blk", s).astype(F32)
-    total = lax.ppermute(total.astype(BF), ("blk",) + plane, turn[0])
-    total = total.reshape(n_b, n_k, FB).transpose(1, 0, 2).reshape(n_k, n_b * FB)
-    grad_right = total.astype(F32)
     return grad_left, grad_right
 
 

time: 123 us -> 102 us (0.83)
  the two profiles are of different devices: /device:TPU:0 before, /device:TPU:15 now
where the time goes in v6:
time: 102 us
  waiting for transfers between devices  40.1 us (39%)
  starting transfers between devices  27.7 us (27%)
  Pallas kernels  21 us (21%)
  local copies, waits for them, and re-layouts  8.61 us (8%)
  matrix products  3.34 us (3%)
    ppermute x18, waiting for transfers between devices, swap(): return lax.ppermute(x, axes, [(i, i ^ s) for i in range(n)])  40.1 us
    ppermute x18, starting transfers between devices, swap(): return lax.ppermute(x, axes, [(i, i ^ s) for i in range(n)])  19.3 us
    pallas_call x1, Pallas kernels, target(): pl.pallas_call(functools.partial(target_kernel, len(tokens)), grid=(cols...  11.3 us
    ppermute x2, starting transfers between devices, per_device(): lax.ppermute(x, ('blk',) + plane, perm)  4.93 us
    pallas_call x1, Pallas kernels, project(): pl.pallas_call(functools.partial(project_kernel, scale, len(hidden), n_z)...  4.61 us
    ppermute x1, starting transfers between devices, per_device(): total = lax.ppermute(total.astype(BF), ('blk',) + plane, turn[0])  3.45 us
    reshape x1, local copies, waits for them, and re-layouts, per_device(): left = left_blocks.reshape(n_b * BI, NB)  2.27 us
    pallas_call x1, Pallas kernels, grad_right_partial(): pl.pallas_call(functools.partial(grad_right_kernel, n_z, parts), grid=(n_...  2.17 us
  transfers between devices with their start and end apart: 21, of which 10 were waited for; matrix products, arithmetic and copies ran while one was open for 11% of the time, Pallas kernels for 17%

profile of v6, /device:TPU:15, one launch (start us, length us, event | category | flops | bytes accessed | tf_op | source)
XLA Modules:
  0.0 101.7 jit_solution(12807575502796720342)
XLA Ops:
  1.7 2.3 %reshape.32 = bf16[2048,64]{1,0:T(8,128)(2,1)} reshape(bf16[16,8192]{1,0:T(8,128)(2,1)} %param.6) | data formatting | bytes 524288 | tf_op jit(solution)/shard_map/reshape | solution.py:236
  4.0 1.8 %reshape.33 = bf16[4,2,2,4,16,224]{5,4,3,2,1,0:T(8,128)(2,1)S(1)} reshape(bf16[16,14336]{1,0:T(8,128)(2,1)} %param.7) | data formatting | bytes 917504 | tf_op jit(solution)/shard_map/reshape | solution.py:258
  5.7 1.6 %fusion = bf16[256,2048]{1,0:T(8,128)(2,1)S(1)} fusion(bf16[2048,64]{1,0:T(8,128)(2,1)} %reshape.32, s32[2048]{0:T(1024)S(1)} %get-tuple-element.42, s32[2048]{0:T(1024)S(1)} %get-tuple-element.43, s32[256]{0:T(256)S(1)} %get-tuple-element.45, s32[256]{0:T(256)S(1)} %get-tuple-element.46, pred[256]{0:T(512)(128)(4,1)S(1)} %get-tuple-element.41, ...), kind=kOutput, calls=%fused_computation.1 | convolution fusion | flops 69779456 | bytes 1333764 | tf_op jit(solution)/shard_map/dot_general | solution.py:246
  8.3 2.4 %collective-permute-start.3 = (bf16[256,256]{1,0:T(8,128)(2,1)S(1)}, bf16[256,256]{1,0:T(8,128)(2,1)S(1)}, u32[]{:S(2)}, u32[]{:S(2)}) collective-permute-start(bf16[256,256]{1,0:T(8,128)(2,1)S(1)} %pad_maximum_fusion.refs_0_), channel_id=1, source_target_pairs={{0,8},{4,12},{8,0},{12,4},{1,9},{5,13},{9,1},{13,5},{2,10},{6,14},... | collective-permute-start | bytes 393224 | tf_op jit(solution)/shard_map/ppermute | solution.py:210
  11.7 3.4 %collective-permute-done.1.refs_2_.refs_6_ = bf16[128,2048]{1,0:T(8,128)(2,1)S(1)} collective-permute-done((bf16[128,2048]{1,0:T(8,128)(2,1)}, bf16[128,2048]{1,0:T(8,128)(2,1)S(1)}, u32[]{:S(2)}, u32[]{:S(2)}) %collective-permute-start.1) | collective-permute-done | bytes 524320 | tf_op jit(solution)/shard_map/ppermute | solution.py:210
  15.1 1.5 %collective-permute-done.3.refs_4_ = bf16[256,256]{1,0:T(8,128)(2,1)S(1)} collective-permute-done((bf16[256,256]{1,0:T(8,128)(2,1)S(1)}, bf16[256,256]{1,0:T(8,128)(2,1)S(1)}, u32[]{:S(2)}, u32[]{:S(2)}) %collective-permute-start.3) | collective-permute-done | bytes 131104 | tf_op jit(solution)/shard_map/ppermute | solution.py:210
  18.1 4.9 %collective-permute-start.8 = (bf16[4,2,4,16,224]{4,3,2,1,0:T(8,128)(2,1)}, bf16[4,2,4,16,224]{4,3,2,1,0:T(8,128)(2,1)S(1)}, u32[]{:S(2)}, u32[]{:S(2)}) collective-permute-start(bf16[4,2,4,16,224]{4,3,2,1,0:T(8,128)(2,1)} %get-tuple-element.16), channel_id=1, source_target_pairs={{0,0},{1,4},{2,8},{3,12},{4,1},{5,5},{6,9},{7,13},{8,2},{9,6},{10,... | collective-permute-start | bytes 688136 | tf_op jit(solution)/shard_map/ppermute | solution.py:265
  25.2 1.3 %collective-permute-start.6 = (bf16[256,256]{1,0:T(8,128)(2,1)S(1)}, bf16[256,256]{1,0:T(8,128)(2,1)S(1)}, u32[]{:S(2)}, u32[]{:S(2)}) collective-permute-start(bf16[256,256]{1,0:T(8,128)(2,1)S(1)} %pad_maximum_fusion.1.refs_1_), channel_id=1, source_target_pairs={{0,8},{4,12},{8,0},{12,4},{1,9},{5,13},{9,1},{13,5},{2,10},{6,14},... | collective-permute-start | bytes 393224 | tf_op jit(solution)/shard_map/ppermute | solution.py:210
  26.7 11.3 %target.1.part_ref = bf16[512,3584]{1,0:T(8,128)(2,1)S(1)} custom-call(bf16[128,2048]{1,0:T(8,128)(2,1)S(1)} %copy-done, bf16[128,2048]{1,0:T(8,128)(2,1)S(1)} %collective-permute-done.refs_1_.refs_5_, bf16[128,2048]{1,0:T(8,128)(2,1)S(1)} %collective-permute-done.1.refs_2_.refs_6_, bf16[128,2048]{1,0:T(8,128)(2,1)S(1)} %collective-permute-done.4.refs_3_.refs_7_, ...), custom_call_target="tpu_custom_call" | custom-call | flops 7516192768 | bytes 14680064 | tf_op jit(solution)/shard_map/target/pallas_call | solution.py:53
  38.0 2.1 %collective-permute-start.16 = (bf16[256,256]{1,0:T(8,128)(2,1)S(1)}, bf16[256,256]{1,0:T(8,128)(2,1)S(1)}, u32[]{:S(2)}, u32[]{:S(2)}) collective-permute-start(bf16[256,256]{1,0:T(8,128)(2,1)S(1)} %collective-permute-done.3.refs_4_), channel_id=1, source_target_pairs={{0,4},{4,0},{8,12},{12,8},{1,5},{5,1},{9,13},{13,9},{2,6},{6,2},{1... | collective-permute-start | bytes 393224 | tf_op jit(solution)/shard_map/ppermute | solution.py:210
  40.1 2.9 %collective-permute-done.6.refs_5_ = bf16[256,256]{1,0:T(8,128)(2,1)S(1)} collective-permute-done((bf16[256,256]{1,0:T(8,128)(2,1)S(1)}, bf16[256,256]{1,0:T(8,128)(2,1)S(1)}, u32[]{:S(2)}, u32[]{:S(2)}) %collective-permute-start.6) | collective-permute-done | bytes 131104 | tf_op jit(solution)/shard_map/ppermute | solution.py:210
  43.0 2.2 %collective-permute-done.7.refs_7_ = bf16[256,256]{1,0:T(8,128)(2,1)S(1)} collective-permute-done((bf16[256,256]{1,0:T(8,128)(2,1)S(1)}, bf16[256,256]{1,0:T(8,128)(2,1)S(1)}, u32[]{:S(2)}, u32[]{:S(2)}) %collective-permute-start.7) | collective-permute-done | bytes 131104 | tf_op jit(solution)/shard_map/ppermute | solution.py:210
  45.1 4.6 %project.1 = (bf16[512,3584]{1,0:T(8,128)(2,1)S(1)}, bf16[4,256,512]{2,1,0:T(8,128)(2,1)S(1)}) custom-call(s32[1]{0:T(128)} %bitcast.1.z_ref, bf16[512,3584]{1,0:T(8,128)(2,1)S(1)} %target.1.part_ref, bf16[256,256]{1,0:T(8,128)(2,1)S(1)} %pad_maximum_fusion.refs_0_, bf16[256,256]{1,0:T(8,128)(2,1)S(1)} %pad_maximum_fusion.1.refs_1_, ...), custom_call_target="tpu_custom_call" | custom-call | flops 1879048192 | bytes 11010048 | tf_op jit(solution)/shard_map/project/pallas_call | solution.py:89
  49.8 2.2 %grad_right.1 = bf16[4,16,3584]{2,1,0:T(8,128)(2,1)S(1)} custom-call(bf16[256,256]{1,0:T(8,128)(2,1)S(1)} %pad_maximum_fusion.refs_0_, bf16[256,256]{1,0:T(8,128)(2,1)S(1)} %pad_maximum_fusion.1.refs_1_, bf16[256,256]{1,0:T(8,128)(2,1)S(1)} %collective-permute-done.2.refs_2_, bf16[256,256]{1,0:T(8,128)(2,1)S(1)} %collective-permute-done.5.refs_3_, ...), custom_call_target="tpu_custom_call" | custom-call | flops 939524096 | bytes 3670016 | tf_op jit(solution)/shard_map/grad_right/pallas_call | solution.py:135
  52.1 2.8 %collective-permute-start.18 = (bf16[16,3584]{1,0:T(8,128)(2,1)S(1)}, bf16[16,3584]{1,0:T(8,128)(2,1)S(1)}, u32[]{:S(2)}, u32[]{:S(2)}) collective-permute-start(bf16[16,3584]{1,0:T(8,128)(2,1)S(1)} %get-tuple-element.35), channel_id=1, source_target_pairs={{0,8},{4,12},{8,0},{12,4},{1,9},{5,13},{9,1},{13,5},{2,10},{6,14},... | collective-permute-start | bytes 344072 | tf_op jit(solution)/shard_map/ppermute | solution.py:210
  56.2 1.5 %collective-permute-start.11 = (bf16[256,512]{1,0:T(8,128)(2,1)S(1)}, bf16[256,512]{1,0:T(8,128)(2,1)S(1)}, u32[]{:S(2)}, u32[]{:S(2)}) collective-permute-start(bf16[256,512]{1,0:T(8,128)(2,1)S(1)} %get-tuple-element.29), channel_id=1, source_target_pairs={{0,8},{4,12},{8,0},{12,4},{1,9},{5,13},{9,1},{13,5},{2,10},{6,14},... | collective-permute-start | bytes 786440 | tf_op jit(solution)/shard_map/ppermute | solution.py:210
  58.6 2.3 %collective-permute-done.18 = bf16[16,3584]{1,0:T(8,128)(2,1)S(1)} collective-permute-done((bf16[16,3584]{1,0:T(8,128)(2,1)S(1)}, bf16[16,3584]{1,0:T(8,128)(2,1)S(1)}, u32[]{:S(2)}, u32[]{:S(2)}) %collective-permute-start.18) | collective-permute-done | bytes 114720 | tf_op jit(solution)/shard_map/ppermute | solution.py:210
  60.9 4.1 %collective-permute-done.19 = bf16[16,3584]{1,0:T(8,128)(2,1)S(1)} collective-permute-done((bf16[16,3584]{1,0:T(8,128)(2,1)S(1)}, bf16[16,3584]{1,0:T(8,128)(2,1)S(1)}, u32[]{:S(2)}, u32[]{:S(2)}) %collective-permute-start.19) | collective-permute-done | bytes 114720 | tf_op jit(solution)/shard_map/ppermute | solution.py:210
  65.0 3.5 %collective-permute-start.20 = (bf16[16,3584]{1,0:T(8,128)(2,1)S(1)}, bf16[16,3584]{1,0:T(8,128)(2,1)S(1)}, u32[]{:S(2)}, u32[]{:S(2)}) collective-permute-start(bf16[16,3584]{1,0:T(8,128)(2,1)S(1)} %fusion.3), channel_id=1, source_target_pairs={{0,0},{1,4},{2,8},{3,12},{4,1},{5,5},{6,9},{7,13},{8,2},{9,6},{10,... | collective-permute-start | bytes 344072 | tf_op jit(solution)/shard_map/ppermute | solution.py:280
  68.5 15.8 %collective-permute-done.11.refs_2_ = bf16[256,512]{1,0:T(8,128)(2,1)S(1)} collective-permute-done((bf16[256,512]{1,0:T(8,128)(2,1)S(1)}, bf16[256,512]{1,0:T(8,128)(2,1)S(1)}, u32[]{:S(2)}, u32[]{:S(2)}) %collective-permute-start.11) | collective-permute-done | bytes 262176 | tf_op jit(solution)/shard_map/ppermute | solution.py:210
  84.3 5.6 %collective-permute-done.12.refs_3_ = bf16[256,512]{1,0:T(8,128)(2,1)S(1)} collective-permute-done((bf16[256,512]{1,0:T(8,128)(2,1)S(1)}, bf16[256,512]{1,0:T(8,128)(2,1)S(1)}, u32[]{:S(2)}, u32[]{:S(2)}) %collective-permute-start.12) | collective-permute-done | bytes 262176 | tf_op jit(solution)/shard_map/ppermute | solution.py:210
  93.5 2.7 %collective-permute-start.14 = (bf16[16,512]{1,0:T(8,128)(2,1)S(1)}, bf16[16,512]{1,0:T(8,128)(2,1)S(1)}, u32[]{:S(2)}, u32[]{:S(2)}) collective-permute-start(bf16[16,512]{1,0:T(8,128)(2,1)S(1)} %get-tuple-element.37), channel_id=1, source_target_pairs={{0,2},{1,3},{2,0},{3,1},{4,6},{5,7},{6,4},{7,5},{8,10},{9,11},{10,... | collective-permute-start | bytes 49160 | tf_op jit(solution)/shard_map/ppermute | solution.py:210
  97.5 1.9 %collective-permute-done.15.refs_3_ = bf16[16,512]{1,0:T(8,128)(2,1)S(1)} collective-permute-done((bf16[16,512]{1,0:T(8,128)(2,1)S(1)}, bf16[16,512]{1,0:T(8,128)(2,1)S(1)}, u32[]{:S(2)}, u32[]{:S(2)}) %collective-permute-start.15) | collective-permute-done | bytes 16416 | tf_op jit(solution)/shard_map/ppermute | solution.py:210
  100.0 1.7 %place.1 = f32[16,2048]{1,0:T(8,128)} custom-call(s32[1]{0:T(128)} %bitcast.c_ref, bf16[16,512]{1,0:T(8,128)(2,1)} %get-tuple-element.39.refs_0_, bf16[16,512]{1,0:T(8,128)(2,1)} %copy-done.1, bf16[16,512]{1,0:T(8,128)(2,1)} %copy-done.2, bf16[16,512]{1,0:T(8,128)(2,1)} %copy-done.3), custom_call_target="tpu_custom_call" | custom-call | tf_op jit(solution)/shard_map/place/pallas_call | solution.py:198
  (56 shorter events, 14.6 us)
Async XLA Ops:
  0.6 7.2 %collective-permute-start = (bf16[128,2048]{1,0:T(8,128)(2,1)}, bf16[128,2048]{1,0:T(8,128)(2,1)S(1)}, u32[]{:S(2)}, u32[]{:S(2)}) collective-permute-start(bf16[128,2048]{1,0:T(8,128)(2,1)} %refs_4_.3), channel_id=1, source_target_pairs={{0,1},{1,0},{2,3},{3,2},{4,5},{5,4},{6,7},{7,6},{8,9},{9,8},{10,11... | collective-permute-start | bytes 1572872 | tf_op jit(solution)/shard_map/ppermute | solution.py:210
  1.4 13.7 %collective-permute-start.1 = (bf16[128,2048]{1,0:T(8,128)(2,1)}, bf16[128,2048]{1,0:T(8,128)(2,1)S(1)}, u32[]{:S(2)}, u32[]{:S(2)}) collective-permute-start(bf16[128,2048]{1,0:T(8,128)(2,1)} %refs_4_.3), channel_id=1, source_target_pairs={{0,2},{2,0},{1,3},{3,1},{4,6},{6,4},{5,7},{7,5},{8,10},{10,8},{9,1... | collective-permute-start | bytes 1572872 | tf_op jit(solution)/shard_map/ppermute | solution.py:210
  5.7 1.6 %copy-start = (bf16[128,2048]{1,0:T(8,128)(2,1)S(1)}, bf16[128,2048]{1,0:T(8,128)(2,1)}, u32[]{:S(2)}) copy-start(bf16[128,2048]{1,0:T(8,128)(2,1)} %refs_4_.3) | copy-start | bytes 1572868
  8.3 8.3 %collective-permute-start.3 = (bf16[256,256]{1,0:T(8,128)(2,1)S(1)}, bf16[256,256]{1,0:T(8,128)(2,1)S(1)}, u32[]{:S(2)}, u32[]{:S(2)}) collective-permute-start(bf16[256,256]{1,0:T(8,128)(2,1)S(1)} %pad_maximum_fusion.refs_0_), channel_id=1, source_target_pairs={{0,8},{4,12},{8,0},{12,4},{1,9},{5,13},{9,1},{13,5},{2,10},{6,14},... | collective-permute-start | bytes 393224 | tf_op jit(solution)/shard_map/ppermute | solution.py:210
  10.7 6.3 %collective-permute-start.2 = (bf16[256,256]{1,0:T(8,128)(2,1)S(1)}, bf16[256,256]{1,0:T(8,128)(2,1)S(1)}, u32[]{:S(2)}, u32[]{:S(2)}) collective-permute-start(bf16[256,256]{1,0:T(8,128)(2,1)S(1)} %pad_maximum_fusion.refs_0_), channel_id=1, source_target_pairs={{0,4},{4,0},{8,12},{12,8},{1,5},{5,1},{9,13},{13,9},{2,6},{6,2},{1... | collective-permute-start | bytes 393224 | tf_op jit(solution)/shard_map/ppermute | solution.py:210
  16.9 6.6 %collective-permute-start.4 = (bf16[128,2048]{1,0:T(8,128)(2,1)S(1)}, bf16[128,2048]{1,0:T(8,128)(2,1)S(1)}, u32[]{:S(2)}, u32[]{:S(2)}) collective-permute-start(bf16[128,2048]{1,0:T(8,128)(2,1)S(1)} %collective-permute-done.1.refs_2_.refs_6_), channel_id=1, source_target_pairs={{0,1},{1,0},{2,3},{3,2},{4,5},{5,4},{6,7},{7,6},{8,9},{9,8},{10,11... | collective-permute-start | bytes 1572872 | tf_op jit(solution)/shard_map/ppermute | solution.py:210
  18.1 19.9 %collective-permute-start.8 = (bf16[4,2,4,16,224]{4,3,2,1,0:T(8,128)(2,1)}, bf16[4,2,4,16,224]{4,3,2,1,0:T(8,128)(2,1)S(1)}, u32[]{:S(2)}, u32[]{:S(2)}) collective-permute-start(bf16[4,2,4,16,224]{4,3,2,1,0:T(8,128)(2,1)} %get-tuple-element.16), channel_id=1, source_target_pairs={{0,0},{1,4},{2,8},{3,12},{4,1},{5,5},{6,9},{7,13},{8,2},{9,6},{10,... | collective-permute-start | bytes 688136 | tf_op jit(solution)/shard_map/ppermute | solution.py:265
  23.0 17.1 %collective-permute-start.9 = (bf16[4,2,4,16,224]{4,3,2,1,0:T(8,128)(2,1)}, bf16[4,2,4,16,224]{4,3,2,1,0:T(8,128)(2,1)S(1)}, u32[]{:S(2)}, u32[]{:S(2)}) collective-permute-start(bf16[4,2,4,16,224]{4,3,2,1,0:T(8,128)(2,1)} %get-tuple-element.17), channel_id=1, source_target_pairs={{0,8},{1,12},{2,0},{3,4},{4,9},{5,13},{6,1},{7,5},{8,10},{9,14},{1... | collective-permute-start | bytes 688136 | tf_op jit(solution)/shard_map/ppermute | solution.py:265
  24.0 16.1 %collective-permute-start.5 = (bf16[256,256]{1,0:T(8,128)(2,1)S(1)}, bf16[256,256]{1,0:T(8,128)(2,1)S(1)}, u32[]{:S(2)}, u32[]{:S(2)}) collective-permute-start(bf16[256,256]{1,0:T(8,128)(2,1)S(1)} %pad_maximum_fusion.1.refs_1_), channel_id=1, source_target_pairs={{0,4},{4,0},{8,12},{12,8},{1,5},{5,1},{9,13},{13,9},{2,6},{6,2},{1... | collective-permute-start | bytes 393224 | tf_op jit(solution)/shard_map/ppermute | solution.py:210
  25.2 17.8 %collective-permute-start.6 = (bf16[256,256]{1,0:T(8,128)(2,1)S(1)}, bf16[256,256]{1,0:T(8,128)(2,1)S(1)}, u32[]{:S(2)}, u32[]{:S(2)}) collective-permute-start(bf16[256,256]{1,0:T(8,128)(2,1)S(1)} %pad_maximum_fusion.1.refs_1_), channel_id=1, source_target_pairs={{0,8},{4,12},{8,0},{12,4},{1,9},{5,13},{9,1},{13,5},{2,10},{6,14},... | collective-permute-start | bytes 393224 | tf_op jit(solution)/shard_map/ppermute | solution.py:210
  26.5 18.7 %collective-permute-start.7 = (bf16[256,256]{1,0:T(8,128)(2,1)S(1)}, bf16[256,256]{1,0:T(8,128)(2,1)S(1)}, u32[]{:S(2)}, u32[]{:S(2)}) collective-permute-start(bf16[256,256]{1,0:T(8,128)(2,1)S(1)} %pad_maximum_fusion.1.refs_1_), channel_id=1, source_target_pairs={{0,12},{4,8},{8,4},{12,0},{1,13},{5,9},{9,5},{13,1},{2,14},{6,10},... | collective-permute-start | bytes 393224 | tf_op jit(solution)/shard_map/ppermute | solution.py:210
  38.0 11.8 %collective-permute-start.16 = (bf16[256,256]{1,0:T(8,128)(2,1)S(1)}, bf16[256,256]{1,0:T(8,128)(2,1)S(1)}, u32[]{:S(2)}, u32[]{:S(2)}) collective-permute-start(bf16[256,256]{1,0:T(8,128)(2,1)S(1)} %collective-permute-done.3.refs_4_), channel_id=1, source_target_pairs={{0,4},{4,0},{8,12},{12,8},{1,5},{5,1},{9,13},{13,9},{2,6},{6,2},{1... | collective-permute-start | bytes 393224 | tf_op jit(solution)/shard_map/ppermute | solution.py:210
  52.0 5.7 %collective-permute-start.17 = (bf16[16,3584]{1,0:T(8,128)(2,1)S(1)}, bf16[16,3584]{1,0:T(8,128)(2,1)S(1)}, u32[]{:S(2)}, u32[]{:S(2)}) collective-permute-start(bf16[16,3584]{1,0:T(8,128)(2,1)S(1)} %get-tuple-element.33), channel_id=1, source_target_pairs={{0,4},{4,0},{8,12},{12,8},{1,5},{5,1},{9,13},{13,9},{2,6},{6,2},{1... | collective-permute-start | bytes 344072 | tf_op jit(solution)/shard_map/ppermute | solution.py:210
  52.1 8.8 %collective-permute-start.18 = (bf16[16,3584]{1,0:T(8,128)(2,1)S(1)}, bf16[16,3584]{1,0:T(8,128)(2,1)S(1)}, u32[]{:S(2)}, u32[]{:S(2)}) collective-permute-start(bf16[16,3584]{1,0:T(8,128)(2,1)S(1)} %get-tuple-element.35), channel_id=1, source_target_pairs={{0,8},{4,12},{8,0},{12,4},{1,9},{5,13},{9,1},{13,5},{2,10},{6,14},... | collective-permute-start | bytes 344072 | tf_op jit(solution)/shard_map/ppermute | solution.py:210
  54.9 10.1 %collective-permute-start.19 = (bf16[16,3584]{1,0:T(8,128)(2,1)S(1)}, bf16[16,3584]{1,0:T(8,128)(2,1)S(1)}, u32[]{:S(2)}, u32[]{:S(2)}) collective-permute-start(bf16[16,3584]{1,0:T(8,128)(2,1)S(1)} %get-tuple-element.34), channel_id=1, source_target_pairs={{0,12},{4,8},{8,4},{12,0},{1,13},{5,9},{9,5},{13,1},{2,14},{6,10},... | collective-permute-start | bytes 344072 | tf_op jit(solution)/shard_map/ppermute | solution.py:210
  54.9 13.5 %collective-permute-start.10 = (bf16[256,512]{1,0:T(8,128)(2,1)S(1)}, bf16[256,512]{1,0:T(8,128)(2,1)S(1)}, u32[]{:S(2)}, u32[]{:S(2)}) collective-permute-start(bf16[256,512]{1,0:T(8,128)(2,1)S(1)} %get-tuple-element.30), channel_id=1, source_target_pairs={{0,4},{4,0},{8,12},{12,8},{1,5},{5,1},{9,13},{13,9},{2,6},{6,2},{1... | collective-permute-start | bytes 786440 | tf_op jit(solution)/shard_map/ppermute | solution.py:210
  56.2 28.1 %collective-permute-start.11 = (bf16[256,512]{1,0:T(8,128)(2,1)S(1)}, bf16[256,512]{1,0:T(8,128)(2,1)S(1)}, u32[]{:S(2)}, u32[]{:S(2)}) collective-permute-start(bf16[256,512]{1,0:T(8,128)(2,1)S(1)} %get-tuple-element.29), channel_id=1, source_target_pairs={{0,8},{4,12},{8,0},{12,4},{1,9},{5,13},{9,1},{13,5},{2,10},{6,14},... | collective-permute-start | bytes 786440 | tf_op jit(solution)/shard_map/ppermute | solution.py:210
  57.6 32.3 %collective-permute-start.12 = (bf16[256,512]{1,0:T(8,128)(2,1)S(1)}, bf16[256,512]{1,0:T(8,128)(2,1)S(1)}, u32[]{:S(2)}, u32[]{:S(2)}) collective-permute-start(bf16[256,512]{1,0:T(8,128)(2,1)S(1)} %get-tuple-element.28), channel_id=1, source_target_pairs={{0,12},{4,8},{8,4},{12,0},{1,13},{5,9},{9,5},{13,1},{2,14},{6,10},... | collective-permute-start | bytes 786440 | tf_op jit(solution)/shard_map/ppermute | solution.py:210
  65.0 31.2 %collective-permute-start.20 = (bf16[16,3584]{1,0:T(8,128)(2,1)S(1)}, bf16[16,3584]{1,0:T(8,128)(2,1)S(1)}, u32[]{:S(2)}, u32[]{:S(2)}) collective-permute-start(bf16[16,3584]{1,0:T(8,128)(2,1)S(1)} %fusion.3), channel_id=1, source_target_pairs={{0,0},{1,4},{2,8},{3,12},{4,1},{5,5},{6,9},{7,13},{8,2},{9,6},{10,... | collective-permute-start | bytes 344072 | tf_op jit(solution)/shard_map/ppermute | solution.py:280
  93.0 4.4 %collective-permute-start.13 = (bf16[16,512]{1,0:T(8,128)(2,1)S(1)}, bf16[16,512]{1,0:T(8,128)(2,1)S(1)}, u32[]{:S(2)}, u32[]{:S(2)}) collective-permute-start(bf16[16,512]{1,0:T(8,128)(2,1)S(1)} %get-tuple-element.38), channel_id=1, source_target_pairs={{0,1},{1,0},{2,3},{3,2},{4,5},{5,4},{6,7},{7,6},{8,9},{9,8},{10,11... | collective-permute-start | bytes 49160 | tf_op jit(solution)/shard_map/ppermute | solution.py:210
  93.5 4.0 %collective-permute-start.14 = (bf16[16,512]{1,0:T(8,128)(2,1)S(1)}, bf16[16,512]{1,0:T(8,128)(2,1)S(1)}, u32[]{:S(2)}, u32[]{:S(2)}) collective-permute-start(bf16[16,512]{1,0:T(8,128)(2,1)S(1)} %get-tuple-element.37), channel_id=1, source_target_pairs={{0,2},{1,3},{2,0},{3,1},{4,6},{5,7},{6,4},{7,5},{8,10},{9,11},{10,... | collective-permute-start | bytes 49160 | tf_op jit(solution)/shard_map/ppermute | solution.py:210
  96.2 3.2 %collective-permute-start.15 = (bf16[16,512]{1,0:T(8,128)(2,1)S(1)}, bf16[16,512]{1,0:T(8,128)(2,1)S(1)}, u32[]{:S(2)}, u32[]{:S(2)}) collective-permute-start(bf16[16,512]{1,0:T(8,128)(2,1)S(1)} %get-tuple-element.36), channel_id=1, source_target_pairs={{0,3},{1,2},{2,1},{3,0},{4,7},{5,6},{6,5},{7,4},{8,11},{9,10},{10,... | collective-permute-start | bytes 49160 | tf_op jit(solution)/shard_map/ppermute | solution.py:210
  97.4 2.0 %copy-start.1 = (bf16[16,512]{1,0:T(8,128)(2,1)}, bf16[16,512]{1,0:T(8,128)(2,1)S(1)}, u32[]{:S(2)}) copy-start(bf16[16,512]{1,0:T(8,128)(2,1)S(1)} %collective-permute-done.13.refs_1_) | copy-start | bytes 49156
  97.5 1.9 %copy-start.2 = (bf16[16,512]{1,0:T(8,128)(2,1)}, bf16[16,512]{1,0:T(8,128)(2,1)S(1)}, u32[]{:S(2)}) copy-start(bf16[16,512]{1,0:T(8,128)(2,1)S(1)} %collective-permute-done.14.refs_2_) | copy-start | bytes 49156
  (1 other events, 0.6 us)

commit v7 on v6

--- a/solution.py
+++ b/solution.py
@@ -63,12 +63,12 @@
     )(*tokens, *[teacher] * SPLIT)
 
 
-def project_kernel(scale, n_hid, n_z, z_ref, part_ref, *refs):
+def project_kernel(scale, n_hid, n_z, n_per, z_ref, part_ref, *refs):
     hid_refs, right_refs, (resid_ref, back_ref) = refs[:n_hid], refs[n_hid:-2], refs[-2:]
-    right = jnp.stack(
-        [jnp.concatenate([a[0, :, 0], b[0, :, 0]], axis=0) for a, b in zip(right_refs[:n_z], right_refs[n_z:])],
-        axis=0,
-    )
+    right = jnp.stack([r[0, :, 0] for r in right_refs[:n_z]], axis=0)
+    if len(right_refs) > n_z:
+        other = jnp.stack([r[0, :, 0] for r in right_refs[n_z:]], axis=0)
+        right = jnp.where(pl.program_id(0) < n_per, right, other)
     right = spread(right)
     rows = right.shape[0] // n_z
     hid = jnp.concatenate([h[...] for h in hid_refs], axis=1)
@@ -81,19 +81,26 @@
 
 def project(z, part, hidden, sides, scale):
     t, cols = part.shape
-    n_q, half, n_z, n_b, _ = sides[0].shape
+    n_per, _, n_z, n_b, _ = sides[0].shape
+    n_q = n_per * len(sides)
     rows = GROUP * n_b
+
+    def at(q, i):
+        return jnp.clip(q - i * n_per, 0, n_per - 1)
+
     right_specs = [
-        pl.BlockSpec((1, half, 1, n_b, FB), lambda q, z, s=s: (q, 0, z[0] ^ s, 0, 0)) for s in range(n_z)
+        pl.BlockSpec((1, GROUP, 1, n_b, FB), lambda q, z, s=s, i=i: (at(q, i), 0, z[0] ^ s, 0, 0))
+        for i in range(len(sides))
+        for s in order_of(n_z)
     ]
     return pl.pallas_call(
-        functools.partial(project_kernel, scale, len(hidden), n_z),
+        functools.partial(project_kernel, scale, len(hidden), n_z, n_per),
         grid_spec=pltpu.PrefetchScalarGridSpec(
             num_scalar_prefetch=1,
             grid=(n_q,),
             in_specs=[pl.BlockSpec((t, COLS), lambda q, z: (0, q))]
             + [pl.BlockSpec((rows, h.shape[1]), lambda q, z: (q, 0)) for h in hidden]
-            + right_specs * 2,
+            + right_specs,
             out_specs=[
                 pl.BlockSpec((t, COLS), lambda q, z: (0, q)),
                 pl.BlockSpec((n_z, rows, t), lambda q, z: (0, q, 0)),
@@ -106,41 +113,41 @@
         compiler_params=pltpu.CompilerParams(vmem_limit_bytes=VMEM),
         cost_estimate=cost(2 * t * cols * n_z * rows * 2, 6 * t * cols),
         name="project",
-    )(z, part, *hidden, *[sides[0]] * n_z, *[sides[1]] * n_z)
-
-
-def grad_right_kernel(n_z, parts, *refs):
-    hid_refs, (resid_ref, out_ref) = refs[:-2], refs[-2:]
+    )(z, part, *hidden, *[x for x in sides for _ in range(n_z)])
+
+
+def grad_right_kernel(*refs):
+    hid_refs, (resid_ref, first_ref, second_ref) = refs[:-3], refs[-3:]
     hid = jnp.concatenate(
-        [
-            jnp.concatenate([r[...] for r in hid_refs[s * parts : (s + 1) * parts]], axis=1)
-            for s in range(n_z)
-        ],
-        axis=0,
+        [jnp.concatenate([r[...] for r in hid_refs[h::2]], axis=2) for h in range(2)], axis=0
     )
-    prod = jnp.dot(hid, resid_ref[...], preferred_element_type=F32)
-    prod = prod.reshape(n_z, GROUP, prod.shape[0] // (n_z * GROUP), COLS)
+    n_z, rows, t = hid.shape
+    prod = jnp.dot(hid.reshape(n_z * rows, t), resid_ref[...], preferred_element_type=F32)
+    prod = prod.reshape(n_z, GROUP, rows // GROUP, COLS)
     block = lax.broadcasted_iota(jnp.int32, (1, 1, COLS), 2) // FB
     total = prod[:, 0]
     for k in range(1, GROUP):
         total = jnp.where(block == k, prod[:, k], total)
-    out_ref[...] = total.astype(BF)
+    first_ref[...] = total[: n_z // 2].astype(BF)
+    second_ref[...] = total[n_z // 2 :].astype(BF)
 
 
 def grad_right_partial(hidden, resid):
     t, cols = resid.shape
-    n_z, parts = len(hidden), len(hidden[0])
     n_q = cols // COLS
-    rows = hidden[0][0].shape[0] // n_q
-    return pl.pallas_call(
-        functools.partial(grad_right_kernel, n_z, parts),
+    half, rows, _ = hidden[0][0].shape
+    rows //= n_q
+    return pl.pallas_call(
+        grad_right_kernel,
         grid=(n_q,),
-        in_specs=[pl.BlockSpec((rows, h.shape[1]), lambda q: (q, 0)) for hs in hidden for h in hs]
+        in_specs=[
+            pl.BlockSpec((half, rows, h.shape[2]), lambda q: (0, q, 0)) for hs in hidden for h in hs
+        ]
         + [pl.BlockSpec((t, COLS), lambda q: (0, q))],
-        out_specs=pl.BlockSpec((n_z, rows // GROUP, COLS), lambda q: (0, 0, q)),
-        out_shape=jax.ShapeDtypeStruct((n_z, rows // GROUP, cols), BF),
+        out_specs=[pl.BlockSpec((half, rows // GROUP, COLS), lambda q: (0, 0, q))] * 2,
+        out_shape=[jax.ShapeDtypeStruct((half, rows // GROUP, cols), BF)] * 2,
         compiler_params=pltpu.CompilerParams(vmem_limit_bytes=VMEM),
-        cost_estimate=cost(2 * t * cols * n_z * rows, 2 * t * cols),
+        cost_estimate=cost(4 * t * cols * half * rows, 2 * t * cols),
         name="grad_right",
     )(*[h for hs in hidden for h in hs], resid)
 
@@ -217,6 +224,24 @@
     return got
 
 
+def doubling(x, axes, second):
+    bit = lax.axis_size(axes) // 4
+    first, second = x[None], second[None]
+    while bit:
+        if second is not None:
+            first = jnp.concatenate([first, second], axis=0)
+        second = swap(first, axes, bit)
+        bit //= 2
+    return first, second
+
+
+def order_of(n):
+    order, bit = [0], n // 2
+    while bit:
+        order, bit = order + [o ^ bit for o in order], bit // 2
+    return order
+
+
 def pick(x, at):
     return lax.dynamic_index_in_dim(x, at, 0, keepdims=False)
 
@@ -251,33 +276,39 @@
             [lax.dot_general(left, p, NT, preferred_element_type=F32).astype(BF) for p in chip], axis=1
         )
 
+    turn = [
+        [(a * n_c + b, (b ^ side) * n_c + a) for a in range(n_z) for b in range(n_c)] for side in (0, n_c // 2)
+    ]
+    n_side = 2 if n_q % 2 == 0 else 1
+    sides = [
+        lax.ppermute(x, ("blk",) + plane, perm).reshape(n_q // n_side, GROUP, n_z, n_b, FB)
+        for x, perm in zip(jnp.split(right_blocks, n_side), turn)
+    ]
+
     far = [swap(tokens, "tok", s) for s in range(1, n_tok)]
     near = gather(tokens, "rep")
     first = hidden_of(near)
-    early = gather(first, "blk")
-    sides = right_blocks.reshape(n_q, 2, GROUP // 2, n_z, n_b, FB)
-    sides = [sides[:, i] for i in range(2)]
-    far, early[1:3], sides = lax.optimization_barrier((far, early[1:3], sides))
-
-    turn = [
-        [(a * n_c + b, (b ^ side) * n_c + a) for a in range(n_z) for b in range(n_c)] for side in (0, n_c // 2)
-    ]
-    sides = [lax.ppermute(x, ("blk",) + plane, perm) for x, perm in zip(sides, turn)]
-
+    early = doubling(first, "blk", swap(first, "blk", n_z // 2))
+    far, _, _ = lax.optimization_barrier((far, early[0], sides))
     chips = [near] + [gather(x, "rep") for x in far]
     pieces = [p for chip in chips for p in chip]
     hid = [first] + [hidden_of(chip) for chip in chips[1:]]
-    late = [[swap(h, "blk", s) for s in range(1, n_z)] for h in hid[1:]]
-    part, late, sides = lax.optimization_barrier((target(pieces, teacher), late, sides))
+    late = [swap(h, "blk", n_z // 2) for h in hid[1:]]
+    part, late = lax.optimization_barrier((target(pieces, teacher), late))
+    late = [doubling(h, "blk", x) for h, x in zip(hid[1:], late)]
     resid, back = project(jnp.reshape(z, (1,)).astype(jnp.int32), part, hid, sides, scale)
-    backs = [back] + [swap(back[s], "blk", s) for s in range(1, n_z)]
-    hidden = list(zip(early, *[[h] + x for h, x in zip(hid[1:], late)]))
-
-    gr = grad_right_partial(hidden, resid)
-    total = gr[0].astype(F32)
-    for s in range(1, n_z):
-        total = total + swap(gr[s], "blk", s).astype(F32)
-    total = lax.ppermute(total.astype(BF), ("blk",) + plane, turn[0])
+    backs = [back] + [swap(back[i], "blk", s) for i, s in enumerate(order_of(n_z)) if s]
+
+    mine, others = grad_right_partial([early] + late, resid)
+    bit = 1
+    while True:
+        mine = mine.astype(F32) + swap(others, "blk", bit).astype(F32)
+        if mine.shape[0] == 1:
+            break
+        mine = mine.astype(BF)
+        mine, others = mine[: mine.shape[0] // 2], mine[mine.shape[0] // 2 :]
+        bit *= 2
+    total = lax.ppermute(mine[0].astype(BF), ("blk",) + plane, turn[0])
     grad_right = total.reshape(n_b, n_k, FB).transpose(1, 0, 2).reshape(n_k, n_b * FB).astype(F32)
 
     gl = grad_left_of(backs, pieces, n_k)

time: 102 us -> 109 us (1.069)
  the two profiles are of different devices: /device:TPU:15 before, /device:TPU:0 now
where the time goes in v7:
time: 109 us; the launch traced here: 108 us
  waiting for transfers between devices  32.3 us (30%)
  starting transfers between devices  27.4 us (25%)
  Pallas kernels  23.1 us (21%)
  local copies, waits for them, and re-layouts  20.3 us (19%)
  matrix products  2.23 us (2%)
  other arithmetic  1.86 us (2%)
    ppermute x15, waiting for transfers between devices, swap(): return lax.ppermute(x, axes, [(i, i ^ s) for i in range(n)])  28.5 us
    ppermute x15, starting transfers between devices, swap(): return lax.ppermute(x, axes, [(i, i ^ s) for i in range(n)])  22.1 us
    pallas_call x1, Pallas kernels, target(): pl.pallas_call(functools.partial(target_kernel, len(tokens)), grid=(cols...  11.3 us
    unnamed x22, local copies, waits for them, and re-layouts  8.43 us
    pallas_call x1, Pallas kernels, project(): pl.pallas_call(functools.partial(project_kernel, scale, len(hidden), n_z,...  4.6 us
    ppermute x2, starting transfers between devices, per_device(): lax.ppermute(x, ('blk',) + plane, perm)  4.56 us
    reshape x2, local copies, waits for them, and re-layouts, per_device(): lax.ppermute(x, ('blk',) + plane, perm)  4.03 us
    ppermute x2, waiting for transfers between devices, per_device(): lax.ppermute(x, ('blk',) + plane, perm)  3.8 us
  transfers between devices with their start and end apart: 18, of which 10 were waited for; matrix products, arithmetic and copies ran while one was open for 13% of the time, Pallas kernels for 18%

profile of v7, /device:TPU:0, one launch (start us, length us, event | category | flops | bytes accessed | tf_op | source)
XLA Modules:
  0.0 108.1 jit_solution(3993942989379916069)
XLA Ops:
  1.1 2.6 %collective-permute-start.1 = (bf16[128,2048]{1,0:T(8,128)(2,1)}, bf16[128,2048]{1,0:T(8,128)(2,1)S(1)}, u32[]{:S(2)}, u32[]{:S(2)}) collective-permute-start(bf16[128,2048]{1,0:T(8,128)(2,1)} %refs_4_.3), channel_id=1, source_target_pairs={{0,2},{2,0},{1,3},{3,1},{4,6},{6,4},{5,7},{7,5},{8,10},{10,8},{9,1... | collective-permute-start | bytes 1572872 | tf_op jit(solution)/shard_map/ppermute | solution.py:217
  3.7 1.8 %fusion.13 = (bf16[8,14336]{1,0:T(8,128)(2,1)S(1)}, bf16[8,14336]{1,0:T(8,128)(2,1)}) fusion(bf16[16,14336]{1,0:T(8,128)(2,1)} %param.7), kind=kLoop, calls=%fused_computation.43 | loop fusion | bytes 917504 | tf_op jit(solution)/shard_map/split | solution.py:285
  5.5 3.5 %collective-permute-start.3 = (bf16[8,14336]{1,0:T(8,128)(2,1)}, bf16[8,14336]{1,0:T(8,128)(2,1)}, u32[]{:S(2)}, u32[]{:S(2)}) collective-permute-start(bf16[8,14336]{1,0:T(8,128)(2,1)} %get-tuple-element.20), channel_id=1, source_target_pairs={{0,0},{1,4},{2,8},{3,12},{4,1},{5,5},{6,9},{7,13},{8,2},{9,6},{10,... | collective-permute-start | bytes 688136 | tf_op jit(solution)/shard_map/ppermute | solution.py:284
  13.5 2.1 %collective-permute-start.2 = (bf16[256,256]{1,0:T(8,128)(2,1)S(1)}, bf16[256,256]{1,0:T(8,128)(2,1)S(1)}, u32[]{:S(2)}, u32[]{:S(2)}) collective-permute-start(bf16[256,256]{1,0:T(8,128)(2,1)S(1)} %get-tuple-element.24.refs_0_), channel_id=1, source_target_pairs={{0,8},{4,12},{8,0},{12,4},{1,9},{5,13},{9,1},{13,5},{2,10},{6,14},... | collective-permute-start | bytes 393224 | tf_op jit(solution)/shard_map/ppermute | solution.py:217
  15.6 2.0 %reshape.35.refs_2_.refs_3_.refs_4_.refs_5_ = bf16[2,4,4,16,224]{4,3,2,1,0:T(8,128)(2,1)} reshape(bf16[8,14336]{1,0:T(8,128)(2,1)} %collective-permute-done.3) | data formatting | bytes 458752 | tf_op jit(solution)/shard_map/reshape | solution.py:284
  17.7 3.8 %collective-permute-done.4 = bf16[8,14336]{1,0:T(8,128)(2,1)} collective-permute-done((bf16[8,14336]{1,0:T(8,128)(2,1)S(1)}, bf16[8,14336]{1,0:T(8,128)(2,1)}, u32[]{:S(2)}, u32[]{:S(2)}) %collective-permute-start.4) | collective-permute-done | bytes 229408 | tf_op jit(solution)/shard_map/ppermute | solution.py:284
  21.5 2.0 %reshape.36.refs_6_.refs_7_.refs_8_.refs_9_ = bf16[2,4,4,16,224]{4,3,2,1,0:T(8,128)(2,1)} reshape(bf16[8,14336]{1,0:T(8,128)(2,1)} %collective-permute-done.4) | data formatting | bytes 458752 | tf_op jit(solution)/shard_map/reshape | solution.py:284
  23.5 3.5 %collective-permute-done.2 = bf16[256,256]{1,0:T(8,128)(2,1)S(1)} collective-permute-done((bf16[256,256]{1,0:T(8,128)(2,1)S(1)}, bf16[256,256]{1,0:T(8,128)(2,1)S(1)}, u32[]{:S(2)}, u32[]{:S(2)}) %collective-permute-start.2) | collective-permute-done | bytes 131104 | tf_op jit(solution)/shard_map/ppermute | solution.py:217
  29.5 4.4 %collective-permute-start.6 = (bf16[256,256]{1,0:T(8,128)(2,1)S(1)}, bf16[256,256]{1,0:T(8,128)(2,1)S(1)}, u32[]{:S(2)}, u32[]{:S(2)}) collective-permute-start(bf16[256,256]{1,0:T(8,128)(2,1)S(1)} %get-tuple-element.22.refs_1_), channel_id=1, source_target_pairs={{0,8},{4,12},{8,0},{12,4},{1,9},{5,13},{9,1},{13,5},{2,10},{6,14},... | collective-permute-start | bytes 393224 | tf_op jit(solution)/shard_map/ppermute | solution.py:217
  33.9 11.3 %target.1.part_ref = bf16[512,3584]{1,0:T(8,128)(2,1)S(1)} custom-call(bf16[128,2048]{1,0:T(8,128)(2,1)S(1)} %copy-done, bf16[128,2048]{1,0:T(8,128)(2,1)S(1)} %collective-permute-done.refs_1_.refs_5_, bf16[128,2048]{1,0:T(8,128)(2,1)S(1)} %collective-permute-done.1.refs_2_.refs_6_, bf16[128,2048]{1,0:T(8,128)(2,1)S(1)} %collective-permute-done.5.refs_3_.refs_7_, ...), custom_call_target="tpu_custom_call" | custom-call | flops 7516192768 | bytes 14680064 | tf_op jit(solution)/shard_map/target/pallas_call | solution.py:53
  45.2 1.8 %copy-done.1 = bf16[512,3584]{1,0:T(8,128)(2,1)} copy-done((bf16[512,3584]{1,0:T(8,128)(2,1)}, bf16[512,3584]{1,0:T(8,128)(2,1)S(1)}, u32[]{:S(2)}) %copy-start.1) | copy-done | bytes 3670040
  48.8 2.0 %copy-done.2 = bf16[512,3584]{1,0:T(8,128)(2,1)S(1)} copy-done((bf16[512,3584]{1,0:T(8,128)(2,1)S(1)}, bf16[512,3584]{1,0:T(8,128)(2,1)}, u32[]{:S(2)}) %copy-start.2) | copy-done | bytes 3670040
  53.7 4.6 %project.1 = (bf16[512,3584]{1,0:T(8,128)(2,1)S(1)}, bf16[4,256,512]{2,1,0:T(8,128)(2,1)S(1)}) custom-call(s32[1]{0:T(128)} %bitcast.1.z_ref, bf16[512,3584]{1,0:T(8,128)(2,1)S(1)} %copy-done.2, bf16[256,256]{1,0:T(8,128)(2,1)S(1)} %get-tuple-element.24.refs_0_, bf16[256,256]{1,0:T(8,128)(2,1)S(1)} %copy-done.6, bf16[2,4,4,16,224]{4,3,2,1,0:T(8,128)(2,1)S(1)} %copy-done.3, ...), custom_call_target="tpu_custom_call" | custom-call | flops 1879048192 | bytes 11010048 | tf_op jit(solution)/shard_map/project/pallas_call | solution.py:96
  58.3 3.4 %grad_right.1 = (bf16[2,16,3584]{2,1,0:T(8,128)(2,1)S(1)}, bf16[2,16,3584]{2,1,0:T(8,128)(2,1)S(1)}) custom-call(bf16[2,256,256]{2,1,0:T(8,128)(2,1)S(1)} %pad_maximum_fusion.refs_0_, bf16[2,256,256]{2,1,0:T(8,128)(2,1)} %collective-permute-done.13.refs_1_, bf16[2,256,256]{2,1,0:T(8,128)(2,1)} %pad_maximum_fusion.1.refs_2_, ...), custom_call_target="tpu_custom_call" | custom-call | flops 939524096 | bytes 3670016 | tf_op jit(solution)/shard_map/grad_right/pallas_call | solution.py:140
  64.7 3.3 %collective-permute-start.9 = (bf16[256,512]{1,0:T(8,128)(2,1)}, bf16[256,512]{1,0:T(8,128)(2,1)}, u32[]{:S(2)}, u32[]{:S(2)}) collective-permute-start(bf16[256,512]{1,0:T(8,128)(2,1)} %get-tuple-element.16), channel_id=1, source_target_pairs={{0,12},{4,8},{8,4},{12,0},{1,13},{5,9},{9,5},{13,1},{2,14},{6,10},... | collective-permute-start | bytes 786440 | tf_op jit(solution)/shard_map/ppermute | solution.py:217
  67.9 4.9 %collective-permute-done.15 = bf16[2,16,3584]{2,1,0:T(8,128)(2,1)S(1)} collective-permute-done((bf16[2,16,3584]{2,1,0:T(8,128)(2,1)S(1)}, bf16[2,16,3584]{2,1,0:T(8,128)(2,1)S(1)}, u32[]{:S(2)}, u32[]{:S(2)}) %collective-permute-start.15) | collective-permute-done | bytes 229408 | tf_op jit(solution)/shard_map/ppermute | solution.py:217
  74.2 5.3 %collective-permute-done.7.refs_1_ = bf16[256,512]{1,0:T(8,128)(2,1)S(1)} collective-permute-done((bf16[256,512]{1,0:T(8,128)(2,1)}, bf16[256,512]{1,0:T(8,128)(2,1)S(1)}, u32[]{:S(2)}, u32[]{:S(2)}) %collective-permute-start.7) | collective-permute-done | bytes 262176 | tf_op jit(solution)/shard_map/ppermute | solution.py:217
  79.5 5.7 %collective-permute-done.8.refs_2_ = bf16[256,512]{1,0:T(8,128)(2,1)} collective-permute-done((bf16[256,512]{1,0:T(8,128)(2,1)}, bf16[256,512]{1,0:T(8,128)(2,1)}, u32[]{:S(2)}, u32[]{:S(2)}) %collective-permute-start.8) | collective-permute-done | bytes 262176 | tf_op jit(solution)/shard_map/ppermute | solution.py:217
  85.2 1.5 %collective-permute-done.9.refs_3_ = bf16[256,512]{1,0:T(8,128)(2,1)} collective-permute-done((bf16[256,512]{1,0:T(8,128)(2,1)}, bf16[256,512]{1,0:T(8,128)(2,1)}, u32[]{:S(2)}, u32[]{:S(2)}) %collective-permute-start.9) | collective-permute-done | bytes 262176 | tf_op jit(solution)/shard_map/ppermute | solution.py:217
  86.8 2.2 %grad_left.1 = bf16[16,2048]{1,0:T(8,128)(2,1)S(1)} custom-call(bf16[4,256,512]{2,1,0:T(8,128)(2,1)S(1)} %get-tuple-element.11.refs_0_, bf16[256,512]{1,0:T(8,128)(2,1)S(1)} %collective-permute-done.7.refs_1_, bf16[256,512]{1,0:T(8,128)(2,1)} %collective-permute-done.8.refs_2_, bf16[256,512]{1,0:T(8,128)(2,1)} %collective-permute-done.9.refs_3_, ...), custom_call_target="tpu_custom_call" | custom-call | flops 536870912 | bytes 2097152 | tf_op jit(solution)/shard_map/grad_left/pallas_call | solution.py:175
  90.2 3.6 %collective-permute-done.16 = bf16[1,16,3584]{2,1,0:T(8,128)(2,1)} collective-permute-done((bf16[1,16,3584]{2,1,0:T(8,128)(2,1)}, bf16[1,16,3584]{2,1,0:T(8,128)(2,1)}, u32[]{:S(2)}, u32[]{:S(2)}) %collective-permute-start.16) | collective-permute-done | bytes 114720 | tf_op jit(solution)/shard_map/ppermute | solution.py:217
  96.0 4.1 %collective-permute-start.10 = (bf16[16,512]{1,0:T(8,128)(2,1)S(1)}, bf16[16,512]{1,0:T(8,128)(2,1)S(1)}, u32[]{:S(2)}, u32[]{:S(2)}) collective-permute-start(bf16[16,512]{1,0:T(8,128)(2,1)S(1)} %get-tuple-element.27), channel_id=1, source_target_pairs={{0,1},{1,0},{2,3},{3,2},{4,5},{5,4},{6,7},{7,6},{8,9},{9,8},{10,11... | collective-permute-start | bytes 49160 | tf_op jit(solution)/shard_map/ppermute | solution.py:217
  101.5 2.4 %collective-permute-done.11.refs_2_ = bf16[16,512]{1,0:T(8,128)(2,1)S(1)} collective-permute-done((bf16[16,512]{1,0:T(8,128)(2,1)S(1)}, bf16[16,512]{1,0:T(8,128)(2,1)S(1)}, u32[]{:S(2)}, u32[]{:S(2)}) %collective-permute-start.11) | collective-permute-done | bytes 16416 | tf_op jit(solution)/shard_map/ppermute | solution.py:217
  105.2 1.7 %place.1 = f32[16,2048]{1,0:T(8,128)} custom-call(s32[1]{0:T(128)} %bitcast.c_ref, bf16[16,512]{1,0:T(8,128)(2,1)} %get-tuple-element.28.refs_0_, bf16[16,512]{1,0:T(8,128)(2,1)} %copy-done.8, bf16[16,512]{1,0:T(8,128)(2,1)} %copy-done.9, bf16[16,512]{1,0:T(8,128)(2,1)} %copy-done.10), custom_call_target="tpu_custom_call" | custom-call | tf_op jit(solution)/shard_map/place/pallas_call | solution.py:205
  (68 shorter events, 23.8 us)
Async XLA Ops:
  0.6 12.4 %collective-permute-start = (bf16[128,2048]{1,0:T(8,128)(2,1)}, bf16[128,2048]{1,0:T(8,128)(2,1)S(1)}, u32[]{:S(2)}, u32[]{:S(2)}) collective-permute-start(bf16[128,2048]{1,0:T(8,128)(2,1)} %refs_4_.3), channel_id=1, source_target_pairs={{0,1},{1,0},{2,3},{3,2},{4,5},{5,4},{6,7},{7,6},{8,9},{9,8},{10,11... | collective-permute-start | bytes 1572872 | tf_op jit(solution)/shard_map/ppermute | solution.py:217
  1.1 25.9 %collective-permute-start.1 = (bf16[128,2048]{1,0:T(8,128)(2,1)}, bf16[128,2048]{1,0:T(8,128)(2,1)S(1)}, u32[]{:S(2)}, u32[]{:S(2)}) collective-permute-start(bf16[128,2048]{1,0:T(8,128)(2,1)} %refs_4_.3), channel_id=1, source_target_pairs={{0,2},{2,0},{1,3},{3,1},{4,6},{6,4},{5,7},{7,5},{8,10},{10,8},{9,1... | collective-permute-start | bytes 1572872 | tf_op jit(solution)/shard_map/ppermute | solution.py:217
  5.5 10.2 %collective-permute-start.3 = (bf16[8,14336]{1,0:T(8,128)(2,1)}, bf16[8,14336]{1,0:T(8,128)(2,1)}, u32[]{:S(2)}, u32[]{:S(2)}) collective-permute-start(bf16[8,14336]{1,0:T(8,128)(2,1)} %get-tuple-element.20), channel_id=1, source_target_pairs={{0,0},{1,4},{2,8},{3,12},{4,1},{5,5},{6,9},{7,13},{8,2},{9,6},{10,... | collective-permute-start | bytes 688136 | tf_op jit(solution)/shard_map/ppermute | solution.py:284
  9.0 12.5 %collective-permute-start.4 = (bf16[8,14336]{1,0:T(8,128)(2,1)S(1)}, bf16[8,14336]{1,0:T(8,128)(2,1)}, u32[]{:S(2)}, u32[]{:S(2)}) collective-permute-start(bf16[8,14336]{1,0:T(8,128)(2,1)S(1)} %get-tuple-element.19), channel_id=1, source_target_pairs={{0,8},{1,12},{2,0},{3,4},{4,9},{5,13},{6,1},{7,5},{8,10},{9,14},{1... | collective-permute-start | bytes 688136 | tf_op jit(solution)/shard_map/ppermute | solution.py:284
  11.6 1.0 copy-start
  13.5 13.5 %collective-permute-start.2 = (bf16[256,256]{1,0:T(8,128)(2,1)S(1)}, bf16[256,256]{1,0:T(8,128)(2,1)S(1)}, u32[]{:S(2)}, u32[]{:S(2)}) collective-permute-start(bf16[256,256]{1,0:T(8,128)(2,1)S(1)} %get-tuple-element.24.refs_0_), channel_id=1, source_target_pairs={{0,8},{4,12},{8,0},{12,4},{1,9},{5,13},{9,1},{13,5},{2,10},{6,14},... | collective-permute-start | bytes 393224 | tf_op jit(solution)/shard_map/ppermute | solution.py:217
  27.0 2.0 %collective-permute-start.5 = (bf16[128,2048]{1,0:T(8,128)(2,1)S(1)}, bf16[128,2048]{1,0:T(8,128)(2,1)S(1)}, u32[]{:S(2)}, u32[]{:S(2)}) collective-permute-start(bf16[128,2048]{1,0:T(8,128)(2,1)S(1)} %collective-permute-done.1.refs_2_.refs_6_), channel_id=1, source_target_pairs={{0,1},{1,0},{2,3},{3,2},{4,5},{5,4},{6,7},{7,6},{8,9},{9,8},{10,11... | collective-permute-start | bytes 1572872 | tf_op jit(solution)/shard_map/ppermute | solution.py:217
  27.1 31.2 %collective-permute-start.13 = (bf16[2,256,256]{2,1,0:T(8,128)(2,1)S(1)}, bf16[2,256,256]{2,1,0:T(8,128)(2,1)}, u32[]{:S(2)}, u32[]{:S(2)}) collective-permute-start(bf16[2,256,256]{2,1,0:T(8,128)(2,1)S(1)} %pad_maximum_fusion.refs_0_), channel_id=1, source_target_pairs={{0,4},{4,0},{8,12},{12,8},{1,5},{5,1},{9,13},{13,9},{2,6},{6,2},{1... | collective-permute-start | bytes 786440 | tf_op jit(solution)/shard_map/ppermute | solution.py:217
  29.5 15.7 %copy-start.5 = (bf16[256,256]{1,0:T(8,128)(2,1)}, bf16[256,256]{1,0:T(8,128)(2,1)S(1)}, u32[]{:S(2)}) copy-start(bf16[256,256]{1,0:T(8,128)(2,1)S(1)} %get-tuple-element.22.refs_1_) | copy-start | bytes 393220
  29.5 17.5 %collective-permute-start.6 = (bf16[256,256]{1,0:T(8,128)(2,1)S(1)}, bf16[256,256]{1,0:T(8,128)(2,1)S(1)}, u32[]{:S(2)}, u32[]{:S(2)}) collective-permute-start(bf16[256,256]{1,0:T(8,128)(2,1)S(1)} %get-tuple-element.22.refs_1_), channel_id=1, source_target_pairs={{0,8},{4,12},{8,0},{12,4},{1,9},{5,13},{9,1},{13,5},{2,10},{6,14},... | collective-permute-start | bytes 393224 | tf_op jit(solution)/shard_map/ppermute | solution.py:217
  45.2 1.8 %copy-start.1 = (bf16[512,3584]{1,0:T(8,128)(2,1)}, bf16[512,3584]{1,0:T(8,128)(2,1)S(1)}, u32[]{:S(2)}) copy-start(bf16[512,3584]{1,0:T(8,128)(2,1)S(1)} %target.1.part_ref) | copy-start | bytes 11010052
  47.7 10.6 %collective-permute-start.14 = (bf16[2,256,256]{2,1,0:T(8,128)(2,1)}, bf16[2,256,256]{2,1,0:T(8,128)(2,1)}, u32[]{:S(2)}, u32[]{:S(2)}) collective-permute-start(bf16[2,256,256]{2,1,0:T(8,128)(2,1)} %pad_maximum_fusion.1.refs_2_), channel_id=1, source_target_pairs={{0,4},{4,0},{8,12},{12,8},{1,5},{5,1},{9,13},{13,9},{2,6},{6,2},{1... | collective-permute-start | bytes 786440 | tf_op jit(solution)/shard_map/ppermute | solution.py:217
  48.8 2.0 %copy-start.2 = (bf16[512,3584]{1,0:T(8,128)(2,1)S(1)}, bf16[512,3584]{1,0:T(8,128)(2,1)}, u32[]{:S(2)}) copy-start(bf16[512,3584]{1,0:T(8,128)(2,1)} %copy-done.1) | copy-start | bytes 11010052
  50.9 0.9 copy-start.3
  61.7 11.2 %collective-permute-start.15 = (bf16[2,16,3584]{2,1,0:T(8,128)(2,1)S(1)}, bf16[2,16,3584]{2,1,0:T(8,128)(2,1)S(1)}, u32[]{:S(2)}, u32[]{:S(2)}) collective-permute-start(bf16[2,16,3584]{2,1,0:T(8,128)(2,1)S(1)} %get-tuple-element.15), channel_id=1, source_target_pairs={{0,4},{4,0},{8,12},{12,8},{1,5},{5,1},{9,13},{13,9},{2,6},{6,2},{1... | collective-permute-start | bytes 688136 | tf_op jit(solution)/shard_map/ppermute | solution.py:217
  63.6 16.0 %collective-permute-start.7 = (bf16[256,512]{1,0:T(8,128)(2,1)}, bf16[256,512]{1,0:T(8,128)(2,1)S(1)}, u32[]{:S(2)}, u32[]{:S(2)}) collective-permute-start(bf16[256,512]{1,0:T(8,128)(2,1)} %get-tuple-element.18), channel_id=1, source_target_pairs={{0,8},{4,12},{8,0},{12,4},{1,9},{5,13},{9,1},{13,5},{2,10},{6,14},... | collective-permute-start | bytes 786440 | tf_op jit(solution)/shard_map/ppermute | solution.py:217
  63.6 21.6 %collective-permute-start.8 = (bf16[256,512]{1,0:T(8,128)(2,1)}, bf16[256,512]{1,0:T(8,128)(2,1)}, u32[]{:S(2)}, u32[]{:S(2)}) collective-permute-start(bf16[256,512]{1,0:T(8,128)(2,1)} %get-tuple-element.17), channel_id=1, source_target_pairs={{0,4},{4,0},{8,12},{12,8},{1,5},{5,1},{9,13},{13,9},{2,6},{6,2},{1... | collective-permute-start | bytes 786440 | tf_op jit(solution)/shard_map/ppermute | solution.py:217
  64.7 22.1 %collective-permute-start.9 = (bf16[256,512]{1,0:T(8,128)(2,1)}, bf16[256,512]{1,0:T(8,128)(2,1)}, u32[]{:S(2)}, u32[]{:S(2)}) collective-permute-start(bf16[256,512]{1,0:T(8,128)(2,1)} %get-tuple-element.16), channel_id=1, source_target_pairs={{0,12},{4,8},{8,4},{12,0},{1,13},{5,9},{9,5},{13,1},{2,14},{6,10},... | collective-permute-start | bytes 786440 | tf_op jit(solution)/shard_map/ppermute | solution.py:217
  74.2 19.5 %collective-permute-start.16 = (bf16[1,16,3584]{2,1,0:T(8,128)(2,1)}, bf16[1,16,3584]{2,1,0:T(8,128)(2,1)}, u32[]{:S(2)}, u32[]{:S(2)}) collective-permute-start(bf16[1,16,3584]{2,1,0:T(8,128)(2,1)} %slice.21), channel_id=1, source_target_pairs={{0,8},{4,12},{8,0},{12,4},{1,9},{5,13},{9,1},{13,5},{2,10},{6,14},... | collective-permute-start | bytes 344072 | tf_op jit(solution)/shard_map/ppermute | solution.py:217
  94.7 12.1 %collective-permute-start.17 = (bf16[16,3584]{1,0:T(8,128)(2,1)S(1)}, bf16[16,3584]{1,0:T(8,128)(2,1)S(1)}, u32[]{:S(2)}, u32[]{:S(2)}) collective-permute-start(bf16[16,3584]{1,0:T(8,128)(2,1)S(1)} %fusion.1), channel_id=1, source_target_pairs={{0,0},{1,4},{2,8},{3,12},{4,1},{5,5},{6,9},{7,13},{8,2},{9,6},{10,... | collective-permute-start | bytes 344072 | tf_op jit(solution)/shard_map/ppermute | solution.py:311
  96.0 5.5 %collective-permute-start.10 = (bf16[16,512]{1,0:T(8,128)(2,1)S(1)}, bf16[16,512]{1,0:T(8,128)(2,1)S(1)}, u32[]{:S(2)}, u32[]{:S(2)}) collective-permute-start(bf16[16,512]{1,0:T(8,128)(2,1)S(1)} %get-tuple-element.27), channel_id=1, source_target_pairs={{0,1},{1,0},{2,3},{3,2},{4,5},{5,4},{6,7},{7,6},{8,9},{9,8},{10,11... | collective-permute-start | bytes 49160 | tf_op jit(solution)/shard_map/ppermute | solution.py:217
  100.2 3.7 %collective-permute-start.11 = (bf16[16,512]{1,0:T(8,128)(2,1)S(1)}, bf16[16,512]{1,0:T(8,128)(2,1)S(1)}, u32[]{:S(2)}, u32[]{:S(2)}) collective-permute-start(bf16[16,512]{1,0:T(8,128)(2,1)S(1)} %get-tuple-element.26), channel_id=1, source_target_pairs={{0,2},{1,3},{2,0},{3,1},{4,6},{5,7},{6,4},{7,5},{8,10},{9,11},{10,... | collective-permute-start | bytes 49160 | tf_op jit(solution)/shard_map/ppermute | solution.py:217
  101.4 3.2 %collective-permute-start.12 = (bf16[16,512]{1,0:T(8,128)(2,1)S(1)}, bf16[16,512]{1,0:T(8,128)(2,1)S(1)}, u32[]{:S(2)}, u32[]{:S(2)}) collective-permute-start(bf16[16,512]{1,0:T(8,128)(2,1)S(1)} %get-tuple-element.25), channel_id=1, source_target_pairs={{0,3},{1,2},{2,1},{3,0},{4,7},{5,6},{6,5},{7,4},{8,11},{9,10},{10,... | collective-permute-start | bytes 49160 | tf_op jit(solution)/shard_map/ppermute | solution.py:217
  101.5 3.0 %copy-start.8 = (bf16[16,512]{1,0:T(8,128)(2,1)}, bf16[16,512]{1,0:T(8,128)(2,1)S(1)}, u32[]{:S(2)}) copy-start(bf16[16,512]{1,0:T(8,128)(2,1)S(1)} %collective-permute-done.10.refs_1_) | copy-start | bytes 49156
  (5 other events, 3.8 us)

commit v8 on v6

--- a/solution.py
+++ b/solution.py
@@ -63,14 +63,10 @@
     )(*tokens, *[teacher] * SPLIT)
 
 
-def project_kernel(scale, n_hid, n_z, z_ref, part_ref, *refs):
+def project_kernel(scale, n_hid, z_ref, part_ref, *refs):
     hid_refs, right_refs, (resid_ref, back_ref) = refs[:n_hid], refs[n_hid:-2], refs[-2:]
-    right = jnp.stack(
-        [jnp.concatenate([a[0, :, 0], b[0, :, 0]], axis=0) for a, b in zip(right_refs[:n_z], right_refs[n_z:])],
-        axis=0,
-    )
-    right = spread(right)
-    rows = right.shape[0] // n_z
+    right = spread(jnp.stack([r[0, :, 0] for r in right_refs], axis=0))
+    rows = right.shape[0] // len(right_refs)
     hid = jnp.concatenate([h[...] for h in hid_refs], axis=1)
     student = lax.dot_general(hid, right[:rows], TN, preferred_element_type=F32)
     resid = ((student - part_ref[...].astype(F32)) * scale).astype(BF)
@@ -79,21 +75,21 @@
     back_ref[...] = back.astype(BF).reshape(back_ref.shape)
 
 
-def project(z, part, hidden, sides, scale):
+def project(z, part, hidden, right, scale):
     t, cols = part.shape
-    n_q, half, n_z, n_b, _ = sides[0].shape
+    n_q, _, n_z, n_b, _ = right.shape
     rows = GROUP * n_b
     right_specs = [
-        pl.BlockSpec((1, half, 1, n_b, FB), lambda q, z, s=s: (q, 0, z[0] ^ s, 0, 0)) for s in range(n_z)
+        pl.BlockSpec((1, GROUP, 1, n_b, FB), lambda q, z, s=s: (q, 0, z[0] ^ s, 0, 0)) for s in order_of(n_z)
     ]
     return pl.pallas_call(
-        functools.partial(project_kernel, scale, len(hidden), n_z),
+        functools.partial(project_kernel, scale, len(hidden)),
         grid_spec=pltpu.PrefetchScalarGridSpec(
             num_scalar_prefetch=1,
             grid=(n_q,),
             in_specs=[pl.BlockSpec((t, COLS), lambda q, z: (0, q))]
             + [pl.BlockSpec((rows, h.shape[1]), lambda q, z: (q, 0)) for h in hidden]
-            + right_specs * 2,
+            + right_specs,
             out_specs=[
                 pl.BlockSpec((t, COLS), lambda q, z: (0, q)),
                 pl.BlockSpec((n_z, rows, t), lambda q, z: (0, q, 0)),
@@ -104,13 +100,13 @@
             jax.ShapeDtypeStruct((n_z, n_q * rows, t), BF),
         ],
         compiler_params=pltpu.CompilerParams(vmem_limit_bytes=VMEM),
-        cost_estimate=cost(2 * t * cols * n_z * rows * 2, 6 * t * cols),
+        cost_estimate=cost(1, 1),
         name="project",
-    )(z, part, *hidden, *[sides[0]] * n_z, *[sides[1]] * n_z)
+    )(z, part, *hidden, *[right] * n_z)
 
 
 def grad_right_kernel(n_z, parts, *refs):
-    hid_refs, (resid_ref, out_ref) = refs[:-2], refs[-2:]
+    hid_refs, (resid_ref, first_ref, second_ref) = refs[:-3], refs[-3:]
     hid = jnp.concatenate(
         [
             jnp.concatenate([r[...] for r in hid_refs[s * parts : (s + 1) * parts]], axis=1)
@@ -124,7 +120,8 @@
     total = prod[:, 0]
     for k in range(1, GROUP):
         total = jnp.where(block == k, prod[:, k], total)
-    out_ref[...] = total.astype(BF)
+    first_ref[...] = total[: n_z // 2].astype(BF)
+    second_ref[...] = total[n_z // 2 :].astype(BF)
 
 
 def grad_right_partial(hidden, resid):
@@ -137,8 +134,8 @@
         grid=(n_q,),
         in_specs=[pl.BlockSpec((rows, h.shape[1]), lambda q: (q, 0)) for hs in hidden for h in hs]
         + [pl.BlockSpec((t, COLS), lambda q: (0, q))],
-        out_specs=pl.BlockSpec((n_z, rows // GROUP, COLS), lambda q: (0, 0, q)),
-        out_shape=jax.ShapeDtypeStruct((n_z, rows // GROUP, cols), BF),
+        out_specs=[pl.BlockSpec((n_z // 2, rows // GROUP, COLS), lambda q: (0, 0, q))] * 2,
+        out_shape=[jax.ShapeDtypeStruct((n_z // 2, rows // GROUP, cols), BF)] * 2,
         compiler_params=pltpu.CompilerParams(vmem_limit_bytes=VMEM),
         cost_estimate=cost(2 * t * cols * n_z * rows, 2 * t * cols),
         name="grad_right",
@@ -217,6 +214,13 @@
     return got
 
 
+def order_of(n):
+    order, bit = [0], n // 2
+    while bit:
+        order, bit = order + [o ^ bit for o in order], bit // 2
+    return order
+
+
 def pick(x, at):
     return lax.dynamic_index_in_dim(x, at, 0, keepdims=False)
 
@@ -255,29 +259,42 @@
     near = gather(tokens, "rep")
     first = hidden_of(near)
     early = gather(first, "blk")
-    sides = right_blocks.reshape(n_q, 2, GROUP // 2, n_z, n_b, FB)
-    sides = [sides[:, i] for i in range(2)]
-    far, early[1:3], sides = lax.optimization_barrier((far, early[1:3], sides))
-
-    turn = [
-        [(a * n_c + b, (b ^ side) * n_c + a) for a in range(n_z) for b in range(n_c)] for side in (0, n_c // 2)
-    ]
-    sides = [lax.ppermute(x, ("blk",) + plane, perm) for x, perm in zip(sides, turn)]
+
+    line = ("blk",) + plane
+    right = right_blocks.reshape(n_q, GROUP, n_z, n_b, FB)
+    bit = n_z // 2
+    while bit:
+        held = [a for a in range(n_z) if a % (2 * bit) == 0]
+        got = lax.ppermute(right, line, [((a ^ b) * n_c + b, (a ^ b ^ bit) * n_c + b) for a in held for b in range(n_c)])
+        if bit == n_z // 2:
+            far, got, early[1:3] = lax.optimization_barrier((far, got, early[1:3]))
+        if bit > 1:
+            right = jnp.where((z ^ c) & (2 * bit - 1) == bit, got, right)
+        bit //= 2
 
     chips = [near] + [gather(x, "rep") for x in far]
     pieces = [p for chip in chips for p in chip]
     hid = [first] + [hidden_of(chip) for chip in chips[1:]]
     late = [[swap(h, "blk", s) for s in range(1, n_z)] for h in hid[1:]]
-    part, late, sides = lax.optimization_barrier((target(pieces, teacher), late, sides))
-    resid, back = project(jnp.reshape(z, (1,)).astype(jnp.int32), part, hid, sides, scale)
-    backs = [back] + [swap(back[s], "blk", s) for s in range(1, n_z)]
+    part, late, got = lax.optimization_barrier((target(pieces, teacher), late, got))
+    right = jnp.where((z ^ c) & 1 == 1, got, right)
+    resid, back = project(jnp.reshape(z, (1,)).astype(jnp.int32), part, hid, right, scale)
+    order = order_of(n_z)
+    backs = [back] + [swap(back[i], "blk", s) for i, s in enumerate(order) if s]
     hidden = list(zip(early, *[[h] + x for h, x in zip(hid[1:], late)]))
 
-    gr = grad_right_partial(hidden, resid)
-    total = gr[0].astype(F32)
-    for s in range(1, n_z):
-        total = total + swap(gr[s], "blk", s).astype(F32)
-    total = lax.ppermute(total.astype(BF), ("blk",) + plane, turn[0])
+    mine, others = grad_right_partial([hidden[s] for s in order], resid)
+    bit = 1
+    while True:
+        mine = mine.astype(F32) + swap(others, "blk", bit).astype(F32)
+        if mine.shape[0] == 1:
+            break
+        mine = mine.astype(BF)
+        mine, others = mine[: mine.shape[0] // 2], mine[mine.shape[0] // 2 :]
+        bit *= 2
+    total = lax.ppermute(
+        mine[0].astype(BF), line, [(a * n_c + b, b * n_c + a) for a in range(n_z) for b in range(n_c)]
+    )
     grad_right = total.reshape(n_b, n_k, FB).transpose(1, 0, 2).reshape(n_k, n_b * FB).astype(F32)
 
     gl = grad_left_of(backs, pieces, n_k)

time: 102 us -> 106 us (1.039)
  the two profiles are of different devices: /device:TPU:15 before, /device:TPU:0 now
where the time goes in v8:
time: 106 us
  starting transfers between devices  39.4 us (37%)
  waiting for transfers between devices  28 us (26%)
  Pallas kernels  21.8 us (21%)
  local copies, waits for them, and re-layouts  9.97 us (9%)
  matrix products  3.34 us (3%)
  other arithmetic  2.27 us (2%)
    ppermute x17, starting transfers between devices, swap(): return lax.ppermute(x, axes, [(i, i ^ s) for i in range(n)])  25.6 us
    ppermute x17, waiting for transfers between devices, swap(): return lax.ppermute(x, axes, [(i, i ^ s) for i in range(n)])  25.4 us
    ppermute x2, starting transfers between devices, per_device(): lax.ppermute(right, line, [((a ^ b) * n_c + b, (a ^ b ^ bit) * n_c + b) f...  13.1 us
    pallas_call x1, Pallas kernels, target(): pl.pallas_call(functools.partial(target_kernel, len(tokens)), grid=(cols...  11.3 us
    pallas_call x1, Pallas kernels, project(): pl.pallas_call(functools.partial(project_kernel, scale, len(hidden)), gri...  4.46 us
    ppermute x2, waiting for transfers between devices, per_device(): lax.ppermute(right, line, [((a ^ b) * n_c + b, (a ^ b ^ bit) * n_c + b) f...  2.57 us
    reshape x1, local copies, waits for them, and re-layouts, per_device(): left = left_blocks.reshape(n_b * BI, NB)  2.28 us
    pallas_call x1, Pallas kernels, grad_right_partial(): pl.pallas_call(functools.partial(grad_right_kernel, n_z, parts), grid=(n_...  2.17 us
  transfers between devices with their start and end apart: 20, of which 9 were waited for; matrix products, arithmetic and copies ran while one was open for 11% of the time, Pallas kernels for 19%

profile of v8, /device:TPU:0, one launch (start us, length us, event | category | flops | bytes accessed | tf_op | source)
XLA Modules:
  0.0 105.7 jit_solution(1913457116151830098)
XLA Ops:
  1.1 2.6 %collective-permute-start.1 = (bf16[128,2048]{1,0:T(8,128)(2,1)}, bf16[128,2048]{1,0:T(8,128)(2,1)S(1)}, u32[]{:S(2)}, u32[]{:S(2)}) collective-permute-start(bf16[128,2048]{1,0:T(8,128)(2,1)} %refs_4_.3), channel_id=1, source_target_pairs={{0,2},{2,0},{1,3},{3,1},{4,6},{6,4},{5,7},{7,5},{8,10},{10,8},{9,1... | collective-permute-start | bytes 1572872 | tf_op jit(solution)/shard_map/ppermute | solution.py:207
  3.7 1.8 %reshape.31 = bf16[4,4,4,16,224]{4,3,2,1,0:T(8,128)(2,1)S(1)} reshape(bf16[16,14336]{1,0:T(8,128)(2,1)} %param.7) | data formatting | bytes 917504 | tf_op jit(solution)/shard_map/reshape | solution.py:264
  5.5 5.3 %collective-permute-start.2 = (bf16[4,4,4,16,224]{4,3,2,1,0:T(8,128)(2,1)S(1)}, bf16[4,4,4,16,224]{4,3,2,1,0:T(8,128)(2,1)}, u32[]{:S(2)}, u32[]{:S(2)}) collective-permute-start(bf16[4,4,4,16,224]{4,3,2,1,0:T(8,128)(2,1)S(1)} %reshape.31), channel_id=1, source_target_pairs={{0,8},{5,13},{10,2},{15,7},{16,24},{21,29},{26,18},{31,23}} | collective-permute-start | bytes 1376264 | tf_op jit(solution)/shard_map/ppermute | solution.py:268
  10.8 2.3 %reshape.32 = bf16[2048,64]{1,0:T(8,128)(2,1)} reshape(bf16[16,8192]{1,0:T(8,128)(2,1)} %param.6) | data formatting | bytes 524288 | tf_op jit(solution)/shard_map/reshape | solution.py:240
  13.1 1.6 %fusion = bf16[256,2048]{1,0:T(8,128)(2,1)S(1)} fusion(bf16[2048,64]{1,0:T(8,128)(2,1)} %reshape.32, s32[2048]{0:T(1024)S(1)} %get-tuple-element.37, s32[2048]{0:T(1024)S(1)} %get-tuple-element.38, s32[256]{0:T(256)S(1)} %get-tuple-element.40, s32[256]{0:T(256)S(1)} %get-tuple-element.41, pred[256]{0:T(512)(128)(4,1)S(1)} %get-tuple-element.36, ...), kind=kOutput, calls=%fused_computation.1 | convolution fusion | flops 69779456 | bytes 1333764 | tf_op jit(solution)/shard_map/dot_general | solution.py:250
  16.1 2.6 %collective-permute-done.2 = bf16[4,4,4,16,224]{4,3,2,1,0:T(8,128)(2,1)} collective-permute-done((bf16[4,4,4,16,224]{4,3,2,1,0:T(8,128)(2,1)S(1)}, bf16[4,4,4,16,224]{4,3,2,1,0:T(8,128)(2,1)}, u32[]{:S(2)}, u32[]{:S(2)}) %collective-permute-start.2) | collective-permute-done | bytes 458784 | tf_op jit(solution)/shard_map/ppermute | solution.py:268
  18.6 4.3 %collective-permute-done.4.refs_2_ = bf16[256,256]{1,0:T(8,128)(2,1)S(1)} collective-permute-done((bf16[256,256]{1,0:T(8,128)(2,1)S(1)}, bf16[256,256]{1,0:T(8,128)(2,1)S(1)}, u32[]{:S(2)}, u32[]{:S(2)}) %collective-permute-start.4) | collective-permute-done | bytes 131104 | tf_op jit(solution)/shard_map/ppermute | solution.py:207
  24.0 7.9 %collective-permute-start.9 = (bf16[4,4,4,16,224]{4,3,2,1,0:T(8,128)(2,1)S(1)}, bf16[4,4,4,16,224]{4,3,2,1,0:T(8,128)(2,1)S(1)}, u32[]{:S(2)}, u32[]{:S(2)}) collective-permute-start(bf16[4,4,4,16,224]{4,3,2,1,0:T(8,128)(2,1)S(1)} %broadcast_select_fusion.1), channel_id=1, source_target_pairs={{0,4},{5,1},{10,14},{15,11},{8,12},{13,9},{2,6},{7,3},{16,20},{21,... | collective-permute-start | bytes 1376264 | tf_op jit(solution)/shard_map/ppermute | solution.py:268
  32.9 2.1 %collective-permute-start.6 = (bf16[256,256]{1,0:T(8,128)(2,1)S(1)}, bf16[256,256]{1,0:T(8,128)(2,1)S(1)}, u32[]{:S(2)}, u32[]{:S(2)}) collective-permute-start(bf16[256,256]{1,0:T(8,128)(2,1)S(1)} %pad_maximum_fusion.1.refs_1_), channel_id=1, source_target_pairs={{0,4},{4,0},{8,12},{12,8},{1,5},{5,1},{9,13},{13,9},{2,6},{6,2},{1... | collective-permute-start | bytes 393224 | tf_op jit(solution)/shard_map/ppermute | solution.py:207
  35.0 3.7 %collective-permute-start.7 = (bf16[256,256]{1,0:T(8,128)(2,1)S(1)}, bf16[256,256]{1,0:T(8,128)(2,1)S(1)}, u32[]{:S(2)}, u32[]{:S(2)}) collective-permute-start(bf16[256,256]{1,0:T(8,128)(2,1)S(1)} %pad_maximum_fusion.1.refs_1_), channel_id=1, source_target_pairs={{0,8},{4,12},{8,0},{12,4},{1,9},{5,13},{9,1},{13,5},{2,10},{6,14},... | collective-permute-start | bytes 393224 | tf_op jit(solution)/shard_map/ppermute | solution.py:207
  38.7 11.3 %target.1.part_ref = bf16[512,3584]{1,0:T(8,128)(2,1)S(1)} custom-call(bf16[128,2048]{1,0:T(8,128)(2,1)S(1)} %copy-done, bf16[128,2048]{1,0:T(8,128)(2,1)S(1)} %collective-permute-done.refs_1_.refs_5_, bf16[128,2048]{1,0:T(8,128)(2,1)S(1)} %collective-permute-done.1.refs_2_.refs_6_, bf16[128,2048]{1,0:T(8,128)(2,1)S(1)} %collective-permute-done.5.refs_3_.refs_7_, ...), custom_call_target="tpu_custom_call" | custom-call | flops 7516192768 | bytes 14680064 | tf_op jit(solution)/shard_map/target/pallas_call | solution.py:53
  50.1 4.5 %project.1 = (bf16[512,3584]{1,0:T(8,128)(2,1)S(1)}, bf16[4,256,512]{2,1,0:T(8,128)(2,1)S(1)}) custom-call(s32[1]{0:T(128)} %bitcast.1.z_ref, bf16[512,3584]{1,0:T(8,128)(2,1)S(1)} %target.1.part_ref, bf16[256,256]{1,0:T(8,128)(2,1)S(1)} %pad_maximum_fusion.refs_0_, bf16[256,256]{1,0:T(8,128)(2,1)S(1)} %pad_maximum_fusion.1.refs_1_, ...), custom_call_target="tpu_custom_call" | custom-call | flops 1 | bytes 1 | tf_op jit(solution)/shard_map/project/pallas_call | solution.py:85
  54.6 2.2 %grad_right.1 = (bf16[2,16,3584]{2,1,0:T(8,128)(2,1)S(1)}, bf16[2,16,3584]{2,1,0:T(8,128)(2,1)S(1)}) custom-call(bf16[256,256]{1,0:T(8,128)(2,1)S(1)} %pad_maximum_fusion.refs_0_, bf16[256,256]{1,0:T(8,128)(2,1)S(1)} %pad_maximum_fusion.1.refs_1_, bf16[256,256]{1,0:T(8,128)(2,1)S(1)} %collective-permute-done.4.refs_2_, ...), custom_call_target="tpu_custom_call" | custom-call | flops 939524096 | bytes 3670016 | tf_op jit(solution)/shard_map/grad_right/pallas_call | solution.py:132
  58.3 4.3 %collective-permute-start.10 = (bf16[256,512]{1,0:T(8,128)(2,1)}, bf16[256,512]{1,0:T(8,128)(2,1)S(1)}, u32[]{:S(2)}, u32[]{:S(2)}) collective-permute-start(bf16[256,512]{1,0:T(8,128)(2,1)} %get-tuple-element.30), channel_id=1, source_target_pairs={{0,8},{4,12},{8,0},{12,4},{1,9},{5,13},{9,1},{13,5},{2,10},{6,14},... | collective-permute-start | bytes 786440 | tf_op jit(solution)/shard_map/ppermute | solution.py:207
  62.6 1.4 %collective-permute-start.12 = (bf16[256,512]{1,0:T(8,128)(2,1)}, bf16[256,512]{1,0:T(8,128)(2,1)}, u32[]{:S(2)}, u32[]{:S(2)}) collective-permute-start(bf16[256,512]{1,0:T(8,128)(2,1)} %get-tuple-element.28), channel_id=1, source_target_pairs={{0,12},{4,8},{8,4},{12,0},{1,13},{5,9},{9,5},{13,1},{2,14},{6,10},... | collective-permute-start | bytes 786440 | tf_op jit(solution)/shard_map/ppermute | solution.py:207
  66.7 4.3 %collective-permute-start.18 = (bf16[1,16,3584]{2,1,0:T(8,128)(2,1)}, bf16[1,16,3584]{2,1,0:T(8,128)(2,1)}, u32[]{:S(2)}, u32[]{:S(2)}) collective-permute-start(bf16[1,16,3584]{2,1,0:T(8,128)(2,1)} %slice.21), channel_id=1, source_target_pairs={{0,8},{4,12},{8,0},{12,4},{1,9},{5,13},{9,1},{13,5},{2,10},{6,14},... | collective-permute-start | bytes 344072 | tf_op jit(solution)/shard_map/ppermute | solution.py:207
  71.0 4.6 %collective-permute-done.10.refs_1_ = bf16[256,512]{1,0:T(8,128)(2,1)S(1)} collective-permute-done((bf16[256,512]{1,0:T(8,128)(2,1)}, bf16[256,512]{1,0:T(8,128)(2,1)S(1)}, u32[]{:S(2)}, u32[]{:S(2)}) %collective-permute-start.10) | collective-permute-done | bytes 262176 | tf_op jit(solution)/shard_map/ppermute | solution.py:207
  76.3 6.1 %collective-permute-done.12.refs_3_ = bf16[256,512]{1,0:T(8,128)(2,1)} collective-permute-done((bf16[256,512]{1,0:T(8,128)(2,1)}, bf16[256,512]{1,0:T(8,128)(2,1)}, u32[]{:S(2)}, u32[]{:S(2)}) %collective-permute-start.12) | collective-permute-done | bytes 262176 | tf_op jit(solution)/shard_map/ppermute | solution.py:207
  82.4 2.2 %grad_left.1 = bf16[16,2048]{1,0:T(8,128)(2,1)S(1)} custom-call(bf16[4,256,512]{2,1,0:T(8,128)(2,1)S(1)} %get-tuple-element.19.refs_0_, bf16[256,512]{1,0:T(8,128)(2,1)S(1)} %collective-permute-done.10.refs_1_, bf16[256,512]{1,0:T(8,128)(2,1)} %collective-permute-done.11.refs_2_, bf16[256,512]{1,0:T(8,128)(2,1)} %collective-permute-done.12.refs_3_, ...), custom_call_target="tpu_custom_call" | custom-call | flops 536870912 | bytes 2097152 | tf_op jit(solution)/shard_map/grad_left/pallas_call | solution.py:165
  85.9 5.4 %collective-permute-done.18 = bf16[1,16,3584]{2,1,0:T(8,128)(2,1)} collective-permute-done((bf16[1,16,3584]{2,1,0:T(8,128)(2,1)}, bf16[1,16,3584]{2,1,0:T(8,128)(2,1)}, u32[]{:S(2)}, u32[]{:S(2)}) %collective-permute-start.18) | collective-permute-done | bytes 114720 | tf_op jit(solution)/shard_map/ppermute | solution.py:207
  93.6 3.5 %collective-permute-start.13 = (bf16[16,512]{1,0:T(8,128)(2,1)S(1)}, bf16[16,512]{1,0:T(8,128)(2,1)S(1)}, u32[]{:S(2)}, u32[]{:S(2)}) collective-permute-start(bf16[16,512]{1,0:T(8,128)(2,1)S(1)} %get-tuple-element.33), channel_id=1, source_target_pairs={{0,1},{1,0},{2,3},{3,2},{4,5},{5,4},{6,7},{7,6},{8,9},{9,8},{10,11... | collective-permute-start | bytes 49160 | tf_op jit(solution)/shard_map/ppermute | solution.py:207
  97.1 1.9 %collective-permute-start.14 = (bf16[16,512]{1,0:T(8,128)(2,1)S(1)}, bf16[16,512]{1,0:T(8,128)(2,1)S(1)}, u32[]{:S(2)}, u32[]{:S(2)}) collective-permute-start(bf16[16,512]{1,0:T(8,128)(2,1)S(1)} %get-tuple-element.32), channel_id=1, source_target_pairs={{0,2},{1,3},{2,0},{3,1},{4,6},{5,7},{6,4},{7,5},{8,10},{9,11},{10,... | collective-permute-start | bytes 49160 | tf_op jit(solution)/shard_map/ppermute | solution.py:207
  99.2 1.7 %collective-permute-done.14.refs_2_ = bf16[16,512]{1,0:T(8,128)(2,1)S(1)} collective-permute-done((bf16[16,512]{1,0:T(8,128)(2,1)S(1)}, bf16[16,512]{1,0:T(8,128)(2,1)S(1)}, u32[]{:S(2)}, u32[]{:S(2)}) %collective-permute-start.14) | collective-permute-done | bytes 16416 | tf_op jit(solution)/shard_map/ppermute | solution.py:207
  102.8 1.7 %place.1 = f32[16,2048]{1,0:T(8,128)} custom-call(s32[1]{0:T(128)} %bitcast.c_ref, bf16[16,512]{1,0:T(8,128)(2,1)} %get-tuple-element.34.refs_0_, bf16[16,512]{1,0:T(8,128)(2,1)} %copy-done.3, bf16[16,512]{1,0:T(8,128)(2,1)} %copy-done.4, bf16[16,512]{1,0:T(8,128)(2,1)} %copy-done.5), custom_call_target="tpu_custom_call" | custom-call | tf_op jit(solution)/shard_map/place/pallas_call | solution.py:195
  (60 shorter events, 15.7 us)
Async XLA Ops:
  0.6 14.6 %collective-permute-start = (bf16[128,2048]{1,0:T(8,128)(2,1)}, bf16[128,2048]{1,0:T(8,128)(2,1)S(1)}, u32[]{:S(2)}, u32[]{:S(2)}) collective-permute-start(bf16[128,2048]{1,0:T(8,128)(2,1)} %refs_4_.3), channel_id=1, source_target_pairs={{0,1},{1,0},{2,3},{3,2},{4,5},{5,4},{6,7},{7,6},{8,9},{9,8},{10,11... | collective-permute-start | bytes 1572872 | tf_op jit(solution)/shard_map/ppermute | solution.py:207
  1.1 17.5 %collective-permute-start.1 = (bf16[128,2048]{1,0:T(8,128)(2,1)}, bf16[128,2048]{1,0:T(8,128)(2,1)S(1)}, u32[]{:S(2)}, u32[]{:S(2)}) collective-permute-start(bf16[128,2048]{1,0:T(8,128)(2,1)} %refs_4_.3), channel_id=1, source_target_pairs={{0,2},{2,0},{1,3},{3,1},{4,6},{6,4},{5,7},{7,5},{8,10},{10,8},{9,1... | collective-permute-start | bytes 1572872 | tf_op jit(solution)/shard_map/ppermute | solution.py:207
  5.5 9.2 %copy-start.1 = (bf16[4,4,4,16,224]{4,3,2,1,0:T(8,128)(2,1)}, bf16[4,4,4,16,224]{4,3,2,1,0:T(8,128)(2,1)S(1)}, u32[]{:S(2)}) copy-start(bf16[4,4,4,16,224]{4,3,2,1,0:T(8,128)(2,1)S(1)} %reshape.31) | copy-start | bytes 1376260
  5.5 13.1 %collective-permute-start.2 = (bf16[4,4,4,16,224]{4,3,2,1,0:T(8,128)(2,1)S(1)}, bf16[4,4,4,16,224]{4,3,2,1,0:T(8,128)(2,1)}, u32[]{:S(2)}, u32[]{:S(2)}) collective-permute-start(bf16[4,4,4,16,224]{4,3,2,1,0:T(8,128)(2,1)S(1)} %reshape.31), channel_id=1, source_target_pairs={{0,8},{5,13},{10,2},{15,7},{16,24},{21,29},{26,18},{31,23}} | collective-permute-start | bytes 1376264 | tf_op jit(solution)/shard_map/ppermute | solution.py:268
  13.1 1.6 %copy-start = (bf16[128,2048]{1,0:T(8,128)(2,1)S(1)}, bf16[128,2048]{1,0:T(8,128)(2,1)}, u32[]{:S(2)}) copy-start(bf16[128,2048]{1,0:T(8,128)(2,1)} %refs_4_.3) | copy-start | bytes 1572868
  15.7 7.3 %collective-permute-start.4 = (bf16[256,256]{1,0:T(8,128)(2,1)S(1)}, bf16[256,256]{1,0:T(8,128)(2,1)S(1)}, u32[]{:S(2)}, u32[]{:S(2)}) collective-permute-start(bf16[256,256]{1,0:T(8,128)(2,1)S(1)} %pad_maximum_fusion.refs_0_), channel_id=1, source_target_pairs={{0,8},{4,12},{8,0},{12,4},{1,9},{5,13},{9,1},{13,5},{2,10},{6,14},... | collective-permute-start | bytes 393224 | tf_op jit(solution)/shard_map/ppermute | solution.py:207
  15.7 7.2 %collective-permute-start.3 = (bf16[256,256]{1,0:T(8,128)(2,1)S(1)}, bf16[256,256]{1,0:T(8,128)(2,1)S(1)}, u32[]{:S(2)}, u32[]{:S(2)}) collective-permute-start(bf16[256,256]{1,0:T(8,128)(2,1)S(1)} %pad_maximum_fusion.refs_0_), channel_id=1, source_target_pairs={{0,4},{4,0},{8,12},{12,8},{1,5},{5,1},{9,13},{13,9},{2,6},{6,2},{1... | collective-permute-start | bytes 393224 | tf_op jit(solution)/shard_map/ppermute | solution.py:207
  22.9 9.5 %collective-permute-start.5 = (bf16[128,2048]{1,0:T(8,128)(2,1)S(1)}, bf16[128,2048]{1,0:T(8,128)(2,1)S(1)}, u32[]{:S(2)}, u32[]{:S(2)}) collective-permute-start(bf16[128,2048]{1,0:T(8,128)(2,1)S(1)} %collective-permute-done.1.refs_2_.refs_6_), channel_id=1, source_target_pairs={{0,1},{1,0},{2,3},{3,2},{4,5},{5,4},{6,7},{7,6},{8,9},{9,8},{10,11... | collective-permute-start | bytes 1572872 | tf_op jit(solution)/shard_map/ppermute | solution.py:207
  24.0 25.9 %collective-permute-start.9 = (bf16[4,4,4,16,224]{4,3,2,1,0:T(8,128)(2,1)S(1)}, bf16[4,4,4,16,224]{4,3,2,1,0:T(8,128)(2,1)S(1)}, u32[]{:S(2)}, u32[]{:S(2)}) collective-permute-start(bf16[4,4,4,16,224]{4,3,2,1,0:T(8,128)(2,1)S(1)} %broadcast_select_fusion.1), channel_id=1, source_target_pairs={{0,4},{5,1},{10,14},{15,11},{8,12},{13,9},{2,6},{7,3},{16,20},{21,... | collective-permute-start | bytes 1376264 | tf_op jit(solution)/shard_map/ppermute | solution.py:268
  31.9 22.7 %collective-permute-start.16 = (bf16[256,256]{1,0:T(8,128)(2,1)S(1)}, bf16[256,256]{1,0:T(8,128)(2,1)S(1)}, u32[]{:S(2)}, u32[]{:S(2)}) collective-permute-start(bf16[256,256]{1,0:T(8,128)(2,1)S(1)} %collective-permute-done.4.refs_2_), channel_id=1, source_target_pairs={{0,4},{4,0},{8,12},{12,8},{1,5},{5,1},{9,13},{13,9},{2,6},{6,2},{1... | collective-permute-start | bytes 393224 | tf_op jit(solution)/shard_map/ppermute | solution.py:207
  32.9 17.1 %collective-permute-start.6 = (bf16[256,256]{1,0:T(8,128)(2,1)S(1)}, bf16[256,256]{1,0:T(8,128)(2,1)S(1)}, u32[]{:S(2)}, u32[]{:S(2)}) collective-permute-start(bf16[256,256]{1,0:T(8,128)(2,1)S(1)} %pad_maximum_fusion.1.refs_1_), channel_id=1, source_target_pairs={{0,4},{4,0},{8,12},{12,8},{1,5},{5,1},{9,13},{13,9},{2,6},{6,2},{1... | collective-permute-start | bytes 393224 | tf_op jit(solution)/shard_map/ppermute | solution.py:207
  35.0 15.0 %collective-permute-start.7 = (bf16[256,256]{1,0:T(8,128)(2,1)S(1)}, bf16[256,256]{1,0:T(8,128)(2,1)S(1)}, u32[]{:S(2)}, u32[]{:S(2)}) collective-permute-start(bf16[256,256]{1,0:T(8,128)(2,1)S(1)} %pad_maximum_fusion.1.refs_1_), channel_id=1, source_target_pairs={{0,8},{4,12},{8,0},{12,4},{1,9},{5,13},{9,1},{13,5},{2,10},{6,14},... | collective-permute-start | bytes 393224 | tf_op jit(solution)/shard_map/ppermute | solution.py:207
  38.7 11.3 %collective-permute-start.8 = (bf16[256,256]{1,0:T(8,128)(2,1)S(1)}, bf16[256,256]{1,0:T(8,128)(2,1)S(1)}, u32[]{:S(2)}, u32[]{:S(2)}) collective-permute-start(bf16[256,256]{1,0:T(8,128)(2,1)S(1)} %pad_maximum_fusion.1.refs_1_), channel_id=1, source_target_pairs={{0,12},{4,8},{8,4},{12,0},{1,13},{5,9},{9,5},{13,1},{2,14},{6,10},... | collective-permute-start | bytes 393224 | tf_op jit(solution)/shard_map/ppermute | solution.py:207
  56.7 8.6 %collective-permute-start.17 = (bf16[2,16,3584]{2,1,0:T(8,128)(2,1)S(1)}, bf16[2,16,3584]{2,1,0:T(8,128)(2,1)S(1)}, u32[]{:S(2)}, u32[]{:S(2)}) collective-permute-start(bf16[2,16,3584]{2,1,0:T(8,128)(2,1)S(1)} %get-tuple-element.27), channel_id=1, source_target_pairs={{0,4},{4,0},{8,12},{12,8},{1,5},{5,1},{9,13},{13,9},{2,6},{6,2},{1... | collective-permute-start | bytes 688136 | tf_op jit(solution)/shard_map/ppermute | solution.py:207
  58.3 17.4 %collective-permute-start.10 = (bf16[256,512]{1,0:T(8,128)(2,1)}, bf16[256,512]{1,0:T(8,128)(2,1)S(1)}, u32[]{:S(2)}, u32[]{:S(2)}) collective-permute-start(bf16[256,512]{1,0:T(8,128)(2,1)} %get-tuple-element.30), channel_id=1, source_target_pairs={{0,8},{4,12},{8,0},{12,4},{1,9},{5,13},{9,1},{13,5},{2,10},{6,14},... | collective-permute-start | bytes 786440 | tf_op jit(solution)/shard_map/ppermute | solution.py:207
  62.6 13.7 %collective-permute-start.11 = (bf16[256,512]{1,0:T(8,128)(2,1)}, bf16[256,512]{1,0:T(8,128)(2,1)}, u32[]{:S(2)}, u32[]{:S(2)}) collective-permute-start(bf16[256,512]{1,0:T(8,128)(2,1)} %get-tuple-element.29), channel_id=1, source_target_pairs={{0,4},{4,0},{8,12},{12,8},{1,5},{5,1},{9,13},{13,9},{2,6},{6,2},{1... | collective-permute-start | bytes 786440 | tf_op jit(solution)/shard_map/ppermute | solution.py:207
  62.6 19.8 %collective-permute-start.12 = (bf16[256,512]{1,0:T(8,128)(2,1)}, bf16[256,512]{1,0:T(8,128)(2,1)}, u32[]{:S(2)}, u32[]{:S(2)}) collective-permute-start(bf16[256,512]{1,0:T(8,128)(2,1)} %get-tuple-element.28), channel_id=1, source_target_pairs={{0,12},{4,8},{8,4},{12,0},{1,13},{5,9},{9,5},{13,1},{2,14},{6,10},... | collective-permute-start | bytes 786440 | tf_op jit(solution)/shard_map/ppermute | solution.py:207
  66.7 24.6 %collective-permute-start.18 = (bf16[1,16,3584]{2,1,0:T(8,128)(2,1)}, bf16[1,16,3584]{2,1,0:T(8,128)(2,1)}, u32[]{:S(2)}, u32[]{:S(2)}) collective-permute-start(bf16[1,16,3584]{2,1,0:T(8,128)(2,1)} %slice.21), channel_id=1, source_target_pairs={{0,8},{4,12},{8,0},{12,4},{1,9},{5,13},{9,1},{13,5},{2,10},{6,14},... | collective-permute-start | bytes 344072 | tf_op jit(solution)/shard_map/ppermute | solution.py:207
  92.3 12.2 %collective-permute-start.19 = (bf16[16,3584]{1,0:T(8,128)(2,1)S(1)}, bf16[16,3584]{1,0:T(8,128)(2,1)S(1)}, u32[]{:S(2)}, u32[]{:S(2)}) collective-permute-start(bf16[16,3584]{1,0:T(8,128)(2,1)S(1)} %fusion.1), channel_id=1, source_target_pairs={{0,0},{1,4},{2,8},{3,12},{4,1},{5,5},{6,9},{7,13},{8,2},{9,6},{10,... | collective-permute-start | bytes 344072 | tf_op jit(solution)/shard_map/ppermute | solution.py:295
  93.6 5.6 %collective-permute-start.13 = (bf16[16,512]{1,0:T(8,128)(2,1)S(1)}, bf16[16,512]{1,0:T(8,128)(2,1)S(1)}, u32[]{:S(2)}, u32[]{:S(2)}) collective-permute-start(bf16[16,512]{1,0:T(8,128)(2,1)S(1)} %get-tuple-element.33), channel_id=1, source_target_pairs={{0,1},{1,0},{2,3},{3,2},{4,5},{5,4},{6,7},{7,6},{8,9},{9,8},{10,11... | collective-permute-start | bytes 49160 | tf_op jit(solution)/shard_map/ppermute | solution.py:207
  97.1 3.7 %collective-permute-start.14 = (bf16[16,512]{1,0:T(8,128)(2,1)S(1)}, bf16[16,512]{1,0:T(8,128)(2,1)S(1)}, u32[]{:S(2)}, u32[]{:S(2)}) collective-permute-start(bf16[16,512]{1,0:T(8,128)(2,1)S(1)} %get-tuple-element.32), channel_id=1, source_target_pairs={{0,2},{1,3},{2,0},{3,1},{4,6},{5,7},{6,4},{7,5},{8,10},{9,11},{10,... | collective-permute-start | bytes 49160 | tf_op jit(solution)/shard_map/ppermute | solution.py:207
  99.0 3.2 %collective-permute-start.15 = (bf16[16,512]{1,0:T(8,128)(2,1)S(1)}, bf16[16,512]{1,0:T(8,128)(2,1)S(1)}, u32[]{:S(2)}, u32[]{:S(2)}) collective-permute-start(bf16[16,512]{1,0:T(8,128)(2,1)S(1)} %get-tuple-element.31), channel_id=1, source_target_pairs={{0,3},{1,2},{2,1},{3,0},{4,7},{5,6},{6,5},{7,4},{8,11},{9,10},{10,... | collective-permute-start | bytes 49160 | tf_op jit(solution)/shard_map/ppermute | solution.py:207
  99.2 3.0 %copy-start.3 = (bf16[16,512]{1,0:T(8,128)(2,1)}, bf16[16,512]{1,0:T(8,128)(2,1)S(1)}, u32[]{:S(2)}) copy-start(bf16[16,512]{1,0:T(8,128)(2,1)S(1)} %collective-permute-done.13.refs_1_) | copy-start | bytes 49156
  100.8 1.4 %copy-start.4 = (bf16[16,512]{1,0:T(8,128)(2,1)}, bf16[16,512]{1,0:T(8,128)(2,1)S(1)}, u32[]{:S(2)}) copy-start(bf16[16,512]{1,0:T(8,128)(2,1)S(1)} %collective-permute-done.14.refs_2_) | copy-start | bytes 49156
  (2 other events, 1.3 us)

commit v9 on v6

--- a/solution.py
+++ b/solution.py
@@ -254,11 +254,10 @@
     far = [swap(tokens, "tok", s) for s in range(1, n_tok)]
     near = gather(tokens, "rep")
     first = hidden_of(near)
-    early = gather(first, "blk")
+
     sides = right_blocks.reshape(n_q, 2, GROUP // 2, n_z, n_b, FB)
     sides = [sides[:, i] for i in range(2)]
-    far, early[1:3], sides = lax.optimization_barrier((far, early[1:3], sides))
-
+    far, first = lax.optimization_barrier((far, first))
     turn = [
         [(a * n_c + b, (b ^ side) * n_c + a) for a in range(n_z) for b in range(n_c)] for side in (0, n_c // 2)
     ]
@@ -266,12 +265,14 @@
 
     chips = [near] + [gather(x, "rep") for x in far]
     pieces = [p for chip in chips for p in chip]
-    hid = [first] + [hidden_of(chip) for chip in chips[1:]]
-    late = [[swap(h, "blk", s) for s in range(1, n_z)] for h in hid[1:]]
-    part, late, sides = lax.optimization_barrier((target(pieces, teacher), late, sides))
+    hid = [jnp.concatenate([first] + [hidden_of(chip) for chip in chips[1:]], axis=1)]
+    hidden = hid + [swap(hid[0], "blk", s) for s in (1, 2)]
+    part, hidden[1:], sides = lax.optimization_barrier((target(pieces, teacher), hidden[1:], sides))
+    for s in range(3, n_z):
+        hidden.append(swap(hidden[s & (s - 1)], "blk", s & -s))
+    hidden = [[h] for h in hidden]
     resid, back = project(jnp.reshape(z, (1,)).astype(jnp.int32), part, hid, sides, scale)
     backs = [back] + [swap(back[s], "blk", s) for s in range(1, n_z)]
-    hidden = list(zip(early, *[[h] + x for h, x in zip(hid[1:], late)]))
 
     gr = grad_right_partial(hidden, resid)
     total = gr[0].astype(F32)

time: 102 us -> 106 us (1.039)
  the two profiles are of different devices: /device:TPU:15 before, /device:TPU:0 now
where the time goes in v9:
time: 106 us
  waiting for transfers between devices  37.5 us (35%)
  starting transfers between devices  28.2 us (27%)
  Pallas kernels  21.9 us (21%)
  local copies, waits for them, and re-layouts  11.2 us (11%)
  matrix products  4.69 us (4%)
  other arithmetic  1.2 us (1%)
    ppermute x15, waiting for transfers between devices, swap(): return lax.ppermute(x, axes, [(i, i ^ s) for i in range(n)])  37.5 us
    ppermute x15, starting transfers between devices, swap(): return lax.ppermute(x, axes, [(i, i ^ s) for i in range(n)])  21.5 us
    pallas_call x1, Pallas kernels, target(): pl.pallas_call(functools.partial(target_kernel, len(tokens)), grid=(cols...  11.3 us
    ppermute x2, starting transfers between devices, per_device(): lax.ppermute(x, ('blk',) + plane, perm)  6.07 us
    pallas_call x1, Pallas kernels, project(): pl.pallas_call(functools.partial(project_kernel, scale, len(hidden), n_z)...  4.6 us
    dot_general x4, matrix products, hidden_of(): lax.dot_general(left, p, NT, preferred_element_type=F32).astype(BF)  4.19 us
    unnamed x18, local copies, waits for them, and re-layouts  3.59 us
    pallas_call x1, Pallas kernels, grad_left_of(): pl.pallas_call(functools.partial(grad_left_kernel, n_z, n_k), grid=(depth...  2.17 us
  transfers between devices with their start and end apart: 18, of which 8 were waited for; matrix products, arithmetic and copies ran while one was open for 11% of the time, Pallas kernels for 21%

profile of v9, /device:TPU:0, one launch (start us, length us, event | category | flops | bytes accessed | tf_op | source)
XLA Modules:
  0.0 105.6 jit_solution(6452258546366591541)
XLA Ops:
  1.1 2.6 %collective-permute-start.1 = (bf16[128,2048]{1,0:T(8,128)(2,1)}, bf16[128,2048]{1,0:T(8,128)(2,1)S(1)}, u32[]{:S(2)}, u32[]{:S(2)}) collective-permute-start(bf16[128,2048]{1,0:T(8,128)(2,1)} %refs_4_.3), channel_id=1, source_target_pairs={{0,2},{2,0},{1,3},{3,1},{4,6},{6,4},{5,7},{7,5},{8,10},{10,8},{9,1... | collective-permute-start | bytes 1572872 | tf_op jit(solution)/shard_map/ppermute | solution.py:210
  3.8 1.5 %reshape.32 = bf16[2048,64]{1,0:T(8,128)(2,1)S(1)} reshape(bf16[16,8192]{1,0:T(8,128)(2,1)} %param.6) | data formatting | bytes 524288 | tf_op jit(solution)/shard_map/reshape | solution.py:236
  7.3 9.2 %collective-permute-done.1.refs_2_.refs_6_ = bf16[128,2048]{1,0:T(8,128)(2,1)S(1)} collective-permute-done((bf16[128,2048]{1,0:T(8,128)(2,1)}, bf16[128,2048]{1,0:T(8,128)(2,1)S(1)}, u32[]{:S(2)}, u32[]{:S(2)}) %collective-permute-start.1) | collective-permute-done | bytes 524320 | tf_op jit(solution)/shard_map/ppermute | solution.py:210
  18.0 1.6 %collective-permute-start.5 = (bf16[4,2,4,16,224]{4,3,2,1,0:T(8,128)(2,1)}, bf16[4,2,4,16,224]{4,3,2,1,0:T(8,128)(2,1)S(1)}, u32[]{:S(2)}, u32[]{:S(2)}) collective-permute-start(bf16[4,2,4,16,224]{4,3,2,1,0:T(8,128)(2,1)} %get-tuple-element.24), channel_id=1, source_target_pairs={{0,0},{1,4},{2,8},{3,12},{4,1},{5,5},{6,9},{7,13},{8,2},{9,6},{10,... | collective-permute-start | bytes 688136 | tf_op jit(solution)/shard_map/ppermute | solution.py:264
  19.5 4.5 %collective-permute-start.6 = (bf16[4,2,4,16,224]{4,3,2,1,0:T(8,128)(2,1)S(1)}, bf16[4,2,4,16,224]{4,3,2,1,0:T(8,128)(2,1)S(1)}, u32[]{:S(2)}, u32[]{:S(2)}) collective-permute-start(bf16[4,2,4,16,224]{4,3,2,1,0:T(8,128)(2,1)S(1)} %get-tuple-element.23), channel_id=1, source_target_pairs={{0,8},{1,12},{2,0},{3,4},{4,9},{5,13},{6,1},{7,5},{8,10},{9,14},{1... | collective-permute-start | bytes 688136 | tf_op jit(solution)/shard_map/ppermute | solution.py:264
  24.0 1.7 %convolution_convert_fusion.1 = bf16[256,128]{1,0:T(8,128)(2,1)S(1)} fusion(bf16[256,2048]{1,0:T(8,128)(2,1)} %copy-done.4, bf16[128,2048]{1,0:T(8,128)(2,1)S(1)} %collective-permute-done.1.refs_2_.refs_6_), kind=kOutput, calls=%fused_computation.4 | convolution fusion | flops 134250496 | bytes 1638400 | tf_op jit(solution)/shard_map/dot_general | solution.py:251
  25.7 1.7 %convolution_convert_fusion = bf16[256,128]{1,0:T(8,128)(2,1)S(1)} fusion(bf16[256,2048]{1,0:T(8,128)(2,1)} %copy-done.4, bf16[128,2048]{1,0:T(8,128)(2,1)S(1)} %collective-permute-done.2.refs_3_.refs_7_), kind=kOutput, calls=%fused_computation.3 | convolution fusion | flops 134250496 | bytes 1638400 | tf_op jit(solution)/shard_map/dot_general | solution.py:251
  27.9 2.6 %collective-permute-start.4 = (bf16[256,512]{1,0:T(8,128)(2,1)S(1)}, bf16[256,512]{1,0:T(8,128)(2,1)S(1)}, u32[]{:S(2)}, u32[]{:S(2)}) collective-permute-start(bf16[256,512]{1,0:T(8,128)(2,1)S(1)} %pad_maximum_fusion.refs_0_), channel_id=1, source_target_pairs={{0,8},{4,12},{8,0},{12,4},{1,9},{5,13},{9,1},{13,5},{2,10},{6,14},... | collective-permute-start | bytes 786440 | tf_op jit(solution)/shard_map/ppermute | solution.py:210
  30.5 11.3 %target.1.part_ref = bf16[512,3584]{1,0:T(8,128)(2,1)S(1)} custom-call(bf16[128,2048]{1,0:T(8,128)(2,1)S(1)} %copy-done, bf16[128,2048]{1,0:T(8,128)(2,1)S(1)} %collective-permute-done.refs_1_.refs_5_, bf16[128,2048]{1,0:T(8,128)(2,1)S(1)} %collective-permute-done.1.refs_2_.refs_6_, bf16[128,2048]{1,0:T(8,128)(2,1)S(1)} %collective-permute-done.2.refs_3_.refs_7_, ...), custom_call_target="tpu_custom_call" | custom-call | flops 7516192768 | bytes 14680064 | tf_op jit(solution)/shard_map/target/pallas_call | solution.py:53
  43.6 4.1 %collective-permute-done.4.refs_2_ = bf16[256,512]{1,0:T(8,128)(2,1)S(1)} collective-permute-done((bf16[256,512]{1,0:T(8,128)(2,1)S(1)}, bf16[256,512]{1,0:T(8,128)(2,1)S(1)}, u32[]{:S(2)}, u32[]{:S(2)}) %collective-permute-start.4) | collective-permute-done | bytes 262176 | tf_op jit(solution)/shard_map/ppermute | solution.py:210
  48.7 4.6 %project.1 = (bf16[512,3584]{1,0:T(8,128)(2,1)S(1)}, bf16[4,256,512]{2,1,0:T(8,128)(2,1)S(1)}) custom-call(s32[1]{0:T(128)} %bitcast.1.z_ref, bf16[512,3584]{1,0:T(8,128)(2,1)S(1)} %target.1.part_ref, bf16[256,512]{1,0:T(8,128)(2,1)S(1)} %pad_maximum_fusion.refs_0_, bf16[4,2,4,16,224]{4,3,2,1,0:T(8,128)(2,1)S(1)} %collective-permute-done.5.refs_1_.refs_2_.refs_3_.refs_4_, ...), custom_call_target="tpu_custom_call" | custom-call | flops 1879048192 | bytes 11010048 | tf_op jit(solution)/shard_map/project/pallas_call | solution.py:89
  54.1 2.0 %collective-permute-start.7 = (bf16[256,512]{1,0:T(8,128)(2,1)S(1)}, bf16[256,512]{1,0:T(8,128)(2,1)S(1)}, u32[]{:S(2)}, u32[]{:S(2)}) collective-permute-start(bf16[256,512]{1,0:T(8,128)(2,1)S(1)} %get-tuple-element.22), channel_id=1, source_target_pairs={{0,4},{4,0},{8,12},{12,8},{1,5},{5,1},{9,13},{13,9},{2,6},{6,2},{1... | collective-permute-start | bytes 786440 | tf_op jit(solution)/shard_map/ppermute | solution.py:210
  57.4 1.5 %collective-permute-start.9 = (bf16[256,512]{1,0:T(8,128)(2,1)}, bf16[256,512]{1,0:T(8,128)(2,1)}, u32[]{:S(2)}, u32[]{:S(2)}) collective-permute-start(bf16[256,512]{1,0:T(8,128)(2,1)} %get-tuple-element.20), channel_id=1, source_target_pairs={{0,12},{4,8},{8,4},{12,0},{1,13},{5,9},{9,5},{13,1},{2,14},{6,10},... | collective-permute-start | bytes 786440 | tf_op jit(solution)/shard_map/ppermute | solution.py:210
  58.9 2.2 %grad_right.1 = bf16[4,16,3584]{2,1,0:T(8,128)(2,1)S(1)} custom-call(bf16[256,512]{1,0:T(8,128)(2,1)S(1)} %pad_maximum_fusion.refs_0_, bf16[256,512]{1,0:T(8,128)(2,1)S(1)} %collective-permute-done.3.refs_1_, bf16[256,512]{1,0:T(8,128)(2,1)S(1)} %collective-permute-done.4.refs_2_, bf16[256,512]{1,0:T(8,128)(2,1)S(1)} %collective-permute-done.13.refs_3_, ...), custom_call_target="tpu_custom_call" | custom-call | flops 939524096 | bytes 3670016 | tf_op jit(solution)/shard_map/grad_right/pallas_call | solution.py:135
  63.3 2.2 %collective-permute-start.15 = (bf16[16,3584]{1,0:T(8,128)(2,1)}, bf16[16,3584]{1,0:T(8,128)(2,1)}, u32[]{:S(2)}, u32[]{:S(2)}) collective-permute-start(bf16[16,3584]{1,0:T(8,128)(2,1)} %get-tuple-element.27), channel_id=1, source_target_pairs={{0,8},{4,12},{8,0},{12,4},{1,9},{5,13},{9,1},{13,5},{2,10},{6,14},... | collective-permute-start | bytes 344072 | tf_op jit(solution)/shard_map/ppermute | solution.py:210
  65.5 2.7 %collective-permute-done.7.refs_1_ = bf16[256,512]{1,0:T(8,128)(2,1)S(1)} collective-permute-done((bf16[256,512]{1,0:T(8,128)(2,1)S(1)}, bf16[256,512]{1,0:T(8,128)(2,1)S(1)}, u32[]{:S(2)}, u32[]{:S(2)}) %collective-permute-start.7) | collective-permute-done | bytes 262176 | tf_op jit(solution)/shard_map/ppermute | solution.py:210
  69.5 8.5 %collective-permute-done.8.refs_2_ = bf16[256,512]{1,0:T(8,128)(2,1)} collective-permute-done((bf16[256,512]{1,0:T(8,128)(2,1)}, bf16[256,512]{1,0:T(8,128)(2,1)}, u32[]{:S(2)}, u32[]{:S(2)}) %collective-permute-start.8) | collective-permute-done | bytes 262176 | tf_op jit(solution)/shard_map/ppermute | solution.py:210
  78.0 2.2 %grad_left.1 = bf16[16,2048]{1,0:T(8,128)(2,1)S(1)} custom-call(bf16[4,256,512]{2,1,0:T(8,128)(2,1)S(1)} %get-tuple-element.16.refs_0_, bf16[256,512]{1,0:T(8,128)(2,1)S(1)} %collective-permute-done.7.refs_1_, bf16[256,512]{1,0:T(8,128)(2,1)} %collective-permute-done.8.refs_2_, bf16[256,512]{1,0:T(8,128)(2,1)} %collective-permute-done.9.refs_3_, ...), custom_call_target="tpu_custom_call" | custom-call | flops 536870912 | bytes 2097152 | tf_op jit(solution)/shard_map/grad_left/pallas_call | solution.py:168
  81.4 8.8 %collective-permute-done.15 = bf16[16,3584]{1,0:T(8,128)(2,1)} collective-permute-done((bf16[16,3584]{1,0:T(8,128)(2,1)}, bf16[16,3584]{1,0:T(8,128)(2,1)}, u32[]{:S(2)}, u32[]{:S(2)}) %collective-permute-start.15) | collective-permute-done | bytes 114720 | tf_op jit(solution)/shard_map/ppermute | solution.py:210
  92.7 3.5 %collective-permute-start.10 = (bf16[16,512]{1,0:T(8,128)(2,1)S(1)}, bf16[16,512]{1,0:T(8,128)(2,1)S(1)}, u32[]{:S(2)}, u32[]{:S(2)}) collective-permute-start(bf16[16,512]{1,0:T(8,128)(2,1)S(1)} %get-tuple-element.30), channel_id=1, source_target_pairs={{0,1},{1,0},{2,3},{3,2},{4,5},{5,4},{6,7},{7,6},{8,9},{9,8},{10,11... | collective-permute-start | bytes 49160 | tf_op jit(solution)/shard_map/ppermute | solution.py:210
  96.2 2.7 %collective-permute-start.11 = (bf16[16,512]{1,0:T(8,128)(2,1)S(1)}, bf16[16,512]{1,0:T(8,128)(2,1)S(1)}, u32[]{:S(2)}, u32[]{:S(2)}) collective-permute-start(bf16[16,512]{1,0:T(8,128)(2,1)S(1)} %get-tuple-element.29), channel_id=1, source_target_pairs={{0,2},{1,3},{2,0},{3,1},{4,6},{5,7},{6,4},{7,5},{8,10},{9,11},{10,... | collective-permute-start | bytes 49160 | tf_op jit(solution)/shard_map/ppermute | solution.py:210
  99.0 1.6 %collective-permute-done.11.refs_2_ = bf16[16,512]{1,0:T(8,128)(2,1)S(1)} collective-permute-done((bf16[16,512]{1,0:T(8,128)(2,1)S(1)}, bf16[16,512]{1,0:T(8,128)(2,1)S(1)}, u32[]{:S(2)}, u32[]{:S(2)}) %collective-permute-start.11) | collective-permute-done | bytes 16416 | tf_op jit(solution)/shard_map/ppermute | solution.py:210
  100.6 1.4 %collective-permute-done.12.refs_3_ = bf16[16,512]{1,0:T(8,128)(2,1)S(1)} collective-permute-done((bf16[16,512]{1,0:T(8,128)(2,1)S(1)}, bf16[16,512]{1,0:T(8,128)(2,1)S(1)}, u32[]{:S(2)}, u32[]{:S(2)}) %collective-permute-start.12) | collective-permute-done | bytes 16416 | tf_op jit(solution)/shard_map/ppermute | solution.py:210
  102.7 1.7 %place.1 = f32[16,2048]{1,0:T(8,128)} custom-call(s32[1]{0:T(128)} %bitcast.c_ref, bf16[16,512]{1,0:T(8,128)(2,1)} %get-tuple-element.31.refs_0_, bf16[16,512]{1,0:T(8,128)(2,1)} %copy-done.6, bf16[16,512]{1,0:T(8,128)(2,1)} %copy-done.7, bf16[16,512]{1,0:T(8,128)(2,1)} %copy-done.8), custom_call_target="tpu_custom_call" | custom-call | tf_op jit(solution)/shard_map/place/pallas_call | solution.py:198
  (60 shorter events, 18.6 us)
Async XLA Ops:
  0.6 6.1 %collective-permute-start = (bf16[128,2048]{1,0:T(8,128)(2,1)}, bf16[128,2048]{1,0:T(8,128)(2,1)S(1)}, u32[]{:S(2)}, u32[]{:S(2)}) collective-permute-start(bf16[128,2048]{1,0:T(8,128)(2,1)} %refs_4_.3), channel_id=1, source_target_pairs={{0,1},{1,0},{2,3},{3,2},{4,5},{5,4},{6,7},{7,6},{8,9},{9,8},{10,11... | collective-permute-start | bytes 1572872 | tf_op jit(solution)/shard_map/ppermute | solution.py:210
  1.1 15.3 %collective-permute-start.1 = (bf16[128,2048]{1,0:T(8,128)(2,1)}, bf16[128,2048]{1,0:T(8,128)(2,1)S(1)}, u32[]{:S(2)}, u32[]{:S(2)}) collective-permute-start(bf16[128,2048]{1,0:T(8,128)(2,1)} %refs_4_.3), channel_id=1, source_target_pairs={{0,2},{2,0},{1,3},{3,1},{4,6},{6,4},{5,7},{7,5},{8,10},{10,8},{9,1... | collective-permute-start | bytes 1572872 | tf_op jit(solution)/shard_map/ppermute | solution.py:210
  5.2 1.0 copy-start
  6.3 1.0 copy-start.4
  6.3 10.2 %copy-start.5 = (bf16[16,14336]{1,0:T(8,128)(2,1)S(1)}, bf16[16,14336]{1,0:T(8,128)(2,1)}, u32[]{:S(2)}) copy-start(bf16[16,14336]{1,0:T(8,128)(2,1)} %param.7) | copy-start | bytes 1376260
  16.4 9.3 %collective-permute-start.2 = (bf16[128,2048]{1,0:T(8,128)(2,1)S(1)}, bf16[128,2048]{1,0:T(8,128)(2,1)S(1)}, u32[]{:S(2)}, u32[]{:S(2)}) collective-permute-start(bf16[128,2048]{1,0:T(8,128)(2,1)S(1)} %collective-permute-done.1.refs_2_.refs_6_), channel_id=1, source_target_pairs={{0,1},{1,0},{2,3},{3,2},{4,5},{5,4},{6,7},{7,6},{8,9},{9,8},{10,11... | collective-permute-start | bytes 1572872 | tf_op jit(solution)/shard_map/ppermute | solution.py:210
  18.0 23.8 %collective-permute-start.5 = (bf16[4,2,4,16,224]{4,3,2,1,0:T(8,128)(2,1)}, bf16[4,2,4,16,224]{4,3,2,1,0:T(8,128)(2,1)S(1)}, u32[]{:S(2)}, u32[]{:S(2)}) collective-permute-start(bf16[4,2,4,16,224]{4,3,2,1,0:T(8,128)(2,1)} %get-tuple-element.24), channel_id=1, source_target_pairs={{0,0},{1,4},{2,8},{3,12},{4,1},{5,5},{6,9},{7,13},{8,2},{9,6},{10,... | collective-permute-start | bytes 688136 | tf_op jit(solution)/shard_map/ppermute | solution.py:264
  19.5 22.2 %collective-permute-start.6 = (bf16[4,2,4,16,224]{4,3,2,1,0:T(8,128)(2,1)S(1)}, bf16[4,2,4,16,224]{4,3,2,1,0:T(8,128)(2,1)S(1)}, u32[]{:S(2)}, u32[]{:S(2)}) collective-permute-start(bf16[4,2,4,16,224]{4,3,2,1,0:T(8,128)(2,1)S(1)} %get-tuple-element.23), channel_id=1, source_target_pairs={{0,8},{1,12},{2,0},{3,4},{4,9},{5,13},{6,1},{7,5},{8,10},{9,14},{1... | collective-permute-start | bytes 688136 | tf_op jit(solution)/shard_map/ppermute | solution.py:264
  27.4 16.2 %collective-permute-start.3 = (bf16[256,512]{1,0:T(8,128)(2,1)S(1)}, bf16[256,512]{1,0:T(8,128)(2,1)S(1)}, u32[]{:S(2)}, u32[]{:S(2)}) collective-permute-start(bf16[256,512]{1,0:T(8,128)(2,1)S(1)} %pad_maximum_fusion.refs_0_), channel_id=1, source_target_pairs={{0,4},{4,0},{8,12},{12,8},{1,5},{5,1},{9,13},{13,9},{2,6},{6,2},{1... | collective-permute-start | bytes 786440 | tf_op jit(solution)/shard_map/ppermute | solution.py:210
  27.9 19.9 %collective-permute-start.4 = (bf16[256,512]{1,0:T(8,128)(2,1)S(1)}, bf16[256,512]{1,0:T(8,128)(2,1)S(1)}, u32[]{:S(2)}, u32[]{:S(2)}) collective-permute-start(bf16[256,512]{1,0:T(8,128)(2,1)S(1)} %pad_maximum_fusion.refs_0_), channel_id=1, source_target_pairs={{0,8},{4,12},{8,0},{12,4},{1,9},{5,13},{9,1},{13,5},{2,10},{6,14},... | collective-permute-start | bytes 786440 | tf_op jit(solution)/shard_map/ppermute | solution.py:210
  47.7 11.2 %collective-permute-start.13 = (bf16[256,512]{1,0:T(8,128)(2,1)S(1)}, bf16[256,512]{1,0:T(8,128)(2,1)S(1)}, u32[]{:S(2)}, u32[]{:S(2)}) collective-permute-start(bf16[256,512]{1,0:T(8,128)(2,1)S(1)} %collective-permute-done.4.refs_2_), channel_id=1, source_target_pairs={{0,4},{4,0},{8,12},{12,8},{1,5},{5,1},{9,13},{13,9},{2,6},{6,2},{1... | collective-permute-start | bytes 786440 | tf_op jit(solution)/shard_map/ppermute | solution.py:210
  47.7 1.0 copy-start.3
  54.1 14.1 %collective-permute-start.7 = (bf16[256,512]{1,0:T(8,128)(2,1)S(1)}, bf16[256,512]{1,0:T(8,128)(2,1)S(1)}, u32[]{:S(2)}, u32[]{:S(2)}) collective-permute-start(bf16[256,512]{1,0:T(8,128)(2,1)S(1)} %get-tuple-element.22), channel_id=1, source_target_pairs={{0,4},{4,0},{8,12},{12,8},{1,5},{5,1},{9,13},{13,9},{2,6},{6,2},{1... | collective-permute-start | bytes 786440 | tf_op jit(solution)/shard_map/ppermute | solution.py:210
  56.2 21.8 %collective-permute-start.8 = (bf16[256,512]{1,0:T(8,128)(2,1)}, bf16[256,512]{1,0:T(8,128)(2,1)}, u32[]{:S(2)}, u32[]{:S(2)}) collective-permute-start(bf16[256,512]{1,0:T(8,128)(2,1)} %get-tuple-element.21), channel_id=1, source_target_pairs={{0,8},{4,12},{8,0},{12,4},{1,9},{5,13},{9,1},{13,5},{2,10},{6,14},... | collective-permute-start | bytes 786440 | tf_op jit(solution)/shard_map/ppermute | solution.py:210
  57.4 20.5 %collective-permute-start.9 = (bf16[256,512]{1,0:T(8,128)(2,1)}, bf16[256,512]{1,0:T(8,128)(2,1)}, u32[]{:S(2)}, u32[]{:S(2)}) collective-permute-start(bf16[256,512]{1,0:T(8,128)(2,1)} %get-tuple-element.20), channel_id=1, source_target_pairs={{0,12},{4,8},{8,4},{12,0},{1,13},{5,9},{9,5},{13,1},{2,14},{6,10},... | collective-permute-start | bytes 786440 | tf_op jit(solution)/shard_map/ppermute | solution.py:210
  62.6 18.9 %collective-permute-start.14 = (bf16[16,3584]{1,0:T(8,128)(2,1)}, bf16[16,3584]{1,0:T(8,128)(2,1)}, u32[]{:S(2)}, u32[]{:S(2)}) collective-permute-start(bf16[16,3584]{1,0:T(8,128)(2,1)} %get-tuple-element.25), channel_id=1, source_target_pairs={{0,4},{4,0},{8,12},{12,8},{1,5},{5,1},{9,13},{13,9},{2,6},{6,2},{1... | collective-permute-start | bytes 344072 | tf_op jit(solution)/shard_map/ppermute | solution.py:210
  63.3 26.9 %collective-permute-start.15 = (bf16[16,3584]{1,0:T(8,128)(2,1)}, bf16[16,3584]{1,0:T(8,128)(2,1)}, u32[]{:S(2)}, u32[]{:S(2)}) collective-permute-start(bf16[16,3584]{1,0:T(8,128)(2,1)} %get-tuple-element.27), channel_id=1, source_target_pairs={{0,8},{4,12},{8,0},{12,4},{1,9},{5,13},{9,1},{13,5},{2,10},{6,14},... | collective-permute-start | bytes 344072 | tf_op jit(solution)/shard_map/ppermute | solution.py:210
  68.2 22.1 %collective-permute-start.16 = (bf16[16,3584]{1,0:T(8,128)(2,1)}, bf16[16,3584]{1,0:T(8,128)(2,1)}, u32[]{:S(2)}, u32[]{:S(2)}) collective-permute-start(bf16[16,3584]{1,0:T(8,128)(2,1)} %get-tuple-element.26), channel_id=1, source_target_pairs={{0,12},{4,8},{8,4},{12,0},{1,13},{5,9},{9,5},{13,1},{2,14},{6,10},... | collective-permute-start | bytes 344072 | tf_op jit(solution)/shard_map/ppermute | solution.py:210
  91.4 13.0 %collective-permute-start.17 = (bf16[16,3584]{1,0:T(8,128)(2,1)S(1)}, bf16[16,3584]{1,0:T(8,128)(2,1)S(1)}, u32[]{:S(2)}, u32[]{:S(2)}) collective-permute-start(bf16[16,3584]{1,0:T(8,128)(2,1)S(1)} %fusion.3), channel_id=1, source_target_pairs={{0,0},{1,4},{2,8},{3,12},{4,1},{5,5},{6,9},{7,13},{8,2},{9,6},{10,... | collective-permute-start | bytes 344072 | tf_op jit(solution)/shard_map/ppermute | solution.py:281
  92.7 6.4 %collective-permute-start.10 = (bf16[16,512]{1,0:T(8,128)(2,1)S(1)}, bf16[16,512]{1,0:T(8,128)(2,1)S(1)}, u32[]{:S(2)}, u32[]{:S(2)}) collective-permute-start(bf16[16,512]{1,0:T(8,128)(2,1)S(1)} %get-tuple-element.30), channel_id=1, source_target_pairs={{0,1},{1,0},{2,3},{3,2},{4,5},{5,4},{6,7},{7,6},{8,9},{9,8},{10,11... | collective-permute-start | bytes 49160 | tf_op jit(solution)/shard_map/ppermute | solution.py:210
  96.2 4.4 %collective-permute-start.11 = (bf16[16,512]{1,0:T(8,128)(2,1)S(1)}, bf16[16,512]{1,0:T(8,128)(2,1)S(1)}, u32[]{:S(2)}, u32[]{:S(2)}) collective-permute-start(bf16[16,512]{1,0:T(8,128)(2,1)S(1)} %get-tuple-element.29), channel_id=1, source_target_pairs={{0,2},{1,3},{2,0},{3,1},{4,6},{5,7},{6,4},{7,5},{8,10},{9,11},{10,... | collective-permute-start | bytes 49160 | tf_op jit(solution)/shard_map/ppermute | solution.py:210
  98.9 3.2 %collective-permute-start.12 = (bf16[16,512]{1,0:T(8,128)(2,1)S(1)}, bf16[16,512]{1,0:T(8,128)(2,1)S(1)}, u32[]{:S(2)}, u32[]{:S(2)}) collective-permute-start(bf16[16,512]{1,0:T(8,128)(2,1)S(1)} %get-tuple-element.28), channel_id=1, source_target_pairs={{0,3},{1,2},{2,1},{3,0},{4,7},{5,6},{6,5},{7,4},{8,11},{9,10},{10,... | collective-permute-start | bytes 49160 | tf_op jit(solution)/shard_map/ppermute | solution.py:210
  99.0 3.0 %copy-start.6 = (bf16[16,512]{1,0:T(8,128)(2,1)}, bf16[16,512]{1,0:T(8,128)(2,1)S(1)}, u32[]{:S(2)}) copy-start(bf16[16,512]{1,0:T(8,128)(2,1)S(1)} %collective-permute-done.10.refs_1_) | copy-start | bytes 49156
  100.6 1.5 %copy-start.7 = (bf16[16,512]{1,0:T(8,128)(2,1)}, bf16[16,512]{1,0:T(8,128)(2,1)S(1)}, u32[]{:S(2)}) copy-start(bf16[16,512]{1,0:T(8,128)(2,1)S(1)} %collective-permute-done.11.refs_2_) | copy-start | bytes 49156
  (3 other events, 2.1 us)

commit v10 on v9

--- a/solution.py
+++ b/solution.py
@@ -256,18 +256,17 @@
     first = hidden_of(near)
 
     sides = right_blocks.reshape(n_q, 2, GROUP // 2, n_z, n_b, FB)
-    sides = [sides[:, i] for i in range(2)]
-    far, first = lax.optimization_barrier((far, first))
     turn = [
         [(a * n_c + b, (b ^ side) * n_c + a) for a in range(n_z) for b in range(n_c)] for side in (0, n_c // 2)
     ]
-    sides = [lax.ppermute(x, ("blk",) + plane, perm) for x, perm in zip(sides, turn)]
+    sides = [lax.ppermute(sides[:, i], ("blk",) + plane, perm) for i, perm in enumerate(turn)]
+    far, first, sides = lax.optimization_barrier((far, first, sides))
 
     chips = [near] + [gather(x, "rep") for x in far]
     pieces = [p for chip in chips for p in chip]
     hid = [jnp.concatenate([first] + [hidden_of(chip) for chip in chips[1:]], axis=1)]
     hidden = hid + [swap(hid[0], "blk", s) for s in (1, 2)]
-    part, hidden[1:], sides = lax.optimization_barrier((target(pieces, teacher), hidden[1:], sides))
+    part, hidden[1:] = lax.optimization_barrier((target(pieces, teacher), hidden[1:]))
     for s in range(3, n_z):
         hidden.append(swap(hidden[s & (s - 1)], "blk", s & -s))
     hidden = [[h] for h in hidden]
@@ -275,11 +274,17 @@
     backs = [back] + [swap(back[s], "blk", s) for s in range(1, n_z)]
 
     gr = grad_right_partial(hidden, resid)
-    total = gr[0].astype(F32)
-    for s in range(1, n_z):
-        total = total + swap(gr[s], "blk", s).astype(F32)
-    total = lax.ppermute(total.astype(BF), ("blk",) + plane, turn[0])
-    grad_right = total.reshape(n_b, n_k, FB).transpose(1, 0, 2).reshape(n_k, n_b * FB).astype(F32)
+    there = []
+    for s in range(n_c):
+        piece = pick(gr, z ^ c ^ s)
+        there.append(swap(piece, plane, s) if s else piece)
+    there = jnp.stack(there, 0)
+    total = None
+    for s in range(n_z):
+        piece = pick(there, c ^ z ^ s)
+        piece = (swap(piece, "blk", s) if s else piece).astype(F32)
+        total = piece if total is None else total + piece
+    grad_right = total.reshape(n_b, n_k, FB).transpose(1, 0, 2).reshape(n_k, n_b * FB)
 
     gl = grad_left_of(backs, pieces, n_k)
     gl = gl.reshape(n_k, n_b, n_c, BI // n_c).transpose(2, 0, 3, 1).reshape(n_c, n_k, -1)

time: 106 us -> 92.9 us (0.88)
  waiting for transfers between devices: 37.5 us -> 26.3 us
  matrix products: 4.69 us -> 3.34 us
  local copies, waits for them, and re-layouts: 11.2 us -> 9.97 us
    ppermute x15 -> x18, waiting for transfers between devices: 37.5 us -> 19.1 us  [swap(): return lax.ppermute(x, axes, [(i, i ^ s) for i in range(n)])]
    ppermute x3 -> x2, waiting for transfers between devices: 0.01 us -> 7.22 us  [per_device(): lax.ppermute(sides[:, i], ('blk',) + plane, perm)]
    ppermute x15 -> x18, starting transfers between devices: 21.5 us -> 24.1 us  [swap(): return lax.ppermute(x, axes, [(i, i ^ s) for i in range(n)])]
    dot_general x4, matrix products: 4.19 us -> 1.74 us  [hidden_of(): lax.dot_general(left, p, NT, preferred_element_type=F32).astype(BF)]
    unnamed x18 -> x14, local copies, waits for them, and re-layouts: 3.59 us -> 1.3 us
    ppermute x3 -> x2, starting transfers between devices: 6.74 us -> 4.56 us  [per_device(): lax.ppermute(sides[:, i], ('blk',) + plane, perm)]
    convert_element_type x3 -> x0, local copies, waits for them, and re-layouts: 1.19 us -> none  [per_device(): total.reshape(n_b, n_k, FB).transpose(1, 0, 2).reshape(n_k, n_b * FB)]
    another operation x0 -> x1, other arithmetic: none -> 1.13 us  [per_device(): there = jnp.stack(there, 0)]
  transfers between devices with their start and end apart: 18 -> 20, of which waited for: 8 -> 7; matrix products, arithmetic and copies ran while one was open for 11% -> 11% of each run, Pallas kernels for 21% -> 24%
where the time goes in v10:
time: 92.9 us; the launch traced here: 92.3 us
  starting transfers between devices  28.7 us (31%)
  waiting for transfers between devices  26.3 us (28%)
  Pallas kernels  21.9 us (24%)
  local copies, waits for them, and re-layouts  9.97 us (11%)
  matrix products  3.34 us (4%)
  other arithmetic  1.26 us (1%)
    ppermute x18, starting transfers between devices, swap(): return lax.ppermute(x, axes, [(i, i ^ s) for i in range(n)])  24.1 us
    ppermute x18, waiting for transfers between devices, swap(): return lax.ppermute(x, axes, [(i, i ^ s) for i in range(n)])  19.1 us
    pallas_call x1, Pallas kernels, target(): pl.pallas_call(functools.partial(target_kernel, len(tokens)), grid=(cols...  11.3 us
    ppermute x2, waiting for transfers between devices, per_device(): lax.ppermute(sides[:, i], ('blk',) + plane, perm)  7.22 us
    pallas_call x1, Pallas kernels, project(): pl.pallas_call(functools.partial(project_kernel, scale, len(hidden), n_z)...  4.6 us
    ppermute x2, starting transfers between devices, per_device(): lax.ppermute(sides[:, i], ('blk',) + plane, perm)  4.56 us
    pallas_call x1, Pallas kernels, grad_left_of(): pl.pallas_call(functools.partial(grad_left_kernel, n_z, n_k), grid=(depth...  2.16 us
    pallas_call x1, Pallas kernels, grad_right_partial(): pl.pallas_call(functools.partial(grad_right_kernel, n_z, parts), grid=(n_...  2.15 us
  transfers between devices with their start and end apart: 20, of which 7 were waited for; matrix products, arithmetic and copies ran while one was open for 11% of the time, Pallas kernels for 24%

profile of v10, /device:TPU:0, one launch (start us, length us, event | category | flops | bytes accessed | tf_op | source)
XLA Modules:
  0.0 92.3 jit_solution(5116419986678526225)
XLA Ops:
  1.2 2.6 %collective-permute-start.1 = (bf16[128,2048]{1,0:T(8,128)(2,1)}, bf16[128,2048]{1,0:T(8,128)(2,1)S(1)}, u32[]{:S(2)}, u32[]{:S(2)}) collective-permute-start(bf16[128,2048]{1,0:T(8,128)(2,1)} %refs_4_.3), channel_id=1, source_target_pairs={{0,2},{2,0},{1,3},{3,1},{4,6},{6,4},{5,7},{7,5},{8,10},{10,8},{9,1... | collective-permute-start | bytes 1572872 | tf_op jit(solution)/shard_map/ppermute | solution.py:210
  3.7 1.8 %reshape.33 = bf16[4,2,2,4,16,224]{5,4,3,2,1,0:T(8,128)(2,1)S(1)} reshape(bf16[16,14336]{1,0:T(8,128)(2,1)} %param.7) | data formatting | bytes 917504 | tf_op jit(solution)/shard_map/reshape | solution.py:258
  6.3 1.6 %collective-permute-start.2 = (bf16[4,2,4,16,224]{4,3,2,1,0:T(8,128)(2,1)}, bf16[4,2,4,16,224]{4,3,2,1,0:T(8,128)(2,1)S(1)}, u32[]{:S(2)}, u32[]{:S(2)}) collective-permute-start(bf16[4,2,4,16,224]{4,3,2,1,0:T(8,128)(2,1)} %get-tuple-element.24), channel_id=1, source_target_pairs={{0,0},{1,4},{2,8},{3,12},{4,1},{5,5},{6,9},{7,13},{8,2},{9,6},{10,... | collective-permute-start | bytes 688136 | tf_op jit(solution)/shard_map/ppermute | solution.py:262
  7.9 3.0 %collective-permute-start.3 = (bf16[4,2,4,16,224]{4,3,2,1,0:T(8,128)(2,1)}, bf16[4,2,4,16,224]{4,3,2,1,0:T(8,128)(2,1)S(1)}, u32[]{:S(2)}, u32[]{:S(2)}) collective-permute-start(bf16[4,2,4,16,224]{4,3,2,1,0:T(8,128)(2,1)} %get-tuple-element.23), channel_id=1, source_target_pairs={{0,8},{1,12},{2,0},{3,4},{4,9},{5,13},{6,1},{7,5},{8,10},{9,14},{1... | collective-permute-start | bytes 688136 | tf_op jit(solution)/shard_map/ppermute | solution.py:262
  11.0 1.3 %reshape.32 = bf16[2048,64]{1,0:T(8,128)(2,1)} reshape(bf16[16,8192]{1,0:T(8,128)(2,1)S(1)} %copy-done.3) | data formatting | bytes 524288 | tf_op jit(solution)/shard_map/reshape | solution.py:236
  12.3 1.6 %fusion = bf16[256,2048]{1,0:T(8,128)(2,1)S(1)} fusion(bf16[2048,64]{1,0:T(8,128)(2,1)} %reshape.32, s32[2048]{0:T(1024)S(1)} %get-tuple-element.38, s32[2048]{0:T(1024)S(1)} %get-tuple-element.39, s32[256]{0:T(256)S(1)} %get-tuple-element.41, s32[256]{0:T(256)S(1)} %get-tuple-element.42, pred[256]{0:T(512)(128)(4,1)S(1)} %get-tuple-element.37, ...), kind=kOutput, calls=%fused_computation.1 | convolution fusion | flops 69779456 | bytes 1333764 | tf_op jit(solution)/shard_map/dot_general | solution.py:246
  14.9 7.2 %collective-permute-done.3.refs_5_.refs_6_.refs_7_.refs_8_ = bf16[4,2,4,16,224]{4,3,2,1,0:T(8,128)(2,1)S(1)} collective-permute-done((bf16[4,2,4,16,224]{4,3,2,1,0:T(8,128)(2,1)}, bf16[4,2,4,16,224]{4,3,2,1,0:T(8,128)(2,1)S(1)}, u32[]{:S(2)}, u32[]{:S(2)}) %collective-permute-start.3) | collective-permute-done | bytes 229408 | tf_op jit(solution)/shard_map/ppermute | solution.py:262
  23.2 1.5 %collective-permute-done.4.refs_3_.refs_7_ = bf16[128,2048]{1,0:T(8,128)(2,1)S(1)} collective-permute-done((bf16[128,2048]{1,0:T(8,128)(2,1)S(1)}, bf16[128,2048]{1,0:T(8,128)(2,1)S(1)}, u32[]{:S(2)}, u32[]{:S(2)}) %collective-permute-start.4) | collective-permute-done | bytes 524320 | tf_op jit(solution)/shard_map/ppermute | solution.py:210
  25.2 2.1 %collective-permute-start.5 = (bf16[256,512]{1,0:T(8,128)(2,1)S(1)}, bf16[256,512]{1,0:T(8,128)(2,1)S(1)}, u32[]{:S(2)}, u32[]{:S(2)}) collective-permute-start(bf16[256,512]{1,0:T(8,128)(2,1)S(1)} %pad_maximum_fusion.1.refs_0_), channel_id=1, source_target_pairs={{0,4},{4,0},{8,12},{12,8},{1,5},{5,1},{9,13},{13,9},{2,6},{6,2},{1... | collective-permute-start | bytes 786440 | tf_op jit(solution)/shard_map/ppermute | solution.py:210
  27.3 3.3 %collective-permute-start.6 = (bf16[256,512]{1,0:T(8,128)(2,1)S(1)}, bf16[256,512]{1,0:T(8,128)(2,1)S(1)}, u32[]{:S(2)}, u32[]{:S(2)}) collective-permute-start(bf16[256,512]{1,0:T(8,128)(2,1)S(1)} %pad_maximum_fusion.1.refs_0_), channel_id=1, source_target_pairs={{0,8},{4,12},{8,0},{12,4},{1,9},{5,13},{9,1},{13,5},{2,10},{6,14},... | collective-permute-start | bytes 786440 | tf_op jit(solution)/shard_map/ppermute | solution.py:210
  30.6 11.3 %target.1.part_ref = bf16[512,3584]{1,0:T(8,128)(2,1)S(1)} custom-call(bf16[128,2048]{1,0:T(8,128)(2,1)S(1)} %copy-done, bf16[128,2048]{1,0:T(8,128)(2,1)S(1)} %collective-permute-done.refs_1_.refs_5_, bf16[128,2048]{1,0:T(8,128)(2,1)S(1)} %collective-permute-done.1.refs_2_.refs_6_, bf16[128,2048]{1,0:T(8,128)(2,1)S(1)} %collective-permute-done.4.refs_3_.refs_7_, ...), custom_call_target="tpu_custom_call" | custom-call | flops 7516192768 | bytes 14680064 | tf_op jit(solution)/shard_map/target/pallas_call | solution.py:53
  43.1 4.6 %project.1 = (bf16[512,3584]{1,0:T(8,128)(2,1)S(1)}, bf16[4,256,512]{2,1,0:T(8,128)(2,1)S(1)}) custom-call(s32[1]{0:T(128)} %bitcast.1.z_ref, bf16[512,3584]{1,0:T(8,128)(2,1)S(1)} %target.1.part_ref, bf16[256,512]{1,0:T(8,128)(2,1)S(1)} %pad_maximum_fusion.1.refs_0_, bf16[4,2,4,16,224]{4,3,2,1,0:T(8,128)(2,1)S(1)} %collective-permute-done.2.refs_1_.refs_2_.refs_3_.refs_4_, ...), custom_call_target="tpu_custom_call" | custom-call | flops 1879048192 | bytes 11010048 | tf_op jit(solution)/shard_map/project/pallas_call | solution.py:89
  48.6 1.7 %collective-permute-start.7 = (bf16[256,512]{1,0:T(8,128)(2,1)S(1)}, bf16[256,512]{1,0:T(8,128)(2,1)S(1)}, u32[]{:S(2)}, u32[]{:S(2)}) collective-permute-start(bf16[256,512]{1,0:T(8,128)(2,1)S(1)} %get-tuple-element.22), channel_id=1, source_target_pairs={{0,4},{4,0},{8,12},{12,8},{1,5},{5,1},{9,13},{13,9},{2,6},{6,2},{1... | collective-permute-start | bytes 786440 | tf_op jit(solution)/shard_map/ppermute | solution.py:210
  51.3 1.7 %collective-permute-start.9 = (bf16[256,512]{1,0:T(8,128)(2,1)}, bf16[256,512]{1,0:T(8,128)(2,1)}, u32[]{:S(2)}, u32[]{:S(2)}) collective-permute-start(bf16[256,512]{1,0:T(8,128)(2,1)} %get-tuple-element.20), channel_id=1, source_target_pairs={{0,12},{4,8},{8,4},{12,0},{1,13},{5,9},{9,5},{13,1},{2,14},{6,10},... | collective-permute-start | bytes 786440 | tf_op jit(solution)/shard_map/ppermute | solution.py:210
  53.0 2.2 %grad_right.1 = bf16[4,16,3584]{2,1,0:T(8,128)(2,1)S(1)} custom-call(bf16[256,512]{1,0:T(8,128)(2,1)S(1)} %pad_maximum_fusion.1.refs_0_, bf16[256,512]{1,0:T(8,128)(2,1)S(1)} %collective-permute-done.5.refs_1_, bf16[256,512]{1,0:T(8,128)(2,1)S(1)} %collective-permute-done.6.refs_2_, bf16[256,512]{1,0:T(8,128)(2,1)S(1)} %collective-permute-done.13.refs_3_, ...), custom_call_target="tpu_custom_call" | custom-call | flops 939524096 | bytes 3670016 | tf_op jit(solution)/shard_map/grad_right/pallas_call | solution.py:135
  55.9 1.6 %collective-permute-start.15 = (bf16[16,3584]{1,0:T(8,128)(2,1)}, bf16[16,3584]{1,0:T(8,128)(2,1)}, u32[]{:S(2)}, u32[]{:S(2)}) collective-permute-start(bf16[16,3584]{1,0:T(8,128)(2,1)} %get-tuple-element.30), channel_id=1, source_target_pairs={{0,2},{1,3},{2,0},{3,1},{4,6},{5,7},{6,4},{7,5},{8,10},{9,11},{10,... | collective-permute-start | bytes 344072 | tf_op jit(solution)/shard_map/ppermute | solution.py:210
  57.5 3.0 %collective-permute-done.7.refs_1_ = bf16[256,512]{1,0:T(8,128)(2,1)S(1)} collective-permute-done((bf16[256,512]{1,0:T(8,128)(2,1)S(1)}, bf16[256,512]{1,0:T(8,128)(2,1)S(1)}, u32[]{:S(2)}, u32[]{:S(2)}) %collective-permute-start.7) | collective-permute-done | bytes 262176 | tf_op jit(solution)/shard_map/ppermute | solution.py:210
  60.5 11.5 %collective-permute-done.8.refs_2_ = bf16[256,512]{1,0:T(8,128)(2,1)} collective-permute-done((bf16[256,512]{1,0:T(8,128)(2,1)}, bf16[256,512]{1,0:T(8,128)(2,1)}, u32[]{:S(2)}, u32[]{:S(2)}) %collective-permute-start.8) | collective-permute-done | bytes 262176 | tf_op jit(solution)/shard_map/ppermute | solution.py:210
  72.0 2.2 %grad_left.1 = bf16[16,2048]{1,0:T(8,128)(2,1)S(1)} custom-call(bf16[4,256,512]{2,1,0:T(8,128)(2,1)S(1)} %get-tuple-element.16.refs_0_, bf16[256,512]{1,0:T(8,128)(2,1)S(1)} %collective-permute-done.7.refs_1_, bf16[256,512]{1,0:T(8,128)(2,1)} %collective-permute-done.8.refs_2_, bf16[256,512]{1,0:T(8,128)(2,1)} %collective-permute-done.9.refs_3_, ...), custom_call_target="tpu_custom_call" | custom-call | flops 536870912 | bytes 2097152 | tf_op jit(solution)/shard_map/grad_left/pallas_call | solution.py:168
  76.6 3.7 %collective-permute-start.17 = (bf16[16,3584]{1,0:T(8,128)(2,1)S(1)}, bf16[16,3584]{1,0:T(8,128)(2,1)S(1)}, u32[]{:S(2)}, u32[]{:S(2)}) collective-permute-start(bf16[16,3584]{1,0:T(8,128)(2,1)S(1)} %get-tuple-element.25), channel_id=1, source_target_pairs={{0,4},{4,0},{8,12},{12,8},{1,5},{5,1},{9,13},{13,9},{2,6},{6,2},{1... | collective-permute-start | bytes 344072 | tf_op jit(solution)/shard_map/ppermute | solution.py:210
  80.3 1.5 %collective-permute-start.18 = (bf16[16,3584]{1,0:T(8,128)(2,1)S(1)}, bf16[16,3584]{1,0:T(8,128)(2,1)S(1)}, u32[]{:S(2)}, u32[]{:S(2)}) collective-permute-start(bf16[16,3584]{1,0:T(8,128)(2,1)S(1)} %get-tuple-element.27), channel_id=1, source_target_pairs={{0,8},{4,12},{8,0},{12,4},{1,9},{5,13},{9,1},{13,5},{2,10},{6,14},... | collective-permute-start | bytes 344072 | tf_op jit(solution)/shard_map/ppermute | solution.py:210
  81.8 1.4 %collective-permute-start.19 = (bf16[16,3584]{1,0:T(8,128)(2,1)S(1)}, bf16[16,3584]{1,0:T(8,128)(2,1)S(1)}, u32[]{:S(2)}, u32[]{:S(2)}) collective-permute-start(bf16[16,3584]{1,0:T(8,128)(2,1)S(1)} %get-tuple-element.26), channel_id=1, source_target_pairs={{0,12},{4,8},{8,4},{12,0},{1,13},{5,9},{9,5},{13,1},{2,14},{6,10},... | collective-permute-start | bytes 344072 | tf_op jit(solution)/shard_map/ppermute | solution.py:210
  83.8 1.8 %collective-permute-start.11 = (bf16[16,512]{1,0:T(8,128)(2,1)S(1)}, bf16[16,512]{1,0:T(8,128)(2,1)S(1)}, u32[]{:S(2)}, u32[]{:S(2)}) collective-permute-start(bf16[16,512]{1,0:T(8,128)(2,1)S(1)} %get-tuple-element.33), channel_id=1, source_target_pairs={{0,2},{1,3},{2,0},{3,1},{4,6},{5,7},{6,4},{7,5},{8,10},{9,11},{10,... | collective-permute-start | bytes 49160 | tf_op jit(solution)/shard_map/ppermute | solution.py:210
  89.3 1.7 %place.1 = f32[16,2048]{1,0:T(8,128)} custom-call(s32[1]{0:T(128)} %bitcast.c_ref, bf16[16,512]{1,0:T(8,128)(2,1)} %get-tuple-element.35.refs_0_, bf16[16,512]{1,0:T(8,128)(2,1)} %copy-done.4, bf16[16,512]{1,0:T(8,128)(2,1)} %copy-done.5, bf16[16,512]{1,0:T(8,128)(2,1)} %copy-done.6), custom_call_target="tpu_custom_call" | custom-call | tf_op jit(solution)/shard_map/place/pallas_call | solution.py:198
  (62 shorter events, 15.8 us)
Async XLA Ops:
  0.6 10.3 %copy-start.3 = (bf16[16,8192]{1,0:T(8,128)(2,1)S(1)}, bf16[16,8192]{1,0:T(8,128)(2,1)}, u32[]{:S(2)}) copy-start(bf16[16,8192]{1,0:T(8,128)(2,1)} %param.6) | copy-start | bytes 786436
  0.6 13.7 %collective-permute-start = (bf16[128,2048]{1,0:T(8,128)(2,1)}, bf16[128,2048]{1,0:T(8,128)(2,1)S(1)}, u32[]{:S(2)}, u32[]{:S(2)}) collective-permute-start(bf16[128,2048]{1,0:T(8,128)(2,1)} %refs_4_.3), channel_id=1, source_target_pairs={{0,1},{1,0},{2,3},{3,2},{4,5},{5,4},{6,7},{7,6},{8,9},{9,8},{10,11... | collective-permute-start | bytes 1572872 | tf_op jit(solution)/shard_map/ppermute | solution.py:210
  1.2 21.6 %collective-permute-start.1 = (bf16[128,2048]{1,0:T(8,128)(2,1)}, bf16[128,2048]{1,0:T(8,128)(2,1)S(1)}, u32[]{:S(2)}, u32[]{:S(2)}) collective-permute-start(bf16[128,2048]{1,0:T(8,128)(2,1)} %refs_4_.3), channel_id=1, source_target_pairs={{0,2},{2,0},{1,3},{3,1},{4,6},{6,4},{5,7},{7,5},{8,10},{10,8},{9,1... | collective-permute-start | bytes 1572872 | tf_op jit(solution)/shard_map/ppermute | solution.py:210
  6.3 8.5 %collective-permute-start.2 = (bf16[4,2,4,16,224]{4,3,2,1,0:T(8,128)(2,1)}, bf16[4,2,4,16,224]{4,3,2,1,0:T(8,128)(2,1)S(1)}, u32[]{:S(2)}, u32[]{:S(2)}) collective-permute-start(bf16[4,2,4,16,224]{4,3,2,1,0:T(8,128)(2,1)} %get-tuple-element.24), channel_id=1, source_target_pairs={{0,0},{1,4},{2,8},{3,12},{4,1},{5,5},{6,9},{7,13},{8,2},{9,6},{10,... | collective-permute-start | bytes 688136 | tf_op jit(solution)/shard_map/ppermute | solution.py:262
  7.9 14.1 %collective-permute-start.3 = (bf16[4,2,4,16,224]{4,3,2,1,0:T(8,128)(2,1)}, bf16[4,2,4,16,224]{4,3,2,1,0:T(8,128)(2,1)S(1)}, u32[]{:S(2)}, u32[]{:S(2)}) collective-permute-start(bf16[4,2,4,16,224]{4,3,2,1,0:T(8,128)(2,1)} %get-tuple-element.23), channel_id=1, source_target_pairs={{0,8},{1,12},{2,0},{3,4},{4,9},{5,13},{6,1},{7,5},{8,10},{9,14},{1... | collective-permute-start | bytes 688136 | tf_op jit(solution)/shard_map/ppermute | solution.py:262
  12.3 1.6 %copy-start = (bf16[128,2048]{1,0:T(8,128)(2,1)S(1)}, bf16[128,2048]{1,0:T(8,128)(2,1)}, u32[]{:S(2)}) copy-start(bf16[128,2048]{1,0:T(8,128)(2,1)} %refs_4_.3) | copy-start | bytes 1572868
  22.8 1.9 %collective-permute-start.4 = (bf16[128,2048]{1,0:T(8,128)(2,1)S(1)}, bf16[128,2048]{1,0:T(8,128)(2,1)S(1)}, u32[]{:S(2)}, u32[]{:S(2)}) collective-permute-start(bf16[128,2048]{1,0:T(8,128)(2,1)S(1)} %collective-permute-done.1.refs_2_.refs_6_), channel_id=1, source_target_pairs={{0,1},{1,0},{2,3},{3,2},{4,5},{5,4},{6,7},{7,6},{8,9},{9,8},{10,11... | collective-permute-start | bytes 1572872 | tf_op jit(solution)/shard_map/ppermute | solution.py:210
  25.1 18.0 %copy-start.2 = (bf16[4,2,4,16,224]{4,3,2,1,0:T(8,128)(2,1)S(1)}, bf16[4,2,4,16,224]{4,3,2,1,0:T(8,128)(2,1)}, u32[]{:S(2)}) copy-start(bf16[4,2,4,16,224]{4,3,2,1,0:T(8,128)(2,1)} %copy-done.1) | copy-start | bytes 688132
  25.2 16.7 %collective-permute-start.5 = (bf16[256,512]{1,0:T(8,128)(2,1)S(1)}, bf16[256,512]{1,0:T(8,128)(2,1)S(1)}, u32[]{:S(2)}, u32[]{:S(2)}) collective-permute-start(bf16[256,512]{1,0:T(8,128)(2,1)S(1)} %pad_maximum_fusion.1.refs_0_), channel_id=1, source_target_pairs={{0,4},{4,0},{8,12},{12,8},{1,5},{5,1},{9,13},{13,9},{2,6},{6,2},{1... | collective-permute-start | bytes 786440 | tf_op jit(solution)/shard_map/ppermute | solution.py:210
  27.3 15.5 %collective-permute-start.6 = (bf16[256,512]{1,0:T(8,128)(2,1)S(1)}, bf16[256,512]{1,0:T(8,128)(2,1)S(1)}, u32[]{:S(2)}, u32[]{:S(2)}) collective-permute-start(bf16[256,512]{1,0:T(8,128)(2,1)S(1)} %pad_maximum_fusion.1.refs_0_), channel_id=1, source_target_pairs={{0,8},{4,12},{8,0},{12,4},{1,9},{5,13},{9,1},{13,5},{2,10},{6,14},... | collective-permute-start | bytes 786440 | tf_op jit(solution)/shard_map/ppermute | solution.py:210
  42.8 10.2 %collective-permute-start.13 = (bf16[256,512]{1,0:T(8,128)(2,1)S(1)}, bf16[256,512]{1,0:T(8,128)(2,1)S(1)}, u32[]{:S(2)}, u32[]{:S(2)}) collective-permute-start(bf16[256,512]{1,0:T(8,128)(2,1)S(1)} %collective-permute-done.6.refs_2_), channel_id=1, source_target_pairs={{0,4},{4,0},{8,12},{12,8},{1,5},{5,1},{9,13},{13,9},{2,6},{6,2},{1... | collective-permute-start | bytes 786440 | tf_op jit(solution)/shard_map/ppermute | solution.py:210
  48.6 11.9 %collective-permute-start.7 = (bf16[256,512]{1,0:T(8,128)(2,1)S(1)}, bf16[256,512]{1,0:T(8,128)(2,1)S(1)}, u32[]{:S(2)}, u32[]{:S(2)}) collective-permute-start(bf16[256,512]{1,0:T(8,128)(2,1)S(1)} %get-tuple-element.22), channel_id=1, source_target_pairs={{0,4},{4,0},{8,12},{12,8},{1,5},{5,1},{9,13},{13,9},{2,6},{6,2},{1... | collective-permute-start | bytes 786440 | tf_op jit(solution)/shard_map/ppermute | solution.py:210
  50.3 21.7 %collective-permute-start.8 = (bf16[256,512]{1,0:T(8,128)(2,1)}, bf16[256,512]{1,0:T(8,128)(2,1)}, u32[]{:S(2)}, u32[]{:S(2)}) collective-permute-start(bf16[256,512]{1,0:T(8,128)(2,1)} %get-tuple-element.21), channel_id=1, source_target_pairs={{0,8},{4,12},{8,0},{12,4},{1,9},{5,13},{9,1},{13,5},{2,10},{6,14},... | collective-permute-start | bytes 786440 | tf_op jit(solution)/shard_map/ppermute | solution.py:210
  51.3 20.7 %collective-permute-start.9 = (bf16[256,512]{1,0:T(8,128)(2,1)}, bf16[256,512]{1,0:T(8,128)(2,1)}, u32[]{:S(2)}, u32[]{:S(2)}) collective-permute-start(bf16[256,512]{1,0:T(8,128)(2,1)} %get-tuple-element.20), channel_id=1, source_target_pairs={{0,12},{4,8},{8,4},{12,0},{1,13},{5,9},{9,5},{13,1},{2,14},{6,10},... | collective-permute-start | bytes 786440 | tf_op jit(solution)/shard_map/ppermute | solution.py:210
  55.9 19.5 %collective-permute-start.14 = (bf16[16,3584]{1,0:T(8,128)(2,1)}, bf16[16,3584]{1,0:T(8,128)(2,1)}, u32[]{:S(2)}, u32[]{:S(2)}) collective-permute-start(bf16[16,3584]{1,0:T(8,128)(2,1)} %get-tuple-element.31), channel_id=1, source_target_pairs={{0,1},{1,0},{2,3},{3,2},{4,5},{5,4},{6,7},{7,6},{8,9},{9,8},{10,11... | collective-permute-start | bytes 344072 | tf_op jit(solution)/shard_map/ppermute | solution.py:210
  55.9 19.5 %collective-permute-start.15 = (bf16[16,3584]{1,0:T(8,128)(2,1)}, bf16[16,3584]{1,0:T(8,128)(2,1)}, u32[]{:S(2)}, u32[]{:S(2)}) collective-permute-start(bf16[16,3584]{1,0:T(8,128)(2,1)} %get-tuple-element.30), channel_id=1, source_target_pairs={{0,2},{1,3},{2,0},{3,1},{4,6},{5,7},{6,4},{7,5},{8,10},{9,11},{10,... | collective-permute-start | bytes 344072 | tf_op jit(solution)/shard_map/ppermute | solution.py:210
  60.5 15.0 %collective-permute-start.16 = (bf16[16,3584]{1,0:T(8,128)(2,1)}, bf16[16,3584]{1,0:T(8,128)(2,1)}, u32[]{:S(2)}, u32[]{:S(2)}) collective-permute-start(bf16[16,3584]{1,0:T(8,128)(2,1)} %get-tuple-element.29), channel_id=1, source_target_pairs={{0,3},{1,2},{2,1},{3,0},{4,7},{5,6},{6,5},{7,4},{8,11},{9,10},{10,... | collective-permute-start | bytes 344072 | tf_op jit(solution)/shard_map/ppermute | solution.py:210
  76.6 14.4 %collective-permute-start.17 = (bf16[16,3584]{1,0:T(8,128)(2,1)S(1)}, bf16[16,3584]{1,0:T(8,128)(2,1)S(1)}, u32[]{:S(2)}, u32[]{:S(2)}) collective-permute-start(bf16[16,3584]{1,0:T(8,128)(2,1)S(1)} %get-tuple-element.25), channel_id=1, source_target_pairs={{0,4},{4,0},{8,12},{12,8},{1,5},{5,1},{9,13},{13,9},{2,6},{6,2},{1... | collective-permute-start | bytes 344072 | tf_op jit(solution)/shard_map/ppermute | solution.py:210
  80.3 10.8 %collective-permute-start.18 = (bf16[16,3584]{1,0:T(8,128)(2,1)S(1)}, bf16[16,3584]{1,0:T(8,128)(2,1)S(1)}, u32[]{:S(2)}, u32[]{:S(2)}) collective-permute-start(bf16[16,3584]{1,0:T(8,128)(2,1)S(1)} %get-tuple-element.27), channel_id=1, source_target_pairs={{0,8},{4,12},{8,0},{12,4},{1,9},{5,13},{9,1},{13,5},{2,10},{6,14},... | collective-permute-start | bytes 344072 | tf_op jit(solution)/shard_map/ppermute | solution.py:210
  81.8 9.3 %collective-permute-start.19 = (bf16[16,3584]{1,0:T(8,128)(2,1)S(1)}, bf16[16,3584]{1,0:T(8,128)(2,1)S(1)}, u32[]{:S(2)}, u32[]{:S(2)}) collective-permute-start(bf16[16,3584]{1,0:T(8,128)(2,1)S(1)} %get-tuple-element.26), channel_id=1, source_target_pairs={{0,12},{4,8},{8,4},{12,0},{1,13},{5,9},{9,5},{13,1},{2,14},{6,10},... | collective-permute-start | bytes 344072 | tf_op jit(solution)/shard_map/ppermute | solution.py:210
  83.8 1.8 %collective-permute-start.10 = (bf16[16,512]{1,0:T(8,128)(2,1)S(1)}, bf16[16,512]{1,0:T(8,128)(2,1)S(1)}, u32[]{:S(2)}, u32[]{:S(2)}) collective-permute-start(bf16[16,512]{1,0:T(8,128)(2,1)S(1)} %get-tuple-element.34), channel_id=1, source_target_pairs={{0,1},{1,0},{2,3},{3,2},{4,5},{5,4},{6,7},{7,6},{8,9},{9,8},{10,11... | collective-permute-start | bytes 49160 | tf_op jit(solution)/shard_map/ppermute | solution.py:210
  83.8 3.7 %collective-permute-start.11 = (bf16[16,512]{1,0:T(8,128)(2,1)S(1)}, bf16[16,512]{1,0:T(8,128)(2,1)S(1)}, u32[]{:S(2)}, u32[]{:S(2)}) collective-permute-start(bf16[16,512]{1,0:T(8,128)(2,1)S(1)} %get-tuple-element.33), channel_id=1, source_target_pairs={{0,2},{1,3},{2,0},{3,1},{4,6},{5,7},{6,4},{7,5},{8,10},{9,11},{10,... | collective-permute-start | bytes 49160 | tf_op jit(solution)/shard_map/ppermute | solution.py:210
  85.6 3.2 %copy-start.4 = (bf16[16,512]{1,0:T(8,128)(2,1)}, bf16[16,512]{1,0:T(8,128)(2,1)S(1)}, u32[]{:S(2)}) copy-start(bf16[16,512]{1,0:T(8,128)(2,1)S(1)} %collective-permute-done.10.refs_1_) | copy-start | bytes 49156
  85.6 3.2 %collective-permute-start.12 = (bf16[16,512]{1,0:T(8,128)(2,1)S(1)}, bf16[16,512]{1,0:T(8,128)(2,1)S(1)}, u32[]{:S(2)}, u32[]{:S(2)}) collective-permute-start(bf16[16,512]{1,0:T(8,128)(2,1)S(1)} %get-tuple-element.32), channel_id=1, source_target_pairs={{0,3},{1,2},{2,1},{3,0},{4,7},{5,6},{6,5},{7,4},{8,11},{9,10},{10,... | collective-permute-start | bytes 49160 | tf_op jit(solution)/shard_map/ppermute | solution.py:210
  (3 other events, 2.5 us)

commit v11 on v10

--- a/solution.py
+++ b/solution.py
@@ -64,7 +64,8 @@
 
 
 def project_kernel(scale, n_hid, n_z, z_ref, part_ref, *refs):
-    hid_refs, right_refs, (resid_ref, back_ref) = refs[:n_hid], refs[n_hid:-2], refs[-2:]
+    hid_refs, right_refs, refs = refs[:n_hid], refs[n_hid : n_hid + 2 * n_z], refs[n_hid + 2 * n_z :]
+    resid_ref, *back_refs = refs
     right = jnp.stack(
         [jnp.concatenate([a[0, :, 0], b[0, :, 0]], axis=0) for a, b in zip(right_refs[:n_z], right_refs[n_z:])],
         axis=0,
@@ -76,7 +77,8 @@
     resid = ((student - part_ref[...].astype(F32)) * scale).astype(BF)
     resid_ref[...] = resid
     back = lax.dot_general(right, resid, NT, preferred_element_type=F32)
-    back_ref[...] = back.astype(BF).reshape(back_ref.shape)
+    for s, ref in enumerate(back_refs):
+        ref[...] = back[s * rows : (s + 1) * rows].astype(BF)
 
 
 def project(z, part, hidden, sides, scale):
@@ -94,32 +96,23 @@
             in_specs=[pl.BlockSpec((t, COLS), lambda q, z: (0, q))]
             + [pl.BlockSpec((rows, h.shape[1]), lambda q, z: (q, 0)) for h in hidden]
             + right_specs * 2,
-            out_specs=[
-                pl.BlockSpec((t, COLS), lambda q, z: (0, q)),
-                pl.BlockSpec((n_z, rows, t), lambda q, z: (0, q, 0)),
-            ],
+            out_specs=[pl.BlockSpec((t, COLS), lambda q, z: (0, q))]
+            + [pl.BlockSpec((rows, t), lambda q, z: (q, 0))] * n_z,
         ),
-        out_shape=[
-            jax.ShapeDtypeStruct((t, cols), BF),
-            jax.ShapeDtypeStruct((n_z, n_q * rows, t), BF),
-        ],
+        out_shape=[jax.ShapeDtypeStruct((t, cols), BF)]
+        + [jax.ShapeDtypeStruct((n_q * rows, t), BF)] * n_z,
         compiler_params=pltpu.CompilerParams(vmem_limit_bytes=VMEM),
         cost_estimate=cost(2 * t * cols * n_z * rows * 2, 6 * t * cols),
         name="project",
     )(z, part, *hidden, *[sides[0]] * n_z, *[sides[1]] * n_z)
 
 
-def grad_right_kernel(n_z, parts, *refs):
-    hid_refs, (resid_ref, out_ref) = refs[:-2], refs[-2:]
-    hid = jnp.concatenate(
-        [
-            jnp.concatenate([r[...] for r in hid_refs[s * parts : (s + 1) * parts]], axis=1)
-            for s in range(n_z)
-        ],
-        axis=0,
-    )
+def grad_right_kernel(*refs):
+    *hid_refs, resid_ref, out_ref = refs
+    n_z, rows = len(hid_refs), hid_refs[0].shape[1]
+    hid = jnp.concatenate([r[0] for r in hid_refs], axis=0)
     prod = jnp.dot(hid, resid_ref[...], preferred_element_type=F32)
-    prod = prod.reshape(n_z, GROUP, prod.shape[0] // (n_z * GROUP), COLS)
+    prod = prod.reshape(n_z, GROUP, rows // GROUP, COLS)
     block = lax.broadcasted_iota(jnp.int32, (1, 1, COLS), 2) // FB
     total = prod[:, 0]
     for k in range(1, GROUP):
@@ -129,25 +122,24 @@
 
 def grad_right_partial(hidden, resid):
     t, cols = resid.shape
-    n_z, parts = len(hidden), len(hidden[0])
-    n_q = cols // COLS
-    rows = hidden[0][0].shape[0] // n_q
-    return pl.pallas_call(
-        functools.partial(grad_right_kernel, n_z, parts),
+    n_z, n_q = len(hidden), cols // COLS
+    rows = hidden[0][0].shape[1] // n_q
+    return pl.pallas_call(
+        grad_right_kernel,
         grid=(n_q,),
-        in_specs=[pl.BlockSpec((rows, h.shape[1]), lambda q: (q, 0)) for hs in hidden for h in hs]
+        in_specs=[pl.BlockSpec((1, rows, t), lambda q, i=i: (i, q, 0)) for _, i in hidden]
         + [pl.BlockSpec((t, COLS), lambda q: (0, q))],
         out_specs=pl.BlockSpec((n_z, rows // GROUP, COLS), lambda q: (0, 0, q)),
         out_shape=jax.ShapeDtypeStruct((n_z, rows // GROUP, cols), BF),
         compiler_params=pltpu.CompilerParams(vmem_limit_bytes=VMEM),
         cost_estimate=cost(2 * t * cols * n_z * rows, 2 * t * cols),
         name="grad_right",
-    )(*[h for hs in hidden for h in hs], resid)
+    )(*[h for h, _ in hidden], resid)
 
 
 def grad_left_kernel(n_z, n_k, *refs):
     back_refs, tok_refs, out_ref = refs[:n_z], refs[n_z:-1], refs[-1]
-    total = back_refs[0][0].astype(F32)
+    total = back_refs[0][...].astype(F32)
     for ref in back_refs[1:]:
         total = total + ref[...].astype(F32)
     prod = jnp.dot(total.astype(BF), rows_of(tok_refs), preferred_element_type=F32)
@@ -168,8 +160,7 @@
     return pl.pallas_call(
         functools.partial(grad_left_kernel, n_z, n_k),
         grid=(depth // block,),
-        in_specs=[pl.BlockSpec((1, rows, t), lambda q: (0, 0, 0))]
-        + [pl.BlockSpec((rows, t), lambda q: (0, 0))] * (n_z - 1)
+        in_specs=[pl.BlockSpec((rows, t), lambda q: (0, 0))] * n_z
         + [pl.BlockSpec((piece, block), lambda q: (0, q))] * len(tokens),
         out_specs=pl.BlockSpec((n_k, block), lambda q: (0, q)),
         out_shape=jax.ShapeDtypeStruct((n_k, depth), BF),
@@ -265,13 +256,21 @@
     chips = [near] + [gather(x, "rep") for x in far]
     pieces = [p for chip in chips for p in chip]
     hid = [jnp.concatenate([first] + [hidden_of(chip) for chip in chips[1:]], axis=1)]
-    hidden = hid + [swap(hid[0], "blk", s) for s in (1, 2)]
-    part, hidden[1:] = lax.optimization_barrier((target(pieces, teacher), hidden[1:]))
-    for s in range(3, n_z):
-        hidden.append(swap(hidden[s & (s - 1)], "blk", s & -s))
-    hidden = [[h] for h in hidden]
-    resid, back = project(jnp.reshape(z, (1,)).astype(jnp.int32), part, hid, sides, scale)
-    backs = [back] + [swap(back[s], "blk", s) for s in range(1, n_z)]
+    bit = n_z // 2
+    got = swap(hid[0], "blk", bit)
+    part, got = lax.optimization_barrier((target(pieces, teacher), got))
+    hidden, order, got = [hid[0][None]], [0], got[None]
+    while True:
+        hidden.append(got)
+        order += [o ^ bit for o in order]
+        bit //= 2
+        if bit == 0:
+            break
+        got = swap(jnp.concatenate(hidden, axis=0), "blk", bit)
+    where = [(x, i) for x in hidden for i in range(x.shape[0])]
+    hidden = [where[order.index(s)] for s in range(n_z)]
+    resid, *back = project(jnp.reshape(z, (1,)).astype(jnp.int32), part, hid, sides, scale)
+    backs = back[:1] + [swap(back[s], "blk", s) for s in range(1, n_z)]
 
     gr = grad_right_partial(hidden, resid)
     there = []

time: 92.9 us -> 96.7 us (1.041)
  local copies, waits for them, and re-layouts: 9.97 us -> 16.3 us
  starting transfers between devices: 28.7 us -> 25.8 us
  matrix products: 3.34 us -> 2.24 us
    unnamed x14 -> x30, local copies, waits for them, and re-layouts: 1.3 us -> 10.9 us
    ppermute x18 -> x17, starting transfers between devices: 24.1 us -> 21.3 us  [swap(): return lax.ppermute(x, axes, [(i, i ^ s) for i in range(n)])]
    ppermute x2, waiting for transfers between devices: 7.22 us -> 8.67 us  [per_device(): lax.ppermute(sides[:, i], ('blk',) + plane, perm)]
    dot_general x1, matrix products: 1.61 us -> 0.5 us  [per_device(): left = lax.dot_general(take, left, NT, preferred_element_type=F32)]
    another operation x1, other arithmetic: 1.13 us -> 0.06 us  [per_device(): there = jnp.stack(there, 0)]
    ppermute x18 -> x17, waiting for transfers between devices: 19.1 us -> 18.5 us  [swap(): return lax.ppermute(x, axes, [(i, i ^ s) for i in range(n)])]
  transfers between devices with their start and end apart: 20 -> 19, of which waited for: 7 -> 7; matrix products, arithmetic and copies ran while one was open for 11% -> 6% of each run, Pallas kernels for 24% -> 23%
where the time goes in v11:
time: 96.7 us; the launch traced here: 96.1 us
  waiting for transfers between devices  27.2 us (28%)
  starting transfers between devices  25.8 us (27%)
  Pallas kernels  22.5 us (23%)
  local copies, waits for them, and re-layouts  16.3 us (17%)
  matrix products  2.24 us (2%)
  other arithmetic  1.05 us (1%)
    ppermute x17, starting transfers between devices, swap(): return lax.ppermute(x, axes, [(i, i ^ s) for i in range(n)])  21.3 us
    ppermute x17, waiting for transfers between devices, swap(): return lax.ppermute(x, axes, [(i, i ^ s) for i in range(n)])  18.5 us
    pallas_call x1, Pallas kernels, target(): pl.pallas_call(functools.partial(target_kernel, len(tokens)), grid=(cols...  11.3 us
    unnamed x30, local copies, waits for them, and re-layouts  10.9 us
    ppermute x2, waiting for transfers between devices, per_device(): lax.ppermute(sides[:, i], ('blk',) + plane, perm)  8.67 us
    pallas_call x1, Pallas kernels, project(): pl.pallas_call(functools.partial(project_kernel, scale, len(hidden), n_z)...  5.19 us
    ppermute x2, starting transfers between devices, per_device(): lax.ppermute(sides[:, i], ('blk',) + plane, perm)  4.56 us
    pallas_call x1, Pallas kernels, grad_left_of(): pl.pallas_call(functools.partial(grad_left_kernel, n_z, n_k), grid=(depth...  2.16 us
  transfers between devices with their start and end apart: 19, of which 7 were waited for; matrix products, arithmetic and copies ran while one was open for 6% of the time, Pallas kernels for 23%

profile of v11, /device:TPU:0, one launch (start us, length us, event | category | flops | bytes accessed | tf_op | source)
XLA Modules:
  0.0 96.1 jit_solution(6888968163239735761)
XLA Ops:
  1.2 2.6 %collective-permute-start.1 = (bf16[128,2048]{1,0:T(8,128)(2,1)}, bf16[128,2048]{1,0:T(8,128)(2,1)S(1)}, u32[]{:S(2)}, u32[]{:S(2)}) collective-permute-start(bf16[128,2048]{1,0:T(8,128)(2,1)} %refs_4_.3), channel_id=1, source_target_pairs={{0,2},{2,0},{1,3},{3,1},{4,6},{6,4},{5,7},{7,5},{8,10},{10,8},{9,1... | collective-permute-start | bytes 1572872 | tf_op jit(solution)/shard_map/ppermute | solution.py:201
  3.7 1.8 %reshape.33 = bf16[4,2,2,4,16,224]{5,4,3,2,1,0:T(8,128)(2,1)S(1)} reshape(bf16[16,14336]{1,0:T(8,128)(2,1)} %param.7) | data formatting | bytes 917504 | tf_op jit(solution)/shard_map/reshape | solution.py:249
  6.2 3.9 %collective-permute-start.3 = (bf16[4,2,4,16,224]{4,3,2,1,0:T(8,128)(2,1)S(1)}, bf16[4,2,4,16,224]{4,3,2,1,0:T(8,128)(2,1)S(1)}, u32[]{:S(2)}, u32[]{:S(2)}) collective-permute-start(bf16[4,2,4,16,224]{4,3,2,1,0:T(8,128)(2,1)S(1)} %get-tuple-element.24), channel_id=1, source_target_pairs={{0,8},{1,12},{2,0},{3,4},{4,9},{5,13},{6,1},{7,5},{8,10},{9,14},{1... | collective-permute-start | bytes 688136 | tf_op jit(solution)/shard_map/ppermute | solution.py:253
  13.4 8.7 %collective-permute-done.3.refs_5_.refs_6_.refs_7_.refs_8_ = bf16[4,2,4,16,224]{4,3,2,1,0:T(8,128)(2,1)S(1)} collective-permute-done((bf16[4,2,4,16,224]{4,3,2,1,0:T(8,128)(2,1)S(1)}, bf16[4,2,4,16,224]{4,3,2,1,0:T(8,128)(2,1)S(1)}, u32[]{:S(2)}, u32[]{:S(2)}) %collective-permute-start.3) | collective-permute-done | bytes 229408 | tf_op jit(solution)/shard_map/ppermute | solution.py:253
  23.2 1.5 %collective-permute-done.4.refs_3_.refs_7_ = bf16[128,2048]{1,0:T(8,128)(2,1)S(1)} collective-permute-done((bf16[128,2048]{1,0:T(8,128)(2,1)S(1)}, bf16[128,2048]{1,0:T(8,128)(2,1)S(1)}, u32[]{:S(2)}, u32[]{:S(2)}) %collective-permute-start.4) | collective-permute-done | bytes 524320 | tf_op jit(solution)/shard_map/ppermute | solution.py:201
  25.2 3.3 %collective-permute-start.5 = (bf16[256,512]{1,0:T(8,128)(2,1)S(1)}, bf16[256,512]{1,0:T(8,128)(2,1)S(1)}, u32[]{:S(2)}, u32[]{:S(2)}) collective-permute-start(bf16[256,512]{1,0:T(8,128)(2,1)S(1)} %get-tuple-element.34.refs_0_), channel_id=1, source_target_pairs={{0,8},{4,12},{8,0},{12,4},{1,9},{5,13},{9,1},{13,5},{2,10},{6,14},... | collective-permute-start | bytes 786440 | tf_op jit(solution)/shard_map/ppermute | solution.py:201
  28.5 11.3 %target.1.part_ref = bf16[512,3584]{1,0:T(8,128)(2,1)S(1)} custom-call(bf16[128,2048]{1,0:T(8,128)(2,1)S(1)} %copy-done, bf16[128,2048]{1,0:T(8,128)(2,1)S(1)} %collective-permute-done.refs_1_.refs_5_, bf16[128,2048]{1,0:T(8,128)(2,1)S(1)} %collective-permute-done.1.refs_2_.refs_6_, bf16[128,2048]{1,0:T(8,128)(2,1)S(1)} %collective-permute-done.4.refs_3_.refs_7_, ...), custom_call_target="tpu_custom_call" | custom-call | flops 7516192768 | bytes 14680064 | tf_op jit(solution)/shard_map/target/pallas_call | solution.py:53
  39.8 1.8 %copy-done.1 = bf16[512,3584]{1,0:T(8,128)(2,1)} copy-done((bf16[512,3584]{1,0:T(8,128)(2,1)}, bf16[512,3584]{1,0:T(8,128)(2,1)S(1)}, u32[]{:S(2)}) %copy-start.1) | copy-done | bytes 3670040
  42.4 1.8 %collective-permute-start.12 = (bf16[2,256,512]{2,1,0:T(8,128)(2,1)}, bf16[2,256,512]{2,1,0:T(8,128)(2,1)S(1)}, u32[]{:S(2)}, u32[]{:S(2)}) collective-permute-start(bf16[2,256,512]{2,1,0:T(8,128)(2,1)} %pad_maximum_fusion), channel_id=1, source_target_pairs={{0,4},{4,0},{8,12},{12,8},{1,5},{5,1},{9,13},{13,9},{2,6},{6,2},{1... | collective-permute-start | bytes 1572872 | tf_op jit(solution)/shard_map/ppermute | solution.py:201
  44.2 2.0 %copy-done.2 = bf16[512,3584]{1,0:T(8,128)(2,1)S(1)} copy-done((bf16[512,3584]{1,0:T(8,128)(2,1)S(1)}, bf16[512,3584]{1,0:T(8,128)(2,1)}, u32[]{:S(2)}) %copy-start.2) | copy-done | bytes 3670040
  47.2 0.9 copy-done.8
  48.2 0.9 copy-done.10
  49.1 5.2 %project.1 = (bf16[512,3584]{1,0:T(8,128)(2,1)S(1)}, bf16[256,512]{1,0:T(8,128)(2,1)S(1)}, bf16[256,512]{1,0:T(8,128)(2,1)S(1)}, bf16[256,512]{1,0:T(8,128)(2,1)}, bf16[256,512]{1,0:T(8,128)(2,1)}) custom-call(s32[1]{0:T(128)} %bitcast.1.z_ref, bf16[512,3584]{1,0:T(8,128)(2,1)S(1)} %copy-done.2, bf16[256,512]{1,0:T(8,128)(2,1)S(1)} %copy-done.6, ...), custom_call_target="tpu_custom_call" | custom-call | flops 1879048192 | bytes 11010048 | tf_op jit(solution)/shard_map/project/pallas_call | solution.py:91
  54.5 1.4 %collective-permute-start.7 = (bf16[256,512]{1,0:T(8,128)(2,1)}, bf16[256,512]{1,0:T(8,128)(2,1)}, u32[]{:S(2)}, u32[]{:S(2)}) collective-permute-start(bf16[256,512]{1,0:T(8,128)(2,1)} %get-tuple-element.20), channel_id=1, source_target_pairs={{0,8},{4,12},{8,0},{12,4},{1,9},{5,13},{9,1},{13,5},{2,10},{6,14},... | collective-permute-start | bytes 786440 | tf_op jit(solution)/shard_map/ppermute | solution.py:201
  56.0 2.7 %collective-permute-start.8 = (bf16[256,512]{1,0:T(8,128)(2,1)}, bf16[256,512]{1,0:T(8,128)(2,1)}, u32[]{:S(2)}, u32[]{:S(2)}) collective-permute-start(bf16[256,512]{1,0:T(8,128)(2,1)} %get-tuple-element.21), channel_id=1, source_target_pairs={{0,12},{4,8},{8,4},{12,0},{1,13},{5,9},{9,5},{13,1},{2,14},{6,10},... | collective-permute-start | bytes 786440 | tf_op jit(solution)/shard_map/ppermute | solution.py:201
  58.7 2.2 %grad_right.1 = bf16[4,16,3584]{2,1,0:T(8,128)(2,1)S(1)} custom-call(bf16[1,256,512]{2,1,0:T(8,128)(2,1)S(1)} %get-tuple-element.33.refs_0_, bf16[2,256,512]{2,1,0:T(8,128)(2,1)S(1)} %collective-permute-done.12.refs_1_.refs_3_, bf16[1,256,512]{2,1,0:T(8,128)(2,1)S(1)} %bitcast.53, bf16[2,256,512]{2,1,0:T(8,128)(2,1)S(1)} %collective-permute-done.12.refs_1_.refs_3_, ...), custom_call_target="tpu_custom_call" | custom-call | flops 939524096 | bytes 3670016 | tf_op jit(solution)/shard_map/grad_right/pallas_call | solution.py:127
  61.6 5.7 %collective-permute-done.6.refs_1_ = bf16[256,512]{1,0:T(8,128)(2,1)S(1)} collective-permute-done((bf16[256,512]{1,0:T(8,128)(2,1)S(1)}, bf16[256,512]{1,0:T(8,128)(2,1)S(1)}, u32[]{:S(2)}, u32[]{:S(2)}) %collective-permute-start.6) | collective-permute-done | bytes 262176 | tf_op jit(solution)/shard_map/ppermute | solution.py:201
  68.0 8.3 %collective-permute-done.7.refs_2_ = bf16[256,512]{1,0:T(8,128)(2,1)} collective-permute-done((bf16[256,512]{1,0:T(8,128)(2,1)}, bf16[256,512]{1,0:T(8,128)(2,1)}, u32[]{:S(2)}, u32[]{:S(2)}) %collective-permute-start.7) | collective-permute-done | bytes 262176 | tf_op jit(solution)/shard_map/ppermute | solution.py:201
  76.2 0.9 copy-done.4
  77.2 2.2 %grad_left.1 = bf16[16,2048]{1,0:T(8,128)(2,1)S(1)} custom-call(bf16[256,512]{1,0:T(8,128)(2,1)S(1)} %get-tuple-element.18.refs_0_, bf16[256,512]{1,0:T(8,128)(2,1)S(1)} %copy-done.4, bf16[256,512]{1,0:T(8,128)(2,1)} %collective-permute-done.7.refs_2_, bf16[256,512]{1,0:T(8,128)(2,1)} %collective-permute-done.8.refs_3_, bf16[128,2048]{1,0:T(8,128)(2,1)S(1)} %copy-done, ...), custom_call_target="tpu_custom_call" | custom-call | flops 536870912 | bytes 2097152 | tf_op jit(solution)/shard_map/grad_left/pallas_call | solution.py:160
  80.7 3.0 %collective-permute-start.18 = (bf16[16,3584]{1,0:T(8,128)(2,1)S(1)}, bf16[16,3584]{1,0:T(8,128)(2,1)S(1)}, u32[]{:S(2)}, u32[]{:S(2)}) collective-permute-start(bf16[16,3584]{1,0:T(8,128)(2,1)S(1)} %get-tuple-element.27), channel_id=1, source_target_pairs={{0,12},{4,8},{8,4},{12,0},{1,13},{5,9},{9,5},{13,1},{2,14},{6,10},... | collective-permute-start | bytes 344072 | tf_op jit(solution)/shard_map/ppermute | solution.py:201
  83.7 3.3 %collective-permute-start.17 = (bf16[16,3584]{1,0:T(8,128)(2,1)S(1)}, bf16[16,3584]{1,0:T(8,128)(2,1)S(1)}, u32[]{:S(2)}, u32[]{:S(2)}) collective-permute-start(bf16[16,3584]{1,0:T(8,128)(2,1)S(1)} %get-tuple-element.28), channel_id=1, source_target_pairs={{0,8},{4,12},{8,0},{12,4},{1,9},{5,13},{9,1},{13,5},{2,10},{6,14},... | collective-permute-start | bytes 344072 | tf_op jit(solution)/shard_map/ppermute | solution.py:201
  90.0 1.9 %collective-permute-done.10.refs_2_ = bf16[16,512]{1,0:T(8,128)(2,1)S(1)} collective-permute-done((bf16[16,512]{1,0:T(8,128)(2,1)S(1)}, bf16[16,512]{1,0:T(8,128)(2,1)S(1)}, u32[]{:S(2)}, u32[]{:S(2)}) %collective-permute-start.10) | collective-permute-done | bytes 16416 | tf_op jit(solution)/shard_map/ppermute | solution.py:201
  93.1 1.7 %place.1 = f32[16,2048]{1,0:T(8,128)} custom-call(s32[1]{0:T(128)} %bitcast.c_ref, bf16[16,512]{1,0:T(8,128)(2,1)} %get-tuple-element.38.refs_0_, bf16[16,512]{1,0:T(8,128)(2,1)} %copy-done.12, bf16[16,512]{1,0:T(8,128)(2,1)} %copy-done.13, bf16[16,512]{1,0:T(8,128)(2,1)} %copy-done.14), custom_call_target="tpu_custom_call" | custom-call | tf_op jit(solution)/shard_map/place/pallas_call | solution.py:189
  (76 shorter events, 16.2 us)
Async XLA Ops:
  0.6 9.5 %copy-start.11 = (bf16[16,8192]{1,0:T(8,128)(2,1)S(1)}, bf16[16,8192]{1,0:T(8,128)(2,1)}, u32[]{:S(2)}) copy-start(bf16[16,8192]{1,0:T(8,128)(2,1)} %param.6) | copy-start | bytes 786436
  0.6 11.6 %collective-permute-start = (bf16[128,2048]{1,0:T(8,128)(2,1)}, bf16[128,2048]{1,0:T(8,128)(2,1)S(1)}, u32[]{:S(2)}, u32[]{:S(2)}) collective-permute-start(bf16[128,2048]{1,0:T(8,128)(2,1)} %refs_4_.3), channel_id=1, source_target_pairs={{0,1},{1,0},{2,3},{3,2},{4,5},{5,4},{6,7},{7,6},{8,9},{9,8},{10,11... | collective-permute-start | bytes 1572872 | tf_op jit(solution)/shard_map/ppermute | solution.py:201
  1.2 21.6 %collective-permute-start.1 = (bf16[128,2048]{1,0:T(8,128)(2,1)}, bf16[128,2048]{1,0:T(8,128)(2,1)S(1)}, u32[]{:S(2)}, u32[]{:S(2)}) collective-permute-start(bf16[128,2048]{1,0:T(8,128)(2,1)} %refs_4_.3), channel_id=1, source_target_pairs={{0,2},{2,0},{1,3},{3,1},{4,6},{6,4},{5,7},{7,5},{8,10},{10,8},{9,1... | collective-permute-start | bytes 1572872 | tf_op jit(solution)/shard_map/ppermute | solution.py:201
  5.5 7.1 %collective-permute-start.2 = (bf16[4,2,4,16,224]{4,3,2,1,0:T(8,128)(2,1)S(1)}, bf16[4,2,4,16,224]{4,3,2,1,0:T(8,128)(2,1)S(1)}, u32[]{:S(2)}, u32[]{:S(2)}) collective-permute-start(bf16[4,2,4,16,224]{4,3,2,1,0:T(8,128)(2,1)S(1)} %get-tuple-element.25), channel_id=1, source_target_pairs={{0,0},{1,4},{2,8},{3,12},{4,1},{5,5},{6,9},{7,13},{8,2},{9,6},{10,... | collective-permute-start | bytes 688136 | tf_op jit(solution)/shard_map/ppermute | solution.py:253
  6.2 15.8 %collective-permute-start.3 = (bf16[4,2,4,16,224]{4,3,2,1,0:T(8,128)(2,1)S(1)}, bf16[4,2,4,16,224]{4,3,2,1,0:T(8,128)(2,1)S(1)}, u32[]{:S(2)}, u32[]{:S(2)}) collective-permute-start(bf16[4,2,4,16,224]{4,3,2,1,0:T(8,128)(2,1)S(1)} %get-tuple-element.24), channel_id=1, source_target_pairs={{0,8},{1,12},{2,0},{3,4},{4,9},{5,13},{6,1},{7,5},{8,10},{9,14},{1... | collective-permute-start | bytes 688136 | tf_op jit(solution)/shard_map/ppermute | solution.py:253
  22.8 1.9 %collective-permute-start.4 = (bf16[128,2048]{1,0:T(8,128)(2,1)S(1)}, bf16[128,2048]{1,0:T(8,128)(2,1)S(1)}, u32[]{:S(2)}, u32[]{:S(2)}) collective-permute-start(bf16[128,2048]{1,0:T(8,128)(2,1)S(1)} %collective-permute-done.1.refs_2_.refs_6_), channel_id=1, source_target_pairs={{0,1},{1,0},{2,3},{3,2},{4,5},{5,4},{6,7},{7,6},{8,9},{9,8},{10,11... | collective-permute-start | bytes 1572872 | tf_op jit(solution)/shard_map/ppermute | solution.py:201
  25.2 14.6 %copy-start.5 = (bf16[256,512]{1,0:T(8,128)(2,1)}, bf16[256,512]{1,0:T(8,128)(2,1)S(1)}, u32[]{:S(2)}) copy-start(bf16[256,512]{1,0:T(8,128)(2,1)S(1)} %get-tuple-element.34.refs_0_) | copy-start | bytes 786436
  25.2 16.4 %collective-permute-start.5 = (bf16[256,512]{1,0:T(8,128)(2,1)S(1)}, bf16[256,512]{1,0:T(8,128)(2,1)S(1)}, u32[]{:S(2)}, u32[]{:S(2)}) collective-permute-start(bf16[256,512]{1,0:T(8,128)(2,1)S(1)} %get-tuple-element.34.refs_0_), channel_id=1, source_target_pairs={{0,8},{4,12},{8,0},{12,4},{1,9},{5,13},{9,1},{13,5},{2,10},{6,14},... | collective-permute-start | bytes 786440 | tf_op jit(solution)/shard_map/ppermute | solution.py:201
  39.8 1.8 %copy-start.1 = (bf16[512,3584]{1,0:T(8,128)(2,1)}, bf16[512,3584]{1,0:T(8,128)(2,1)S(1)}, u32[]{:S(2)}) copy-start(bf16[512,3584]{1,0:T(8,128)(2,1)S(1)} %target.1.part_ref) | copy-start | bytes 11010052
  42.4 16.3 %collective-permute-start.12 = (bf16[2,256,512]{2,1,0:T(8,128)(2,1)}, bf16[2,256,512]{2,1,0:T(8,128)(2,1)S(1)}, u32[]{:S(2)}, u32[]{:S(2)}) collective-permute-start(bf16[2,256,512]{2,1,0:T(8,128)(2,1)} %pad_maximum_fusion), channel_id=1, source_target_pairs={{0,4},{4,0},{8,12},{12,8},{1,5},{5,1},{9,13},{13,9},{2,6},{6,2},{1... | collective-permute-start | bytes 1572872 | tf_op jit(solution)/shard_map/ppermute | solution.py:201
  44.2 2.0 %copy-start.2 = (bf16[512,3584]{1,0:T(8,128)(2,1)S(1)}, bf16[512,3584]{1,0:T(8,128)(2,1)}, u32[]{:S(2)}) copy-start(bf16[512,3584]{1,0:T(8,128)(2,1)} %copy-done.1) | copy-start | bytes 11010052
  54.3 12.9 %collective-permute-start.6 = (bf16[256,512]{1,0:T(8,128)(2,1)S(1)}, bf16[256,512]{1,0:T(8,128)(2,1)S(1)}, u32[]{:S(2)}, u32[]{:S(2)}) collective-permute-start(bf16[256,512]{1,0:T(8,128)(2,1)S(1)} %get-tuple-element.19), channel_id=1, source_target_pairs={{0,4},{4,0},{8,12},{12,8},{1,5},{5,1},{9,13},{13,9},{2,6},{6,2},{1... | collective-permute-start | bytes 786440 | tf_op jit(solution)/shard_map/ppermute | solution.py:201
  54.5 21.7 %collective-permute-start.7 = (bf16[256,512]{1,0:T(8,128)(2,1)}, bf16[256,512]{1,0:T(8,128)(2,1)}, u32[]{:S(2)}, u32[]{:S(2)}) collective-permute-start(bf16[256,512]{1,0:T(8,128)(2,1)} %get-tuple-element.20), channel_id=1, source_target_pairs={{0,8},{4,12},{8,0},{12,4},{1,9},{5,13},{9,1},{13,5},{2,10},{6,14},... | collective-permute-start | bytes 786440 | tf_op jit(solution)/shard_map/ppermute | solution.py:201
  56.0 20.2 %collective-permute-start.8 = (bf16[256,512]{1,0:T(8,128)(2,1)}, bf16[256,512]{1,0:T(8,128)(2,1)}, u32[]{:S(2)}, u32[]{:S(2)}) collective-permute-start(bf16[256,512]{1,0:T(8,128)(2,1)} %get-tuple-element.21), channel_id=1, source_target_pairs={{0,12},{4,8},{8,4},{12,0},{1,13},{5,9},{9,5},{13,1},{2,14},{6,10},... | collective-permute-start | bytes 786440 | tf_op jit(solution)/shard_map/ppermute | solution.py:201
  60.9 19.7 %collective-permute-start.15 = (bf16[16,3584]{1,0:T(8,128)(2,1)S(1)}, bf16[16,3584]{1,0:T(8,128)(2,1)S(1)}, u32[]{:S(2)}, u32[]{:S(2)}) collective-permute-start(bf16[16,3584]{1,0:T(8,128)(2,1)S(1)} %get-tuple-element.30), channel_id=1, source_target_pairs={{0,3},{1,2},{2,1},{3,0},{4,7},{5,6},{6,5},{7,4},{8,11},{9,10},{10,... | collective-permute-start | bytes 344072 | tf_op jit(solution)/shard_map/ppermute | solution.py:201
  61.0 19.6 %collective-permute-start.14 = (bf16[16,3584]{1,0:T(8,128)(2,1)S(1)}, bf16[16,3584]{1,0:T(8,128)(2,1)S(1)}, u32[]{:S(2)}, u32[]{:S(2)}) collective-permute-start(bf16[16,3584]{1,0:T(8,128)(2,1)S(1)} %get-tuple-element.31), channel_id=1, source_target_pairs={{0,2},{1,3},{2,0},{3,1},{4,6},{5,7},{6,4},{7,5},{8,10},{9,11},{10,... | collective-permute-start | bytes 344072 | tf_op jit(solution)/shard_map/ppermute | solution.py:201
  67.9 12.7 %collective-permute-start.13 = (bf16[16,3584]{1,0:T(8,128)(2,1)S(1)}, bf16[16,3584]{1,0:T(8,128)(2,1)S(1)}, u32[]{:S(2)}, u32[]{:S(2)}) collective-permute-start(bf16[16,3584]{1,0:T(8,128)(2,1)S(1)} %get-tuple-element.32), channel_id=1, source_target_pairs={{0,1},{1,0},{2,3},{3,2},{4,5},{5,4},{6,7},{7,6},{8,9},{9,8},{10,11... | collective-permute-start | bytes 344072 | tf_op jit(solution)/shard_map/ppermute | solution.py:201
  80.7 14.0 %collective-permute-start.18 = (bf16[16,3584]{1,0:T(8,128)(2,1)S(1)}, bf16[16,3584]{1,0:T(8,128)(2,1)S(1)}, u32[]{:S(2)}, u32[]{:S(2)}) collective-permute-start(bf16[16,3584]{1,0:T(8,128)(2,1)S(1)} %get-tuple-element.27), channel_id=1, source_target_pairs={{0,12},{4,8},{8,4},{12,0},{1,13},{5,9},{9,5},{13,1},{2,14},{6,10},... | collective-permute-start | bytes 344072 | tf_op jit(solution)/shard_map/ppermute | solution.py:201
  83.7 11.0 %collective-permute-start.17 = (bf16[16,3584]{1,0:T(8,128)(2,1)S(1)}, bf16[16,3584]{1,0:T(8,128)(2,1)S(1)}, u32[]{:S(2)}, u32[]{:S(2)}) collective-permute-start(bf16[16,3584]{1,0:T(8,128)(2,1)S(1)} %get-tuple-element.28), channel_id=1, source_target_pairs={{0,8},{4,12},{8,0},{12,4},{1,9},{5,13},{9,1},{13,5},{2,10},{6,14},... | collective-permute-start | bytes 344072 | tf_op jit(solution)/shard_map/ppermute | solution.py:201
  87.1 7.7 %collective-permute-start.16 = (bf16[16,3584]{1,0:T(8,128)(2,1)S(1)}, bf16[16,3584]{1,0:T(8,128)(2,1)S(1)}, u32[]{:S(2)}, u32[]{:S(2)}) collective-permute-start(bf16[16,3584]{1,0:T(8,128)(2,1)S(1)} %get-tuple-element.26), channel_id=1, source_target_pairs={{0,4},{4,0},{8,12},{12,8},{1,5},{5,1},{9,13},{13,9},{2,6},{6,2},{1... | collective-permute-start | bytes 344072 | tf_op jit(solution)/shard_map/ppermute | solution.py:201
  88.1 1.2 %collective-permute-start.9 = (bf16[16,512]{1,0:T(8,128)(2,1)S(1)}, bf16[16,512]{1,0:T(8,128)(2,1)S(1)}, u32[]{:S(2)}, u32[]{:S(2)}) collective-permute-start(bf16[16,512]{1,0:T(8,128)(2,1)S(1)} %get-tuple-element.37), channel_id=1, source_target_pairs={{0,1},{1,0},{2,3},{3,2},{4,5},{5,4},{6,7},{7,6},{8,9},{9,8},{10,11... | collective-permute-start | bytes 49160 | tf_op jit(solution)/shard_map/ppermute | solution.py:201
  88.1 3.7 %collective-permute-start.10 = (bf16[16,512]{1,0:T(8,128)(2,1)S(1)}, bf16[16,512]{1,0:T(8,128)(2,1)S(1)}, u32[]{:S(2)}, u32[]{:S(2)}) collective-permute-start(bf16[16,512]{1,0:T(8,128)(2,1)S(1)} %get-tuple-element.36), channel_id=1, source_target_pairs={{0,2},{1,3},{2,0},{3,1},{4,6},{5,7},{6,4},{7,5},{8,10},{9,11},{10,... | collective-permute-start | bytes 49160 | tf_op jit(solution)/shard_map/ppermute | solution.py:201
  89.3 3.2 %copy-start.12 = (bf16[16,512]{1,0:T(8,128)(2,1)}, bf16[16,512]{1,0:T(8,128)(2,1)S(1)}, u32[]{:S(2)}) copy-start(bf16[16,512]{1,0:T(8,128)(2,1)S(1)} %collective-permute-done.9.refs_1_) | copy-start | bytes 49156
  89.3 3.2 %collective-permute-start.11 = (bf16[16,512]{1,0:T(8,128)(2,1)S(1)}, bf16[16,512]{1,0:T(8,128)(2,1)S(1)}, u32[]{:S(2)}, u32[]{:S(2)}) collective-permute-start(bf16[16,512]{1,0:T(8,128)(2,1)S(1)} %get-tuple-element.35), channel_id=1, source_target_pairs={{0,3},{1,2},{2,1},{3,0},{4,7},{5,6},{6,5},{7,4},{8,11},{9,10},{10,... | collective-permute-start | bytes 49160 | tf_op jit(solution)/shard_map/ppermute | solution.py:201
  (10 other events, 8.2 us)

commit v12 on v11

--- a/solution.py
+++ b/solution.py
@@ -19,7 +19,7 @@
 NT = (((1,), (1,)), ((), ()))
 TN = (((0,), (0,)), ((), ()))
 SPLIT = 4
-VMEM = 40 * 1024 * 1024
+VMEM = 20 * 1024 * 1024
 
 
 def cost(flops, nbytes):

time: 96.7 us -> 100 us (1.034)
  local copies, waits for them, and re-layouts: 16.3 us -> 21.5 us
  Pallas kernels: 22.5 us -> 21.2 us
    unnamed x30 -> x32, local copies, waits for them, and re-layouts: 10.9 us -> 16.1 us
    pallas_call x1, Pallas kernels: 11.3 us -> 9.95 us  [target(): pl.pallas_call(functools.partial(target_kernel, len(tokens)), grid=(cols...]
  transfers between devices with their start and end apart: 19 -> 19, of which waited for: 7 -> 8; matrix products, arithmetic and copies ran while one was open for 6% -> 6% of each run, Pallas kernels for 23% -> 21%
where the time goes in v12:
time: 100 us; the launch traced here: 99.9 us
  waiting for transfers between devices  27.4 us (27%)
  starting transfers between devices  25.6 us (26%)
  local copies, waits for them, and re-layouts  21.5 us (22%)
  Pallas kernels  21.2 us (21%)
  matrix products  2.24 us (2%)
  other arithmetic  1.05 us (1%)
    ppermute x17, starting transfers between devices, swap(): return lax.ppermute(x, axes, [(i, i ^ s) for i in range(n)])  21 us
    ppermute x17, waiting for transfers between devices, swap(): return lax.ppermute(x, axes, [(i, i ^ s) for i in range(n)])  18.7 us
    unnamed x32, local copies, waits for them, and re-layouts  16.1 us
    pallas_call x1, Pallas kernels, target(): pl.pallas_call(functools.partial(target_kernel, len(tokens)), grid=(cols...  9.95 us
    ppermute x2, waiting for transfers between devices, per_device(): lax.ppermute(sides[:, i], ('blk',) + plane, perm)  8.65 us
    pallas_call x1, Pallas kernels, project(): pl.pallas_call(functools.partial(project_kernel, scale, len(hidden), n_z)...  5.19 us
    ppermute x2, starting transfers between devices, per_device(): lax.ppermute(sides[:, i], ('blk',) + plane, perm)  4.56 us
    pallas_call x1, Pallas kernels, grad_left_of(): pl.pallas_call(functools.partial(grad_left_kernel, n_z, n_k), grid=(depth...  2.17 us
  transfers between devices with their start and end apart: 19, of which 8 were waited for; matrix products, arithmetic and copies ran while one was open for 6% of the time, Pallas kernels for 21%

profile of v12, /device:TPU:0, one launch (start us, length us, event | category | flops | bytes accessed | tf_op | source)
XLA Modules:
  0.0 99.9 jit_solution(14195931380388238180)
XLA Ops:
  1.2 2.6 %collective-permute-start.1 = (bf16[128,2048]{1,0:T(8,128)(2,1)}, bf16[128,2048]{1,0:T(8,128)(2,1)S(1)}, u32[]{:S(2)}, u32[]{:S(2)}) collective-permute-start(bf16[128,2048]{1,0:T(8,128)(2,1)} %refs_4_.3), channel_id=1, source_target_pairs={{0,2},{2,0},{1,3},{3,1},{4,6},{6,4},{5,7},{7,5},{8,10},{10,8},{9,1... | collective-permute-start | bytes 1572872 | tf_op jit(solution)/shard_map/ppermute | solution.py:201
  3.7 1.8 %reshape.33 = bf16[4,2,2,4,16,224]{5,4,3,2,1,0:T(8,128)(2,1)S(1)} reshape(bf16[16,14336]{1,0:T(8,128)(2,1)} %param.7) | data formatting | bytes 917504 | tf_op jit(solution)/shard_map/reshape | solution.py:249
  6.2 3.9 %collective-permute-start.3 = (bf16[4,2,4,16,224]{4,3,2,1,0:T(8,128)(2,1)S(1)}, bf16[4,2,4,16,224]{4,3,2,1,0:T(8,128)(2,1)S(1)}, u32[]{:S(2)}, u32[]{:S(2)}) collective-permute-start(bf16[4,2,4,16,224]{4,3,2,1,0:T(8,128)(2,1)S(1)} %get-tuple-element.24), channel_id=1, source_target_pairs={{0,8},{1,12},{2,0},{3,4},{4,9},{5,13},{6,1},{7,5},{8,10},{9,14},{1... | collective-permute-start | bytes 688136 | tf_op jit(solution)/shard_map/ppermute | solution.py:253
  13.4 8.7 %collective-permute-done.3.refs_5_.refs_6_.refs_7_.refs_8_ = bf16[4,2,4,16,224]{4,3,2,1,0:T(8,128)(2,1)S(1)} collective-permute-done((bf16[4,2,4,16,224]{4,3,2,1,0:T(8,128)(2,1)S(1)}, bf16[4,2,4,16,224]{4,3,2,1,0:T(8,128)(2,1)S(1)}, u32[]{:S(2)}, u32[]{:S(2)}) %collective-permute-start.3) | collective-permute-done | bytes 229408 | tf_op jit(solution)/shard_map/ppermute | solution.py:253
  23.2 1.5 %collective-permute-done.4.refs_3_.refs_7_ = bf16[128,2048]{1,0:T(8,128)(2,1)S(1)} collective-permute-done((bf16[128,2048]{1,0:T(8,128)(2,1)S(1)}, bf16[128,2048]{1,0:T(8,128)(2,1)S(1)}, u32[]{:S(2)}, u32[]{:S(2)}) %collective-permute-start.4) | collective-permute-done | bytes 524320 | tf_op jit(solution)/shard_map/ppermute | solution.py:201
  25.2 3.3 %collective-permute-start.5 = (bf16[256,512]{1,0:T(8,128)(2,1)S(1)}, bf16[256,512]{1,0:T(8,128)(2,1)S(1)}, u32[]{:S(2)}, u32[]{:S(2)}) collective-permute-start(bf16[256,512]{1,0:T(8,128)(2,1)S(1)} %get-tuple-element.34.refs_0_), channel_id=1, source_target_pairs={{0,8},{4,12},{8,0},{12,4},{1,9},{5,13},{9,1},{13,5},{2,10},{6,14},... | collective-permute-start | bytes 786440 | tf_op jit(solution)/shard_map/ppermute | solution.py:201
  28.5 5.2 %copy-done = bf16[2048,3584]{1,0:T(8,128)(2,1)S(1)} copy-done((bf16[2048,3584]{1,0:T(8,128)(2,1)S(1)}, bf16[2048,3584]{1,0:T(8,128)(2,1)}, u32[]{:S(2)}) %copy-start) | copy-done | bytes 14680088
  33.7 10.0 %target.1.part_ref = bf16[512,3584]{1,0:T(8,128)(2,1)S(1)} custom-call(bf16[128,2048]{1,0:T(8,128)(2,1)S(1)} %copy-done.1, bf16[128,2048]{1,0:T(8,128)(2,1)S(1)} %collective-permute-done.refs_1_.refs_5_, bf16[128,2048]{1,0:T(8,128)(2,1)S(1)} %collective-permute-done.1.refs_2_.refs_6_, bf16[128,2048]{1,0:T(8,128)(2,1)S(1)} %collective-permute-done.4.refs_3_.refs_7_, ...), custom_call_target="tpu_custom_call" | custom-call | flops 7516192768 | bytes 14680064 | tf_op jit(solution)/shard_map/target/pallas_call | solution.py:53
  43.6 1.8 %copy-done.2 = bf16[512,3584]{1,0:T(8,128)(2,1)} copy-done((bf16[512,3584]{1,0:T(8,128)(2,1)}, bf16[512,3584]{1,0:T(8,128)(2,1)S(1)}, u32[]{:S(2)}) %copy-start.2) | copy-done | bytes 3670040
  46.3 1.8 %collective-permute-start.12 = (bf16[2,256,512]{2,1,0:T(8,128)(2,1)}, bf16[2,256,512]{2,1,0:T(8,128)(2,1)S(1)}, u32[]{:S(2)}, u32[]{:S(2)}) collective-permute-start(bf16[2,256,512]{2,1,0:T(8,128)(2,1)} %pad_maximum_fusion), channel_id=1, source_target_pairs={{0,4},{4,0},{8,12},{12,8},{1,5},{5,1},{9,13},{13,9},{2,6},{6,2},{1... | collective-permute-start | bytes 1572872 | tf_op jit(solution)/shard_map/ppermute | solution.py:201
  48.1 2.0 %copy-done.3 = bf16[512,3584]{1,0:T(8,128)(2,1)S(1)} copy-done((bf16[512,3584]{1,0:T(8,128)(2,1)S(1)}, bf16[512,3584]{1,0:T(8,128)(2,1)}, u32[]{:S(2)}) %copy-start.3) | copy-done | bytes 3670040
  51.1 0.9 copy-done.9
  52.0 0.9 copy-done.11
  53.0 5.2 %project.1 = (bf16[512,3584]{1,0:T(8,128)(2,1)S(1)}, bf16[256,512]{1,0:T(8,128)(2,1)S(1)}, bf16[256,512]{1,0:T(8,128)(2,1)S(1)}, bf16[256,512]{1,0:T(8,128)(2,1)}, bf16[256,512]{1,0:T(8,128)(2,1)}) custom-call(s32[1]{0:T(128)} %bitcast.1.z_ref, bf16[512,3584]{1,0:T(8,128)(2,1)S(1)} %copy-done.3, bf16[256,512]{1,0:T(8,128)(2,1)S(1)} %copy-done.7, ...), custom_call_target="tpu_custom_call" | custom-call | flops 1879048192 | bytes 11010048 | tf_op jit(solution)/shard_map/project/pallas_call | solution.py:91
  58.4 4.1 %collective-permute-start.8 = (bf16[256,512]{1,0:T(8,128)(2,1)}, bf16[256,512]{1,0:T(8,128)(2,1)}, u32[]{:S(2)}, u32[]{:S(2)}) collective-permute-start(bf16[256,512]{1,0:T(8,128)(2,1)} %get-tuple-element.21), channel_id=1, source_target_pairs={{0,12},{4,8},{8,4},{12,0},{1,13},{5,9},{9,5},{13,1},{2,14},{6,10},... | collective-permute-start | bytes 786440 | tf_op jit(solution)/shard_map/ppermute | solution.py:201
  62.6 2.2 %grad_right.1 = bf16[4,16,3584]{2,1,0:T(8,128)(2,1)S(1)} custom-call(bf16[1,256,512]{2,1,0:T(8,128)(2,1)S(1)} %get-tuple-element.33.refs_0_, bf16[2,256,512]{2,1,0:T(8,128)(2,1)S(1)} %collective-permute-done.12.refs_1_.refs_3_, bf16[1,256,512]{2,1,0:T(8,128)(2,1)S(1)} %bitcast.53, bf16[2,256,512]{2,1,0:T(8,128)(2,1)S(1)} %collective-permute-done.12.refs_1_.refs_3_, ...), custom_call_target="tpu_custom_call" | custom-call | flops 939524096 | bytes 3670016 | tf_op jit(solution)/shard_map/grad_right/pallas_call | solution.py:127
  65.4 5.0 %collective-permute-done.6.refs_1_ = bf16[256,512]{1,0:T(8,128)(2,1)S(1)} collective-permute-done((bf16[256,512]{1,0:T(8,128)(2,1)S(1)}, bf16[256,512]{1,0:T(8,128)(2,1)S(1)}, u32[]{:S(2)}, u32[]{:S(2)}) %collective-permute-start.6) | collective-permute-done | bytes 262176 | tf_op jit(solution)/shard_map/ppermute | solution.py:201
  71.2 8.9 %collective-permute-done.7.refs_2_ = bf16[256,512]{1,0:T(8,128)(2,1)} collective-permute-done((bf16[256,512]{1,0:T(8,128)(2,1)}, bf16[256,512]{1,0:T(8,128)(2,1)}, u32[]{:S(2)}, u32[]{:S(2)}) %collective-permute-start.7) | collective-permute-done | bytes 262176 | tf_op jit(solution)/shard_map/ppermute | solution.py:201
  80.1 0.9 copy-done.5
  81.0 2.2 %grad_left.1 = bf16[16,2048]{1,0:T(8,128)(2,1)S(1)} custom-call(bf16[256,512]{1,0:T(8,128)(2,1)S(1)} %get-tuple-element.18.refs_0_, bf16[256,512]{1,0:T(8,128)(2,1)S(1)} %copy-done.5, bf16[256,512]{1,0:T(8,128)(2,1)} %collective-permute-done.7.refs_2_, bf16[256,512]{1,0:T(8,128)(2,1)} %collective-permute-done.8.refs_3_, bf16[128,2048]{1,0:T(8,128)(2,1)S(1)} %copy-done.1, ...), custom_call_target="tpu_custom_call" | custom-call | flops 536870912 | bytes 2097152 | tf_op jit(solution)/shard_map/grad_left/pallas_call | solution.py:160
  84.6 1.3 %collective-permute-start.18 = (bf16[16,3584]{1,0:T(8,128)(2,1)S(1)}, bf16[16,3584]{1,0:T(8,128)(2,1)S(1)}, u32[]{:S(2)}, u32[]{:S(2)}) collective-permute-start(bf16[16,3584]{1,0:T(8,128)(2,1)S(1)} %get-tuple-element.27), channel_id=1, source_target_pairs={{0,12},{4,8},{8,4},{12,0},{1,13},{5,9},{9,5},{13,1},{2,14},{6,10},... | collective-permute-start | bytes 344072 | tf_op jit(solution)/shard_map/ppermute | solution.py:201
  85.9 5.0 %collective-permute-start.17 = (bf16[16,3584]{1,0:T(8,128)(2,1)S(1)}, bf16[16,3584]{1,0:T(8,128)(2,1)S(1)}, u32[]{:S(2)}, u32[]{:S(2)}) collective-permute-start(bf16[16,3584]{1,0:T(8,128)(2,1)S(1)} %get-tuple-element.28), channel_id=1, source_target_pairs={{0,8},{4,12},{8,0},{12,4},{1,9},{5,13},{9,1},{13,5},{2,10},{6,14},... | collective-permute-start | bytes 344072 | tf_op jit(solution)/shard_map/ppermute | solution.py:201
  93.4 1.9 %collective-permute-done.10.refs_2_ = bf16[16,512]{1,0:T(8,128)(2,1)S(1)} collective-permute-done((bf16[16,512]{1,0:T(8,128)(2,1)S(1)}, bf16[16,512]{1,0:T(8,128)(2,1)S(1)}, u32[]{:S(2)}, u32[]{:S(2)}) %collective-permute-start.10) | collective-permute-done | bytes 16416 | tf_op jit(solution)/shard_map/ppermute | solution.py:201
  96.5 1.7 %place.1 = f32[16,2048]{1,0:T(8,128)} custom-call(s32[1]{0:T(128)} %bitcast.c_ref, bf16[16,512]{1,0:T(8,128)(2,1)} %get-tuple-element.38.refs_0_, bf16[16,512]{1,0:T(8,128)(2,1)} %copy-done.13, bf16[16,512]{1,0:T(8,128)(2,1)} %copy-done.14, bf16[16,512]{1,0:T(8,128)(2,1)} %copy-done.15), custom_call_target="tpu_custom_call" | custom-call | tf_op jit(solution)/shard_map/place/pallas_call | solution.py:189
  (78 shorter events, 16.2 us)
Async XLA Ops:
  0.6 9.5 %copy-start.12 = (bf16[16,8192]{1,0:T(8,128)(2,1)S(1)}, bf16[16,8192]{1,0:T(8,128)(2,1)}, u32[]{:S(2)}) copy-start(bf16[16,8192]{1,0:T(8,128)(2,1)} %param.6) | copy-start | bytes 786436
  0.6 11.6 %collective-permute-start = (bf16[128,2048]{1,0:T(8,128)(2,1)}, bf16[128,2048]{1,0:T(8,128)(2,1)S(1)}, u32[]{:S(2)}, u32[]{:S(2)}) collective-permute-start(bf16[128,2048]{1,0:T(8,128)(2,1)} %refs_4_.3), channel_id=1, source_target_pairs={{0,1},{1,0},{2,3},{3,2},{4,5},{5,4},{6,7},{7,6},{8,9},{9,8},{10,11... | collective-permute-start | bytes 1572872 | tf_op jit(solution)/shard_map/ppermute | solution.py:201
  1.2 21.6 %collective-permute-start.1 = (bf16[128,2048]{1,0:T(8,128)(2,1)}, bf16[128,2048]{1,0:T(8,128)(2,1)S(1)}, u32[]{:S(2)}, u32[]{:S(2)}) collective-permute-start(bf16[128,2048]{1,0:T(8,128)(2,1)} %refs_4_.3), channel_id=1, source_target_pairs={{0,2},{2,0},{1,3},{3,1},{4,6},{6,4},{5,7},{7,5},{8,10},{10,8},{9,1... | collective-permute-start | bytes 1572872 | tf_op jit(solution)/shard_map/ppermute | solution.py:201
  5.5 7.1 %collective-permute-start.2 = (bf16[4,2,4,16,224]{4,3,2,1,0:T(8,128)(2,1)S(1)}, bf16[4,2,4,16,224]{4,3,2,1,0:T(8,128)(2,1)S(1)}, u32[]{:S(2)}, u32[]{:S(2)}) collective-permute-start(bf16[4,2,4,16,224]{4,3,2,1,0:T(8,128)(2,1)S(1)} %get-tuple-element.25), channel_id=1, source_target_pairs={{0,0},{1,4},{2,8},{3,12},{4,1},{5,5},{6,9},{7,13},{8,2},{9,6},{10,... | collective-permute-start | bytes 688136 | tf_op jit(solution)/shard_map/ppermute | solution.py:253
  6.2 15.8 %collective-permute-start.3 = (bf16[4,2,4,16,224]{4,3,2,1,0:T(8,128)(2,1)S(1)}, bf16[4,2,4,16,224]{4,3,2,1,0:T(8,128)(2,1)S(1)}, u32[]{:S(2)}, u32[]{:S(2)}) collective-permute-start(bf16[4,2,4,16,224]{4,3,2,1,0:T(8,128)(2,1)S(1)} %get-tuple-element.24), channel_id=1, source_target_pairs={{0,8},{1,12},{2,0},{3,4},{4,9},{5,13},{6,1},{7,5},{8,10},{9,14},{1... | collective-permute-start | bytes 688136 | tf_op jit(solution)/shard_map/ppermute | solution.py:253
  22.8 1.9 %collective-permute-start.4 = (bf16[128,2048]{1,0:T(8,128)(2,1)S(1)}, bf16[128,2048]{1,0:T(8,128)(2,1)S(1)}, u32[]{:S(2)}, u32[]{:S(2)}) collective-permute-start(bf16[128,2048]{1,0:T(8,128)(2,1)S(1)} %collective-permute-done.1.refs_2_.refs_6_), channel_id=1, source_target_pairs={{0,1},{1,0},{2,3},{3,2},{4,5},{5,4},{6,7},{7,6},{8,9},{9,8},{10,11... | collective-permute-start | bytes 1572872 | tf_op jit(solution)/shard_map/ppermute | solution.py:201
  25.2 18.5 %copy-start.6 = (bf16[256,512]{1,0:T(8,128)(2,1)}, bf16[256,512]{1,0:T(8,128)(2,1)S(1)}, u32[]{:S(2)}) copy-start(bf16[256,512]{1,0:T(8,128)(2,1)S(1)} %get-tuple-element.34.refs_0_) | copy-start | bytes 786436
  25.2 20.3 %collective-permute-start.5 = (bf16[256,512]{1,0:T(8,128)(2,1)S(1)}, bf16[256,512]{1,0:T(8,128)(2,1)S(1)}, u32[]{:S(2)}, u32[]{:S(2)}) collective-permute-start(bf16[256,512]{1,0:T(8,128)(2,1)S(1)} %get-tuple-element.34.refs_0_), channel_id=1, source_target_pairs={{0,8},{4,12},{8,0},{12,4},{1,9},{5,13},{9,1},{13,5},{2,10},{6,14},... | collective-permute-start | bytes 786440 | tf_op jit(solution)/shard_map/ppermute | solution.py:201
  28.5 5.2 %copy-start = (bf16[2048,3584]{1,0:T(8,128)(2,1)S(1)}, bf16[2048,3584]{1,0:T(8,128)(2,1)}, u32[]{:S(2)}) copy-start(bf16[2048,3584]{1,0:T(8,128)(2,1)} %refs_7_.1) | copy-start | bytes 44040196
  46.3 16.3 %collective-permute-start.12 = (bf16[2,256,512]{2,1,0:T(8,128)(2,1)}, bf16[2,256,512]{2,1,0:T(8,128)(2,1)S(1)}, u32[]{:S(2)}, u32[]{:S(2)}) collective-permute-start(bf16[2,256,512]{2,1,0:T(8,128)(2,1)} %pad_maximum_fusion), channel_id=1, source_target_pairs={{0,4},{4,0},{8,12},{12,8},{1,5},{5,1},{9,13},{13,9},{2,6},{6,2},{1... | collective-permute-start | bytes 1572872 | tf_op jit(solution)/shard_map/ppermute | solution.py:201
  48.1 2.0 %copy-start.3 = (bf16[512,3584]{1,0:T(8,128)(2,1)S(1)}, bf16[512,3584]{1,0:T(8,128)(2,1)}, u32[]{:S(2)}) copy-start(bf16[512,3584]{1,0:T(8,128)(2,1)} %copy-done.2) | copy-start | bytes 11010052
  58.2 12.3 %collective-permute-start.6 = (bf16[256,512]{1,0:T(8,128)(2,1)S(1)}, bf16[256,512]{1,0:T(8,128)(2,1)S(1)}, u32[]{:S(2)}, u32[]{:S(2)}) collective-permute-start(bf16[256,512]{1,0:T(8,128)(2,1)S(1)} %get-tuple-element.19), channel_id=1, source_target_pairs={{0,4},{4,0},{8,12},{12,8},{1,5},{5,1},{9,13},{13,9},{2,6},{6,2},{1... | collective-permute-start | bytes 786440 | tf_op jit(solution)/shard_map/ppermute | solution.py:201
  58.4 21.7 %collective-permute-start.7 = (bf16[256,512]{1,0:T(8,128)(2,1)}, bf16[256,512]{1,0:T(8,128)(2,1)}, u32[]{:S(2)}, u32[]{:S(2)}) collective-permute-start(bf16[256,512]{1,0:T(8,128)(2,1)} %get-tuple-element.20), channel_id=1, source_target_pairs={{0,8},{4,12},{8,0},{12,4},{1,9},{5,13},{9,1},{13,5},{2,10},{6,14},... | collective-permute-start | bytes 786440 | tf_op jit(solution)/shard_map/ppermute | solution.py:201
  58.4 21.7 %collective-permute-start.8 = (bf16[256,512]{1,0:T(8,128)(2,1)}, bf16[256,512]{1,0:T(8,128)(2,1)}, u32[]{:S(2)}, u32[]{:S(2)}) collective-permute-start(bf16[256,512]{1,0:T(8,128)(2,1)} %get-tuple-element.21), channel_id=1, source_target_pairs={{0,12},{4,8},{8,4},{12,0},{1,13},{5,9},{9,5},{13,1},{2,14},{6,10},... | collective-permute-start | bytes 786440 | tf_op jit(solution)/shard_map/ppermute | solution.py:201
  64.8 19.7 %collective-permute-start.15 = (bf16[16,3584]{1,0:T(8,128)(2,1)S(1)}, bf16[16,3584]{1,0:T(8,128)(2,1)S(1)}, u32[]{:S(2)}, u32[]{:S(2)}) collective-permute-start(bf16[16,3584]{1,0:T(8,128)(2,1)S(1)} %get-tuple-element.30), channel_id=1, source_target_pairs={{0,3},{1,2},{2,1},{3,0},{4,7},{5,6},{6,5},{7,4},{8,11},{9,10},{10,... | collective-permute-start | bytes 344072 | tf_op jit(solution)/shard_map/ppermute | solution.py:201
  64.9 19.6 %collective-permute-start.14 = (bf16[16,3584]{1,0:T(8,128)(2,1)S(1)}, bf16[16,3584]{1,0:T(8,128)(2,1)S(1)}, u32[]{:S(2)}, u32[]{:S(2)}) collective-permute-start(bf16[16,3584]{1,0:T(8,128)(2,1)S(1)} %get-tuple-element.31), channel_id=1, source_target_pairs={{0,2},{1,3},{2,0},{3,1},{4,6},{5,7},{6,4},{7,5},{8,10},{9,11},{10,... | collective-permute-start | bytes 344072 | tf_op jit(solution)/shard_map/ppermute | solution.py:201
  71.2 13.3 %collective-permute-start.13 = (bf16[16,3584]{1,0:T(8,128)(2,1)S(1)}, bf16[16,3584]{1,0:T(8,128)(2,1)S(1)}, u32[]{:S(2)}, u32[]{:S(2)}) collective-permute-start(bf16[16,3584]{1,0:T(8,128)(2,1)S(1)} %get-tuple-element.32), channel_id=1, source_target_pairs={{0,1},{1,0},{2,3},{3,2},{4,5},{5,4},{6,7},{7,6},{8,9},{9,8},{10,11... | collective-permute-start | bytes 344072 | tf_op jit(solution)/shard_map/ppermute | solution.py:201
  84.6 13.6 %collective-permute-start.18 = (bf16[16,3584]{1,0:T(8,128)(2,1)S(1)}, bf16[16,3584]{1,0:T(8,128)(2,1)S(1)}, u32[]{:S(2)}, u32[]{:S(2)}) collective-permute-start(bf16[16,3584]{1,0:T(8,128)(2,1)S(1)} %get-tuple-element.27), channel_id=1, source_target_pairs={{0,12},{4,8},{8,4},{12,0},{1,13},{5,9},{9,5},{13,1},{2,14},{6,10},... | collective-permute-start | bytes 344072 | tf_op jit(solution)/shard_map/ppermute | solution.py:201
  85.9 12.7 %collective-permute-start.17 = (bf16[16,3584]{1,0:T(8,128)(2,1)S(1)}, bf16[16,3584]{1,0:T(8,128)(2,1)S(1)}, u32[]{:S(2)}, u32[]{:S(2)}) collective-permute-start(bf16[16,3584]{1,0:T(8,128)(2,1)S(1)} %get-tuple-element.28), channel_id=1, source_target_pairs={{0,8},{4,12},{8,0},{12,4},{1,9},{5,13},{9,1},{13,5},{2,10},{6,14},... | collective-permute-start | bytes 344072 | tf_op jit(solution)/shard_map/ppermute | solution.py:201
  90.9 7.7 %collective-permute-start.16 = (bf16[16,3584]{1,0:T(8,128)(2,1)S(1)}, bf16[16,3584]{1,0:T(8,128)(2,1)S(1)}, u32[]{:S(2)}, u32[]{:S(2)}) collective-permute-start(bf16[16,3584]{1,0:T(8,128)(2,1)S(1)} %get-tuple-element.26), channel_id=1, source_target_pairs={{0,4},{4,0},{8,12},{12,8},{1,5},{5,1},{9,13},{13,9},{2,6},{6,2},{1... | collective-permute-start | bytes 344072 | tf_op jit(solution)/shard_map/ppermute | solution.py:201
  91.5 1.2 %collective-permute-start.9 = (bf16[16,512]{1,0:T(8,128)(2,1)S(1)}, bf16[16,512]{1,0:T(8,128)(2,1)S(1)}, u32[]{:S(2)}, u32[]{:S(2)}) collective-permute-start(bf16[16,512]{1,0:T(8,128)(2,1)S(1)} %get-tuple-element.37), channel_id=1, source_target_pairs={{0,1},{1,0},{2,3},{3,2},{4,5},{5,4},{6,7},{7,6},{8,9},{9,8},{10,11... | collective-permute-start | bytes 49160 | tf_op jit(solution)/shard_map/ppermute | solution.py:201
  91.6 3.7 %collective-permute-start.10 = (bf16[16,512]{1,0:T(8,128)(2,1)S(1)}, bf16[16,512]{1,0:T(8,128)(2,1)S(1)}, u32[]{:S(2)}, u32[]{:S(2)}) collective-permute-start(bf16[16,512]{1,0:T(8,128)(2,1)S(1)} %get-tuple-element.36), channel_id=1, source_target_pairs={{0,2},{1,3},{2,0},{3,1},{4,6},{5,7},{6,4},{7,5},{8,10},{9,11},{10,... | collective-permute-start | bytes 49160 | tf_op jit(solution)/shard_map/ppermute | solution.py:201
  92.7 3.2 %copy-start.13 = (bf16[16,512]{1,0:T(8,128)(2,1)}, bf16[16,512]{1,0:T(8,128)(2,1)S(1)}, u32[]{:S(2)}) copy-start(bf16[16,512]{1,0:T(8,128)(2,1)S(1)} %collective-permute-done.9.refs_1_) | copy-start | bytes 49156
  92.7 3.2 %collective-permute-start.11 = (bf16[16,512]{1,0:T(8,128)(2,1)S(1)}, bf16[16,512]{1,0:T(8,128)(2,1)S(1)}, u32[]{:S(2)}, u32[]{:S(2)}) collective-permute-start(bf16[16,512]{1,0:T(8,128)(2,1)S(1)} %get-tuple-element.35), channel_id=1, source_target_pairs={{0,3},{1,2},{2,1},{3,0},{4,7},{5,6},{6,5},{7,4},{8,11},{9,10},{10,... | collective-permute-start | bytes 49160 | tf_op jit(solution)/shard_map/ppermute | solution.py:201
  (11 other events, 10.0 us)

commit v13 on v10

--- a/solution.py
+++ b/solution.py
@@ -265,13 +265,15 @@
     chips = [near] + [gather(x, "rep") for x in far]
     pieces = [p for chip in chips for p in chip]
     hid = [jnp.concatenate([first] + [hidden_of(chip) for chip in chips[1:]], axis=1)]
-    hidden = hid + [swap(hid[0], "blk", s) for s in (1, 2)]
+    two = swap(hid[0], "blk", 2)
+    hidden = hid + [swap(hid[0], "blk", 1), two]
     part, hidden[1:] = lax.optimization_barrier((target(pieces, teacher), hidden[1:]))
     for s in range(3, n_z):
         hidden.append(swap(hidden[s & (s - 1)], "blk", s & -s))
     hidden = [[h] for h in hidden]
     resid, back = project(jnp.reshape(z, (1,)).astype(jnp.int32), part, hid, sides, scale)
-    backs = [back] + [swap(back[s], "blk", s) for s in range(1, n_z)]
+    far_first = list(range(2, n_z)) + [1]
+    backs = [back] + [swap(back[s], "blk", s) for s in far_first]
 
     gr = grad_right_partial(hidden, resid)
     there = []
@@ -279,11 +281,9 @@
         piece = pick(gr, z ^ c ^ s)
         there.append(swap(piece, plane, s) if s else piece)
     there = jnp.stack(there, 0)
-    total = None
-    for s in range(n_z):
-        piece = pick(there, c ^ z ^ s)
-        piece = (swap(piece, "blk", s) if s else piece).astype(F32)
-        total = piece if total is None else total + piece
+    total = pick(there, c ^ z).astype(F32)
+    for s in far_first:
+        total = total + swap(pick(there, c ^ z ^ s), "blk", s).astype(F32)
     grad_right = total.reshape(n_b, n_k, FB).transpose(1, 0, 2).reshape(n_k, n_b * FB)
 
     gl = grad_left_of(backs, pieces, n_k)

time: 92.9 us -> 91.1 us (0.981)
  waiting for transfers between devices: 26.3 us -> 24.8 us
    ppermute x18, waiting for transfers between devices: 19.1 us -> 17.6 us  [swap(): return lax.ppermute(x, axes, [(i, i ^ s) for i in range(n)])]
  transfers between devices with their start and end apart: 20 -> 20, of which waited for: 7 -> 8; matrix products, arithmetic and copies ran while one was open for 11% -> 11% of each run, Pallas kernels for 24% -> 24%
where the time goes in v13:
time: 91.1 us; the launch traced here: 90.6 us
  starting transfers between devices  28.5 us (31%)
  waiting for transfers between devices  24.8 us (27%)
  Pallas kernels  21.9 us (24%)
  local copies, waits for them, and re-layouts  9.97 us (11%)
  matrix products  3.34 us (4%)
  other arithmetic  1.26 us (1%)
    ppermute x18, starting transfers between devices, swap(): return lax.ppermute(x, axes, [(i, i ^ s) for i in range(n)])  23.9 us
    ppermute x18, waiting for transfers between devices, swap(): return lax.ppermute(x, axes, [(i, i ^ s) for i in range(n)])  17.6 us
    pallas_call x1, Pallas kernels, target(): pl.pallas_call(functools.partial(target_kernel, len(tokens)), grid=(cols...  11.3 us
    ppermute x2, waiting for transfers between devices, per_device(): lax.ppermute(sides[:, i], ('blk',) + plane, perm)  7.22 us
    pallas_call x1, Pallas kernels, project(): pl.pallas_call(functools.partial(project_kernel, scale, len(hidden), n_z)...  4.6 us
    ppermute x2, starting transfers between devices, per_device(): lax.ppermute(sides[:, i], ('blk',) + plane, perm)  4.56 us
    pallas_call x1, Pallas kernels, grad_left_of(): pl.pallas_call(functools.partial(grad_left_kernel, n_z, n_k), grid=(depth...  2.16 us
    pallas_call x1, Pallas kernels, grad_right_partial(): pl.pallas_call(functools.partial(grad_right_kernel, n_z, parts), grid=(n_...  2.15 us
  transfers between devices with their start and end apart: 20, of which 8 were waited for; matrix products, arithmetic and copies ran while one was open for 11% of the time, Pallas kernels for 24%

profile of v13, /device:TPU:0, one launch (start us, length us, event | category | flops | bytes accessed | tf_op | source)
XLA Modules:
  0.0 90.6 jit_solution(8034759254929376089)
XLA Ops:
  1.2 2.6 %collective-permute-start.1 = (bf16[128,2048]{1,0:T(8,128)(2,1)}, bf16[128,2048]{1,0:T(8,128)(2,1)S(1)}, u32[]{:S(2)}, u32[]{:S(2)}) collective-permute-start(bf16[128,2048]{1,0:T(8,128)(2,1)} %refs_4_.3), channel_id=1, source_target_pairs={{0,2},{2,0},{1,3},{3,1},{4,6},{6,4},{5,7},{7,5},{8,10},{10,8},{9,1... | collective-permute-start | bytes 1572872 | tf_op jit(solution)/shard_map/ppermute | solution.py:210
  3.7 1.8 %reshape.33 = bf16[4,2,2,4,16,224]{5,4,3,2,1,0:T(8,128)(2,1)S(1)} reshape(bf16[16,14336]{1,0:T(8,128)(2,1)} %param.7) | data formatting | bytes 917504 | tf_op jit(solution)/shard_map/reshape | solution.py:258
  6.3 1.6 %collective-permute-start.2 = (bf16[4,2,4,16,224]{4,3,2,1,0:T(8,128)(2,1)}, bf16[4,2,4,16,224]{4,3,2,1,0:T(8,128)(2,1)S(1)}, u32[]{:S(2)}, u32[]{:S(2)}) collective-permute-start(bf16[4,2,4,16,224]{4,3,2,1,0:T(8,128)(2,1)} %get-tuple-element.24), channel_id=1, source_target_pairs={{0,0},{1,4},{2,8},{3,12},{4,1},{5,5},{6,9},{7,13},{8,2},{9,6},{10,... | collective-permute-start | bytes 688136 | tf_op jit(solution)/shard_map/ppermute | solution.py:262
  7.9 3.0 %collective-permute-start.3 = (bf16[4,2,4,16,224]{4,3,2,1,0:T(8,128)(2,1)}, bf16[4,2,4,16,224]{4,3,2,1,0:T(8,128)(2,1)S(1)}, u32[]{:S(2)}, u32[]{:S(2)}) collective-permute-start(bf16[4,2,4,16,224]{4,3,2,1,0:T(8,128)(2,1)} %get-tuple-element.23), channel_id=1, source_target_pairs={{0,8},{1,12},{2,0},{3,4},{4,9},{5,13},{6,1},{7,5},{8,10},{9,14},{1... | collective-permute-start | bytes 688136 | tf_op jit(solution)/shard_map/ppermute | solution.py:262
  11.0 1.3 %reshape.32 = bf16[2048,64]{1,0:T(8,128)(2,1)} reshape(bf16[16,8192]{1,0:T(8,128)(2,1)S(1)} %copy-done.3) | data formatting | bytes 524288 | tf_op jit(solution)/shard_map/reshape | solution.py:236
  12.3 1.6 %fusion = bf16[256,2048]{1,0:T(8,128)(2,1)S(1)} fusion(bf16[2048,64]{1,0:T(8,128)(2,1)} %reshape.32, s32[2048]{0:T(1024)S(1)} %get-tuple-element.38, s32[2048]{0:T(1024)S(1)} %get-tuple-element.39, s32[256]{0:T(256)S(1)} %get-tuple-element.41, s32[256]{0:T(256)S(1)} %get-tuple-element.42, pred[256]{0:T(512)(128)(4,1)S(1)} %get-tuple-element.37, ...), kind=kOutput, calls=%fused_computation.1 | convolution fusion | flops 69779456 | bytes 1333764 | tf_op jit(solution)/shard_map/dot_general | solution.py:246
  14.9 7.2 %collective-permute-done.3.refs_5_.refs_6_.refs_7_.refs_8_ = bf16[4,2,4,16,224]{4,3,2,1,0:T(8,128)(2,1)S(1)} collective-permute-done((bf16[4,2,4,16,224]{4,3,2,1,0:T(8,128)(2,1)}, bf16[4,2,4,16,224]{4,3,2,1,0:T(8,128)(2,1)S(1)}, u32[]{:S(2)}, u32[]{:S(2)}) %collective-permute-start.3) | collective-permute-done | bytes 229408 | tf_op jit(solution)/shard_map/ppermute | solution.py:262
  23.2 1.5 %collective-permute-done.4.refs_3_.refs_7_ = bf16[128,2048]{1,0:T(8,128)(2,1)S(1)} collective-permute-done((bf16[128,2048]{1,0:T(8,128)(2,1)S(1)}, bf16[128,2048]{1,0:T(8,128)(2,1)S(1)}, u32[]{:S(2)}, u32[]{:S(2)}) %collective-permute-start.4) | collective-permute-done | bytes 524320 | tf_op jit(solution)/shard_map/ppermute | solution.py:210
  25.2 2.1 %collective-permute-start.5 = (bf16[256,512]{1,0:T(8,128)(2,1)S(1)}, bf16[256,512]{1,0:T(8,128)(2,1)S(1)}, u32[]{:S(2)}, u32[]{:S(2)}) collective-permute-start(bf16[256,512]{1,0:T(8,128)(2,1)S(1)} %pad_maximum_fusion.1.refs_0_), channel_id=1, source_target_pairs={{0,4},{4,0},{8,12},{12,8},{1,5},{5,1},{9,13},{13,9},{2,6},{6,2},{1... | collective-permute-start | bytes 786440 | tf_op jit(solution)/shard_map/ppermute | solution.py:210
  27.3 3.3 %collective-permute-start.6 = (bf16[256,512]{1,0:T(8,128)(2,1)S(1)}, bf16[256,512]{1,0:T(8,128)(2,1)S(1)}, u32[]{:S(2)}, u32[]{:S(2)}) collective-permute-start(bf16[256,512]{1,0:T(8,128)(2,1)S(1)} %pad_maximum_fusion.1.refs_0_), channel_id=1, source_target_pairs={{0,8},{4,12},{8,0},{12,4},{1,9},{5,13},{9,1},{13,5},{2,10},{6,14},... | collective-permute-start | bytes 786440 | tf_op jit(solution)/shard_map/ppermute | solution.py:210
  30.6 11.3 %target.1.part_ref = bf16[512,3584]{1,0:T(8,128)(2,1)S(1)} custom-call(bf16[128,2048]{1,0:T(8,128)(2,1)S(1)} %copy-done, bf16[128,2048]{1,0:T(8,128)(2,1)S(1)} %collective-permute-done.refs_1_.refs_5_, bf16[128,2048]{1,0:T(8,128)(2,1)S(1)} %collective-permute-done.1.refs_2_.refs_6_, bf16[128,2048]{1,0:T(8,128)(2,1)S(1)} %collective-permute-done.4.refs_3_.refs_7_, ...), custom_call_target="tpu_custom_call" | custom-call | flops 7516192768 | bytes 14680064 | tf_op jit(solution)/shard_map/target/pallas_call | solution.py:53
  43.1 4.6 %project.1 = (bf16[512,3584]{1,0:T(8,128)(2,1)S(1)}, bf16[4,256,512]{2,1,0:T(8,128)(2,1)S(1)}) custom-call(s32[1]{0:T(128)} %bitcast.1.z_ref, bf16[512,3584]{1,0:T(8,128)(2,1)S(1)} %target.1.part_ref, bf16[256,512]{1,0:T(8,128)(2,1)S(1)} %pad_maximum_fusion.1.refs_0_, bf16[4,2,4,16,224]{4,3,2,1,0:T(8,128)(2,1)S(1)} %collective-permute-done.2.refs_1_.refs_2_.refs_3_.refs_4_, ...), custom_call_target="tpu_custom_call" | custom-call | flops 1879048192 | bytes 11010048 | tf_op jit(solution)/shard_map/project/pallas_call | solution.py:89
  48.6 2.7 %collective-permute-start.7 = (bf16[256,512]{1,0:T(8,128)(2,1)S(1)}, bf16[256,512]{1,0:T(8,128)(2,1)S(1)}, u32[]{:S(2)}, u32[]{:S(2)}) collective-permute-start(bf16[256,512]{1,0:T(8,128)(2,1)S(1)} %get-tuple-element.22), channel_id=1, source_target_pairs={{0,8},{4,12},{8,0},{12,4},{1,9},{5,13},{9,1},{13,5},{2,10},{6,14},... | collective-permute-start | bytes 786440 | tf_op jit(solution)/shard_map/ppermute | solution.py:210
  51.2 1.4 %collective-permute-start.8 = (bf16[256,512]{1,0:T(8,128)(2,1)}, bf16[256,512]{1,0:T(8,128)(2,1)}, u32[]{:S(2)}, u32[]{:S(2)}) collective-permute-start(bf16[256,512]{1,0:T(8,128)(2,1)} %get-tuple-element.21), channel_id=1, source_target_pairs={{0,12},{4,8},{8,4},{12,0},{1,13},{5,9},{9,5},{13,1},{2,14},{6,10},... | collective-permute-start | bytes 786440 | tf_op jit(solution)/shard_map/ppermute | solution.py:210
  52.6 2.2 %grad_right.1 = bf16[4,16,3584]{2,1,0:T(8,128)(2,1)S(1)} custom-call(bf16[256,512]{1,0:T(8,128)(2,1)S(1)} %pad_maximum_fusion.1.refs_0_, bf16[256,512]{1,0:T(8,128)(2,1)S(1)} %collective-permute-done.5.refs_1_, bf16[256,512]{1,0:T(8,128)(2,1)S(1)} %collective-permute-done.6.refs_2_, bf16[256,512]{1,0:T(8,128)(2,1)S(1)} %collective-permute-done.13.refs_3_, ...), custom_call_target="tpu_custom_call" | custom-call | flops 939524096 | bytes 3670016 | tf_op jit(solution)/shard_map/grad_right/pallas_call | solution.py:135
  55.6 1.9 %collective-permute-start.15 = (bf16[16,3584]{1,0:T(8,128)(2,1)}, bf16[16,3584]{1,0:T(8,128)(2,1)}, u32[]{:S(2)}, u32[]{:S(2)}) collective-permute-start(bf16[16,3584]{1,0:T(8,128)(2,1)} %get-tuple-element.30), channel_id=1, source_target_pairs={{0,2},{1,3},{2,0},{3,1},{4,6},{5,7},{6,4},{7,5},{8,10},{9,11},{10,... | collective-permute-start | bytes 344072 | tf_op jit(solution)/shard_map/ppermute | solution.py:210
  57.5 11.4 %collective-permute-done.7.refs_1_ = bf16[256,512]{1,0:T(8,128)(2,1)S(1)} collective-permute-done((bf16[256,512]{1,0:T(8,128)(2,1)S(1)}, bf16[256,512]{1,0:T(8,128)(2,1)S(1)}, u32[]{:S(2)}, u32[]{:S(2)}) %collective-permute-start.7) | collective-permute-done | bytes 262176 | tf_op jit(solution)/shard_map/ppermute | solution.py:210
  69.9 2.2 %grad_left.1 = bf16[16,2048]{1,0:T(8,128)(2,1)S(1)} custom-call(bf16[4,256,512]{2,1,0:T(8,128)(2,1)S(1)} %get-tuple-element.16.refs_0_, bf16[256,512]{1,0:T(8,128)(2,1)S(1)} %collective-permute-done.7.refs_1_, bf16[256,512]{1,0:T(8,128)(2,1)} %collective-permute-done.8.refs_2_, bf16[256,512]{1,0:T(8,128)(2,1)} %collective-permute-done.9.refs_3_, ...), custom_call_target="tpu_custom_call" | custom-call | flops 536870912 | bytes 2097152 | tf_op jit(solution)/shard_map/grad_left/pallas_call | solution.py:168
  73.9 1.1 %pad_maximum_fusion = bf16[4,16,3584]{2,1,0:T(8,128)(2,1)S(1)} fusion(bf16[1,16,3584]{2,1,0:T(8,128)(2,1)} %bitcast.17, bf16[1,16,3584]{2,1,0:T(8,128)(2,1)} %bitcast.15, bf16[1,16,3584]{2,1,0:T(8,128)(2,1)} %bitcast.13, bf16[1,16,3584]{2,1,0:T(8,128)(2,1)} %get-tuple-element.28), kind=kLoop, calls=%fused_computation.7 | loop fusion | flops 688128 | bytes 917504 | tf_op jit(solution)/shard_map/stack | solution.py:283
  75.1 4.9 %collective-permute-start.17 = (bf16[16,3584]{1,0:T(8,128)(2,1)S(1)}, bf16[16,3584]{1,0:T(8,128)(2,1)S(1)}, u32[]{:S(2)}, u32[]{:S(2)}) collective-permute-start(bf16[16,3584]{1,0:T(8,128)(2,1)S(1)} %get-tuple-element.25), channel_id=1, source_target_pairs={{0,8},{4,12},{8,0},{12,4},{1,9},{5,13},{9,1},{13,5},{2,10},{6,14},... | collective-permute-start | bytes 344072 | tf_op jit(solution)/shard_map/ppermute | solution.py:210
  80.0 1.6 %collective-permute-start.18 = (bf16[16,3584]{1,0:T(8,128)(2,1)S(1)}, bf16[16,3584]{1,0:T(8,128)(2,1)S(1)}, u32[]{:S(2)}, u32[]{:S(2)}) collective-permute-start(bf16[16,3584]{1,0:T(8,128)(2,1)S(1)} %get-tuple-element.27), channel_id=1, source_target_pairs={{0,12},{4,8},{8,4},{12,0},{1,13},{5,9},{9,5},{13,1},{2,14},{6,10},... | collective-permute-start | bytes 344072 | tf_op jit(solution)/shard_map/ppermute | solution.py:210
  82.3 1.6 %collective-permute-start.11 = (bf16[16,512]{1,0:T(8,128)(2,1)S(1)}, bf16[16,512]{1,0:T(8,128)(2,1)S(1)}, u32[]{:S(2)}, u32[]{:S(2)}) collective-permute-start(bf16[16,512]{1,0:T(8,128)(2,1)S(1)} %get-tuple-element.33), channel_id=1, source_target_pairs={{0,2},{1,3},{2,0},{3,1},{4,6},{5,7},{6,4},{7,5},{8,10},{9,11},{10,... | collective-permute-start | bytes 49160 | tf_op jit(solution)/shard_map/ppermute | solution.py:210
  84.8 1.2 %collective-permute-done.11.refs_2_ = bf16[16,512]{1,0:T(8,128)(2,1)S(1)} collective-permute-done((bf16[16,512]{1,0:T(8,128)(2,1)S(1)}, bf16[16,512]{1,0:T(8,128)(2,1)S(1)}, u32[]{:S(2)}, u32[]{:S(2)}) %collective-permute-start.11) | collective-permute-done | bytes 16416 | tf_op jit(solution)/shard_map/ppermute | solution.py:210
  87.6 1.7 %place.1 = f32[16,2048]{1,0:T(8,128)} custom-call(s32[1]{0:T(128)} %bitcast.c_ref, bf16[16,512]{1,0:T(8,128)(2,1)} %get-tuple-element.35.refs_0_, bf16[16,512]{1,0:T(8,128)(2,1)} %copy-done.4, bf16[16,512]{1,0:T(8,128)(2,1)} %copy-done.5, bf16[16,512]{1,0:T(8,128)(2,1)} %copy-done.6), custom_call_target="tpu_custom_call" | custom-call | tf_op jit(solution)/shard_map/place/pallas_call | solution.py:198
  (62 shorter events, 14.0 us)
Async XLA Ops:
  0.6 10.3 %copy-start.3 = (bf16[16,8192]{1,0:T(8,128)(2,1)S(1)}, bf16[16,8192]{1,0:T(8,128)(2,1)}, u32[]{:S(2)}) copy-start(bf16[16,8192]{1,0:T(8,128)(2,1)} %param.6) | copy-start | bytes 786436
  0.6 13.7 %collective-permute-start = (bf16[128,2048]{1,0:T(8,128)(2,1)}, bf16[128,2048]{1,0:T(8,128)(2,1)S(1)}, u32[]{:S(2)}, u32[]{:S(2)}) collective-permute-start(bf16[128,2048]{1,0:T(8,128)(2,1)} %refs_4_.3), channel_id=1, source_target_pairs={{0,1},{1,0},{2,3},{3,2},{4,5},{5,4},{6,7},{7,6},{8,9},{9,8},{10,11... | collective-permute-start | bytes 1572872 | tf_op jit(solution)/shard_map/ppermute | solution.py:210
  1.2 21.6 %collective-permute-start.1 = (bf16[128,2048]{1,0:T(8,128)(2,1)}, bf16[128,2048]{1,0:T(8,128)(2,1)S(1)}, u32[]{:S(2)}, u32[]{:S(2)}) collective-permute-start(bf16[128,2048]{1,0:T(8,128)(2,1)} %refs_4_.3), channel_id=1, source_target_pairs={{0,2},{2,0},{1,3},{3,1},{4,6},{6,4},{5,7},{7,5},{8,10},{10,8},{9,1... | collective-permute-start | bytes 1572872 | tf_op jit(solution)/shard_map/ppermute | solution.py:210
  6.3 8.5 %collective-permute-start.2 = (bf16[4,2,4,16,224]{4,3,2,1,0:T(8,128)(2,1)}, bf16[4,2,4,16,224]{4,3,2,1,0:T(8,128)(2,1)S(1)}, u32[]{:S(2)}, u32[]{:S(2)}) collective-permute-start(bf16[4,2,4,16,224]{4,3,2,1,0:T(8,128)(2,1)} %get-tuple-element.24), channel_id=1, source_target_pairs={{0,0},{1,4},{2,8},{3,12},{4,1},{5,5},{6,9},{7,13},{8,2},{9,6},{10,... | collective-permute-start | bytes 688136 | tf_op jit(solution)/shard_map/ppermute | solution.py:262
  7.9 14.1 %collective-permute-start.3 = (bf16[4,2,4,16,224]{4,3,2,1,0:T(8,128)(2,1)}, bf16[4,2,4,16,224]{4,3,2,1,0:T(8,128)(2,1)S(1)}, u32[]{:S(2)}, u32[]{:S(2)}) collective-permute-start(bf16[4,2,4,16,224]{4,3,2,1,0:T(8,128)(2,1)} %get-tuple-element.23), channel_id=1, source_target_pairs={{0,8},{1,12},{2,0},{3,4},{4,9},{5,13},{6,1},{7,5},{8,10},{9,14},{1... | collective-permute-start | bytes 688136 | tf_op jit(solution)/shard_map/ppermute | solution.py:262
  12.3 1.6 %copy-start = (bf16[128,2048]{1,0:T(8,128)(2,1)S(1)}, bf16[128,2048]{1,0:T(8,128)(2,1)}, u32[]{:S(2)}) copy-start(bf16[128,2048]{1,0:T(8,128)(2,1)} %refs_4_.3) | copy-start | bytes 1572868
  22.8 1.9 %collective-permute-start.4 = (bf16[128,2048]{1,0:T(8,128)(2,1)S(1)}, bf16[128,2048]{1,0:T(8,128)(2,1)S(1)}, u32[]{:S(2)}, u32[]{:S(2)}) collective-permute-start(bf16[128,2048]{1,0:T(8,128)(2,1)S(1)} %collective-permute-done.1.refs_2_.refs_6_), channel_id=1, source_target_pairs={{0,1},{1,0},{2,3},{3,2},{4,5},{5,4},{6,7},{7,6},{8,9},{9,8},{10,11... | collective-permute-start | bytes 1572872 | tf_op jit(solution)/shard_map/ppermute | solution.py:210
  25.1 18.0 %copy-start.2 = (bf16[4,2,4,16,224]{4,3,2,1,0:T(8,128)(2,1)S(1)}, bf16[4,2,4,16,224]{4,3,2,1,0:T(8,128)(2,1)}, u32[]{:S(2)}) copy-start(bf16[4,2,4,16,224]{4,3,2,1,0:T(8,128)(2,1)} %copy-done.1) | copy-start | bytes 688132
  25.2 16.7 %collective-permute-start.5 = (bf16[256,512]{1,0:T(8,128)(2,1)S(1)}, bf16[256,512]{1,0:T(8,128)(2,1)S(1)}, u32[]{:S(2)}, u32[]{:S(2)}) collective-permute-start(bf16[256,512]{1,0:T(8,128)(2,1)S(1)} %pad_maximum_fusion.1.refs_0_), channel_id=1, source_target_pairs={{0,4},{4,0},{8,12},{12,8},{1,5},{5,1},{9,13},{13,9},{2,6},{6,2},{1... | collective-permute-start | bytes 786440 | tf_op jit(solution)/shard_map/ppermute | solution.py:210
  27.3 15.5 %collective-permute-start.6 = (bf16[256,512]{1,0:T(8,128)(2,1)S(1)}, bf16[256,512]{1,0:T(8,128)(2,1)S(1)}, u32[]{:S(2)}, u32[]{:S(2)}) collective-permute-start(bf16[256,512]{1,0:T(8,128)(2,1)S(1)} %pad_maximum_fusion.1.refs_0_), channel_id=1, source_target_pairs={{0,8},{4,12},{8,0},{12,4},{1,9},{5,13},{9,1},{13,5},{2,10},{6,14},... | collective-permute-start | bytes 786440 | tf_op jit(solution)/shard_map/ppermute | solution.py:210
  42.8 9.9 %collective-permute-start.13 = (bf16[256,512]{1,0:T(8,128)(2,1)S(1)}, bf16[256,512]{1,0:T(8,128)(2,1)S(1)}, u32[]{:S(2)}, u32[]{:S(2)}) collective-permute-start(bf16[256,512]{1,0:T(8,128)(2,1)S(1)} %collective-permute-done.6.refs_2_), channel_id=1, source_target_pairs={{0,4},{4,0},{8,12},{12,8},{1,5},{5,1},{9,13},{13,9},{2,6},{6,2},{1... | collective-permute-start | bytes 786440 | tf_op jit(solution)/shard_map/ppermute | solution.py:210
  48.6 20.4 %collective-permute-start.7 = (bf16[256,512]{1,0:T(8,128)(2,1)S(1)}, bf16[256,512]{1,0:T(8,128)(2,1)S(1)}, u32[]{:S(2)}, u32[]{:S(2)}) collective-permute-start(bf16[256,512]{1,0:T(8,128)(2,1)S(1)} %get-tuple-element.22), channel_id=1, source_target_pairs={{0,8},{4,12},{8,0},{12,4},{1,9},{5,13},{9,1},{13,5},{2,10},{6,14},... | collective-permute-start | bytes 786440 | tf_op jit(solution)/shard_map/ppermute | solution.py:210
  51.2 17.7 %collective-permute-start.8 = (bf16[256,512]{1,0:T(8,128)(2,1)}, bf16[256,512]{1,0:T(8,128)(2,1)}, u32[]{:S(2)}, u32[]{:S(2)}) collective-permute-start(bf16[256,512]{1,0:T(8,128)(2,1)} %get-tuple-element.21), channel_id=1, source_target_pairs={{0,12},{4,8},{8,4},{12,0},{1,13},{5,9},{9,5},{13,1},{2,14},{6,10},... | collective-permute-start | bytes 786440 | tf_op jit(solution)/shard_map/ppermute | solution.py:210
  52.6 17.3 %collective-permute-start.9 = (bf16[256,512]{1,0:T(8,128)(2,1)}, bf16[256,512]{1,0:T(8,128)(2,1)}, u32[]{:S(2)}, u32[]{:S(2)}) collective-permute-start(bf16[256,512]{1,0:T(8,128)(2,1)} %get-tuple-element.20), channel_id=1, source_target_pairs={{0,4},{4,0},{8,12},{12,8},{1,5},{5,1},{9,13},{13,9},{2,6},{6,2},{1... | collective-permute-start | bytes 786440 | tf_op jit(solution)/shard_map/ppermute | solution.py:210
  55.6 17.8 %collective-permute-start.14 = (bf16[16,3584]{1,0:T(8,128)(2,1)}, bf16[16,3584]{1,0:T(8,128)(2,1)}, u32[]{:S(2)}, u32[]{:S(2)}) collective-permute-start(bf16[16,3584]{1,0:T(8,128)(2,1)} %get-tuple-element.31), channel_id=1, source_target_pairs={{0,1},{1,0},{2,3},{3,2},{4,5},{5,4},{6,7},{7,6},{8,9},{9,8},{10,11... | collective-permute-start | bytes 344072 | tf_op jit(solution)/shard_map/ppermute | solution.py:210
  55.6 17.8 %collective-permute-start.15 = (bf16[16,3584]{1,0:T(8,128)(2,1)}, bf16[16,3584]{1,0:T(8,128)(2,1)}, u32[]{:S(2)}, u32[]{:S(2)}) collective-permute-start(bf16[16,3584]{1,0:T(8,128)(2,1)} %get-tuple-element.30), channel_id=1, source_target_pairs={{0,2},{1,3},{2,0},{3,1},{4,6},{5,7},{6,4},{7,5},{8,10},{9,11},{10,... | collective-permute-start | bytes 344072 | tf_op jit(solution)/shard_map/ppermute | solution.py:210
  68.9 5.0 %collective-permute-start.16 = (bf16[16,3584]{1,0:T(8,128)(2,1)}, bf16[16,3584]{1,0:T(8,128)(2,1)}, u32[]{:S(2)}, u32[]{:S(2)}) collective-permute-start(bf16[16,3584]{1,0:T(8,128)(2,1)} %get-tuple-element.29), channel_id=1, source_target_pairs={{0,3},{1,2},{2,1},{3,0},{4,7},{5,6},{6,5},{7,4},{8,11},{9,10},{10,... | collective-permute-start | bytes 344072 | tf_op jit(solution)/shard_map/ppermute | solution.py:210
  75.1 14.2 %collective-permute-start.17 = (bf16[16,3584]{1,0:T(8,128)(2,1)S(1)}, bf16[16,3584]{1,0:T(8,128)(2,1)S(1)}, u32[]{:S(2)}, u32[]{:S(2)}) collective-permute-start(bf16[16,3584]{1,0:T(8,128)(2,1)S(1)} %get-tuple-element.25), channel_id=1, source_target_pairs={{0,8},{4,12},{8,0},{12,4},{1,9},{5,13},{9,1},{13,5},{2,10},{6,14},... | collective-permute-start | bytes 344072 | tf_op jit(solution)/shard_map/ppermute | solution.py:210
  80.0 9.3 %collective-permute-start.18 = (bf16[16,3584]{1,0:T(8,128)(2,1)S(1)}, bf16[16,3584]{1,0:T(8,128)(2,1)S(1)}, u32[]{:S(2)}, u32[]{:S(2)}) collective-permute-start(bf16[16,3584]{1,0:T(8,128)(2,1)S(1)} %get-tuple-element.27), channel_id=1, source_target_pairs={{0,12},{4,8},{8,4},{12,0},{1,13},{5,9},{9,5},{13,1},{2,14},{6,10},... | collective-permute-start | bytes 344072 | tf_op jit(solution)/shard_map/ppermute | solution.py:210
  81.7 7.7 %collective-permute-start.19 = (bf16[16,3584]{1,0:T(8,128)(2,1)S(1)}, bf16[16,3584]{1,0:T(8,128)(2,1)S(1)}, u32[]{:S(2)}, u32[]{:S(2)}) collective-permute-start(bf16[16,3584]{1,0:T(8,128)(2,1)S(1)} %get-tuple-element.26), channel_id=1, source_target_pairs={{0,4},{4,0},{8,12},{12,8},{1,5},{5,1},{9,13},{13,9},{2,6},{6,2},{1... | collective-permute-start | bytes 344072 | tf_op jit(solution)/shard_map/ppermute | solution.py:210
  82.3 1.6 %collective-permute-start.10 = (bf16[16,512]{1,0:T(8,128)(2,1)S(1)}, bf16[16,512]{1,0:T(8,128)(2,1)S(1)}, u32[]{:S(2)}, u32[]{:S(2)}) collective-permute-start(bf16[16,512]{1,0:T(8,128)(2,1)S(1)} %get-tuple-element.34), channel_id=1, source_target_pairs={{0,1},{1,0},{2,3},{3,2},{4,5},{5,4},{6,7},{7,6},{8,9},{9,8},{10,11... | collective-permute-start | bytes 49160 | tf_op jit(solution)/shard_map/ppermute | solution.py:210
  82.3 3.7 %collective-permute-start.11 = (bf16[16,512]{1,0:T(8,128)(2,1)S(1)}, bf16[16,512]{1,0:T(8,128)(2,1)S(1)}, u32[]{:S(2)}, u32[]{:S(2)}) collective-permute-start(bf16[16,512]{1,0:T(8,128)(2,1)S(1)} %get-tuple-element.33), channel_id=1, source_target_pairs={{0,2},{1,3},{2,0},{3,1},{4,6},{5,7},{6,4},{7,5},{8,10},{9,11},{10,... | collective-permute-start | bytes 49160 | tf_op jit(solution)/shard_map/ppermute | solution.py:210
  83.8 3.2 %copy-start.4 = (bf16[16,512]{1,0:T(8,128)(2,1)}, bf16[16,512]{1,0:T(8,128)(2,1)S(1)}, u32[]{:S(2)}) copy-start(bf16[16,512]{1,0:T(8,128)(2,1)S(1)} %collective-permute-done.10.refs_1_) | copy-start | bytes 49156
  83.8 3.2 %collective-permute-start.12 = (bf16[16,512]{1,0:T(8,128)(2,1)S(1)}, bf16[16,512]{1,0:T(8,128)(2,1)S(1)}, u32[]{:S(2)}, u32[]{:S(2)}) collective-permute-start(bf16[16,512]{1,0:T(8,128)(2,1)S(1)} %get-tuple-element.32), channel_id=1, source_target_pairs={{0,3},{1,2},{2,1},{3,0},{4,7},{5,6},{6,5},{7,4},{8,11},{9,10},{10,... | collective-permute-start | bytes 49160 | tf_op jit(solution)/shard_map/ppermute | solution.py:210
  (3 other events, 2.3 us)

commit v14 on v13

--- a/solution.py
+++ b/solution.py
@@ -265,9 +265,9 @@
     chips = [near] + [gather(x, "rep") for x in far]
     pieces = [p for chip in chips for p in chip]
     hid = [jnp.concatenate([first] + [hidden_of(chip) for chip in chips[1:]], axis=1)]
-    two = swap(hid[0], "blk", 2)
-    hidden = hid + [swap(hid[0], "blk", 1), two]
-    part, hidden[1:] = lax.optimization_barrier((target(pieces, teacher), hidden[1:]))
+    two, one = swap(hid[0], "blk", 2), swap(hid[0], "blk", 1)
+    part, two, one = lax.optimization_barrier((target(pieces, teacher), two, one))
+    hidden = hid + [one, two]
     for s in range(3, n_z):
         hidden.append(swap(hidden[s & (s - 1)], "blk", s & -s))
     hidden = [[h] for h in hidden]

time: 91.1 us -> 91 us (level)
  starting transfers between devices: 28.5 us -> 26.9 us
  waiting for transfers between devices: 24.8 us -> 26.3 us
    ppermute x18, starting transfers between devices: 23.9 us -> 22.3 us  [swap(): return lax.ppermute(x, axes, [(i, i ^ s) for i in range(n)])]
    ppermute x18, waiting for transfers between devices: 17.6 us -> 19.1 us  [swap(): return lax.ppermute(x, axes, [(i, i ^ s) for i in range(n)])]
  transfers between devices with their start and end apart: 20 -> 20, of which waited for: 8 -> 9; matrix products, arithmetic and copies ran while one was open for 11% -> 11% of each run, Pallas kernels for 24% -> 24%
where the time goes in v14:
time: 91 us; the launch traced here: 90.5 us
  starting transfers between devices  26.9 us (30%)
  waiting for transfers between devices  26.3 us (29%)
  Pallas kernels  21.9 us (24%)
  local copies, waits for them, and re-layouts  9.97 us (11%)
  matrix products  3.34 us (4%)
  other arithmetic  1.25 us (1%)
    ppermute x18, starting transfers between devices, swap(): return lax.ppermute(x, axes, [(i, i ^ s) for i in range(n)])  22.3 us
    ppermute x18, waiting for transfers between devices, swap(): return lax.ppermute(x, axes, [(i, i ^ s) for i in range(n)])  19.1 us
    pallas_call x1, Pallas kernels, target(): pl.pallas_call(functools.partial(target_kernel, len(tokens)), grid=(cols...  11.3 us
    ppermute x2, waiting for transfers between devices, per_device(): lax.ppermute(sides[:, i], ('blk',) + plane, perm)  7.22 us
    pallas_call x1, Pallas kernels, project(): pl.pallas_call(functools.partial(project_kernel, scale, len(hidden), n_z)...  4.6 us
    ppermute x2, starting transfers between devices, per_device(): lax.ppermute(sides[:, i], ('blk',) + plane, perm)  4.56 us
    pallas_call x1, Pallas kernels, grad_left_of(): pl.pallas_call(functools.partial(grad_left_kernel, n_z, n_k), grid=(depth...  2.16 us
    pallas_call x1, Pallas kernels, grad_right_partial(): pl.pallas_call(functools.partial(grad_right_kernel, n_z, parts), grid=(n_...  2.15 us
  transfers between devices with their start and end apart: 20, of which 9 were waited for; matrix products, arithmetic and copies ran while one was open for 11% of the time, Pallas kernels for 24%

profile of v14, /device:TPU:0, one launch (start us, length us, event | category | flops | bytes accessed | tf_op | source)
XLA Modules:
  0.0 90.5 jit_solution(16648592056234908371)
XLA Ops:
  1.2 2.6 %collective-permute-start.1 = (bf16[128,2048]{1,0:T(8,128)(2,1)}, bf16[128,2048]{1,0:T(8,128)(2,1)S(1)}, u32[]{:S(2)}, u32[]{:S(2)}) collective-permute-start(bf16[128,2048]{1,0:T(8,128)(2,1)} %refs_4_.3), channel_id=1, source_target_pairs={{0,2},{2,0},{1,3},{3,1},{4,6},{6,4},{5,7},{7,5},{8,10},{10,8},{9,1... | collective-permute-start | bytes 1572872 | tf_op jit(solution)/shard_map/ppermute | solution.py:210
  3.7 1.8 %reshape.33 = bf16[4,2,2,4,16,224]{5,4,3,2,1,0:T(8,128)(2,1)S(1)} reshape(bf16[16,14336]{1,0:T(8,128)(2,1)} %param.7) | data formatting | bytes 917504 | tf_op jit(solution)/shard_map/reshape | solution.py:258
  6.3 1.6 %collective-permute-start.2 = (bf16[4,2,4,16,224]{4,3,2,1,0:T(8,128)(2,1)}, bf16[4,2,4,16,224]{4,3,2,1,0:T(8,128)(2,1)S(1)}, u32[]{:S(2)}, u32[]{:S(2)}) collective-permute-start(bf16[4,2,4,16,224]{4,3,2,1,0:T(8,128)(2,1)} %get-tuple-element.24), channel_id=1, source_target_pairs={{0,0},{1,4},{2,8},{3,12},{4,1},{5,5},{6,9},{7,13},{8,2},{9,6},{10,... | collective-permute-start | bytes 688136 | tf_op jit(solution)/shard_map/ppermute | solution.py:262
  7.9 3.0 %collective-permute-start.3 = (bf16[4,2,4,16,224]{4,3,2,1,0:T(8,128)(2,1)}, bf16[4,2,4,16,224]{4,3,2,1,0:T(8,128)(2,1)S(1)}, u32[]{:S(2)}, u32[]{:S(2)}) collective-permute-start(bf16[4,2,4,16,224]{4,3,2,1,0:T(8,128)(2,1)} %get-tuple-element.23), channel_id=1, source_target_pairs={{0,8},{1,12},{2,0},{3,4},{4,9},{5,13},{6,1},{7,5},{8,10},{9,14},{1... | collective-permute-start | bytes 688136 | tf_op jit(solution)/shard_map/ppermute | solution.py:262
  11.0 1.3 %reshape.32 = bf16[2048,64]{1,0:T(8,128)(2,1)} reshape(bf16[16,8192]{1,0:T(8,128)(2,1)S(1)} %copy-done.3) | data formatting | bytes 524288 | tf_op jit(solution)/shard_map/reshape | solution.py:236
  12.3 1.6 %fusion = bf16[256,2048]{1,0:T(8,128)(2,1)S(1)} fusion(bf16[2048,64]{1,0:T(8,128)(2,1)} %reshape.32, s32[2048]{0:T(1024)S(1)} %get-tuple-element.38, s32[2048]{0:T(1024)S(1)} %get-tuple-element.39, s32[256]{0:T(256)S(1)} %get-tuple-element.41, s32[256]{0:T(256)S(1)} %get-tuple-element.42, pred[256]{0:T(512)(128)(4,1)S(1)} %get-tuple-element.37, ...), kind=kOutput, calls=%fused_computation.1 | convolution fusion | flops 69779456 | bytes 1333764 | tf_op jit(solution)/shard_map/dot_general | solution.py:246
  14.9 7.2 %collective-permute-done.3.refs_5_.refs_6_.refs_7_.refs_8_ = bf16[4,2,4,16,224]{4,3,2,1,0:T(8,128)(2,1)S(1)} collective-permute-done((bf16[4,2,4,16,224]{4,3,2,1,0:T(8,128)(2,1)}, bf16[4,2,4,16,224]{4,3,2,1,0:T(8,128)(2,1)S(1)}, u32[]{:S(2)}, u32[]{:S(2)}) %collective-permute-start.3) | collective-permute-done | bytes 229408 | tf_op jit(solution)/shard_map/ppermute | solution.py:262
  23.2 1.5 %collective-permute-done.4.refs_3_.refs_7_ = bf16[128,2048]{1,0:T(8,128)(2,1)S(1)} collective-permute-done((bf16[128,2048]{1,0:T(8,128)(2,1)S(1)}, bf16[128,2048]{1,0:T(8,128)(2,1)S(1)}, u32[]{:S(2)}, u32[]{:S(2)}) %collective-permute-start.4) | collective-permute-done | bytes 524320 | tf_op jit(solution)/shard_map/ppermute | solution.py:210
  25.2 3.6 %collective-permute-start.5 = (bf16[256,512]{1,0:T(8,128)(2,1)S(1)}, bf16[256,512]{1,0:T(8,128)(2,1)S(1)}, u32[]{:S(2)}, u32[]{:S(2)}) collective-permute-start(bf16[256,512]{1,0:T(8,128)(2,1)S(1)} %pad_maximum_fusion.1.refs_0_), channel_id=1, source_target_pairs={{0,8},{4,12},{8,0},{12,4},{1,9},{5,13},{9,1},{13,5},{2,10},{6,14},... | collective-permute-start | bytes 786440 | tf_op jit(solution)/shard_map/ppermute | solution.py:210
  28.8 1.8 %collective-permute-start.6 = (bf16[256,512]{1,0:T(8,128)(2,1)S(1)}, bf16[256,512]{1,0:T(8,128)(2,1)S(1)}, u32[]{:S(2)}, u32[]{:S(2)}) collective-permute-start(bf16[256,512]{1,0:T(8,128)(2,1)S(1)} %pad_maximum_fusion.1.refs_0_), channel_id=1, source_target_pairs={{0,4},{4,0},{8,12},{12,8},{1,5},{5,1},{9,13},{13,9},{2,6},{6,2},{1... | collective-permute-start | bytes 786440 | tf_op jit(solution)/shard_map/ppermute | solution.py:210
  30.6 11.3 %target.1.part_ref = bf16[512,3584]{1,0:T(8,128)(2,1)S(1)} custom-call(bf16[128,2048]{1,0:T(8,128)(2,1)S(1)} %copy-done, bf16[128,2048]{1,0:T(8,128)(2,1)S(1)} %collective-permute-done.refs_1_.refs_5_, bf16[128,2048]{1,0:T(8,128)(2,1)S(1)} %collective-permute-done.1.refs_2_.refs_6_, bf16[128,2048]{1,0:T(8,128)(2,1)S(1)} %collective-permute-done.4.refs_3_.refs_7_, ...), custom_call_target="tpu_custom_call" | custom-call | flops 7516192768 | bytes 14680064 | tf_op jit(solution)/shard_map/target/pallas_call | solution.py:53
  41.9 1.1 %collective-permute-start.13 = (bf16[256,512]{1,0:T(8,128)(2,1)S(1)}, bf16[256,512]{1,0:T(8,128)(2,1)S(1)}, u32[]{:S(2)}, u32[]{:S(2)}) collective-permute-start(bf16[256,512]{1,0:T(8,128)(2,1)S(1)} %collective-permute-done.5.refs_2_), channel_id=1, source_target_pairs={{0,4},{4,0},{8,12},{12,8},{1,5},{5,1},{9,13},{13,9},{2,6},{6,2},{1... | collective-permute-start | bytes 786440 | tf_op jit(solution)/shard_map/ppermute | solution.py:210
  43.0 4.6 %project.1 = (bf16[512,3584]{1,0:T(8,128)(2,1)S(1)}, bf16[4,256,512]{2,1,0:T(8,128)(2,1)S(1)}) custom-call(s32[1]{0:T(128)} %bitcast.1.z_ref, bf16[512,3584]{1,0:T(8,128)(2,1)S(1)} %target.1.part_ref, bf16[256,512]{1,0:T(8,128)(2,1)S(1)} %pad_maximum_fusion.1.refs_0_, bf16[4,2,4,16,224]{4,3,2,1,0:T(8,128)(2,1)S(1)} %collective-permute-done.2.refs_1_.refs_2_.refs_3_.refs_4_, ...), custom_call_target="tpu_custom_call" | custom-call | flops 1879048192 | bytes 11010048 | tf_op jit(solution)/shard_map/project/pallas_call | solution.py:89
  48.4 2.3 %collective-permute-start.7 = (bf16[256,512]{1,0:T(8,128)(2,1)S(1)}, bf16[256,512]{1,0:T(8,128)(2,1)S(1)}, u32[]{:S(2)}, u32[]{:S(2)}) collective-permute-start(bf16[256,512]{1,0:T(8,128)(2,1)S(1)} %get-tuple-element.22), channel_id=1, source_target_pairs={{0,8},{4,12},{8,0},{12,4},{1,9},{5,13},{9,1},{13,5},{2,10},{6,14},... | collective-permute-start | bytes 786440 | tf_op jit(solution)/shard_map/ppermute | solution.py:210
  51.9 2.2 %grad_right.1 = bf16[4,16,3584]{2,1,0:T(8,128)(2,1)S(1)} custom-call(bf16[256,512]{1,0:T(8,128)(2,1)S(1)} %pad_maximum_fusion.1.refs_0_, bf16[256,512]{1,0:T(8,128)(2,1)S(1)} %collective-permute-done.6.refs_1_, bf16[256,512]{1,0:T(8,128)(2,1)S(1)} %collective-permute-done.5.refs_2_, bf16[256,512]{1,0:T(8,128)(2,1)S(1)} %collective-permute-done.13.refs_3_, ...), custom_call_target="tpu_custom_call" | custom-call | flops 939524096 | bytes 3670016 | tf_op jit(solution)/shard_map/grad_right/pallas_call | solution.py:135
  54.9 1.7 %collective-permute-start.15 = (bf16[16,3584]{1,0:T(8,128)(2,1)}, bf16[16,3584]{1,0:T(8,128)(2,1)}, u32[]{:S(2)}, u32[]{:S(2)}) collective-permute-start(bf16[16,3584]{1,0:T(8,128)(2,1)} %get-tuple-element.30), channel_id=1, source_target_pairs={{0,2},{1,3},{2,0},{3,1},{4,6},{5,7},{6,4},{7,5},{8,10},{9,11},{10,... | collective-permute-start | bytes 344072 | tf_op jit(solution)/shard_map/ppermute | solution.py:210
  56.6 12.4 %collective-permute-done.7.refs_1_ = bf16[256,512]{1,0:T(8,128)(2,1)S(1)} collective-permute-done((bf16[256,512]{1,0:T(8,128)(2,1)S(1)}, bf16[256,512]{1,0:T(8,128)(2,1)S(1)}, u32[]{:S(2)}, u32[]{:S(2)}) %collective-permute-start.7) | collective-permute-done | bytes 262176 | tf_op jit(solution)/shard_map/ppermute | solution.py:210
  69.9 2.2 %grad_left.1 = bf16[16,2048]{1,0:T(8,128)(2,1)S(1)} custom-call(bf16[4,256,512]{2,1,0:T(8,128)(2,1)S(1)} %get-tuple-element.16.refs_0_, bf16[256,512]{1,0:T(8,128)(2,1)S(1)} %collective-permute-done.7.refs_1_, bf16[256,512]{1,0:T(8,128)(2,1)} %collective-permute-done.8.refs_2_, bf16[256,512]{1,0:T(8,128)(2,1)} %collective-permute-done.9.refs_3_, ...), custom_call_target="tpu_custom_call" | custom-call | flops 536870912 | bytes 2097152 | tf_op jit(solution)/shard_map/grad_left/pallas_call | solution.py:168
  73.4 1.2 %collective-permute-done.16 = bf16[16,3584]{1,0:T(8,128)(2,1)} collective-permute-done((bf16[16,3584]{1,0:T(8,128)(2,1)}, bf16[16,3584]{1,0:T(8,128)(2,1)}, u32[]{:S(2)}, u32[]{:S(2)}) %collective-permute-start.16) | collective-permute-done | bytes 114720 | tf_op jit(solution)/shard_map/ppermute | solution.py:210
  74.6 1.1 %pad_maximum_fusion = bf16[4,16,3584]{2,1,0:T(8,128)(2,1)S(1)} fusion(bf16[1,16,3584]{2,1,0:T(8,128)(2,1)} %bitcast.17, bf16[1,16,3584]{2,1,0:T(8,128)(2,1)} %bitcast.15, bf16[1,16,3584]{2,1,0:T(8,128)(2,1)} %bitcast.13, bf16[1,16,3584]{2,1,0:T(8,128)(2,1)} %get-tuple-element.28), kind=kLoop, calls=%fused_computation.7 | loop fusion | flops 688128 | bytes 917504 | tf_op jit(solution)/shard_map/stack | solution.py:283
  75.7 4.5 %collective-permute-start.17 = (bf16[16,3584]{1,0:T(8,128)(2,1)S(1)}, bf16[16,3584]{1,0:T(8,128)(2,1)S(1)}, u32[]{:S(2)}, u32[]{:S(2)}) collective-permute-start(bf16[16,3584]{1,0:T(8,128)(2,1)S(1)} %get-tuple-element.25), channel_id=1, source_target_pairs={{0,8},{4,12},{8,0},{12,4},{1,9},{5,13},{9,1},{13,5},{2,10},{6,14},... | collective-permute-start | bytes 344072 | tf_op jit(solution)/shard_map/ppermute | solution.py:210
  80.2 1.4 %collective-permute-start.18 = (bf16[16,3584]{1,0:T(8,128)(2,1)S(1)}, bf16[16,3584]{1,0:T(8,128)(2,1)S(1)}, u32[]{:S(2)}, u32[]{:S(2)}) collective-permute-start(bf16[16,3584]{1,0:T(8,128)(2,1)S(1)} %get-tuple-element.27), channel_id=1, source_target_pairs={{0,12},{4,8},{8,4},{12,0},{1,13},{5,9},{9,5},{13,1},{2,14},{6,10},... | collective-permute-start | bytes 344072 | tf_op jit(solution)/shard_map/ppermute | solution.py:210
  84.1 1.9 %collective-permute-done.11.refs_2_ = bf16[16,512]{1,0:T(8,128)(2,1)S(1)} collective-permute-done((bf16[16,512]{1,0:T(8,128)(2,1)S(1)}, bf16[16,512]{1,0:T(8,128)(2,1)S(1)}, u32[]{:S(2)}, u32[]{:S(2)}) %collective-permute-start.11) | collective-permute-done | bytes 16416 | tf_op jit(solution)/shard_map/ppermute | solution.py:210
  87.2 1.7 %place.1 = f32[16,2048]{1,0:T(8,128)} custom-call(s32[1]{0:T(128)} %bitcast.c_ref, bf16[16,512]{1,0:T(8,128)(2,1)} %get-tuple-element.35.refs_0_, bf16[16,512]{1,0:T(8,128)(2,1)} %copy-done.4, bf16[16,512]{1,0:T(8,128)(2,1)} %copy-done.5, bf16[16,512]{1,0:T(8,128)(2,1)} %copy-done.6), custom_call_target="tpu_custom_call" | custom-call | tf_op jit(solution)/shard_map/place/pallas_call | solution.py:198
  (62 shorter events, 14.2 us)
Async XLA Ops:
  0.6 10.3 %copy-start.3 = (bf16[16,8192]{1,0:T(8,128)(2,1)S(1)}, bf16[16,8192]{1,0:T(8,128)(2,1)}, u32[]{:S(2)}) copy-start(bf16[16,8192]{1,0:T(8,128)(2,1)} %param.6) | copy-start | bytes 786436
  0.6 13.7 %collective-permute-start = (bf16[128,2048]{1,0:T(8,128)(2,1)}, bf16[128,2048]{1,0:T(8,128)(2,1)S(1)}, u32[]{:S(2)}, u32[]{:S(2)}) collective-permute-start(bf16[128,2048]{1,0:T(8,128)(2,1)} %refs_4_.3), channel_id=1, source_target_pairs={{0,1},{1,0},{2,3},{3,2},{4,5},{5,4},{6,7},{7,6},{8,9},{9,8},{10,11... | collective-permute-start | bytes 1572872 | tf_op jit(solution)/shard_map/ppermute | solution.py:210
  1.2 21.6 %collective-permute-start.1 = (bf16[128,2048]{1,0:T(8,128)(2,1)}, bf16[128,2048]{1,0:T(8,128)(2,1)S(1)}, u32[]{:S(2)}, u32[]{:S(2)}) collective-permute-start(bf16[128,2048]{1,0:T(8,128)(2,1)} %refs_4_.3), channel_id=1, source_target_pairs={{0,2},{2,0},{1,3},{3,1},{4,6},{6,4},{5,7},{7,5},{8,10},{10,8},{9,1... | collective-permute-start | bytes 1572872 | tf_op jit(solution)/shard_map/ppermute | solution.py:210
  6.3 8.5 %collective-permute-start.2 = (bf16[4,2,4,16,224]{4,3,2,1,0:T(8,128)(2,1)}, bf16[4,2,4,16,224]{4,3,2,1,0:T(8,128)(2,1)S(1)}, u32[]{:S(2)}, u32[]{:S(2)}) collective-permute-start(bf16[4,2,4,16,224]{4,3,2,1,0:T(8,128)(2,1)} %get-tuple-element.24), channel_id=1, source_target_pairs={{0,0},{1,4},{2,8},{3,12},{4,1},{5,5},{6,9},{7,13},{8,2},{9,6},{10,... | collective-permute-start | bytes 688136 | tf_op jit(solution)/shard_map/ppermute | solution.py:262
  7.9 14.1 %collective-permute-start.3 = (bf16[4,2,4,16,224]{4,3,2,1,0:T(8,128)(2,1)}, bf16[4,2,4,16,224]{4,3,2,1,0:T(8,128)(2,1)S(1)}, u32[]{:S(2)}, u32[]{:S(2)}) collective-permute-start(bf16[4,2,4,16,224]{4,3,2,1,0:T(8,128)(2,1)} %get-tuple-element.23), channel_id=1, source_target_pairs={{0,8},{1,12},{2,0},{3,4},{4,9},{5,13},{6,1},{7,5},{8,10},{9,14},{1... | collective-permute-start | bytes 688136 | tf_op jit(solution)/shard_map/ppermute | solution.py:262
  12.3 1.6 %copy-start = (bf16[128,2048]{1,0:T(8,128)(2,1)S(1)}, bf16[128,2048]{1,0:T(8,128)(2,1)}, u32[]{:S(2)}) copy-start(bf16[128,2048]{1,0:T(8,128)(2,1)} %refs_4_.3) | copy-start | bytes 1572868
  22.8 1.9 %collective-permute-start.4 = (bf16[128,2048]{1,0:T(8,128)(2,1)S(1)}, bf16[128,2048]{1,0:T(8,128)(2,1)S(1)}, u32[]{:S(2)}, u32[]{:S(2)}) collective-permute-start(bf16[128,2048]{1,0:T(8,128)(2,1)S(1)} %collective-permute-done.1.refs_2_.refs_6_), channel_id=1, source_target_pairs={{0,1},{1,0},{2,3},{3,2},{4,5},{5,4},{6,7},{7,6},{8,9},{9,8},{10,11... | collective-permute-start | bytes 1572872 | tf_op jit(solution)/shard_map/ppermute | solution.py:210
  25.1 17.8 %copy-start.2 = (bf16[4,2,4,16,224]{4,3,2,1,0:T(8,128)(2,1)S(1)}, bf16[4,2,4,16,224]{4,3,2,1,0:T(8,128)(2,1)}, u32[]{:S(2)}) copy-start(bf16[4,2,4,16,224]{4,3,2,1,0:T(8,128)(2,1)} %copy-done.1) | copy-start | bytes 688132
  25.2 16.7 %collective-permute-start.5 = (bf16[256,512]{1,0:T(8,128)(2,1)S(1)}, bf16[256,512]{1,0:T(8,128)(2,1)S(1)}, u32[]{:S(2)}, u32[]{:S(2)}) collective-permute-start(bf16[256,512]{1,0:T(8,128)(2,1)S(1)} %pad_maximum_fusion.1.refs_0_), channel_id=1, source_target_pairs={{0,8},{4,12},{8,0},{12,4},{1,9},{5,13},{9,1},{13,5},{2,10},{6,14},... | collective-permute-start | bytes 786440 | tf_op jit(solution)/shard_map/ppermute | solution.py:210
  28.8 13.1 %collective-permute-start.6 = (bf16[256,512]{1,0:T(8,128)(2,1)S(1)}, bf16[256,512]{1,0:T(8,128)(2,1)S(1)}, u32[]{:S(2)}, u32[]{:S(2)}) collective-permute-start(bf16[256,512]{1,0:T(8,128)(2,1)S(1)} %pad_maximum_fusion.1.refs_0_), channel_id=1, source_target_pairs={{0,4},{4,0},{8,12},{12,8},{1,5},{5,1},{9,13},{13,9},{2,6},{6,2},{1... | collective-permute-start | bytes 786440 | tf_op jit(solution)/shard_map/ppermute | solution.py:210
  41.9 10.1 %collective-permute-start.13 = (bf16[256,512]{1,0:T(8,128)(2,1)S(1)}, bf16[256,512]{1,0:T(8,128)(2,1)S(1)}, u32[]{:S(2)}, u32[]{:S(2)}) collective-permute-start(bf16[256,512]{1,0:T(8,128)(2,1)S(1)} %collective-permute-done.5.refs_2_), channel_id=1, source_target_pairs={{0,4},{4,0},{8,12},{12,8},{1,5},{5,1},{9,13},{13,9},{2,6},{6,2},{1... | collective-permute-start | bytes 786440 | tf_op jit(solution)/shard_map/ppermute | solution.py:210
  48.4 20.5 %collective-permute-start.7 = (bf16[256,512]{1,0:T(8,128)(2,1)S(1)}, bf16[256,512]{1,0:T(8,128)(2,1)S(1)}, u32[]{:S(2)}, u32[]{:S(2)}) collective-permute-start(bf16[256,512]{1,0:T(8,128)(2,1)S(1)} %get-tuple-element.22), channel_id=1, source_target_pairs={{0,8},{4,12},{8,0},{12,4},{1,9},{5,13},{9,1},{13,5},{2,10},{6,14},... | collective-permute-start | bytes 786440 | tf_op jit(solution)/shard_map/ppermute | solution.py:210
  50.8 18.2 %collective-permute-start.8 = (bf16[256,512]{1,0:T(8,128)(2,1)}, bf16[256,512]{1,0:T(8,128)(2,1)}, u32[]{:S(2)}, u32[]{:S(2)}) collective-permute-start(bf16[256,512]{1,0:T(8,128)(2,1)} %get-tuple-element.21), channel_id=1, source_target_pairs={{0,12},{4,8},{8,4},{12,0},{1,13},{5,9},{9,5},{13,1},{2,14},{6,10},... | collective-permute-start | bytes 786440 | tf_op jit(solution)/shard_map/ppermute | solution.py:210
  51.8 18.1 %collective-permute-start.9 = (bf16[256,512]{1,0:T(8,128)(2,1)}, bf16[256,512]{1,0:T(8,128)(2,1)}, u32[]{:S(2)}, u32[]{:S(2)}) collective-permute-start(bf16[256,512]{1,0:T(8,128)(2,1)} %get-tuple-element.20), channel_id=1, source_target_pairs={{0,4},{4,0},{8,12},{12,8},{1,5},{5,1},{9,13},{13,9},{2,6},{6,2},{1... | collective-permute-start | bytes 786440 | tf_op jit(solution)/shard_map/ppermute | solution.py:210
  54.9 18.5 %collective-permute-start.14 = (bf16[16,3584]{1,0:T(8,128)(2,1)}, bf16[16,3584]{1,0:T(8,128)(2,1)}, u32[]{:S(2)}, u32[]{:S(2)}) collective-permute-start(bf16[16,3584]{1,0:T(8,128)(2,1)} %get-tuple-element.31), channel_id=1, source_target_pairs={{0,1},{1,0},{2,3},{3,2},{4,5},{5,4},{6,7},{7,6},{8,9},{9,8},{10,11... | collective-permute-start | bytes 344072 | tf_op jit(solution)/shard_map/ppermute | solution.py:210
  54.9 18.5 %collective-permute-start.15 = (bf16[16,3584]{1,0:T(8,128)(2,1)}, bf16[16,3584]{1,0:T(8,128)(2,1)}, u32[]{:S(2)}, u32[]{:S(2)}) collective-permute-start(bf16[16,3584]{1,0:T(8,128)(2,1)} %get-tuple-element.30), channel_id=1, source_target_pairs={{0,2},{1,3},{2,0},{3,1},{4,6},{5,7},{6,4},{7,5},{8,10},{9,11},{10,... | collective-permute-start | bytes 344072 | tf_op jit(solution)/shard_map/ppermute | solution.py:210
  68.9 5.6 %collective-permute-start.16 = (bf16[16,3584]{1,0:T(8,128)(2,1)}, bf16[16,3584]{1,0:T(8,128)(2,1)}, u32[]{:S(2)}, u32[]{:S(2)}) collective-permute-start(bf16[16,3584]{1,0:T(8,128)(2,1)} %get-tuple-element.29), channel_id=1, source_target_pairs={{0,3},{1,2},{2,1},{3,0},{4,7},{5,6},{6,5},{7,4},{8,11},{9,10},{10,... | collective-permute-start | bytes 344072 | tf_op jit(solution)/shard_map/ppermute | solution.py:210
  75.7 13.2 %collective-permute-start.17 = (bf16[16,3584]{1,0:T(8,128)(2,1)S(1)}, bf16[16,3584]{1,0:T(8,128)(2,1)S(1)}, u32[]{:S(2)}, u32[]{:S(2)}) collective-permute-start(bf16[16,3584]{1,0:T(8,128)(2,1)S(1)} %get-tuple-element.25), channel_id=1, source_target_pairs={{0,8},{4,12},{8,0},{12,4},{1,9},{5,13},{9,1},{13,5},{2,10},{6,14},... | collective-permute-start | bytes 344072 | tf_op jit(solution)/shard_map/ppermute | solution.py:210
  80.2 8.7 %collective-permute-start.18 = (bf16[16,3584]{1,0:T(8,128)(2,1)S(1)}, bf16[16,3584]{1,0:T(8,128)(2,1)S(1)}, u32[]{:S(2)}, u32[]{:S(2)}) collective-permute-start(bf16[16,3584]{1,0:T(8,128)(2,1)S(1)} %get-tuple-element.27), channel_id=1, source_target_pairs={{0,12},{4,8},{8,4},{12,0},{1,13},{5,9},{9,5},{13,1},{2,14},{6,10},... | collective-permute-start | bytes 344072 | tf_op jit(solution)/shard_map/ppermute | solution.py:210
  81.6 7.6 %collective-permute-start.19 = (bf16[16,3584]{1,0:T(8,128)(2,1)S(1)}, bf16[16,3584]{1,0:T(8,128)(2,1)S(1)}, u32[]{:S(2)}, u32[]{:S(2)}) collective-permute-start(bf16[16,3584]{1,0:T(8,128)(2,1)S(1)} %get-tuple-element.26), channel_id=1, source_target_pairs={{0,4},{4,0},{8,12},{12,8},{1,5},{5,1},{9,13},{13,9},{2,6},{6,2},{1... | collective-permute-start | bytes 344072 | tf_op jit(solution)/shard_map/ppermute | solution.py:210
  82.3 1.2 %collective-permute-start.10 = (bf16[16,512]{1,0:T(8,128)(2,1)S(1)}, bf16[16,512]{1,0:T(8,128)(2,1)S(1)}, u32[]{:S(2)}, u32[]{:S(2)}) collective-permute-start(bf16[16,512]{1,0:T(8,128)(2,1)S(1)} %get-tuple-element.34), channel_id=1, source_target_pairs={{0,1},{1,0},{2,3},{3,2},{4,5},{5,4},{6,7},{7,6},{8,9},{9,8},{10,11... | collective-permute-start | bytes 49160 | tf_op jit(solution)/shard_map/ppermute | solution.py:210
  82.3 3.7 %collective-permute-start.11 = (bf16[16,512]{1,0:T(8,128)(2,1)S(1)}, bf16[16,512]{1,0:T(8,128)(2,1)S(1)}, u32[]{:S(2)}, u32[]{:S(2)}) collective-permute-start(bf16[16,512]{1,0:T(8,128)(2,1)S(1)} %get-tuple-element.33), channel_id=1, source_target_pairs={{0,2},{1,3},{2,0},{3,1},{4,6},{5,7},{6,4},{7,5},{8,10},{9,11},{10,... | collective-permute-start | bytes 49160 | tf_op jit(solution)/shard_map/ppermute | solution.py:210
  83.4 3.2 %copy-start.4 = (bf16[16,512]{1,0:T(8,128)(2,1)}, bf16[16,512]{1,0:T(8,128)(2,1)S(1)}, u32[]{:S(2)}) copy-start(bf16[16,512]{1,0:T(8,128)(2,1)S(1)} %collective-permute-done.10.refs_1_) | copy-start | bytes 49156
  83.4 3.2 %collective-permute-start.12 = (bf16[16,512]{1,0:T(8,128)(2,1)S(1)}, bf16[16,512]{1,0:T(8,128)(2,1)S(1)}, u32[]{:S(2)}, u32[]{:S(2)}) collective-permute-start(bf16[16,512]{1,0:T(8,128)(2,1)S(1)} %get-tuple-element.32), channel_id=1, source_target_pairs={{0,3},{1,2},{2,1},{3,0},{4,7},{5,6},{6,5},{7,4},{8,11},{9,10},{10,... | collective-permute-start | bytes 49160 | tf_op jit(solution)/shard_map/ppermute | solution.py:210
  (3 other events, 1.9 us)
